TPU v7x, 32 devices: a whole 2x2x4 slice. The times are simulated.
32 devices in a mesh: dp: 4 (over y, core), seq: 8 (over z, x).
Axes of the slice: x: 2, y: 2, z: 4, core: 2. Of those that a mesh axis runs over, the one named last changes fastest.
Arguments:
- tokens: bfloat16 [4096, 2048], P(('dp', 'seq')), may hold values from -6 to 6
- cotangent: bfloat16 [4096, 2048], P(('dp', 'seq')), may hold values from -6 to 6
- short_lengths: int32 [4, 4], P('dp'), may hold values from 1 to 256, 512 in all within a row
- w_query: bfloat16 [2048, 2048], P(('dp', 'seq')), may hold values from -0.125 to 0.125
- w_key: bfloat16 [2048, 2048], P(('dp', 'seq')), may hold values from -0.125 to 0.125
- w_value: bfloat16 [2048, 2048], P(('dp', 'seq')), may hold values from -0.125 to 0.125
- w_unit: bfloat16 [2048, 2048], P(('dp', 'seq')), may hold values from -0.125 to 0.125
- w_output: bfloat16 [2048, 2048], P(('dp', 'seq')), may hold values from -0.125 to 0.125
- w_gate: bfloat16 [2048, 5632], P(('dp', 'seq')), may hold values from -0.125 to 0.125
- w_up: bfloat16 [2048, 5632], P(('dp', 'seq')), may hold values from -0.125 to 0.125
- w_down: bfloat16 [5632, 2048], P(('dp', 'seq')), may hold values from -0.078125 to 0.078125
Outputs:
- mixed: bfloat16 [4096, 2048], P(('dp', 'seq'))
- tokens_grad: bfloat16 [4096, 2048], P(('dp', 'seq'))
- grad_query: float32 [2048, 2048], P(('dp', 'seq'))
- grad_key: float32 [2048, 2048], P(('dp', 'seq'))
- grad_value: float32 [2048, 2048], P(('dp', 'seq'))
- grad_unit: float32 [2048, 2048], P(('dp', 'seq'))
- grad_output: float32 [2048, 2048], P(('dp', 'seq'))
- grad_gate: float32 [2048, 5632], P(('dp', 'seq'))
- grad_up: float32 [2048, 5632], P(('dp', 'seq'))
- grad_down: float32 [5632, 2048], P(('dp', 'seq'))
Inputs may be any that keep to these rules, and one draw needn't show every extreme that they name: `short_lengths`: row g gives, in order, the lengths of the 4 short sequences that fill group g's 512 short rows; they sum to 512 and the largest is exactly 256.
All inputs are finite; a program needn't handle non-finite values.
Results may differ from a plain program's by a relative error of at most 0.017.
Values may be sent and summed in bfloat16 or wider, within the bound.
A program may use at most 344 MiB of HBM per device.

v0:
```python
import math

import jax
import jax.numpy as jnp
from jax import lax
from jax.sharding import PartitionSpec as P

H = 16
DH = 128
FF = 5632
LONG_DEV = 64
SHORT_DEV = 64


epsilon = 1e-06
highest = lax.Precision.HIGHEST
layer_number = 14
total_layers = 16


def carried_in(array, axis, join, neutral, backward):
    count = lax.axis_size(axis)
    place = lax.axis_index(axis)
    ahead = count - 1 - place if backward else place
    gathered = jax.tree.map(
        lambda a, kind: lax.all_gather(a.astype(kind), axis), array, (jnp.bfloat16, jnp.bfloat16)
    )
    state = jax.tree.map(lambda a, e: jnp.zeros_like(a) + jnp.asarray(e, a.dtype), array, neutral)

    def one(hop, state):
        source = count - 1 - hop if backward else hop
        return join(
            state,
            jax.tree.map(
                lambda a, own: lax.dynamic_index_in_dim(a, source, 0, False).astype(own.dtype),
                gathered,
                array,
            ),
        )

    return lax.fori_loop(0, ahead, one, state)


def normalize(values):
    return values * lax.rsqrt(jnp.mean(values * values, axis=-1, keepdims=True) + epsilon)


def norm_back(values, upstream):
    scale = lax.rsqrt(jnp.mean(values * values, axis=-1, keepdims=True) + epsilon)
    inner = jnp.mean(upstream * values, axis=-1, keepdims=True)
    return scale * upstream - values * (scale * scale * scale) * inner


def silu_slope(inputs):
    sigma = jax.nn.sigmoid(inputs)
    return sigma * (1.0 + inputs * (1.0 - sigma))


def head_rates(heads):
    order = jnp.arange(heads).astype(jnp.float32)
    factor = 1.0 - layer_number / (total_layers - 1.0) + 1e-05
    return jnp.exp(-(order + 1.0) * (8.0 / heads) * math.log(2.0)) * factor


def block_layout(lengths, block_index, long_rows, short_rows, decays):
    ends = jnp.cumsum(lengths)
    starts = ends - lengths
    places = block_index * short_rows + jnp.arange(short_rows, dtype=jnp.int32)
    segment = jnp.sum((places[:, None] >= ends[None, :]).astype(jnp.int32), axis=1)
    opening = jnp.sum((places[:, None] == starts[None, :]).astype(jnp.int32), axis=1)
    long_pos = jnp.arange(long_rows).astype(jnp.float32)
    short_pos = jnp.arange(short_rows).astype(jnp.float32)
    enter_mask = ((segment == segment[0]) & (opening[0] == 0)).astype(jnp.float32)
    leave_mask = (segment == segment[short_rows - 1]).astype(jnp.float32)
    into_long = jnp.exp(-(long_pos[:, None] + 1.0) * decays[None, :])
    into_short = jnp.exp(-(short_pos[:, None] + 1.0) * decays[None, :]) * enter_mask[:, None]
    from_long = jnp.exp(-(long_rows - 1.0 - long_pos)[:, None] * decays[None, :])
    from_short = (
        jnp.exp(-(short_rows - 1.0 - short_pos)[:, None] * decays[None, :]) * leave_mask[:, None]
    )
    unbroken = (jnp.sum(opening) == 0).astype(jnp.float32)
    carry_decay = jnp.stack(
        [jnp.exp(-long_rows * decays), jnp.exp(-short_rows * decays) * unbroken]
    )
    all_segments = jnp.concatenate([jnp.full((long_rows,), -1, jnp.int32), segment])
    all_pos = jnp.concatenate([long_pos, short_pos])
    spacing = all_pos[:, None] - all_pos[None, :]
    linked = (all_segments[:, None] == all_segments[None, :]) & (spacing >= 0.0)
    decay_matrix = jnp.where(
        linked[None], jnp.exp(-decays[:, None, None] * jnp.where(linked, spacing, 0.0)[None]), 0.0
    )
    return (into_long, into_short, from_long, from_short, carry_decay, decay_matrix)


def chain_forward(earlier, later):
    return (earlier[0] * later[0], later[0][:, :, None, None] * earlier[1] + later[1])


def chain_backward(earlier, later):
    return (later[0] * earlier[0], later[1] + later[0][:, :, None, None] * earlier[1])


def fold_rows(left, carry, pieces):
    totals, stored = carry
    totals = tuple((jnp.dot(left, piece, preferred_element_type=jnp.float32) for piece in pieces))
    return (totals, stored)


def fold_start(pieces, row_count):
    totals = tuple((jnp.zeros((row_count, piece.shape[1]), jnp.float32) for piece in pieces))
    stored = ()
    return (totals, stored)


def fold_back(grads, pieces):
    part = sum(
        (
            jnp.einsum("tf,cf->tc", grad, piece, preferred_element_type=jnp.float32)
            for grad, piece in zip(grads, pieces)
        )
    )
    return part


def outer_rows(left, right):
    return jnp.einsum("tc,tf->cf", left, right, preferred_element_type=jnp.float32)


def local(
    tokens,
    cotangent,
    short_lengths,
    w_query,
    w_key,
    w_value,
    w_unit,
    w_output,
    w_gate,
    w_up,
    w_down,
):
    row_count, model_width = tokens.shape
    long_rows = LONG_DEV
    short_rows = SHORT_DEV
    decays = head_rates(H)
    into_long, into_short, from_long, from_short, carry_decay, decay_matrix = block_layout(
        short_lengths[0], lax.axis_index("seq"), long_rows, short_rows, decays
    )
    inputs = tokens.astype(jnp.float32)
    normed_low = normalize(inputs).astype(jnp.bfloat16)
    attn_weights = (w_query, w_key, w_value, w_unit)
    projected, kept_attn = fold_rows(
        normed_low,
        fold_start(attn_weights, row_count),
        (
            lax.all_gather(w_query, ("dp", "seq"), axis=0, tiled=True),
            lax.all_gather(w_key, ("dp", "seq"), axis=0, tiled=True),
            lax.all_gather(w_value, ("dp", "seq"), axis=0, tiled=True),
            lax.all_gather(w_unit, ("dp", "seq"), axis=0, tiled=True),
        ),
    )
    z_query, z_key, z_value, z_unit = projected
    head_shape = (row_count, H, DH)
    query_low = jax.nn.silu(z_query).astype(jnp.bfloat16).reshape(head_shape)
    key_low = jax.nn.silu(z_key).astype(jnp.bfloat16).reshape(head_shape)
    value_low = z_value.astype(jnp.bfloat16).reshape(head_shape)
    scores = jnp.einsum("thd,shd->hts", query_low, key_low, preferred_element_type=jnp.float32)
    weights_low = (scores * decay_matrix).astype(jnp.bfloat16)
    local_out = jnp.einsum(
        "hts,shd->thd", weights_low, value_low, preferred_element_type=jnp.float32
    )
    key_long = (key_low[:long_rows].astype(jnp.float32) * from_long[:, :, None]).astype(
        jnp.bfloat16
    )
    key_short = (key_low[long_rows:].astype(jnp.float32) * from_short[:, :, None]).astype(
        jnp.bfloat16
    )
    increment = jnp.stack(
        [
            jnp.einsum(
                "thd,the->hde", key_long, value_low[:long_rows], preferred_element_type=jnp.float32
            ),
            jnp.einsum(
                "thd,the->hde", key_short, value_low[long_rows:], preferred_element_type=jnp.float32
            ),
        ]
    )
    identity = (jnp.ones_like(carry_decay), jnp.zeros_like(increment))
    entering = carried_in((carry_decay, increment), "seq", chain_forward, identity, False)
    state_low = entering[1].astype(jnp.bfloat16)
    carried = jnp.concatenate(
        [
            jnp.einsum(
                "thd,hde->the",
                query_low[:long_rows],
                state_low[0],
                preferred_element_type=jnp.float32,
            )
            * into_long[:, :, None],
            jnp.einsum(
                "thd,hde->the",
                query_low[long_rows:],
                state_low[1],
                preferred_element_type=jnp.float32,
            )
            * into_short[:, :, None],
        ],
        axis=0,
    )
    mixed_heads = (local_out + carried).reshape(row_count, model_width)
    normed_heads = normalize(mixed_heads)
    gated_low = (normed_heads * z_unit).astype(jnp.bfloat16)
    attn_proj, kept_out = fold_rows(
        gated_low,
        fold_start((w_output,), row_count),
        (lax.all_gather(w_output, ("dp", "seq"), axis=0, tiled=True),),
    )
    middle = inputs + attn_proj[0]
    second_low = normalize(middle).astype(jnp.bfloat16)
    mlp_proj, kept_mlp = fold_rows(
        second_low,
        fold_start((w_gate, w_up), row_count),
        (
            lax.all_gather(w_gate, ("dp", "seq"), axis=0, tiled=True),
            lax.all_gather(w_up, ("dp", "seq"), axis=0, tiled=True),
        ),
    )
    gate_val, up_val = mlp_proj
    hidden_low = (gate_val * up_val).astype(jnp.bfloat16)
    down_proj, kept_down = fold_rows(
        hidden_low,
        fold_start((w_down,), row_count),
        (lax.all_gather(w_down, ("dp", "seq"), axis=0, tiled=True),),
    )
    mixed = (middle + down_proj[0]).astype(jnp.bfloat16)
    grad_down = lax.psum_scatter(
        outer_rows(hidden_low, cotangent), ("dp", "seq"), scatter_dimension=0, tiled=True
    )
    hidden_grad = jnp.einsum(
        "td,fd->tf",
        cotangent,
        lax.all_gather(w_down, ("dp", "seq"), axis=0, tiled=True),
        preferred_element_type=jnp.float32,
    )
    gate_grad_low = (hidden_grad * up_val).astype(jnp.bfloat16)
    up_grad_low = (hidden_grad * gate_val).astype(jnp.bfloat16)
    grad_pair = lax.psum_scatter(
        outer_rows(second_low, jnp.concatenate([gate_grad_low, up_grad_low], axis=1)),
        ("dp", "seq"),
        scatter_dimension=0,
        tiled=True,
    )
    grad_gate = grad_pair[:, :FF]
    grad_up = grad_pair[:, FF:]
    second_grad = fold_back(
        (gate_grad_low, up_grad_low),
        (
            lax.all_gather(w_gate, ("dp", "seq"), axis=0, tiled=True),
            lax.all_gather(w_up, ("dp", "seq"), axis=0, tiled=True),
        ),
    )
    middle_grad = cotangent.astype(jnp.float32) + norm_back(middle, second_grad)
    middle_low = middle_grad.astype(jnp.bfloat16)
    grad_output = lax.psum_scatter(
        outer_rows(gated_low, middle_low), ("dp", "seq"), scatter_dimension=0, tiled=True
    )
    gated_grad = jnp.einsum(
        "td,cd->tc",
        middle_low,
        lax.all_gather(w_output, ("dp", "seq"), axis=0, tiled=True),
        preferred_element_type=jnp.float32,
    )
    unit_low = (gated_grad * normed_heads).astype(jnp.bfloat16)
    heads_grad = (
        norm_back(mixed_heads, gated_grad * z_unit).astype(jnp.bfloat16).reshape(head_shape)
    )
    weights_grad = jnp.einsum(
        "the,she->hts", heads_grad, value_low, preferred_element_type=jnp.float32
    )
    scores_low = (weights_grad * decay_matrix).astype(jnp.bfloat16)
    value_grad = jnp.einsum(
        "hts,the->she", weights_low, heads_grad, preferred_element_type=jnp.float32
    )
    query_grad = jnp.einsum(
        "hts,shd->thd", scores_low, key_low, preferred_element_type=jnp.float32
    ) + jnp.concatenate(
        [
            jnp.einsum(
                "the,hde->thd",
                heads_grad[:long_rows],
                state_low[0],
                preferred_element_type=jnp.float32,
            )
            * into_long[:, :, None],
            jnp.einsum(
                "the,hde->thd",
                heads_grad[long_rows:],
                state_low[1],
                preferred_element_type=jnp.float32,
            )
            * into_short[:, :, None],
        ],
        axis=0,
    )
    key_grad = jnp.einsum("hts,thd->shd", scores_low, query_low, preferred_element_type=jnp.float32)
    query_wide = query_low.astype(jnp.float32)
    grad_wide = heads_grad.astype(jnp.float32)
    local_state = jnp.stack(
        [
            jnp.einsum(
                "thd,the->hde",
                query_wide[:long_rows],
                grad_wide[:long_rows] * into_long[:, :, None],
                precision=highest,
            ),
            jnp.einsum(
                "thd,the->hde",
                query_wide[long_rows:],
                grad_wide[long_rows:] * into_short[:, :, None],
                precision=highest,
            ),
        ]
    )
    leaving = carried_in((carry_decay, local_state), "seq", chain_backward, identity, True)
    state_grad = leaving[1]
    value_wide = value_low.astype(jnp.float32)
    key_grad = key_grad + jnp.concatenate(
        [
            jnp.einsum("the,hde->thd", value_wide[:long_rows], state_grad[0], precision=highest)
            * from_long[:, :, None],
            jnp.einsum("the,hde->thd", value_wide[long_rows:], state_grad[1], precision=highest)
            * from_short[:, :, None],
        ],
        axis=0,
    )
    value_grad = value_grad + jnp.concatenate(
        [
            jnp.einsum(
                "thd,hde->the", key_long.astype(jnp.float32), state_grad[0], precision=highest
            ),
            jnp.einsum(
                "thd,hde->the", key_short.astype(jnp.float32), state_grad[1], precision=highest
            ),
        ],
        axis=0,
    )
    query_in_low = (query_grad.reshape(row_count, model_width) * silu_slope(z_query)).astype(
        jnp.bfloat16
    )
    key_in_low = (key_grad.reshape(row_count, model_width) * silu_slope(z_key)).astype(jnp.bfloat16)
    value_in_low = value_grad.reshape(row_count, model_width).astype(jnp.bfloat16)
    four_grads = jnp.concatenate([query_in_low, key_in_low, value_in_low, unit_low], axis=1)
    grad_four = lax.psum_scatter(
        outer_rows(normed_low, four_grads), ("dp", "seq"), scatter_dimension=0, tiled=True
    )
    grad_query = grad_four[:, :model_width]
    grad_key = grad_four[:, model_width : 2 * model_width]
    grad_value = grad_four[:, 2 * model_width : 3 * model_width]
    grad_unit = grad_four[:, 3 * model_width :]
    first_grad = fold_back(
        (query_in_low, key_in_low, value_in_low, unit_low),
        (
            lax.all_gather(w_query, ("dp", "seq"), axis=0, tiled=True),
            lax.all_gather(w_key, ("dp", "seq"), axis=0, tiled=True),
            lax.all_gather(w_value, ("dp", "seq"), axis=0, tiled=True),
            lax.all_gather(w_unit, ("dp", "seq"), axis=0, tiled=True),
        ),
    )
    tokens_grad = (middle_grad + norm_back(inputs, first_grad)).astype(jnp.bfloat16)
    return (
        mixed,
        tokens_grad,
        grad_query,
        grad_key,
        grad_value,
        grad_unit,
        grad_output,
        grad_gate,
        grad_up,
        grad_down,
    )


def solution(mesh):
    in_specs = (
        P(("dp", "seq"), None),
        P(("dp", "seq"), None),
        P("dp", None),
        P(("dp", "seq"), None),
        P(("dp", "seq"), None),
        P(("dp", "seq"), None),
        P(("dp", "seq"), None),
        P(("dp", "seq"), None),
        P(("dp", "seq"), None),
        P(("dp", "seq"), None),
        P(("dp", "seq"), None),
    )
    out_specs = (
        P(("dp", "seq"), None),
        P(("dp", "seq"), None),
        P(("dp", "seq"), None),
        P(("dp", "seq"), None),
        P(("dp", "seq"), None),
        P(("dp", "seq"), None),
        P(("dp", "seq"), None),
        P(("dp", "seq"), None),
        P(("dp", "seq"), None),
        P(("dp", "seq"), None),
    )
    return jax.shard_map(local, mesh=mesh, in_specs=in_specs, out_specs=out_specs, check_vma=False)
```

profile of v0, /device:TPU:0, one launch (start us, length us, event | category | flops | bytes accessed | tf_op | source)
XLA Modules:
  0.0 5865.5 jit_solution(10490122040806232496)
XLA Ops:
  15.5 75.6 %all-gather.15.cloned.1.call-done = bf16[2048,2048]{1,0:T(8,128)(2,1)} async-done(((bf16[64,2048]{1,0:T(8,128)(2,1)}), bf16[2048,2048]{1,0:T(8,128)(2,1)}) %all-gather.15.cloned.1.call-update) | async-done | bytes 8388624 | tf_op jit(solution)/shard_map/all_gather | solution.py:157
  91.1 5.9 multiply_convert_fusion.7
  97.4 72.8 %all-gather.11.cloned.1.call-done = bf16[2048,2048]{1,0:T(8,128)(2,1)} async-done(((bf16[64,2048]{1,0:T(8,128)(2,1)}), bf16[2048,2048]{1,0:T(8,128)(2,1)}) %all-gather.11.cloned.1.call-update) | async-done | bytes 8388624 | tf_op jit(solution)/shard_map/all_gather | solution.py:158
  170.2 4.7 convolution_convert_fusion
  182.2 19.5 all_gather.49
  202.3 46.8 all-gather.13.cloned.1.call-done
  249.1 5.8 multiply_convert_fusion.8
  257.3 117.9 %all-gather.17.cloned.1.call-done = bf16[8,2,16,128,128]{4,3,2,1,0:T(8,128)(2,1)} async-done(((bf16[1,2,16,128,128]{4,3,2,1,0:T(8,128)(2,1)}), bf16[8,2,16,128,128]{4,3,2,1,0:T(8,128)(2,1)}) %all-gather.17.cloned.1.call-update) | async-done | bytes 8388624 | tf_op jit(solution)/shard_map/all_gather | solution.py:26
  380.1 73.6 %all-gather.19.cloned.1.call-done = bf16[2048,2048]{1,0:T(8,128)(2,1)} async-done(((bf16[64,2048]{1,0:T(8,128)(2,1)}), bf16[2048,2048]{1,0:T(8,128)(2,1)}) %all-gather.19.cloned.1.call-update) | async-done | bytes 8388624 | tf_op jit(solution)/shard_map/all_gather | solution.py:159
  453.7 5.7 multiply_convert_fusion.6
  459.4 73.2 %all-gather.21.cloned.1.call-done = bf16[2048,2048]{1,0:T(8,128)(2,1)} async-done(((bf16[64,2048]{1,0:T(8,128)(2,1)}), bf16[2048,2048]{1,0:T(8,128)(2,1)}) %all-gather.21.cloned.1.call-update) | async-done | bytes 8388624 | tf_op jit(solution)/shard_map/all_gather | solution.py:216
  532.5 4.8 multiply_reduce_fusion.2
  538.0 140.7 %all-gather.23.cloned.1.call-done = bf16[2048,5632]{1,0:T(8,128)(2,1)} async-done(((bf16[64,5632]{1,0:T(8,128)(2,1)}), bf16[2048,5632]{1,0:T(8,128)(2,1)}) %all-gather.23.cloned.1.call-update) | async-done | bytes 23068688 | tf_op jit(solution)/shard_map/all_gather | solution.py:224
  678.7 12.3 fusion.97
  690.9 133.5 %all-gather.25.cloned.1.call-done = bf16[2048,5632]{1,0:T(8,128)(2,1)} async-done(((bf16[64,5632]{1,0:T(8,128)(2,1)}), bf16[2048,5632]{1,0:T(8,128)(2,1)}) %all-gather.25.cloned.1.call-update) | async-done | bytes 23068688 | tf_op jit(solution)/shard_map/all_gather | solution.py:225
  824.4 12.3 fusion.98
  836.7 133.4 %all-gather.27.cloned.1.call-done = bf16[5632,2048]{1,0:T(8,128)(2,1)} async-done(((bf16[176,2048]{1,0:T(8,128)(2,1)}), bf16[5632,2048]{1,0:T(8,128)(2,1)}) %all-gather.27.cloned.1.call-update) | async-done | bytes 23068688 | tf_op jit(solution)/shard_map/all_gather | solution.py:233
  970.1 14.9 multiply_convert_fusion
  985.0 12.3 fusion.99
  997.3 13.2 multiply_reduce_fusion.1
  1010.5 1.8 subtract_add_fusion
  1012.5 6.6 multiply_reduce_fusion
  1029.3 1.7 copy.186
  1033.9 2.4 multiply_convert_fusion.4
  1036.3 111.5 %all-gather.29.cloned.1.call-done = bf16[8,2,16,128,128]{4,3,2,1,0:T(8,128)(2,1)} async-done(((bf16[1,2,16,128,128]{4,3,2,1,0:T(8,128)(2,1)}), bf16[8,2,16,128,128]{4,3,2,1,0:T(8,128)(2,1)}) %all-gather.29.cloned.1.call-update) | async-done | bytes 8388624 | tf_op jit(solution)/shard_map/all_gather | solution.py:26
  1148.0 16.1 while.27
  1148.7 1.6 convert_add_fusion.5
  1150.9 1.6 convert_add_fusion.5
  1153.2 1.6 convert_add_fusion.5
  1155.5 1.6 convert_add_fusion.5
  1157.9 1.6 convert_add_fusion.5
  1164.2 2.2 fusion.36
  1166.4 2.1 fusion.39
  1177.7 23.2 fusion.5
  1202.3 33.3 fusion
  1236.9 8.2 fusion.65
  1246.6 18.2 fusion.102
  1265.9 6.5 fusion.100
  1272.4 11.8 fusion.4
  1284.3 3.9 convolution_add_fusion.4
  1288.2 4.3 convolution_add_fusion.3
  1292.5 3.0 fusion.33
  1296.8 1304.0 %reduce-scatter.5.cloned.1.call-done = f32[64,8192]{1,0:T(8,128)} async-done(((f32[2048,8192]{1,0:T(8,128)}), f32[64,8192]{1,0:T(8,128)}) %reduce-scatter.5.cloned.1.call-update) | async-done | bytes 2097168 | tf_op jit(solution)/shard_map/reduce_scatter | solution.py:353
  2600.8 2.9 fusion.95
  2603.7 1924.5 %reduce-scatter.9.cloned.1.call-done = f32[64,11264]{1,0:T(8,128)} async-done(((f32[2048,11264]{1,0:T(8,128)}), f32[64,11264]{1,0:T(8,128)}) %reduce-scatter.9.cloned.1.call-update) | async-done | bytes 2883600 | tf_op jit(solution)/shard_map/reduce_scatter | solution.py:247
  4528.2 3.6 fusion.94
  4531.8 357.3 %reduce-scatter.7.cloned.1.call-done = f32[64,2048]{1,0:T(8,128)} async-done(((f32[2048,2048]{1,0:T(8,128)}), f32[64,2048]{1,0:T(8,128)}) %reduce-scatter.7.cloned.1.call-update) | async-done | bytes 524304 | tf_op jit(solution)/shard_map/reduce_scatter | solution.py:264
  4889.1 969.4 %reduce-scatter.11.cloned.1.call-done = f32[176,2048]{1,0:T(8,128)} async-done(((f32[5632,2048]{1,0:T(8,128)}), f32[176,2048]{1,0:T(8,128)}) %reduce-scatter.11.cloned.1.call-update) | async-done | bytes 1441808 | tf_op jit(solution)/shard_map/reduce_scatter | solution.py:236
  (246 shorter events, 60.2 us)
Async XLA Ops:
  7.2 84.0 %all-gather.15.cloned.1.call-start = ((), (), s32[]{:S(2)}) async-start(), calls=%async_computation.6 | async-start | bytes 8650752 | tf_op jit(solution)/shard_map/all_gather | solution.py:157
  7.9 162.3 %all-gather.11.cloned.1.call-start = ((), (), s32[]{:S(2)}) async-start(), calls=%async_computation.4 | async-start | bytes 8650752 | tf_op jit(solution)/shard_map/all_gather | solution.py:158
  8.7 240.4 %all-gather.13.cloned.1.call-start = ((), (), s32[]{:S(2)}) async-start(), calls=%async_computation.5 | async-start | bytes 8650752 | tf_op jit(solution)/shard_map/all_gather | solution.py:156
  9.4 365.8 %all-gather.17.cloned.1.call-start = ((), (), s32[]{:S(2)}) async-start(), calls=%async_computation.7 | async-start | bytes 9437184 | tf_op jit(solution)/shard_map/all_gather | solution.py:26
  14.1 156.0 %copy-start.48 = (f32[128]{0:T(128)}, f32[128]{0:T(128)S(1)}, u32[]{:S(2)}) copy-start(f32[128]{0:T(128)S(1)} %get-tuple-element.187) | copy-start | bytes 1540
  97.0 73.1 %copy-start = (bf16[128,2048]{1,0:T(8,128)(2,1)S(1)}, bf16[128,2048]{1,0:T(8,128)(2,1)}, u32[]{:S(2)}) copy-start(bf16[128,2048]{1,0:T(8,128)(2,1)} %param.15) | copy-start | bytes 1572868
  174.9 202.5 %copy-start.24 = (bf16[128,2048]{1,0:T(8,128)(2,1)}, bf16[128,2048]{1,0:T(8,128)(2,1)S(1)}, u32[]{:S(2)}) copy-start(bf16[128,2048]{1,0:T(8,128)(2,1)S(1)} %convolution_convert_fusion) | copy-start | bytes 1572868
  176.7 5.3 copy-start.53
  177.8 71.3 %copy-start.49 = (f32[128]{0:T(128)S(1)}, f32[128]{0:T(128)}, u32[]{:S(2)}) copy-start(f32[128]{0:T(128)} %copy-done.48) | copy-start | bytes 1540
  177.8 275.8 %all-gather.19.cloned.1.call-start = ((), (), s32[]{:S(2)}) async-start(), calls=%async_computation.8 | async-start | bytes 8650752 | tf_op jit(solution)/shard_map/all_gather | solution.py:159
  178.4 354.1 %all-gather.21.cloned.1.call-start = ((), (), s32[]{:S(2)}) async-start(), calls=%async_computation.9 | async-start | bytes 8650752 | tf_op jit(solution)/shard_map/all_gather | solution.py:216
  179.0 499.7 %all-gather.23.cloned.1.call-start = ((), (), s32[]{:S(2)}) async-start(), calls=%async_computation.10 | async-start | bytes 23789568 | tf_op jit(solution)/shard_map/all_gather | solution.py:224
  179.7 644.7 %all-gather.25.cloned.1.call-start = ((), (), s32[]{:S(2)}) async-start(), calls=%async_computation.11 | async-start | bytes 23789568 | tf_op jit(solution)/shard_map/all_gather | solution.py:225
  180.5 789.6 %all-gather.27.cloned.1.call-start = ((), (), s32[]{:S(2)}) async-start(), calls=%async_computation.12 | async-start | bytes 23789568 | tf_op jit(solution)/shard_map/all_gather | solution.py:233
  181.2 966.6 %all-gather.29.cloned.1.call-start = ((), (), s32[]{:S(2)}) async-start(), calls=%async_computation.13 | async-start | bytes 9437184 | tf_op jit(solution)/shard_map/all_gather | solution.py:26
  201.7 54.3 copy-start.61
  201.9 54.1 copy-start.51
  202.3 53.8 copy-start.44
  378.9 80.5 %copy-start.9 = (f32[128,2048]{1,0:T(8,128)}, f32[128,2048]{1,0:T(8,128)S(1)}, u32[]{:S(2)}) copy-start(f32[128,2048]{1,0:T(8,128)S(1)} %copy.185) | copy-start | bytes 3145732
  380.1 79.3 %copy-start.54 = (f32[128]{0:T(128)}, f32[128]{0:T(128)S(1)}, u32[]{:S(2)}) copy-start(f32[128]{0:T(128)S(1)} %get-tuple-element.189) | copy-start | bytes 1540
  459.4 77.9 %copy-start.14 = (bf16[128,2048]{1,0:T(8,128)(2,1)}, bf16[128,2048]{1,0:T(8,128)(2,1)S(1)}, u32[]{:S(2)}) copy-start(bf16[128,2048]{1,0:T(8,128)(2,1)S(1)} %get-tuple-element.204) | copy-start | bytes 1572868
  537.3 473.2 %copy-start.1 = (f32[128,2048]{1,0:T(8,128)}, f32[128,2048]{1,0:T(8,128)S(1)}, u32[]{:S(2)}) copy-start(f32[128,2048]{1,0:T(8,128)S(1)} %get-tuple-element.207) | copy-start | bytes 3145732
  537.9 140.8 %copy-start.56 = (f32[128]{0:T(128)}, f32[128]{0:T(128)S(1)}, u32[]{:S(2)}) copy-start(f32[128]{0:T(128)S(1)} %get-tuple-element.191) | copy-start | bytes 1540
  690.9 279.2 %copy-start.16 = (bf16[128,2048]{1,0:T(8,128)(2,1)S(1)}, bf16[128,2048]{1,0:T(8,128)(2,1)}, u32[]{:S(2)}) copy-start(bf16[128,2048]{1,0:T(8,128)(2,1)} %param.16) | copy-start | bytes 1572868
  985.0 12.3 copy-start.3
  997.3 13.2 copy-start.57
  997.3 13.2 copy-start.60
  1012.3 6.8 copy-start.6
  1012.5 6.6 copy-start.55
  1012.5 6.6 copy-start.59
  1020.6 5.2 copy-start.26
  1024.5 1576.3 %reduce-scatter.5.cloned.1.call-start = ((), (), s32[]{:S(2)}) async-start(), calls=%async_computation.14 | async-start | bytes 69206016 | tf_op jit(solution)/shard_map/reduce_scatter | solution.py:353
  1164.2 4.3 copy-start.33
  1168.5 4.3 copy-start.27
  1168.5 4.3 copy-start.42
  1177.1 23.7 copy-start.22
  1200.9 3327.3 %reduce-scatter.9.cloned.1.call-start = ((), (), s32[]{:S(2)}) async-start(), calls=%async_computation.16 | async-start | bytes 95158272 | tf_op jit(solution)/shard_map/reduce_scatter | solution.py:247
  1235.6 3653.6 %reduce-scatter.7.cloned.1.call-start = ((), (), s32[]{:S(2)}) async-start(), calls=%async_computation.15 | async-start | bytes 17301504 | tf_op jit(solution)/shard_map/reduce_scatter | solution.py:264
  1245.1 4613.4 %reduce-scatter.11.cloned.1.call-start = ((), (), s32[]{:S(2)}) async-start(), calls=%async_computation.17 | async-start | bytes 47579136 | tf_op jit(solution)/shard_map/reduce_scatter | solution.py:236
  1265.9 6.5 copy-start.2
  1265.9 18.4 slice-start.4
  1265.9 22.3 slice-start.2
  1272.4 11.9 slice-start.5
  1272.4 11.9 copy-start.23
  1272.4 15.8 slice-start.3
  1284.3 8.2 slice-start
  1288.2 4.3 slice-start.1
  1288.2 4.3 copy-start.19
  (34 other events, 68.2 us)
Sparse Core Ops, SparseCore 0:
  11.0 80.1 all-gather.14
  94.1 75.9 all-gather.10
  173.1 75.8 all-gather.12
  251.6 123.5 all-gather.16
  378.0 75.5 all-gather.18
  456.5 75.9 all-gather.20
  535.4 143.1 all-gather.22
  681.6 142.7 all-gather.24
  827.3 142.7 all-gather.26
  1024.7 123.0 all-gather.28
  1201.0 1399.7 reduce-scatter.4
  2603.0 1925.1 reduce-scatter.8
  4531.1 357.9 reduce-scatter.6
  4891.9 966.6 reduce-scatter.10
where the time goes:
time: 5870 us
  waiting for transfers between devices  5540 us (94%)
  matrix products  229 us (4%)
    reduce_scatter x1, waiting for transfers between devices, local(): lax.psum_scatter(outer_rows(second_low, jnp.concatenate([gate_grad_low, u...  1920 us
    reduce_scatter x1, waiting for transfers between devices, local(): lax.psum_scatter(outer_rows(normed_low, four_grads), ('dp', 'seq'), scatt...  1300 us
    reduce_scatter x1, waiting for transfers between devices, local(): lax.psum_scatter(outer_rows(hidden_low, cotangent), ('dp', 'seq'), scatte...  969 us
    reduce_scatter x1, waiting for transfers between devices, local(): lax.psum_scatter(outer_rows(gated_low, middle_low), ('dp', 'seq'), scatte...  357 us
    all_gather x2, waiting for transfers between devices, carried_in(): lax.all_gather(a.astype(kind), axis)  229 us
    all_gather x1, waiting for transfers between devices, local(): lax.all_gather(w_gate, ('dp', 'seq'), axis=0, tiled=True)  141 us
    all_gather x1, waiting for transfers between devices, local(): lax.all_gather(w_up, ('dp', 'seq'), axis=0, tiled=True)  133 us
    all_gather x1, waiting for transfers between devices, local(): lax.all_gather(w_down, ('dp', 'seq'), axis=0, tiled=True)  133 us
  transfers between devices with their start and end apart: 14, of which 14 were waited for; matrix products, arithmetic and copies ran while one was open for 3% of the time, Pallas kernels for 0%

commit v1 on v0

v1 whole, which is shorter than its diff:
```python
import math

import jax
import jax.numpy as jnp
from jax import lax
from jax.sharding import PartitionSpec as P

H = 16
DH = 128
LONG_DEV = 64
SHORT_DEV = 64
HEADS_DEV = 2
TEAM = H // HEADS_DEV
RING = (0, 2, 4, 6, 7, 5, 3, 1)
PLACE = tuple(RING.index(i) for i in range(TEAM))

epsilon = 1e-06
layer_number = 14
total_layers = 16
low = jnp.bfloat16
wide = jnp.float32


def normalize(values):
    return values * lax.rsqrt(jnp.mean(values * values, axis=-1, keepdims=True) + epsilon)


def norm_back(values, upstream):
    scale = lax.rsqrt(jnp.mean(values * values, axis=-1, keepdims=True) + epsilon)
    inner = jnp.mean(upstream * values, axis=-1, keepdims=True)
    return scale * upstream - values * (scale * scale * scale) * inner


def dot(left, right):
    return jnp.dot(left, right, preferred_element_type=wide)


def dot_t(left, right):
    return lax.dot_general(left, right, (((1,), (1,)), ((), ())), preferred_element_type=wide)


def outer(left, right):
    return lax.dot_general(left, right, (((0,), (0,)), ((), ())), preferred_element_type=wide)


def head_rates(order):
    factor = 1.0 - layer_number / (total_layers - 1.0) + 1e-05
    return jnp.exp(-(order + 1.0) * (8.0 / H) * math.log(2.0)) * factor


class Plan:
    def __init__(self, mesh):
        self.dp = mesh.shape["dp"]
        self.seq = mesh.shape["seq"]
        self.subs = self.seq // TEAM
        self.groups = self.dp * self.subs
        teams = [[sub * TEAM + i for i in range(TEAM)] for sub in range(self.subs)]
        self.team_groups = None if self.subs == 1 else teams
        self.sub_groups = [[sub * TEAM + i for sub in range(self.subs)] for i in range(TEAM)]
        self.up = [(t[RING[i]], t[RING[(i + 1) % TEAM]]) for t in teams for i in range(TEAM)]
        self.down = [(b, a) for a, b in self.up]

    def to_next(self, x):
        return lax.ppermute(x, "seq", self.up)

    def to_previous(self, x):
        return lax.ppermute(x, "seq", self.down)

    def ring_gather(self, x):
        half = x.shape[0] // 2
        blocks = [x] + [None] * (TEAM - 1)
        forth = back = x
        for k in range(1, TEAM // 2):
            forth, back = self.to_next(forth), self.to_previous(back)
            blocks[k], blocks[TEAM - k] = forth, back
        blocks[TEAM // 2] = jnp.concatenate(
            [self.to_next(forth[:half]), self.to_previous(back[half:])], axis=0
        )
        return blocks

    def ring_reduce(self, part):
        middle = part(TEAM // 2)
        half = middle.shape[0] // 2
        back = self.to_previous(middle[:half].astype(low))
        forth = self.to_next(middle[half:].astype(low))
        for k in range(TEAM // 2 - 1, 0, -1):
            a, b = part(k), part(TEAM - k)
            if k == TEAM // 2 - 1:
                a = jnp.concatenate([a[:half] + back.astype(wide), a[half:]], axis=0)
                b = jnp.concatenate([b[:half], b[half:] + forth.astype(wide)], axis=0)
            else:
                a, b = a + back.astype(wide), b + forth.astype(wide)
            back = self.to_previous(a.astype(low))
            forth = self.to_next(b.astype(low))
        return part(0) + back.astype(wide) + forth.astype(wide)

    def across(self, x):
        if self.subs > 1:
            x = lax.all_gather(x, "seq", axis=0, tiled=True, axis_index_groups=self.sub_groups)
        return lax.all_gather(x, "dp", axis=0, tiled=True)

    def across_sum(self, x):
        rows = x.shape[0] // self.groups
        count = self.dp
        mine = lax.axis_index("dp")
        x = x.reshape((self.dp, self.subs * rows) + x.shape[1:])
        bit = 1
        while bit < count:
            pairs = x.reshape((x.shape[0] // 2, 2) + x.shape[1:])
            own = (mine // bit) % 2
            keep = lax.dynamic_index_in_dim(pairs, own, 1, False)
            send = lax.dynamic_index_in_dim(pairs, 1 - own, 1, False)
            got = lax.ppermute(send.astype(low), "dp", [(i, i ^ bit) for i in range(count)])
            x = keep.astype(wide) + got.astype(wide)
            bit *= 2
        x = x[0]
        if self.subs > 1:
            x = lax.psum_scatter(
                x, "seq", scatter_dimension=0, tiled=True, axis_index_groups=self.sub_groups
            )
        return x

    def swap(self, x):
        return lax.all_to_all(x, "seq", 0, 0, tiled=True, axis_index_groups=self.team_groups)

    def team_rows(self, x):
        count = self.groups
        spot = lax.axis_index("dp") * self.subs + lax.axis_index("seq") // TEAM
        got = []
        for i in range(count):
            pairs = [
                (count * s + (g + i) % count, g * TEAM + s) for g in range(count) for s in range(TEAM)
            ]
            got.append(lax.ppermute(x, ("dp", "seq"), pairs))
        got = jnp.stack(got)
        return jnp.concatenate(
            [
                lax.dynamic_index_in_dim(got, (j - spot + count) % count, 0, False)
                for j in range(count)
            ],
            axis=0,
        )

    def team_rows_back(self, x):
        count = self.groups
        pairs = [(g * TEAM + s, count * s + g) for g in range(count) for s in range(TEAM)]
        return lax.ppermute(x, ("dp", "seq"), pairs)


def decay_tables(plan, lengths, long_rows, short_rows):
    team_place = lax.axis_index("seq") % TEAM
    sub = lax.axis_index("seq") // TEAM
    spot = jnp.asarray(PLACE, jnp.int32)[team_place]
    blocks = jnp.asarray(RING, jnp.int32)[(spot + TEAM - jnp.arange(TEAM)) % TEAM]
    rates = head_rates((team_place * HEADS_DEV + jnp.arange(HEADS_DEV)).astype(wide))
    ends = jnp.cumsum(lengths)
    starts = ends - lengths

    def places(rows):
        return (blocks[:, None] * rows + jnp.arange(rows, dtype=jnp.int32)[None]).reshape(-1)

    def segment_of(place):
        return jnp.sum((place[..., None] >= ends).astype(jnp.int32), axis=-1)

    long_place, short_place = places(long_rows), places(short_rows)
    first = sub * short_rows * TEAM
    last = first + short_rows * TEAM - 1
    segment = segment_of(first + short_place)
    place = jnp.stack([long_place, short_place])
    segments = jnp.stack([jnp.full_like(long_place, -1), segment])
    spacing = (place[:, :, None] - place[:, None, :]).astype(wide)
    linked = (segments[:, :, None] == segments[:, None, :]) & (spacing >= 0.0)
    decay = jnp.where(
        linked[:, None],
        jnp.exp(-rates[None, :, None, None] * jnp.where(linked, spacing, 0.0)[:, None]),
        0.0,
    )
    if plan.subs == 1:
        return decay, None
    rows = (long_rows * TEAM, short_rows * TEAM)
    enter = (segment == segment_of(first)) & (jnp.sum((starts == first).astype(jnp.int32)) == 0)
    leave = segment == segment_of(last)
    masks_in = jnp.stack([jnp.ones_like(enter), enter]).astype(wide)
    masks_out = jnp.stack([jnp.ones_like(leave), leave]).astype(wide)
    size = jnp.asarray(rows, wide)[:, None]
    into = jnp.exp(-rates[None, :, None] * (place.astype(wide) + 1.0)[:, None]) * masks_in[:, None]
    out = (
        jnp.exp(-rates[None, :, None] * (size - 1.0 - place.astype(wide))[:, None])
        * masks_out[:, None]
    )
    broken = jnp.sum(((starts >= first) & (starts <= last)).astype(jnp.int32)) > 0
    unbroken = jnp.stack([jnp.ones((), bool), ~broken]).astype(wide)
    carry = jnp.exp(-rates[None, :] * size) * unbroken[:, None]
    return decay, (into[..., None], out[..., None], carry[..., None, None])


def carried(plan, carry, increment, backward):
    sub = lax.axis_index("seq") // TEAM
    groups = plan.sub_groups
    all_carry = lax.all_gather(carry, "seq", axis_index_groups=groups)
    all_increment = lax.all_gather(increment.astype(low), "seq", axis_index_groups=groups)
    state = jnp.zeros_like(increment)
    for hop in range(plan.subs):
        source = plan.subs - 1 - hop if backward else hop
        ahead = source > sub if backward else source < sub
        update = all_carry[source] * state + all_increment[source].astype(wide)
        state = jnp.where(ahead, update, state)
    return state


def bmm(left, right, left_dim, right_dim):
    return lax.dot_general(
        left,
        right,
        (((left_dim,), (right_dim,)), ((0, 1), (0, 1))),
        preferred_element_type=wide,
    )


def local(
    plan,
    tokens,
    cotangent,
    short_lengths,
    w_query,
    w_key,
    w_value,
    w_unit,
    w_output,
    w_gate,
    w_up,
    w_down,
):
    row_count, model_width = tokens.shape
    weight_rows = w_query.shape[0]
    groups = plan.groups
    piece = w_down.shape[0]
    hidden = piece * groups
    head_width = HEADS_DEV * DH
    team_tokens = row_count * TEAM

    def by_heads(w):
        return w.reshape(weight_rows, TEAM, head_width).transpose(1, 0, 2)

    def by_units(w):
        return w.reshape(weight_rows, groups, TEAM, piece).transpose(2, 0, 1, 3).reshape(TEAM, weight_rows, hidden)

    attn_pieces = jnp.concatenate([by_heads(w) for w in (w_query, w_key, w_value, w_unit)], axis=2)
    mlp_pieces = jnp.concatenate([by_units(w_gate), by_units(w_up)], axis=2)
    attn_w = plan.across(plan.swap(attn_pieces).reshape(TEAM * weight_rows, 4 * head_width))
    mlp_w = plan.across(plan.swap(mlp_pieces).reshape(TEAM * weight_rows, 2 * hidden))
    down_w = plan.across(w_down)
    output_w = plan.team_rows(w_output)

    inputs = tokens.astype(wide)
    normed = plan.ring_gather(normalize(inputs).astype(low))
    z_all = jnp.concatenate([dot(block, attn_w) for block in normed], axis=0)
    z_query, z_key, z_value, z_unit = jnp.split(z_all, 4, axis=1)

    def to_heads(x):
        x = x.reshape(TEAM, 2, LONG_DEV, HEADS_DEV, DH).transpose(1, 3, 0, 2, 4)
        return x.reshape(2, HEADS_DEV, TEAM * LONG_DEV, DH)

    def from_heads(x):
        x = x.reshape(2, HEADS_DEV, TEAM, LONG_DEV, DH).transpose(2, 0, 3, 1, 4)
        return x.reshape(team_tokens, head_width)

    decay, passing = decay_tables(plan, short_lengths[0], LONG_DEV, SHORT_DEV)
    query = to_heads(jax.nn.silu(z_query).astype(low))
    key = to_heads(jax.nn.silu(z_key).astype(low))
    value = to_heads(z_value.astype(low))
    weights = (bmm(query, key, 3, 3) * decay).astype(low)
    heads_out = bmm(weights, value, 3, 2)
    if passing is not None:
        into, out, carry = passing
        key_out = (key.astype(wide) * out).astype(low)
        state = carried(plan, carry, bmm(key_out, value, 2, 2), False).astype(low)
        heads_out = heads_out + bmm(query, state, 3, 2) * into
    heads_out = from_heads(heads_out)
    ring_spot = jnp.asarray(PLACE, jnp.int32)[lax.axis_index("seq") % TEAM]
    from_ring = (ring_spot + TEAM - jnp.asarray(PLACE, jnp.int32)) % TEAM
    to_ring = jnp.asarray(RING, jnp.int32)[(ring_spot + TEAM - jnp.arange(TEAM)) % TEAM]
    squares = lax.psum(
        jnp.sum(heads_out * heads_out, axis=1).reshape(TEAM, row_count)[from_ring],
        "seq",
        axis_index_groups=plan.team_groups,
    )
    scales = lax.rsqrt(squares[to_ring] / model_width + epsilon)
    scale_rows = scales.reshape(team_tokens, 1)
    gated_raw = (heads_out * z_unit).astype(low)

    def rows(x, k):
        return x[k * row_count : (k + 1) * row_count]

    attn_proj = plan.ring_reduce(lambda k: dot(rows(gated_raw, k), output_w)) * scales[0][:, None]
    middle = inputs + attn_proj

    cotangents = plan.ring_gather(cotangent)
    second = plan.ring_gather(normalize(middle).astype(low))
    hidden_blocks, pair_grads = [], []
    for block, above in zip(second, cotangents):
        pair = dot(block, mlp_w)
        gate_val, up_val = pair[:, :hidden], pair[:, hidden:]
        hidden_grad = dot_t(above, down_w)
        hidden_blocks.append((gate_val * up_val).astype(low))
        pair_grads.append(
            jnp.concatenate([hidden_grad * up_val, hidden_grad * gate_val], axis=1).astype(low)
        )
    second_grad = plan.ring_reduce(lambda k: dot_t(pair_grads[k], mlp_w))
    mixed = (middle + plan.ring_reduce(lambda k: dot(hidden_blocks[k], down_w))).astype(low)
    cotangent_all = jnp.concatenate(cotangents, axis=0)
    grad_down = plan.across_sum(outer(jnp.concatenate(hidden_blocks, axis=0), cotangent_all))
    grad_pair = plan.across_sum(
        outer(jnp.concatenate(second, axis=0), jnp.concatenate(pair_grads, axis=0))
    )

    def from_units(x):
        x = x.reshape(TEAM, weight_rows, groups, piece).transpose(1, 2, 0, 3)
        return x.reshape(weight_rows, TEAM * hidden).astype(wide)

    grad_pair = plan.swap(grad_pair.astype(low).reshape(TEAM, weight_rows, 2 * hidden))
    grad_gate = from_units(grad_pair[:, :, :hidden])
    grad_up = from_units(grad_pair[:, :, hidden:])

    middle_grad = cotangent.astype(wide) + norm_back(middle, second_grad)
    middle_low = middle_grad.astype(low)
    inner = jnp.sum(middle_low.astype(wide) * attn_proj, axis=1) / model_width
    inner = (scales[0] * scales[0] * inner).reshape(1, row_count)
    middle_blocks = plan.ring_gather(middle_low)
    inner_all = lax.all_gather(
        inner, "seq", axis=0, tiled=True, axis_index_groups=plan.team_groups
    )
    inner_rows = inner_all[to_ring].reshape(team_tokens, 1)
    gated_grad = jnp.concatenate([dot_t(block, output_w) for block in middle_blocks], axis=0)
    normed_heads = heads_out * scale_rows
    gated = (normed_heads * z_unit).astype(low)
    grad_output = plan.across_sum(outer(gated, jnp.concatenate(middle_blocks, axis=0)))
    grad_output = plan.team_rows_back(grad_output)
    unit_grad = (gated_grad * normed_heads).astype(low)
    heads_grad = to_heads(
        (scale_rows * gated_grad * z_unit - heads_out * inner_rows).astype(low)
    )
    scores = (bmm(heads_grad, value, 3, 3) * decay).astype(low)
    query_grad = bmm(scores, key, 3, 2)
    key_grad = bmm(scores, query, 2, 2)
    value_grad = bmm(weights, heads_grad, 2, 2)
    if passing is not None:
        query_grad = query_grad + bmm(heads_grad, state, 3, 3) * into
        local_state = bmm(query, (heads_grad.astype(wide) * into).astype(low), 2, 2)
        state_grad = carried(plan, carry, local_state, True).astype(low)
        key_grad = key_grad + bmm(value, state_grad, 3, 3) * out
        value_grad = value_grad + bmm(key_out, state_grad, 3, 2)

    def silu_slope(z):
        sigma = jax.nn.sigmoid(z)
        return sigma * (1.0 + z * (1.0 - sigma))

    z_grads = jnp.concatenate(
        [
            (from_heads(query_grad) * silu_slope(z_query)).astype(low),
            (from_heads(key_grad) * silu_slope(z_key)).astype(low),
            from_heads(value_grad).astype(low),
            unit_grad,
        ],
        axis=1,
    )
    first_grad = plan.ring_reduce(lambda k: dot_t(rows(z_grads, k), attn_w))
    grad_four = plan.across_sum(outer(jnp.concatenate(normed, axis=0), z_grads))
    grad_four = plan.swap(grad_four.astype(low).reshape(TEAM, weight_rows, 4 * head_width))

    def from_columns(x):
        return x.transpose(1, 0, 2).reshape(weight_rows, TEAM * head_width).astype(wide)

    grad_query, grad_key, grad_value, grad_unit = (
        from_columns(grad_four[:, :, i * head_width : (i + 1) * head_width]) for i in range(4)
    )
    tokens_grad = (middle_grad + norm_back(inputs, first_grad)).astype(low)
    return (
        mixed,
        tokens_grad,
        grad_query,
        grad_key,
        grad_value,
        grad_unit,
        grad_output,
        grad_gate,
        grad_up,
        grad_down,
    )


def solution(mesh):
    plan = Plan(mesh)
    rows = P(("dp", "seq"), None)
    in_specs = (rows, rows, P("dp", None)) + (rows,) * 8

    def layer(*args):
        return local(plan, *args)

    return jax.shard_map(layer, mesh=mesh, in_specs=in_specs, out_specs=(rows,) * 10, check_vma=False)
```

time: 5870 us -> 758 us (0.13)
  waiting for transfers between devices: 5540 us -> 178 us
  starting transfers between devices: 0.93 us -> 155 us
  matrix products: 229 us -> 128 us
  blocking collectives: 19.5 us -> 107 us
  local copies, waits for them, and re-layouts: 23.1 us -> 99 us
    reduce_scatter x4 -> x0, waiting for transfers between devices: 4560 us -> none  [the longest x1 1920 us: local(): lax.psum_scatter(outer_rows(second_low, jnp.concatenate([gate_grad_low, u...]
    all_gather x10 -> x3, waiting for transfers between devices: 979 us -> 0.01 us  [across(): return lax.all_gather(x, 'dp', axis=0, tiled=True)]
    ppermute x0 -> x77, waiting for transfers between devices: none -> 178 us  [the longest x32 123 us: to_previous(): return lax.ppermute(x, 'seq', self.down)]
    ppermute x0 -> x77, starting transfers between devices: none -> 135 us  [the longest x32 83.6 us: to_next(): return lax.ppermute(x, 'seq', self.up)]
    dot_general x38 -> x74, matrix products: 229 us -> 128 us  [the longest x32 55.8 us: dot_t(): lax.dot_general(left, right, (((1,), (1,)), ((), ())), preferred_element_...]
    all_to_all x0 -> x2, blocking collectives: none -> 70.8 us  [swap(): lax.all_to_all(x, 'seq', 0, 0, tiled=True, axis_index_groups=self.team_gr...]
  transfers between devices with their start and end apart: 14 -> 82, of which waited for: 14 -> 24; matrix products, arithmetic and copies ran while one was open for 3% -> 36% of each run, Pallas kernels for 0% -> 0%
where the time goes in v1:
time: 758 us; the launch traced here: 747 us
  waiting for transfers between devices  178 us (23%)
  starting transfers between devices  155 us (20%)
  matrix products  128 us (17%)
  blocking collectives  107 us (14%)
  local copies, waits for them, and re-layouts  99 us (13%)
  other arithmetic  62.8 us (8%)
  between operations  17.3 us (2%)
    ppermute x32, waiting for transfers between devices, to_previous(): return lax.ppermute(x, 'seq', self.down)  123 us
    ppermute x32, starting transfers between devices, to_next(): return lax.ppermute(x, 'seq', self.up)  83.6 us
    all_to_all x2, blocking collectives, swap(): lax.all_to_all(x, 'seq', 0, 0, tiled=True, axis_index_groups=self.team_gr...  70.8 us
    dot_general x32, matrix products, dot_t(): lax.dot_general(left, right, (((1,), (1,)), ((), ())), preferred_element_...  55.8 us
    ppermute x32, waiting for transfers between devices, to_next(): return lax.ppermute(x, 'seq', self.up)  52.2 us
    dot_general x32, matrix products, dot(): return jnp.dot(left, right, preferred_element_type=wide)  43.5 us
    unnamed x228, local copies, waits for them, and re-layouts  39.4 us
    ppermute x32, starting transfers between devices, to_previous(): return lax.ppermute(x, 'seq', self.down)  22.4 us
  transfers between devices with their start and end apart: 82, of which 24 were waited for; matrix products, arithmetic and copies ran while one was open for 36% of the time, Pallas kernels for 0%

profile of v1, /device:TPU:0, one launch (start us, length us, event | category | flops | bytes accessed | tf_op | source)
XLA Modules:
  0.0 747.2 jit_solution(857090046690297677)
XLA Ops:
  12.0 32.9 %all_to_all.20 = bf16[8,64,1024]{2,1,0:T(8,128)(2,1)} all-to-all(bf16[8,64,1024]{2,1,0:T(8,128)(2,1)S(1)} %copy.193), channel_id=1, replica_groups=mesh['dp'=4,'seq'=8] {'seq'}, dimensions={0} | all-to-all | bytes 2097152 | tf_op jit(solution)/shard_map/all_to_all | solution.py:124
  53.2 37.8 %all_to_all.21 = bf16[8,64,1408]{2,1,0:T(8,128)(2,1)} all-to-all(bf16[8,64,1408]{2,1,0:T(8,128)(2,1)S(1)} %pad_maximum_fusion.1), channel_id=1, replica_groups=mesh['dp'=4,'seq'=8] {'seq'}, dimensions={0} | all-to-all | bytes 2883584 | tf_op jit(solution)/shard_map/all_to_all | solution.py:124
  94.7 3.2 collective-permute-start.11
  99.7 4.7 collective-permute-start.4
  106.9 25.4 %collective-permute-done.4 = bf16[128,2048]{1,0:T(8,128)(2,1)S(1)} collective-permute-done((bf16[128,2048]{1,0:T(8,128)(2,1)S(1)}, bf16[128,2048]{1,0:T(8,128)(2,1)S(1)}, u32[]{:S(2)}, u32[]{:S(2)}) %collective-permute-start.4) | collective-permute-done | bytes 524320 | tf_op jit(solution)/shard_map/ppermute | solution.py:67
  132.4 8.6 %collective-permute-start.1 = (bf16[128,2048]{1,0:T(8,128)(2,1)S(1)}, bf16[128,2048]{1,0:T(8,128)(2,1)}, u32[]{:S(2)}, u32[]{:S(2)}) collective-permute-start(bf16[128,2048]{1,0:T(8,128)(2,1)S(1)} %collective-permute-done), channel_id=1, source_target_pairs={{0,2},{2,4},{4,6},{6,7},{7,5},{5,3},{3,1},{1,0},{8,10},{10,12},{12... | collective-permute-start | bytes 1572872 | tf_op jit(solution)/shard_map/ppermute | solution.py:64
  146.1 7.5 %collective-permute-done.5 = bf16[128,2048]{1,0:T(8,128)(2,1)S(1)} collective-permute-done((bf16[128,2048]{1,0:T(8,128)(2,1)S(1)}, bf16[128,2048]{1,0:T(8,128)(2,1)S(1)}, u32[]{:S(2)}, u32[]{:S(2)}) %collective-permute-start.5) | collective-permute-done | bytes 524320 | tf_op jit(solution)/shard_map/ppermute | solution.py:67
  153.6 7.7 %collective-permute-start.2 = (bf16[128,2048]{1,0:T(8,128)(2,1)}, bf16[128,2048]{1,0:T(8,128)(2,1)S(1)}, u32[]{:S(2)}, u32[]{:S(2)}) collective-permute-start(bf16[128,2048]{1,0:T(8,128)(2,1)} %collective-permute-done.1), channel_id=1, source_target_pairs={{0,2},{2,4},{4,6},{6,7},{7,5},{5,3},{3,1},{1,0},{8,10},{10,12},{12... | collective-permute-start | bytes 1572872 | tf_op jit(solution)/shard_map/ppermute | solution.py:64
  167.1 9.1 %collective-permute-done.40 = bf16[128,2048]{1,0:T(8,128)(2,1)} collective-permute-done((bf16[128,2048]{1,0:T(8,128)(2,1)}, bf16[128,2048]{1,0:T(8,128)(2,1)}, u32[]{:S(2)}, u32[]{:S(2)}) %collective-permute-start.40) | collective-permute-done | bytes 524320 | tf_op jit(solution)/shard_map/ppermute | solution.py:67
  177.9 9.4 %collective-permute-done.6 = bf16[128,2048]{1,0:T(8,128)(2,1)S(1)} collective-permute-done((bf16[128,2048]{1,0:T(8,128)(2,1)S(1)}, bf16[128,2048]{1,0:T(8,128)(2,1)S(1)}, u32[]{:S(2)}, u32[]{:S(2)}) %collective-permute-start.6) | collective-permute-done | bytes 524320 | tf_op jit(solution)/shard_map/ppermute | solution.py:67
  191.1 3.2 convolution_dynamic-update-slice_fusion.7
  216.6 4.6 collective-permute-start.16
  222.0 4.1 collective-permute-done.16
  234.5 7.7 %collective-permute-done.17 = bf16[128,2048]{1,0:T(8,128)(2,1)} collective-permute-done((bf16[128,2048]{1,0:T(8,128)(2,1)}, bf16[128,2048]{1,0:T(8,128)(2,1)}, u32[]{:S(2)}, u32[]{:S(2)}) %collective-permute-start.17) | collective-permute-done | bytes 524320 | tf_op jit(solution)/shard_map/ppermute | solution.py:64
  249.9 3.6 collective-permute-done.38
  258.3 6.2 collective-permute-done.18
  273.8 19.8 %psum.7 = f32[8,128]{1,0:T(8,128)S(1)} all-reduce(f32[8,128]{1,0:T(8,128)S(1)} %gather_fusion.1), channel_id=1, replica_groups=mesh['dp'=4,'seq'=8] {'seq'}, use_global_device_ids=true, to_apply=%region_4.5 | all-reduce | flops 1024 | bytes 8192 | tf_op jit(solution)/shard_map/psum | solution.py:283
  304.0 8.3 %collective-permute-done.24 = bf16[128,2048]{1,0:T(8,128)(2,1)S(1)} collective-permute-done((bf16[128,2048]{1,0:T(8,128)(2,1)S(1)}, bf16[128,2048]{1,0:T(8,128)(2,1)S(1)}, u32[]{:S(2)}, u32[]{:S(2)}) %collective-permute-start.24) | collective-permute-done | bytes 524320 | tf_op jit(solution)/shard_map/ppermute | solution.py:67
  316.9 10.0 %collective-permute-done.25 = bf16[128,2048]{1,0:T(8,128)(2,1)} collective-permute-done((bf16[128,2048]{1,0:T(8,128)(2,1)S(1)}, bf16[128,2048]{1,0:T(8,128)(2,1)}, u32[]{:S(2)}, u32[]{:S(2)}) %collective-permute-start.25) | collective-permute-done | bytes 524320 | tf_op jit(solution)/shard_map/ppermute | solution.py:67
  326.9 10.5 %collective-permute-start.22 = (bf16[128,2048]{1,0:T(8,128)(2,1)}, bf16[128,2048]{1,0:T(8,128)(2,1)}, u32[]{:S(2)}, u32[]{:S(2)}) collective-permute-start(bf16[128,2048]{1,0:T(8,128)(2,1)} %collective-permute-done.21), channel_id=1, source_target_pairs={{0,2},{2,4},{4,6},{6,7},{7,5},{5,3},{3,1},{1,0},{8,10},{10,12},{12... | collective-permute-start | bytes 1572872 | tf_op jit(solution)/shard_map/ppermute | solution.py:64
  339.3 3.9 fusion.120
  350.0 3.3 multiply_convert_fusion.23
  353.4 3.1 multiply_convert_fusion.21
  356.7 3.6 fusion.128
  423.2 10.3 %collective-permute-done.45 = bf16[128,2048]{1,0:T(8,128)(2,1)S(1)} collective-permute-done((bf16[128,2048]{1,0:T(8,128)(2,1)S(1)}, bf16[128,2048]{1,0:T(8,128)(2,1)S(1)}, u32[]{:S(2)}, u32[]{:S(2)}) %collective-permute-start.45) | collective-permute-done | bytes 524320 | tf_op jit(solution)/shard_map/ppermute | solution.py:67
  435.9 9.4 %collective-permute-done.33 = bf16[128,2048]{1,0:T(8,128)(2,1)S(1)} collective-permute-done((bf16[128,2048]{1,0:T(8,128)(2,1)S(1)}, bf16[128,2048]{1,0:T(8,128)(2,1)S(1)}, u32[]{:S(2)}, u32[]{:S(2)}) %collective-permute-start.33) | collective-permute-done | bytes 524320 | tf_op jit(solution)/shard_map/ppermute | solution.py:64
  447.6 8.4 %collective-permute-done.46 = bf16[128,2048]{1,0:T(8,128)(2,1)S(1)} collective-permute-done((bf16[128,2048]{1,0:T(8,128)(2,1)S(1)}, bf16[128,2048]{1,0:T(8,128)(2,1)S(1)}, u32[]{:S(2)}, u32[]{:S(2)}) %collective-permute-start.46) | collective-permute-done | bytes 524320 | tf_op jit(solution)/shard_map/ppermute | solution.py:67
  458.3 9.4 %collective-permute-done.34 = bf16[128,2048]{1,0:T(8,128)(2,1)S(1)} collective-permute-done((bf16[128,2048]{1,0:T(8,128)(2,1)S(1)}, bf16[128,2048]{1,0:T(8,128)(2,1)S(1)}, u32[]{:S(2)}, u32[]{:S(2)}) %collective-permute-start.34) | collective-permute-done | bytes 524320 | tf_op jit(solution)/shard_map/ppermute | solution.py:64
  470.0 8.7 %fusion.136 = f32[2048,1408]{1,0:T(8,128)S(1)} fusion(bf16[1024,2048]{1,0:T(8,128)(2,1)} %constant_dynamic-update-slice_fusion.18, bf16[1024,1408]{1,0:T(8,128)(2,1)S(1)} %fusion.61), kind=kOutput, calls=%fused_computation.361 | convolution fusion | flops 5905580032 | bytes 18612224 | tf_op jit(solution)/shard_map/dot_general | solution.py:43
  494.7 6.4 fusion.137
  501.1 16.8 %all-gather = f32[8,1,128]{2,1,0:T(1,128)S(1)} all-gather(f32[1,1,128]{2,1,0:T(1,128)S(1)} %fusion.99), channel_id=1, replica_groups=mesh['dp'=4,'seq'=8] {'seq'}, dimensions={0}, use_global_device_ids=true | all-gather | bytes 4608 | tf_op jit(solution)/shard_map/all_gather | solution.py:330
  528.0 4.1 bitcast_add_fusion
  544.6 5.7 collective-permute-done.58
  554.2 3.2 collective-permute-done.59
  585.4 4.7 fusion.113
  612.5 4.3 all-to-all-start.3
  621.4 3.5 collective-permute-start.62
  624.9 3.5 bitcast_add_fusion.1
  628.6 7.9 %collective-permute-start.69 = (bf16[1,512,1024]{2,1,0:T(8,128)(2,1)S(1)}, bf16[1,512,1024]{2,1,0:T(8,128)(2,1)S(1)}, u32[]{:S(2)}, u32[]{:S(2)}) collective-permute-start(bf16[1,512,1024]{2,1,0:T(8,128)(2,1)S(1)} %dynamic-slice_convert_fusion.3), channel_id=1, source_target_pairs={{0,16},{8,24},{16,0},{24,8},{1,17},{9,25},{17,1},{25,9},{2,18},{10... | collective-permute-start | bytes 3145736 | tf_op jit(solution)/shard_map/ppermute | solution.py:113
  637.4 5.3 collective-permute-start.72
  642.7 9.5 %collective-permute-done.66 = bf16[128,2048]{1,0:T(8,128)(2,1)S(1)} collective-permute-done((bf16[128,2048]{1,0:T(8,128)(2,1)S(1)}, bf16[128,2048]{1,0:T(8,128)(2,1)S(1)}, u32[]{:S(2)}, u32[]{:S(2)}) %collective-permute-start.66) | collective-permute-done | bytes 524320 | tf_op jit(solution)/shard_map/ppermute | solution.py:64
  653.1 9.3 %collective-permute-start.67 = (bf16[128,2048]{1,0:T(8,128)(2,1)}, bf16[128,2048]{1,0:T(8,128)(2,1)}, u32[]{:S(2)}, u32[]{:S(2)}) collective-permute-start(bf16[128,2048]{1,0:T(8,128)(2,1)} %add_convert_fusion.2), channel_id=1, source_target_pairs={{0,2},{2,4},{4,6},{6,7},{7,5},{5,3},{3,1},{1,0},{8,10},{10,12},{12... | collective-permute-start | bytes 1572872 | tf_op jit(solution)/shard_map/ppermute | solution.py:64
  664.7 15.8 %all-to-all-start.2 = ((bf16[8,64,1024]{2,1,0:T(8,128)(2,1)}), bf16[8,64,1024]{2,1,0:T(8,128)(2,1)}, u32[]{:S(2)}, u32[]{:S(2)}) async-start(bf16[8,64,1024]{2,1,0:T(8,128)(2,1)} %bitcast.287), calls=%async_computation.2 | async-start | bytes 2097152 | tf_op jit(solution)/shard_map/all_to_all | solution.py:124
  682.9 22.6 %collective-permute-done.63 = bf16[128,2048]{1,0:T(8,128)(2,1)} collective-permute-done((bf16[128,2048]{1,0:T(8,128)(2,1)}, bf16[128,2048]{1,0:T(8,128)(2,1)}, u32[]{:S(2)}, u32[]{:S(2)}) %collective-permute-start.63) | collective-permute-done | bytes 524320 | tf_op jit(solution)/shard_map/ppermute | solution.py:67
  705.5 4.2 fusion.10
  712.4 3.5 slice_convert_fusion.1
  721.5 3.3 reshape.460
  730.3 3.3 reshape.459
  (590 shorter events, 308.3 us)
Async XLA Ops:
  7.2 183.9 %all-gather.5.cloned.1.call-start = ((), (), s32[]{:S(2)}) async-start(), calls=%async_computation.4 | async-start | bytes 5242880 | tf_op jit(solution)/shard_map/all_gather | solution.py:100
  44.9 294.4 %all-gather.7.cloned.1.call-start = ((), (), s32[]{:S(2)}) async-start(), calls=%async_computation.5 | async-start | bytes 7208960 | tf_op jit(solution)/shard_map/all_gather | solution.py:100
  91.1 258.9 %all-gather.9.cloned.1.call-start = ((), (), s32[]{:S(2)}) async-start(), calls=%async_computation.6 | async-start | bytes 3604480 | tf_op jit(solution)/shard_map/all_gather | solution.py:100
  91.1 52.9 %collective-permute-start.9 = (bf16[64,2048]{1,0:T(8,128)(2,1)}, bf16[64,2048]{1,0:T(8,128)(2,1)S(1)}, u32[]{:S(2)}, u32[]{:S(2)}) collective-permute-start(bf16[64,2048]{1,0:T(8,128)(2,1)} %param.23), channel_id=1, source_target_pairs={{1,0},{5,1},{9,2},{13,3},{17,4},{21,5},{25,6},{29,7},{2,8},{6,9},{... | collective-permute-start | bytes 786440 | tf_op jit(solution)/shard_map/ppermute | solution.py:134
  93.1 51.0 %collective-permute-start.8 = (bf16[64,2048]{1,0:T(8,128)(2,1)}, bf16[64,2048]{1,0:T(8,128)(2,1)S(1)}, u32[]{:S(2)}, u32[]{:S(2)}) collective-permute-start(bf16[64,2048]{1,0:T(8,128)(2,1)} %param.23), channel_id=1, source_target_pairs={{0,0},{4,1},{8,2},{12,3},{16,4},{20,5},{24,6},{28,7},{1,8},{5,9},{... | collective-permute-start | bytes 786440 | tf_op jit(solution)/shard_map/ppermute | solution.py:134
  94.7 51.4 %collective-permute-start.11 = (bf16[64,2048]{1,0:T(8,128)(2,1)}, bf16[64,2048]{1,0:T(8,128)(2,1)}, u32[]{:S(2)}, u32[]{:S(2)}) collective-permute-start(bf16[64,2048]{1,0:T(8,128)(2,1)} %param.23), channel_id=1, source_target_pairs={{3,0},{7,1},{11,2},{15,3},{19,4},{23,5},{27,6},{31,7},{0,8},{4,9},... | collective-permute-start | bytes 786440 | tf_op jit(solution)/shard_map/ppermute | solution.py:134
  99.7 32.7 %collective-permute-start.4 = (bf16[128,2048]{1,0:T(8,128)(2,1)S(1)}, bf16[128,2048]{1,0:T(8,128)(2,1)S(1)}, u32[]{:S(2)}, u32[]{:S(2)}) collective-permute-start(bf16[128,2048]{1,0:T(8,128)(2,1)S(1)} %get-tuple-element.32), channel_id=1, source_target_pairs={{2,0},{4,2},{6,4},{7,6},{5,7},{3,5},{1,3},{0,1},{10,8},{12,10},{14... | collective-permute-start | bytes 1572872 | tf_op jit(solution)/shard_map/ppermute | solution.py:67
  104.3 28.0 %collective-permute-start = (bf16[128,2048]{1,0:T(8,128)(2,1)S(1)}, bf16[128,2048]{1,0:T(8,128)(2,1)S(1)}, u32[]{:S(2)}, u32[]{:S(2)}) collective-permute-start(bf16[128,2048]{1,0:T(8,128)(2,1)S(1)} %get-tuple-element.32), channel_id=1, source_target_pairs={{0,2},{2,4},{4,6},{6,7},{7,5},{5,3},{3,1},{1,0},{8,10},{10,12},{12... | collective-permute-start | bytes 1572872 | tf_op jit(solution)/shard_map/ppermute | solution.py:64
  132.4 21.3 %collective-permute-start.5 = (bf16[128,2048]{1,0:T(8,128)(2,1)S(1)}, bf16[128,2048]{1,0:T(8,128)(2,1)S(1)}, u32[]{:S(2)}, u32[]{:S(2)}) collective-permute-start(bf16[128,2048]{1,0:T(8,128)(2,1)S(1)} %collective-permute-done.4), channel_id=1, source_target_pairs={{2,0},{4,2},{6,4},{7,6},{5,7},{3,5},{1,3},{0,1},{10,8},{12,10},{14... | collective-permute-start | bytes 1572872 | tf_op jit(solution)/shard_map/ppermute | solution.py:67
  132.4 21.3 %collective-permute-start.1 = (bf16[128,2048]{1,0:T(8,128)(2,1)S(1)}, bf16[128,2048]{1,0:T(8,128)(2,1)}, u32[]{:S(2)}, u32[]{:S(2)}) collective-permute-start(bf16[128,2048]{1,0:T(8,128)(2,1)S(1)} %collective-permute-done), channel_id=1, source_target_pairs={{0,2},{2,4},{4,6},{6,7},{7,5},{5,3},{3,1},{1,0},{8,10},{10,12},{12... | collective-permute-start | bytes 1572872 | tf_op jit(solution)/shard_map/ppermute | solution.py:64
  144.0 21.7 %collective-permute-start.36 = (bf16[128,2048]{1,0:T(8,128)(2,1)}, bf16[128,2048]{1,0:T(8,128)(2,1)}, u32[]{:S(2)}, u32[]{:S(2)}) collective-permute-start(bf16[128,2048]{1,0:T(8,128)(2,1)} %param.17), channel_id=1, source_target_pairs={{0,2},{2,4},{4,6},{6,7},{7,5},{5,3},{3,1},{1,0},{8,10},{10,12},{12... | collective-permute-start | bytes 1572872 | tf_op jit(solution)/shard_map/ppermute | solution.py:64
  146.1 30.1 %collective-permute-start.40 = (bf16[128,2048]{1,0:T(8,128)(2,1)}, bf16[128,2048]{1,0:T(8,128)(2,1)}, u32[]{:S(2)}, u32[]{:S(2)}) collective-permute-start(bf16[128,2048]{1,0:T(8,128)(2,1)} %param.17), channel_id=1, source_target_pairs={{2,0},{4,2},{6,4},{7,6},{5,7},{3,5},{1,3},{0,1},{10,8},{12,10},{14... | collective-permute-start | bytes 1572872 | tf_op jit(solution)/shard_map/ppermute | solution.py:67
  153.6 33.7 %collective-permute-start.6 = (bf16[128,2048]{1,0:T(8,128)(2,1)S(1)}, bf16[128,2048]{1,0:T(8,128)(2,1)S(1)}, u32[]{:S(2)}, u32[]{:S(2)}) collective-permute-start(bf16[128,2048]{1,0:T(8,128)(2,1)S(1)} %collective-permute-done.5), channel_id=1, source_target_pairs={{2,0},{4,2},{6,4},{7,6},{5,7},{3,5},{1,3},{0,1},{10,8},{12,10},{14... | collective-permute-start | bytes 1572872 | tf_op jit(solution)/shard_map/ppermute | solution.py:67
  153.6 34.4 %collective-permute-start.2 = (bf16[128,2048]{1,0:T(8,128)(2,1)}, bf16[128,2048]{1,0:T(8,128)(2,1)S(1)}, u32[]{:S(2)}, u32[]{:S(2)}) collective-permute-start(bf16[128,2048]{1,0:T(8,128)(2,1)} %collective-permute-done.1), channel_id=1, source_target_pairs={{0,2},{2,4},{4,6},{6,7},{7,5},{5,3},{3,1},{1,0},{8,10},{10,12},{12... | collective-permute-start | bytes 1572872 | tf_op jit(solution)/shard_map/ppermute | solution.py:64
  165.7 66.8 %collective-permute-start.37 = (bf16[128,2048]{1,0:T(8,128)(2,1)}, bf16[128,2048]{1,0:T(8,128)(2,1)}, u32[]{:S(2)}, u32[]{:S(2)}) collective-permute-start(bf16[128,2048]{1,0:T(8,128)(2,1)} %collective-permute-done.36), channel_id=1, source_target_pairs={{0,2},{2,4},{4,6},{6,7},{7,5},{5,3},{3,1},{1,0},{8,10},{10,12},{12... | collective-permute-start | bytes 1572872 | tf_op jit(solution)/shard_map/ppermute | solution.py:64
  176.2 58.3 %collective-permute-start.41 = (bf16[128,2048]{1,0:T(8,128)(2,1)}, bf16[128,2048]{1,0:T(8,128)(2,1)}, u32[]{:S(2)}, u32[]{:S(2)}) collective-permute-start(bf16[128,2048]{1,0:T(8,128)(2,1)} %collective-permute-done.40), channel_id=1, source_target_pairs={{2,0},{4,2},{6,4},{7,6},{5,7},{3,5},{1,3},{0,1},{10,8},{12,10},{14... | collective-permute-start | bytes 1572872 | tf_op jit(solution)/shard_map/ppermute | solution.py:67
  234.5 22.3 %collective-permute-start.42 = (bf16[128,2048]{1,0:T(8,128)(2,1)}, bf16[128,2048]{1,0:T(8,128)(2,1)S(1)}, u32[]{:S(2)}, u32[]{:S(2)}) collective-permute-start(bf16[128,2048]{1,0:T(8,128)(2,1)} %collective-permute-done.41), channel_id=1, source_target_pairs={{2,0},{4,2},{6,4},{7,6},{5,7},{3,5},{1,3},{0,1},{10,8},{12,10},{14... | collective-permute-start | bytes 1572872 | tf_op jit(solution)/shard_map/ppermute | solution.py:67
  247.9 21.1 %collective-permute-start.14 = (bf16[128,2048]{1,0:T(8,128)(2,1)S(1)}, bf16[128,2048]{1,0:T(8,128)(2,1)S(1)}, u32[]{:S(2)}, u32[]{:S(2)}) collective-permute-start(bf16[128,2048]{1,0:T(8,128)(2,1)S(1)} %add_convert_fusion.18), channel_id=1, source_target_pairs={{2,0},{4,2},{6,4},{7,6},{5,7},{3,5},{1,3},{0,1},{10,8},{12,10},{14... | collective-permute-start | bytes 1572872 | tf_op jit(solution)/shard_map/ppermute | solution.py:67
  254.2 144.4 %collective-permute-start.39 = (bf16[64,2048]{1,0:T(8,128)(2,1)}, bf16[64,2048]{1,0:T(8,128)(2,1)}, u32[]{:S(2)}, u32[]{:S(2)}) collective-permute-start(bf16[64,2048]{1,0:T(8,128)(2,1)} %slice.351), channel_id=1, source_target_pairs={{0,2},{2,4},{4,6},{6,7},{7,5},{5,3},{3,1},{1,0},{8,10},{10,12},{12... | collective-permute-start | bytes 786440 | tf_op jit(solution)/shard_map/ppermute | solution.py:64
  257.5 141.1 %collective-permute-start.43 = (bf16[64,2048]{1,0:T(8,128)(2,1)}, bf16[64,2048]{1,0:T(8,128)(2,1)}, u32[]{:S(2)}, u32[]{:S(2)}) collective-permute-start(bf16[64,2048]{1,0:T(8,128)(2,1)} %slice.352), channel_id=1, source_target_pairs={{2,0},{4,2},{6,4},{7,6},{5,7},{3,5},{1,3},{0,1},{10,8},{12,10},{14... | collective-permute-start | bytes 786440 | tf_op jit(solution)/shard_map/ppermute | solution.py:67
  266.5 27.6 %collective-permute-start.19 = (bf16[128,2048]{1,0:T(8,128)(2,1)}, bf16[128,2048]{1,0:T(8,128)(2,1)}, u32[]{:S(2)}, u32[]{:S(2)}) collective-permute-start(bf16[128,2048]{1,0:T(8,128)(2,1)} %add_convert_fusion.15), channel_id=1, source_target_pairs={{0,2},{2,4},{4,6},{6,7},{7,5},{5,3},{3,1},{1,0},{8,10},{10,12},{12... | collective-permute-start | bytes 1572872 | tf_op jit(solution)/shard_map/ppermute | solution.py:64
  271.0 23.2 %collective-permute-start.15 = (bf16[128,2048]{1,0:T(8,128)(2,1)}, bf16[128,2048]{1,0:T(8,128)(2,1)}, u32[]{:S(2)}, u32[]{:S(2)}) collective-permute-start(bf16[128,2048]{1,0:T(8,128)(2,1)} %add_convert_fusion.17), channel_id=1, source_target_pairs={{2,0},{4,2},{6,4},{7,6},{5,7},{3,5},{1,3},{0,1},{10,8},{12,10},{14... | collective-permute-start | bytes 1572872 | tf_op jit(solution)/shard_map/ppermute | solution.py:67
  326.9 54.7 %collective-permute-start.26 = (bf16[128,2048]{1,0:T(8,128)(2,1)}, bf16[128,2048]{1,0:T(8,128)(2,1)S(1)}, u32[]{:S(2)}, u32[]{:S(2)}) collective-permute-start(bf16[128,2048]{1,0:T(8,128)(2,1)} %collective-permute-done.25), channel_id=1, source_target_pairs={{2,0},{4,2},{6,4},{7,6},{5,7},{3,5},{1,3},{0,1},{10,8},{12,10},{14... | collective-permute-start | bytes 1572872 | tf_op jit(solution)/shard_map/ppermute | solution.py:67
  326.9 55.1 %collective-permute-start.22 = (bf16[128,2048]{1,0:T(8,128)(2,1)}, bf16[128,2048]{1,0:T(8,128)(2,1)}, u32[]{:S(2)}, u32[]{:S(2)}) collective-permute-start(bf16[128,2048]{1,0:T(8,128)(2,1)} %collective-permute-done.21), channel_id=1, source_target_pairs={{0,2},{2,4},{4,6},{6,7},{7,5},{5,3},{3,1},{1,0},{8,10},{10,12},{12... | collective-permute-start | bytes 1572872 | tf_op jit(solution)/shard_map/ppermute | solution.py:64
  420.9 24.3 %collective-permute-start.33 = (bf16[128,2048]{1,0:T(8,128)(2,1)S(1)}, bf16[128,2048]{1,0:T(8,128)(2,1)S(1)}, u32[]{:S(2)}, u32[]{:S(2)}) collective-permute-start(bf16[128,2048]{1,0:T(8,128)(2,1)S(1)} %pad_maximum_fusion.8), channel_id=1, source_target_pairs={{0,2},{2,4},{4,6},{6,7},{7,5},{5,3},{3,1},{1,0},{8,10},{10,12},{12... | collective-permute-start | bytes 1572872 | tf_op jit(solution)/shard_map/ppermute | solution.py:64
  421.1 26.0 %collective-permute-start.29 = (bf16[128,2048]{1,0:T(8,128)(2,1)S(1)}, bf16[128,2048]{1,0:T(8,128)(2,1)S(1)}, u32[]{:S(2)}, u32[]{:S(2)}) collective-permute-start(bf16[128,2048]{1,0:T(8,128)(2,1)S(1)} %pad_maximum_fusion.7), channel_id=1, source_target_pairs={{2,0},{4,2},{6,4},{7,6},{5,7},{3,5},{1,3},{0,1},{10,8},{12,10},{14... | collective-permute-start | bytes 1572872 | tf_op jit(solution)/shard_map/ppermute | solution.py:67
  433.6 22.4 %collective-permute-start.46 = (bf16[128,2048]{1,0:T(8,128)(2,1)S(1)}, bf16[128,2048]{1,0:T(8,128)(2,1)S(1)}, u32[]{:S(2)}, u32[]{:S(2)}) collective-permute-start(bf16[128,2048]{1,0:T(8,128)(2,1)S(1)} %add_convert_fusion.9), channel_id=1, source_target_pairs={{2,0},{4,2},{6,4},{7,6},{5,7},{3,5},{1,3},{0,1},{10,8},{12,10},{14... | collective-permute-start | bytes 1572872 | tf_op jit(solution)/shard_map/ppermute | solution.py:67
  434.1 22.4 %collective-permute-start.50 = (bf16[128,2048]{1,0:T(8,128)(2,1)S(1)}, bf16[128,2048]{1,0:T(8,128)(2,1)S(1)}, u32[]{:S(2)}, u32[]{:S(2)}) collective-permute-start(bf16[128,2048]{1,0:T(8,128)(2,1)S(1)} %add_convert_fusion.7), channel_id=1, source_target_pairs={{0,2},{2,4},{4,6},{6,7},{7,5},{5,3},{3,1},{1,0},{8,10},{10,12},{12... | collective-permute-start | bytes 1572872 | tf_op jit(solution)/shard_map/ppermute | solution.py:64
  445.3 22.4 %collective-permute-start.34 = (bf16[128,2048]{1,0:T(8,128)(2,1)S(1)}, bf16[128,2048]{1,0:T(8,128)(2,1)S(1)}, u32[]{:S(2)}, u32[]{:S(2)}) collective-permute-start(bf16[128,2048]{1,0:T(8,128)(2,1)S(1)} %add_convert_fusion.12), channel_id=1, source_target_pairs={{0,2},{2,4},{4,6},{6,7},{7,5},{5,3},{3,1},{1,0},{8,10},{10,12},{12... | collective-permute-start | bytes 1572872 | tf_op jit(solution)/shard_map/ppermute | solution.py:64
  447.2 22.4 %collective-permute-start.30 = (bf16[128,2048]{1,0:T(8,128)(2,1)S(1)}, bf16[128,2048]{1,0:T(8,128)(2,1)S(1)}, u32[]{:S(2)}, u32[]{:S(2)}) collective-permute-start(bf16[128,2048]{1,0:T(8,128)(2,1)S(1)} %add_convert_fusion.14), channel_id=1, source_target_pairs={{2,0},{4,2},{6,4},{7,6},{5,7},{3,5},{1,3},{0,1},{10,8},{12,10},{14... | collective-permute-start | bytes 1572872 | tf_op jit(solution)/shard_map/ppermute | solution.py:67
  456.1 24.7 %collective-permute-start.47 = (bf16[128,2048]{1,0:T(8,128)(2,1)S(1)}, bf16[128,2048]{1,0:T(8,128)(2,1)S(1)}, u32[]{:S(2)}, u32[]{:S(2)}) collective-permute-start(bf16[128,2048]{1,0:T(8,128)(2,1)S(1)} %add_convert_fusion.8), channel_id=1, source_target_pairs={{2,0},{4,2},{6,4},{7,6},{5,7},{3,5},{1,3},{0,1},{10,8},{12,10},{14... | collective-permute-start | bytes 1572872 | tf_op jit(solution)/shard_map/ppermute | solution.py:67
  456.6 24.2 %collective-permute-start.51 = (bf16[128,2048]{1,0:T(8,128)(2,1)S(1)}, bf16[128,2048]{1,0:T(8,128)(2,1)S(1)}, u32[]{:S(2)}, u32[]{:S(2)}) collective-permute-start(bf16[128,2048]{1,0:T(8,128)(2,1)S(1)} %add_convert_fusion.6), channel_id=1, source_target_pairs={{0,2},{2,4},{4,6},{6,7},{7,5},{5,3},{3,1},{1,0},{8,10},{10,12},{12... | collective-permute-start | bytes 1572872 | tf_op jit(solution)/shard_map/ppermute | solution.py:64
  480.8 47.2 %collective-permute-start.73 = (bf16[2,512,1408]{2,1,0:T(8,128)(2,1)}, bf16[2,512,1408]{2,1,0:T(8,128)(2,1)}, u32[]{:S(2)}, u32[]{:S(2)}) collective-permute-start(bf16[2,512,1408]{2,1,0:T(8,128)(2,1)} %fusion), channel_id=1, source_target_pairs={{0,8},{8,0},{16,24},{24,16},{1,9},{9,1},{17,25},{25,17},{2,10},{10... | collective-permute-start | bytes 8650760 | tf_op jit(solution)/shard_map/ppermute | solution.py:113
  484.7 37.5 %collective-permute-start.56 = (bf16[128,2048]{1,0:T(8,128)(2,1)S(1)}, bf16[128,2048]{1,0:T(8,128)(2,1)}, u32[]{:S(2)}, u32[]{:S(2)}) collective-permute-start(bf16[128,2048]{1,0:T(8,128)(2,1)S(1)} %get-tuple-element.29), channel_id=1, source_target_pairs={{2,0},{4,2},{6,4},{7,6},{5,7},{3,5},{1,3},{0,1},{10,8},{12,10},{14... | collective-permute-start | bytes 1572872 | tf_op jit(solution)/shard_map/ppermute | solution.py:67
  484.8 39.0 %collective-permute-start.52 = (bf16[128,2048]{1,0:T(8,128)(2,1)S(1)}, bf16[128,2048]{1,0:T(8,128)(2,1)}, u32[]{:S(2)}, u32[]{:S(2)}) collective-permute-start(bf16[128,2048]{1,0:T(8,128)(2,1)S(1)} %get-tuple-element.29), channel_id=1, source_target_pairs={{0,2},{2,4},{4,6},{6,7},{7,5},{5,3},{3,1},{1,0},{8,10},{10,12},{12... | collective-permute-start | bytes 1572872 | tf_op jit(solution)/shard_map/ppermute | solution.py:64
  533.5 73.4 %collective-permute-start.74 = (bf16[1,512,1408]{2,1,0:T(8,128)(2,1)}, bf16[1,512,1408]{2,1,0:T(8,128)(2,1)}, u32[]{:S(2)}, u32[]{:S(2)}) collective-permute-start(bf16[1,512,1408]{2,1,0:T(8,128)(2,1)} %dynamic-slice_convert_fusion.2), channel_id=1, source_target_pairs={{0,16},{8,24},{16,0},{24,8},{1,17},{9,25},{17,1},{25,9},{2,18},{10... | collective-permute-start | bytes 4325384 | tf_op jit(solution)/shard_map/ppermute | solution.py:113
  541.8 138.7 %collective-permute-start.76 = (bf16[1,176,2048]{2,1,0:T(8,128)(2,1)}, bf16[1,176,2048]{2,1,0:T(8,128)(2,1)}, u32[]{:S(2)}, u32[]{:S(2)}) collective-permute-start(bf16[1,176,2048]{2,1,0:T(8,128)(2,1)} %dynamic-slice_convert_fusion.4), channel_id=1, source_target_pairs={{0,16},{8,24},{16,0},{24,8},{1,17},{9,25},{17,1},{25,9},{2,18},{10... | collective-permute-start | bytes 2162696 | tf_op jit(solution)/shard_map/ppermute | solution.py:113
  576.2 28.0 %collective-permute-start.70 = (bf16[2,64,2048]{2,1,0:T(8,128)(2,1)S(1)}, bf16[2,64,2048]{2,1,0:T(8,128)(2,1)S(1)}, u32[]{:S(2)}, u32[]{:S(2)}) collective-permute-start(bf16[2,64,2048]{2,1,0:T(8,128)(2,1)S(1)} %fusion.18), channel_id=1, source_target_pairs={{0,8},{8,0},{16,24},{24,16},{1,9},{9,1},{17,25},{25,17},{2,10},{10... | collective-permute-start | bytes 1572872 | tf_op jit(solution)/shard_map/ppermute | solution.py:113
  601.9 23.0 %collective-permute-start.68 = (bf16[2,512,1024]{2,1,0:T(8,128)(2,1)}, bf16[2,512,1024]{2,1,0:T(8,128)(2,1)}, u32[]{:S(2)}, u32[]{:S(2)}) collective-permute-start(bf16[2,512,1024]{2,1,0:T(8,128)(2,1)} %fusion.1), channel_id=1, source_target_pairs={{0,8},{8,0},{16,24},{24,16},{1,9},{9,1},{17,25},{25,17},{2,10},{10... | collective-permute-start | bytes 6291464 | tf_op jit(solution)/shard_map/ppermute | solution.py:113
  606.9 29.6 %collective-permute-start.71 = (bf16[1,64,2048]{2,1,0:T(8,128)(2,1)}, bf16[1,64,2048]{2,1,0:T(8,128)(2,1)S(1)}, u32[]{:S(2)}, u32[]{:S(2)}) collective-permute-start(bf16[1,64,2048]{2,1,0:T(8,128)(2,1)} %dynamic-slice_convert_fusion.5), channel_id=1, source_target_pairs={{0,16},{8,24},{16,0},{24,8},{1,17},{9,25},{17,1},{25,9},{2,18},{10... | collective-permute-start | bytes 786440 | tf_op jit(solution)/shard_map/ppermute | solution.py:113
  612.5 52.2 %all-to-all-start.3 = ((bf16[8,64,1408]{2,1,0:T(8,128)(2,1)}), bf16[8,64,1408]{2,1,0:T(8,128)(2,1)}, u32[]{:S(2)}, u32[]{:S(2)}) async-start(bf16[8,64,1408]{2,1,0:T(8,128)(2,1)} %bitcast.60), calls=%async_computation.3 | async-start | bytes 2883584 | tf_op jit(solution)/shard_map/all_to_all | solution.py:124
  618.9 33.2 %collective-permute-start.66 = (bf16[128,2048]{1,0:T(8,128)(2,1)S(1)}, bf16[128,2048]{1,0:T(8,128)(2,1)S(1)}, u32[]{:S(2)}, u32[]{:S(2)}) collective-permute-start(bf16[128,2048]{1,0:T(8,128)(2,1)S(1)} %add_convert_fusion.3), channel_id=1, source_target_pairs={{0,2},{2,4},{4,6},{6,7},{7,5},{5,3},{3,1},{1,0},{8,10},{10,12},{12... | collective-permute-start | bytes 1572872 | tf_op jit(solution)/shard_map/ppermute | solution.py:64
  621.4 41.0 %collective-permute-start.62 = (bf16[128,2048]{1,0:T(8,128)(2,1)S(1)}, bf16[128,2048]{1,0:T(8,128)(2,1)S(1)}, u32[]{:S(2)}, u32[]{:S(2)}) collective-permute-start(bf16[128,2048]{1,0:T(8,128)(2,1)S(1)} %add_convert_fusion.5), channel_id=1, source_target_pairs={{2,0},{4,2},{6,4},{7,6},{5,7},{3,5},{1,3},{0,1},{10,8},{12,10},{14... | collective-permute-start | bytes 1572872 | tf_op jit(solution)/shard_map/ppermute | solution.py:67
  628.6 34.7 %collective-permute-start.69 = (bf16[1,512,1024]{2,1,0:T(8,128)(2,1)S(1)}, bf16[1,512,1024]{2,1,0:T(8,128)(2,1)S(1)}, u32[]{:S(2)}, u32[]{:S(2)}) collective-permute-start(bf16[1,512,1024]{2,1,0:T(8,128)(2,1)S(1)} %dynamic-slice_convert_fusion.3), channel_id=1, source_target_pairs={{0,16},{8,24},{16,0},{24,8},{1,17},{9,25},{17,1},{25,9},{2,18},{10... | collective-permute-start | bytes 3145736 | tf_op jit(solution)/shard_map/ppermute | solution.py:113
  637.4 45.5 %collective-permute-start.72 = (f32[64,2048]{1,0:T(8,128)}, f32[64,2048]{1,0:T(8,128)}, u32[]{:S(2)}, u32[]{:S(2)}) collective-permute-start(f32[64,2048]{1,0:T(8,128)} %add_bitcast_fusion.1), channel_id=1, source_target_pairs={{0,0},{1,4},{2,8},{3,12},{4,16},{5,20},{6,24},{7,28},{8,1},{9,5},{... | collective-permute-start | bytes 1572872 | tf_op jit(solution)/shard_map/ppermute | solution.py:147
  653.1 29.8 %collective-permute-start.67 = (bf16[128,2048]{1,0:T(8,128)(2,1)}, bf16[128,2048]{1,0:T(8,128)(2,1)}, u32[]{:S(2)}, u32[]{:S(2)}) collective-permute-start(bf16[128,2048]{1,0:T(8,128)(2,1)} %add_convert_fusion.2), channel_id=1, source_target_pairs={{0,2},{2,4},{4,6},{6,7},{7,5},{5,3},{3,1},{1,0},{8,10},{10,12},{12... | collective-permute-start | bytes 1572872 | tf_op jit(solution)/shard_map/ppermute | solution.py:64
  663.3 42.2 %collective-permute-start.63 = (bf16[128,2048]{1,0:T(8,128)(2,1)}, bf16[128,2048]{1,0:T(8,128)(2,1)}, u32[]{:S(2)}, u32[]{:S(2)}) collective-permute-start(bf16[128,2048]{1,0:T(8,128)(2,1)} %add_convert_fusion.4), channel_id=1, source_target_pairs={{2,0},{4,2},{6,4},{7,6},{5,7},{3,5},{1,3},{0,1},{10,8},{12,10},{14... | collective-permute-start | bytes 1572872 | tf_op jit(solution)/shard_map/ppermute | solution.py:67
  664.7 68.9 %all-to-all-start.2 = ((bf16[8,64,1024]{2,1,0:T(8,128)(2,1)}), bf16[8,64,1024]{2,1,0:T(8,128)(2,1)}, u32[]{:S(2)}, u32[]{:S(2)}) async-start(bf16[8,64,1024]{2,1,0:T(8,128)(2,1)} %bitcast.287), calls=%async_computation.2 | async-start | bytes 2097152 | tf_op jit(solution)/shard_map/all_to_all | solution.py:124
  (131 other events, 1677.8 us)
Sparse Core Ops, SparseCore 0:
  45.1 33.5 all-gather.4
  91.2 51.5 all-gather.6
  144.4 31.3 all-gather.8

commit v2 on v1

--- a/solution.py
+++ b/solution.py
@@ -1,8 +1,11 @@
+import functools
 import math
 
 import jax
 import jax.numpy as jnp
 from jax import lax
+from jax.experimental import pallas as pl
+from jax.experimental.pallas import tpu as pltpu
 from jax.sharding import PartitionSpec as P
 
 H = 16
@@ -13,6 +16,9 @@
 TEAM = H // HEADS_DEV
 RING = (0, 2, 4, 6, 7, 5, 3, 1)
 PLACE = tuple(RING.index(i) for i in range(TEAM))
+ORDER = (0, 1, 7, 2, 6, 3, 5, 4)
+CHUNK = 64
+MESH = pl.DeviceIdType.MESH
 
 epsilon = 1e-06
 layer_number = 14
@@ -76,9 +82,12 @@
         blocks[TEAM // 2] = jnp.concatenate(
             [self.to_next(forth[:half]), self.to_previous(back[half:])], axis=0
         )
-        return blocks
-
-    def ring_reduce(self, part):
+        return [blocks[k] for k in ORDER]
+
+    def ring_reduce(self, slot_part):
+        def part(k):
+            return slot_part(ORDER.index(k))
+
         middle = part(TEAM // 2)
         half = middle.shape[0] // 2
         back = self.to_previous(middle[:half].astype(low))
@@ -147,11 +156,334 @@
         return lax.ppermute(x, ("dp", "seq"), pairs)
 
 
+def middle_kernel(
+    model_width,
+    hidden,
+    squares_ref,
+    raw_ref,
+    tokens_ref,
+    cotangents_hbm,
+    output_ref,
+    mlp_hbm,
+    down_hbm,
+    middle_ref,
+    middle_grad_ref,
+    second_hbm,
+    hidden_hbm,
+    pairs_hbm,
+    gathered_hbm,
+    coefficients_ref,
+    cotangents,
+    mlp,
+    down,
+    second,
+    hiddens,
+    pairs,
+    gathered,
+    part,
+    proj,
+    own_squares,
+    stage,
+    landed,
+    load_sems,
+    store_sems,
+    gather_send,
+    gather_recv,
+    reduce_send,
+    reduce_recv,
+    square_send,
+    square_recv,
+    coef_send,
+    coef_recv,
+):
+    dp, seq = lax.axis_index("dp"), lax.axis_index("seq")
+    place = seq % TEAM
+    base = seq - place
+    spot = place // 2 + (place % 2) * (TEAM - 1 - 2 * (place // 2))
+    rows = tokens_ref.shape[0]
+
+    def device(steps):
+        at = (spot + TEAM + steps) % TEAM
+        side = at // (TEAM // 2)
+        return (dp, base + 2 * (at + side * (TEAM - 1 - 2 * at)) + side)
+
+    ahead, behind = device(1), device(-1)
+    barrier = pltpu.get_barrier_semaphore()
+    for k in range(1, TEAM):
+        pl.semaphore_signal(barrier, inc=1, device_id=device(k), device_id_type=MESH)
+    pl.semaphore_wait(barrier, TEAM - 1)
+
+    def remote(src, dst, send, recv, target):
+        return pltpu.make_async_remote_copy(
+            src, dst, send, recv, device_id=target, device_id_type=MESH
+        )
+
+    def slab(ref, slot, chunk):
+        return ref.at[pl.ds(slot * rows + chunk * CHUNK, CHUNK)]
+
+    loads = [
+        pltpu.make_async_copy(src, dst, load_sems.at[i])
+        for i, (src, dst) in enumerate(
+            ((mlp_hbm, mlp), (down_hbm, down), (cotangents_hbm, cotangents))
+        )
+    ]
+    for load in loads:
+        load.start()
+
+    square_copies = [
+        remote(
+            squares_ref.at[ORDER.index(k)],
+            own_squares.at[k],
+            square_send.at[k],
+            square_recv.at[k],
+            device(-k),
+        )
+        for k in range(1, TEAM)
+    ]
+    for copy in square_copies:
+        copy.start()
+
+    def gather_copy(buffer, way, step, chunk):
+        source = max(2 * (step - 1) - 1 + way, 0)
+        target = 2 * step - 1 + way if step < TEAM // 2 else TEAM - 1
+        return remote(
+            slab(buffer, source, chunk),
+            slab(buffer, target, chunk),
+            gather_send.at[way, step - 1, chunk],
+            gather_recv.at[way, step - 1, chunk],
+            behind if way else ahead,
+        )
+
+    def gather_chunks(way, step):
+        return (0, 1) if step < TEAM // 2 else (way,)
+
+    def gather_start(buffer):
+        for chunk in range(2):
+            for way in range(2):
+                gather_copy(buffer, way, 1, chunk).start()
+
+    def gather_step(buffer, step):
+        for chunk in range(2):
+            for way in range(2):
+                if chunk in gather_chunks(way, step):
+                    gather_copy(buffer, way, step, chunk).wait_recv()
+                    if step < TEAM // 2 and chunk in gather_chunks(way, step + 1):
+                        gather_copy(buffer, way, step + 1, chunk).start()
+
+    def gather_end(buffer):
+        for step in range(1, TEAM // 2 + 1):
+            for way in range(2):
+                for chunk in gather_chunks(way, step):
+                    gather_copy(buffer, way, step, chunk).wait_send()
+
+    def reduce_copy(way, step, chunk):
+        return remote(
+            stage.at[way, step, chunk],
+            landed.at[way, step, chunk],
+            reduce_send.at[way, step, chunk],
+            reduce_recv.at[way, step, chunk],
+            ahead if way else behind,
+        )
+
+    def ring_sum(fill):
+        last = TEAM // 2 - 1
+        fill(TEAM - 1, 1)
+        for way in range(2):
+            stage[way, 0, way] = part[way * CHUNK : (way + 1) * CHUNK].astype(low)
+            reduce_copy(way, 0, way).start()
+        for step in range(1, last + 1):
+            slot = 2 * (last - step) + 1
+            fill(slot, 2)
+            for turn in range(2):
+                for way in range(2):
+                    chunk = 1 - way if turn == 0 else way
+                    start = way * rows + chunk * CHUNK
+                    value = part[start : start + CHUNK]
+                    if step > 1 or chunk == way:
+                        reduce_copy(way, step - 1, chunk).wait_recv()
+                        value = value + landed[way, step - 1, chunk].astype(wide)
+                    stage[way, step, chunk] = value.astype(low)
+                    reduce_copy(way, step, chunk).start()
+        fill(0, 1)
+        for chunk in range(2):
+            at = pl.ds(chunk * CHUNK, CHUNK)
+            for way in range(2):
+                reduce_copy(way, last, chunk).wait_recv()
+            part[at] = (
+                part[at]
+                + landed[0, last, chunk].astype(wide)
+                + landed[1, last, chunk].astype(wide)
+            )
+        for way in range(2):
+            reduce_copy(way, 0, way).wait_send()
+            for step in range(1, last + 1):
+                for chunk in range(2):
+                    reduce_copy(way, step, chunk).wait_send()
+
+    tile = 512
+
+    def fill_output(slot, count):
+        left = raw_ref[slot * rows : (slot + count) * rows]
+
+        @pl.loop(0, model_width // tile)
+        def _(i):
+            at = pl.ds(pl.multiple_of(i * tile, tile), tile)
+            part[: count * rows, at] = dot(left, output_ref[:, at])
+
+    def fill_pairs(slot, count):
+        left = pairs[slot * rows : (slot + count) * rows]
+
+        @pl.loop(0, model_width // tile)
+        def _(i):
+            at = pl.ds(pl.multiple_of(i * tile, tile), tile)
+            part[: count * rows, at] = dot_t(left, mlp[at])
+
+    eye = lax.broadcasted_iota(jnp.int32, (rows, rows), 0) == lax.broadcasted_iota(
+        jnp.int32, (rows, rows), 1
+    )
+
+    def column(row):
+        return jnp.sum(jnp.where(eye, jnp.broadcast_to(row, (rows, rows)), 0.0), axis=1, keepdims=True)
+
+    def row_of(column):
+        return jnp.sum(jnp.where(eye, jnp.broadcast_to(column, (rows, rows)), 0.0), axis=0, keepdims=True)
+
+    ring_sum(fill_output)
+    total = squares_ref[0, 0:1]
+    for copy in square_copies:
+        copy.wait_recv()
+    for k in range(1, TEAM):
+        total = total + own_squares[k, 0:1]
+    scale = lax.rsqrt(column(total) / model_width + epsilon)
+    proj[...] = part[:rows] * scale
+    middle_ref[...] = tokens_ref[...].astype(wide) + proj[...]
+    second[:rows] = normalize(middle_ref[...]).astype(low)
+    gather_start(second)
+
+    def units(slot, count):
+        at = pl.ds(slot * rows, count * rows)
+        pair = dot(second[at], mlp[...])
+        turned = pltpu.roll(pair, hidden, 1)
+        hiddens[at] = (pair * turned)[:, : hiddens.shape[1]].astype(low)
+        above = dot_t(cotangents[at], down[...])
+        above = jnp.concatenate(
+            [above, jnp.zeros((count * rows, 2 * hidden - above.shape[1]), wide)], axis=1
+        )
+        pairs[at] = ((above + pltpu.roll(above, hidden, 1)) * turned).astype(low)
+
+    for load in loads:
+        load.wait()
+    units(0, 1)
+    for step in range(1, TEAM // 2):
+        gather_step(second, step)
+        units(2 * step - 1, 2)
+    gather_step(second, TEAM // 2)
+    units(TEAM - 1, 1)
+    stores = [
+        pltpu.make_async_copy(src, dst, store_sems.at[i])
+        for i, (src, dst) in enumerate(
+            (
+                (second, second_hbm),
+                (hiddens, hidden_hbm),
+                (pairs, pairs_hbm),
+                (gathered, gathered_hbm),
+            )
+        )
+    ]
+    for store in stores[:3]:
+        store.start()
+
+    ring_sum(fill_pairs)
+    middle_grad_ref[...] = cotangents[:rows].astype(wide) + norm_back(middle_ref[...], part[:rows])
+    middle_low = middle_grad_ref[...].astype(low)
+    gathered[:rows] = middle_low
+    gather_start(gathered)
+    inner = jnp.sum(middle_low.astype(wide) * proj[...], axis=1, keepdims=True) / model_width
+    coefficients_ref[0, 0:1] = row_of(scale)
+    coefficients_ref[0, 1:2] = row_of(scale * scale * inner)
+    coefficients_ref[0, 2:8] = jnp.zeros((6, rows), wide)
+    coef_copies = [
+        remote(
+            coefficients_ref.at[0],
+            coefficients_ref.at[ORDER.index(k)],
+            coef_send.at[k],
+            coef_recv.at[k],
+            device(k),
+        )
+        for k in range(1, TEAM)
+    ]
+    for copy in coef_copies:
+        copy.start()
+    for step in range(1, TEAM // 2 + 1):
+        gather_step(gathered, step)
+    stores[3].start()
+    gather_end(second)
+    gather_end(gathered)
+    for copy in coef_copies:
+        copy.wait()
+    for copy in square_copies:
+        copy.wait_send()
+    for store in stores:
+        store.wait()
+
+
+def middle_call(plan, squares, raw, tokens, cotangents, output_w, mlp_w, down_w):
+    rows, width = tokens.shape
+    team_rows = rows * TEAM
+    hidden = mlp_w.shape[1] // 2
+    padded = down_w.shape[0]
+    vmem, anywhere = pl.BlockSpec(memory_space=pltpu.VMEM), pl.BlockSpec(memory_space=pl.ANY)
+    steps = TEAM // 2
+    flops = 2 * team_rows * width * (2 * raw.shape[1] + 4 * hidden + padded)
+    return pl.pallas_call(
+        functools.partial(middle_kernel, width, hidden),
+        out_shape=(
+            jax.ShapeDtypeStruct((rows, width), wide),
+            jax.ShapeDtypeStruct((rows, width), wide),
+            jax.ShapeDtypeStruct((team_rows, width), low),
+            jax.ShapeDtypeStruct((team_rows, padded), low),
+            jax.ShapeDtypeStruct((team_rows, 2 * hidden), low),
+            jax.ShapeDtypeStruct((team_rows, width), low),
+            jax.ShapeDtypeStruct((TEAM, 8, rows), wide),
+        ),
+        in_specs=[vmem, vmem, vmem, anywhere, vmem, anywhere, anywhere],
+        out_specs=(vmem, vmem, anywhere, anywhere, anywhere, anywhere, vmem),
+        scratch_shapes=[
+            pltpu.VMEM((team_rows, width), low),
+            pltpu.VMEM((width, 2 * hidden), low),
+            pltpu.VMEM((padded, width), low),
+            pltpu.VMEM((team_rows, width), low),
+            pltpu.VMEM((team_rows, padded), low),
+            pltpu.VMEM((team_rows, 2 * hidden), low),
+            pltpu.VMEM((team_rows, width), low),
+            pltpu.VMEM((2 * rows, width), wide),
+            pltpu.VMEM((rows, width), wide),
+            pltpu.VMEM((TEAM, 8, rows), wide),
+            pltpu.VMEM((2, steps, 2, CHUNK, width), low),
+            pltpu.VMEM((2, steps, 2, CHUNK, width), low),
+            pltpu.SemaphoreType.DMA((3,)),
+            pltpu.SemaphoreType.DMA((4,)),
+            pltpu.SemaphoreType.DMA((2, steps, 2)),
+            pltpu.SemaphoreType.DMA((2, steps, 2)),
+            pltpu.SemaphoreType.DMA((2, steps, 2)),
+            pltpu.SemaphoreType.DMA((2, steps, 2)),
+            pltpu.SemaphoreType.DMA((TEAM,)),
+            pltpu.SemaphoreType.DMA((TEAM,)),
+            pltpu.SemaphoreType.DMA((TEAM,)),
+            pltpu.SemaphoreType.DMA((TEAM,)),
+        ],
+        compiler_params=pltpu.CompilerParams(
+            collective_id=0, has_side_effects=True, vmem_limit_bytes=60 * 2**20
+        ),
+        cost_estimate=pl.CostEstimate(flops=flops, bytes_accessed=60 * 2**20, transcendentals=0),
+    )(squares, raw, tokens, cotangents, output_w, mlp_w, down_w)
+
+
 def decay_tables(plan, lengths, long_rows, short_rows):
     team_place = lax.axis_index("seq") % TEAM
     sub = lax.axis_index("seq") // TEAM
     spot = jnp.asarray(PLACE, jnp.int32)[team_place]
-    blocks = jnp.asarray(RING, jnp.int32)[(spot + TEAM - jnp.arange(TEAM)) % TEAM]
+    blocks = jnp.asarray(RING, jnp.int32)[(spot + TEAM - jnp.asarray(ORDER)) % TEAM]
     rates = head_rates((team_place * HEADS_DEV + jnp.arange(HEADS_DEV)).astype(wide))
     ends = jnp.cumsum(lengths)
     starts = ends - lengths
@@ -277,42 +609,23 @@
         state = carried(plan, carry, bmm(key_out, value, 2, 2), False).astype(low)
         heads_out = heads_out + bmm(query, state, 3, 2) * into
     heads_out = from_heads(heads_out)
-    ring_spot = jnp.asarray(PLACE, jnp.int32)[lax.axis_index("seq") % TEAM]
-    from_ring = (ring_spot + TEAM - jnp.asarray(PLACE, jnp.int32)) % TEAM
-    to_ring = jnp.asarray(RING, jnp.int32)[(ring_spot + TEAM - jnp.arange(TEAM)) % TEAM]
-    squares = lax.psum(
-        jnp.sum(heads_out * heads_out, axis=1).reshape(TEAM, row_count)[from_ring],
-        "seq",
-        axis_index_groups=plan.team_groups,
-    )
-    scales = lax.rsqrt(squares[to_ring] / model_width + epsilon)
-    scale_rows = scales.reshape(team_tokens, 1)
+    squares = jnp.sum(heads_out * heads_out, axis=1).reshape(TEAM, 1, row_count)
     gated_raw = (heads_out * z_unit).astype(low)
 
     def rows(x, k):
         return x[k * row_count : (k + 1) * row_count]
 
-    attn_proj = plan.ring_reduce(lambda k: dot(rows(gated_raw, k), output_w)) * scales[0][:, None]
-    middle = inputs + attn_proj
-
-    cotangents = plan.ring_gather(cotangent)
-    second = plan.ring_gather(normalize(middle).astype(low))
-    hidden_blocks, pair_grads = [], []
-    for block, above in zip(second, cotangents):
-        pair = dot(block, mlp_w)
-        gate_val, up_val = pair[:, :hidden], pair[:, hidden:]
-        hidden_grad = dot_t(above, down_w)
-        hidden_blocks.append((gate_val * up_val).astype(low))
-        pair_grads.append(
-            jnp.concatenate([hidden_grad * up_val, hidden_grad * gate_val], axis=1).astype(low)
-        )
-    second_grad = plan.ring_reduce(lambda k: dot_t(pair_grads[k], mlp_w))
-    mixed = (middle + plan.ring_reduce(lambda k: dot(hidden_blocks[k], down_w))).astype(low)
-    cotangent_all = jnp.concatenate(cotangents, axis=0)
-    grad_down = plan.across_sum(outer(jnp.concatenate(hidden_blocks, axis=0), cotangent_all))
-    grad_pair = plan.across_sum(
-        outer(jnp.concatenate(second, axis=0), jnp.concatenate(pair_grads, axis=0))
-    )
+    cotangents = jnp.concatenate(plan.ring_gather(cotangent), axis=0)
+    spare = -hidden % 128
+    down_w = jnp.pad(down_w, ((0, spare), (0, 0)))
+    middle, middle_grad, second, hidden_low, pair_grads, middle_all, coefficients = middle_call(
+        plan, jnp.broadcast_to(squares, (TEAM, 8, row_count)), gated_raw, tokens, cotangents, output_w, mlp_w, down_w
+    )
+    scale_rows = coefficients[:, 0].reshape(team_tokens, 1)
+    inner_rows = coefficients[:, 1].reshape(team_tokens, 1)
+    mixed = (middle + plan.ring_reduce(lambda i: dot(rows(hidden_low, i), down_w))).astype(low)
+    grad_down = plan.across_sum(outer(hidden_low, cotangents)[:hidden])
+    grad_pair = plan.across_sum(outer(second, pair_grads))
 
     def from_units(x):
         x = x.reshape(TEAM, weight_rows, groups, piece).transpose(1, 2, 0, 3)
@@ -322,19 +635,10 @@
     grad_gate = from_units(grad_pair[:, :, :hidden])
     grad_up = from_units(grad_pair[:, :, hidden:])
 
-    middle_grad = cotangent.astype(wide) + norm_back(middle, second_grad)
-    middle_low = middle_grad.astype(low)
-    inner = jnp.sum(middle_low.astype(wide) * attn_proj, axis=1) / model_width
-    inner = (scales[0] * scales[0] * inner).reshape(1, row_count)
-    middle_blocks = plan.ring_gather(middle_low)
-    inner_all = lax.all_gather(
-        inner, "seq", axis=0, tiled=True, axis_index_groups=plan.team_groups
-    )
-    inner_rows = inner_all[to_ring].reshape(team_tokens, 1)
-    gated_grad = jnp.concatenate([dot_t(block, output_w) for block in middle_blocks], axis=0)
+    gated_grad = dot_t(middle_all, output_w)
     normed_heads = heads_out * scale_rows
     gated = (normed_heads * z_unit).astype(low)
-    grad_output = plan.across_sum(outer(gated, jnp.concatenate(middle_blocks, axis=0)))
+    grad_output = plan.across_sum(outer(gated, middle_all))
     grad_output = plan.team_rows_back(grad_output)
     unit_grad = (gated_grad * normed_heads).astype(low)
     heads_grad = to_heads(

time: 758 us -> 726 us (0.958)
  Pallas kernels: 0 us -> 188 us
  blocking collectives: 107 us -> 32.9 us
  starting transfers between devices: 155 us -> 90.6 us
  matrix products: 128 us -> 72.6 us
  other arithmetic: 62.8 us -> 48.8 us
  local copies, waits for them, and re-layouts: 99 us -> 87.8 us
    pallas_call x0 -> x1, Pallas kernels: none -> 188 us  [middle_call(): pl.pallas_call(functools.partial(middle_kernel, width, hidden), out_shape...]
    ppermute x32 -> x16, waiting for transfers between devices: 123 us -> 48.5 us  [to_previous(): return lax.ppermute(x, 'seq', self.down)]
    all_to_all x2 -> x3, waiting for transfers between devices: 0.01 us -> 54.8 us  [swap(): lax.all_to_all(x, 'seq', 0, 0, tiled=True, axis_index_groups=self.team_gr...]
    ppermute x32 -> x16, starting transfers between devices: 83.6 us -> 29.2 us  [to_next(): return lax.ppermute(x, 'seq', self.up)]
    all_to_all x2 -> x1, blocking collectives: 70.8 us -> 32.9 us  [swap(): lax.all_to_all(x, 'seq', 0, 0, tiled=True, axis_index_groups=self.team_gr...]
    dot_general x32 -> x9, matrix products: 55.8 us -> 18.3 us  [dot_t(): lax.dot_general(left, right, (((1,), (1,)), ((), ())), preferred_element_...]
    ppermute x8, waiting for transfers between devices: 0.02 us -> 33.1 us  [across_sum(): lax.ppermute(send.astype(low), 'dp', [(i, i ^ bit) for i in range(count)])]
    dot_general x32 -> x16, matrix products: 43.5 us -> 17.1 us  [dot(): return jnp.dot(left, right, preferred_element_type=wide)]
  transfers between devices with their start and end apart: 82 -> 51, of which waited for: 24 -> 15; matrix products, arithmetic and copies ran while one was open for 36% -> 21% of each run, Pallas kernels for 0% -> 0%
where the time goes in v2:
time: 726 us; the launch traced here: 716 us
  Pallas kernels  188 us (26%)
  waiting for transfers between devices  178 us (25%)
  starting transfers between devices  90.6 us (12%)
  local copies, waits for them, and re-layouts  87.8 us (12%)
  matrix products  72.6 us (10%)
  other arithmetic  48.8 us (7%)
  blocking collectives  32.9 us (5%)
  between operations  16.3 us (2%)
    pallas_call x1, Pallas kernels, middle_call(): pl.pallas_call(functools.partial(middle_kernel, width, hidden), out_shape...  188 us
    all_to_all x3, waiting for transfers between devices, swap(): lax.all_to_all(x, 'seq', 0, 0, tiled=True, axis_index_groups=self.team_gr...  54.8 us
    ppermute x16, waiting for transfers between devices, to_previous(): return lax.ppermute(x, 'seq', self.down)  48.5 us
    ppermute x16, waiting for transfers between devices, to_next(): return lax.ppermute(x, 'seq', self.up)  41 us
    unnamed x127, local copies, waits for them, and re-layouts  34.1 us
    ppermute x8, waiting for transfers between devices, across_sum(): lax.ppermute(send.astype(low), 'dp', [(i, i ^ bit) for i in range(count)])  33.1 us
    all_to_all x1, blocking collectives, swap(): lax.all_to_all(x, 'seq', 0, 0, tiled=True, axis_index_groups=self.team_gr...  32.9 us
    dot_general x4, matrix products, outer(): lax.dot_general(left, right, (((0,), (0,)), ((), ())), preferred_element_...  29.5 us
  transfers between devices with their start and end apart: 51, of which 15 were waited for; matrix products, arithmetic and copies ran while one was open for 21% of the time, Pallas kernels for 0%

profile of v2, /device:TPU:0, one launch (start us, length us, event | category | flops | bytes accessed | tf_op | source)
XLA Modules:
  0.0 715.5 jit_solution(5653769851705572387)
XLA Ops:
  12.8 32.9 %all_to_all.20 = bf16[8,64,1024]{2,1,0:T(8,128)(2,1)} all-to-all(bf16[8,64,1024]{2,1,0:T(8,128)(2,1)S(1)} %copy.120), channel_id=1, replica_groups=mesh['dp'=4,'seq'=8] {'seq'}, dimensions={0} | all-to-all | bytes 2097152 | tf_op jit(solution)/shard_map/all_to_all | solution.py:133
  47.7 3.6 collective-permute-start.16
  53.2 4.9 collective-permute-start.18
  61.4 3.0 reshape.289
  67.4 4.6 all-to-all-start.1
  82.7 6.4 collective-permute-start.1
  90.5 38.1 %all-to-all-done.1 = bf16[8,64,1408]{2,1,0:T(8,128)(2,1)S(1)} async-done(((bf16[8,64,1408]{2,1,0:T(8,128)(2,1)}), bf16[8,64,1408]{2,1,0:T(8,128)(2,1)S(1)}, u32[]{:S(2)}, u32[]{:S(2)}) %all-to-all-start.1) | async-done | bytes 1441824 | tf_op jit(solution)/shard_map/all_to_all | solution.py:133
  131.0 8.3 %collective-permute-start.10 = (bf16[128,2048]{1,0:T(8,128)(2,1)}, bf16[128,2048]{1,0:T(8,128)(2,1)S(1)}, u32[]{:S(2)}, u32[]{:S(2)}) collective-permute-start(bf16[128,2048]{1,0:T(8,128)(2,1)} %collective-permute-done.8), channel_id=1, source_target_pairs={{0,2},{2,4},{4,6},{6,7},{7,5},{5,3},{3,1},{1,0},{8,10},{10,12},{12... | collective-permute-start | bytes 1572872 | tf_op jit(solution)/shard_map/ppermute | solution.py:70
  139.3 3.9 collective-permute-start.11
  145.2 3.8 collective-permute-start.2
  158.3 8.0 %collective-permute-done.3 = bf16[128,2048]{1,0:T(8,128)(2,1)S(1)} collective-permute-done((bf16[128,2048]{1,0:T(8,128)(2,1)S(1)}, bf16[128,2048]{1,0:T(8,128)(2,1)S(1)}, u32[]{:S(2)}, u32[]{:S(2)}) %collective-permute-start.3) | collective-permute-done | bytes 524320 | tf_op jit(solution)/shard_map/ppermute | solution.py:73
  168.7 2.8 collective-permute-start.4
  174.9 3.2 collective-permute-done.12
  180.3 8.4 %collective-permute-done.5 = bf16[128,2048]{1,0:T(8,128)(2,1)S(1)} collective-permute-done((bf16[128,2048]{1,0:T(8,128)(2,1)S(1)}, bf16[128,2048]{1,0:T(8,128)(2,1)S(1)}, u32[]{:S(2)}, u32[]{:S(2)}) %collective-permute-start.5) | collective-permute-done | bytes 524320 | tf_op jit(solution)/shard_map/ppermute | solution.py:73
  188.7 2.8 collective-permute-start.7
  191.5 2.8 collective-permute-start.6
  201.5 3.9 pad.5.down_hbm
  205.4 3.1 convolution_dynamic-update-slice_fusion.7
  220.4 3.1 multiply_convert_fusion.1
  230.1 188.5 %shard_map.213 = (f32[128,2048]{1,0:T(8,128)}, f32[128,2048]{1,0:T(8,128)}, bf16[1024,2048]{1,0:T(8,128)(2,1)}, bf16[1024,768]{1,0:T(8,128)(2,1)}, bf16[1024,140...) custom-call(f32[8,8,128]{2,1,0:T(8,128)} %broadcast_in_dim.20.squares_ref, ...), custom_call_target="tpu_custom_call" | custom-call | flops 17179869184 | bytes 62914560 | tf_op jit(solution)/shard_map/pallas_call | solution.py:438
  419.5 5.3 fusion.24
  424.9 3.6 fusion.22
  436.7 5.1 fusion.8
  452.4 6.5 fusion.62
  458.9 12.6 %fusion.86 = f32[2048,1408]{1,0:T(8,128)S(1)} fusion(bf16[1024,2048]{1,0:T(8,128)(2,1)} %get-tuple-element.22, bf16[1024,1408]{1,0:T(8,128)(2,1)} %get-tuple-element.23), kind=kOutput, calls=%fused_computation.206 | convolution fusion | flops 5905580032 | bytes 18612224 | tf_op jit(solution)/shard_map/dot_general | solution.py:49
  486.6 3.1 fusion.10
  498.6 18.9 %collective-permute-done.33 = bf16[128,2048]{1,0:T(8,128)(2,1)S(1)} collective-permute-done((bf16[128,2048]{1,0:T(8,128)(2,1)S(1)}, bf16[128,2048]{1,0:T(8,128)(2,1)S(1)}, u32[]{:S(2)}, u32[]{:S(2)}) %collective-permute-start.33) | collective-permute-done | bytes 524320 | tf_op jit(solution)/shard_map/ppermute | solution.py:70
  518.0 4.1 collective-permute-start.39
  522.3 5.3 collective-permute-done.39
  531.8 10.6 %collective-permute-done.34 = bf16[128,2048]{1,0:T(8,128)(2,1)S(1)} collective-permute-done((bf16[128,2048]{1,0:T(8,128)(2,1)S(1)}, bf16[128,2048]{1,0:T(8,128)(2,1)S(1)}, u32[]{:S(2)}, u32[]{:S(2)}) %collective-permute-start.34) | collective-permute-done | bytes 524320 | tf_op jit(solution)/shard_map/ppermute | solution.py:70
  544.0 6.8 collective-permute-done.26
  554.7 3.2 bitcast_add_fusion.1
  558.2 31.6 %collective-permute-done.22 = bf16[128,2048]{1,0:T(8,128)(2,1)S(1)} collective-permute-done((bf16[128,2048]{1,0:T(8,128)(2,1)S(1)}, bf16[128,2048]{1,0:T(8,128)(2,1)S(1)}, u32[]{:S(2)}, u32[]{:S(2)}) %collective-permute-start.22) | collective-permute-done | bytes 524320 | tf_op jit(solution)/shard_map/ppermute | solution.py:73
  600.8 12.0 %collective-permute-done.37 = bf16[1,512,1024]{2,1,0:T(8,128)(2,1)S(1)} collective-permute-done((bf16[1,512,1024]{2,1,0:T(8,128)(2,1)S(1)}, bf16[1,512,1024]{2,1,0:T(8,128)(2,1)S(1)}, u32[]{:S(2)}, u32[]{:S(2)}) %collective-permute-start.37) | collective-permute-done | bytes 1048608 | tf_op jit(solution)/shard_map/ppermute | solution.py:122
  614.1 4.7 all-to-all-start.2
  623.4 2.8 bitcast_add_fusion.2
  628.8 15.8 %collective-permute-done.42 = bf16[1,512,1408]{2,1,0:T(8,128)(2,1)} collective-permute-done((bf16[1,512,1408]{2,1,0:T(8,128)(2,1)}, bf16[1,512,1408]{2,1,0:T(8,128)(2,1)}, u32[]{:S(2)}, u32[]{:S(2)}) %collective-permute-start.42) | collective-permute-done | bytes 1441824 | tf_op jit(solution)/shard_map/ppermute | solution.py:122
  644.6 2.8 add_convert_fusion
  647.4 6.0 all-to-all-start.3
  655.9 3.1 fusion.17
  660.0 2.7 fusion.16
  669.9 16.8 %all-to-all-done.3 = bf16[8,64,1408]{2,1,0:T(8,128)(2,1)} async-done(((bf16[8,64,1408]{2,1,0:T(8,128)(2,1)}), bf16[8,64,1408]{2,1,0:T(8,128)(2,1)}, u32[]{:S(2)}, u32[]{:S(2)}) %all-to-all-start.3) | async-done | bytes 1441824 | tf_op jit(solution)/shard_map/all_to_all | solution.py:133
  686.7 3.5 slice_convert_fusion.1
  690.2 3.0 reshape.305
  693.2 2.5 copy.141
  695.7 3.3 reshape.303
  699.0 3.0 reshape.304
  704.6 3.3 reshape.302
  (329 shorter events, 161.1 us)
Async XLA Ops:
  7.2 194.3 %all-gather.8.cloned.1.call-start = ((), (), s32[]{:S(2)}) async-start(), calls=%async_computation.6 | async-start | bytes 3604480 | tf_op jit(solution)/shard_map/all_gather | solution.py:109
  7.9 197.5 %all-gather.4.cloned.1.call-start = ((), (), s32[]{:S(2)}) async-start(), calls=%async_computation.4 | async-start | bytes 5242880 | tf_op jit(solution)/shard_map/all_gather | solution.py:109
  45.7 35.0 %collective-permute-start.17 = (bf16[64,2048]{1,0:T(8,128)(2,1)}, bf16[64,2048]{1,0:T(8,128)(2,1)}, u32[]{:S(2)}, u32[]{:S(2)}) collective-permute-start(bf16[64,2048]{1,0:T(8,128)(2,1)} %param.21), channel_id=1, source_target_pairs={{1,0},{5,1},{9,2},{13,3},{17,4},{21,5},{25,6},{29,7},{2,8},{6,9},{... | collective-permute-start | bytes 786440 | tf_op jit(solution)/shard_map/ppermute | solution.py:143
  47.7 35.1 %collective-permute-start.16 = (bf16[64,2048]{1,0:T(8,128)(2,1)}, bf16[64,2048]{1,0:T(8,128)(2,1)}, u32[]{:S(2)}, u32[]{:S(2)}) collective-permute-start(bf16[64,2048]{1,0:T(8,128)(2,1)} %param.21), channel_id=1, source_target_pairs={{0,0},{4,1},{8,2},{12,3},{16,4},{20,5},{24,6},{28,7},{1,8},{5,9},{... | collective-permute-start | bytes 786440 | tf_op jit(solution)/shard_map/ppermute | solution.py:143
  51.3 37.9 %collective-permute-start.19 = (bf16[64,2048]{1,0:T(8,128)(2,1)}, bf16[64,2048]{1,0:T(8,128)(2,1)}, u32[]{:S(2)}, u32[]{:S(2)}) collective-permute-start(bf16[64,2048]{1,0:T(8,128)(2,1)} %param.21), channel_id=1, source_target_pairs={{3,0},{7,1},{11,2},{15,3},{19,4},{23,5},{27,6},{31,7},{0,8},{4,9},... | collective-permute-start | bytes 786440 | tf_op jit(solution)/shard_map/ppermute | solution.py:143
  53.2 36.0 %collective-permute-start.18 = (bf16[64,2048]{1,0:T(8,128)(2,1)}, bf16[64,2048]{1,0:T(8,128)(2,1)}, u32[]{:S(2)}, u32[]{:S(2)}) collective-permute-start(bf16[64,2048]{1,0:T(8,128)(2,1)} %param.21), channel_id=1, source_target_pairs={{2,0},{6,1},{10,2},{14,3},{18,4},{22,5},{26,6},{30,7},{3,8},{7,9},... | collective-permute-start | bytes 786440 | tf_op jit(solution)/shard_map/ppermute | solution.py:143
  58.1 72.9 %collective-permute-start.8 = (bf16[128,2048]{1,0:T(8,128)(2,1)}, bf16[128,2048]{1,0:T(8,128)(2,1)}, u32[]{:S(2)}, u32[]{:S(2)}) collective-permute-start(bf16[128,2048]{1,0:T(8,128)(2,1)} %param.15), channel_id=1, source_target_pairs={{0,2},{2,4},{4,6},{6,7},{7,5},{5,3},{3,1},{1,0},{8,10},{10,12},{12... | collective-permute-start | bytes 1572872 | tf_op jit(solution)/shard_map/ppermute | solution.py:70
  67.4 61.1 %all-to-all-start.1 = ((bf16[8,64,1408]{2,1,0:T(8,128)(2,1)}), bf16[8,64,1408]{2,1,0:T(8,128)(2,1)S(1)}, u32[]{:S(2)}, u32[]{:S(2)}) async-start(bf16[8,64,1408]{2,1,0:T(8,128)(2,1)} %pad_maximum_fusion.1), calls=%async_computation.1 | async-start | bytes 2883584 | tf_op jit(solution)/shard_map/all_to_all | solution.py:133
  72.0 157.5 %all-gather.6.cloned.1.call-start = ((), (), s32[]{:S(2)}) async-start(), calls=%async_computation.5 | async-start | bytes 7208960 | tf_op jit(solution)/shard_map/all_gather | solution.py:109
  80.8 58.5 %collective-permute-start.9 = (bf16[128,2048]{1,0:T(8,128)(2,1)}, bf16[128,2048]{1,0:T(8,128)(2,1)}, u32[]{:S(2)}, u32[]{:S(2)}) collective-permute-start(bf16[128,2048]{1,0:T(8,128)(2,1)} %param.15), channel_id=1, source_target_pairs={{2,0},{4,2},{6,4},{7,6},{5,7},{3,5},{1,3},{0,1},{10,8},{12,10},{14... | collective-permute-start | bytes 1572872 | tf_op jit(solution)/shard_map/ppermute | solution.py:73
  82.7 60.5 %collective-permute-start.1 = (bf16[128,2048]{1,0:T(8,128)(2,1)S(1)}, bf16[128,2048]{1,0:T(8,128)(2,1)S(1)}, u32[]{:S(2)}, u32[]{:S(2)}) collective-permute-start(bf16[128,2048]{1,0:T(8,128)(2,1)S(1)} %get-tuple-element.25), channel_id=1, source_target_pairs={{2,0},{4,2},{6,4},{7,6},{5,7},{3,5},{1,3},{0,1},{10,8},{12,10},{14... | collective-permute-start | bytes 1572872 | tf_op jit(solution)/shard_map/ppermute | solution.py:73
  89.1 56.0 %collective-permute-start = (bf16[128,2048]{1,0:T(8,128)(2,1)S(1)}, bf16[128,2048]{1,0:T(8,128)(2,1)}, u32[]{:S(2)}, u32[]{:S(2)}) collective-permute-start(bf16[128,2048]{1,0:T(8,128)(2,1)S(1)} %get-tuple-element.25), channel_id=1, source_target_pairs={{0,2},{2,4},{4,6},{6,7},{7,5},{5,3},{3,1},{1,0},{8,10},{10,12},{12... | collective-permute-start | bytes 1572872 | tf_op jit(solution)/shard_map/ppermute | solution.py:70
  131.0 25.2 %collective-permute-start.10 = (bf16[128,2048]{1,0:T(8,128)(2,1)}, bf16[128,2048]{1,0:T(8,128)(2,1)S(1)}, u32[]{:S(2)}, u32[]{:S(2)}) collective-permute-start(bf16[128,2048]{1,0:T(8,128)(2,1)} %collective-permute-done.8), channel_id=1, source_target_pairs={{0,2},{2,4},{4,6},{6,7},{7,5},{5,3},{3,1},{1,0},{8,10},{10,12},{12... | collective-permute-start | bytes 1572872 | tf_op jit(solution)/shard_map/ppermute | solution.py:70
  139.3 18.4 %collective-permute-start.11 = (bf16[128,2048]{1,0:T(8,128)(2,1)}, bf16[128,2048]{1,0:T(8,128)(2,1)S(1)}, u32[]{:S(2)}, u32[]{:S(2)}) collective-permute-start(bf16[128,2048]{1,0:T(8,128)(2,1)} %collective-permute-done.9), channel_id=1, source_target_pairs={{2,0},{4,2},{6,4},{7,6},{5,7},{3,5},{1,3},{0,1},{10,8},{12,10},{14... | collective-permute-start | bytes 1572872 | tf_op jit(solution)/shard_map/ppermute | solution.py:73
  143.2 23.0 %collective-permute-start.3 = (bf16[128,2048]{1,0:T(8,128)(2,1)S(1)}, bf16[128,2048]{1,0:T(8,128)(2,1)S(1)}, u32[]{:S(2)}, u32[]{:S(2)}) collective-permute-start(bf16[128,2048]{1,0:T(8,128)(2,1)S(1)} %collective-permute-done.1), channel_id=1, source_target_pairs={{2,0},{4,2},{6,4},{7,6},{5,7},{3,5},{1,3},{0,1},{10,8},{12,10},{14... | collective-permute-start | bytes 1572872 | tf_op jit(solution)/shard_map/ppermute | solution.py:73
  145.2 23.5 %collective-permute-start.2 = (bf16[128,2048]{1,0:T(8,128)(2,1)}, bf16[128,2048]{1,0:T(8,128)(2,1)S(1)}, u32[]{:S(2)}, u32[]{:S(2)}) collective-permute-start(bf16[128,2048]{1,0:T(8,128)(2,1)} %collective-permute-done), channel_id=1, source_target_pairs={{0,2},{2,4},{4,6},{6,7},{7,5},{5,3},{3,1},{1,0},{8,10},{10,12},{12... | collective-permute-start | bytes 1572872 | tf_op jit(solution)/shard_map/ppermute | solution.py:70
  156.2 21.9 %collective-permute-start.12 = (bf16[128,2048]{1,0:T(8,128)(2,1)S(1)}, bf16[128,2048]{1,0:T(8,128)(2,1)S(1)}, u32[]{:S(2)}, u32[]{:S(2)}) collective-permute-start(bf16[128,2048]{1,0:T(8,128)(2,1)S(1)} %collective-permute-done.10), channel_id=1, source_target_pairs={{0,2},{2,4},{4,6},{6,7},{7,5},{5,3},{3,1},{1,0},{8,10},{10,12},{12... | collective-permute-start | bytes 1572872 | tf_op jit(solution)/shard_map/ppermute | solution.py:70
  157.7 20.5 %collective-permute-start.13 = (bf16[128,2048]{1,0:T(8,128)(2,1)S(1)}, bf16[128,2048]{1,0:T(8,128)(2,1)S(1)}, u32[]{:S(2)}, u32[]{:S(2)}) collective-permute-start(bf16[128,2048]{1,0:T(8,128)(2,1)S(1)} %collective-permute-done.11), channel_id=1, source_target_pairs={{2,0},{4,2},{6,4},{7,6},{5,7},{3,5},{1,3},{0,1},{10,8},{12,10},{14... | collective-permute-start | bytes 1572872 | tf_op jit(solution)/shard_map/ppermute | solution.py:73
  166.2 22.5 %collective-permute-start.5 = (bf16[128,2048]{1,0:T(8,128)(2,1)S(1)}, bf16[128,2048]{1,0:T(8,128)(2,1)S(1)}, u32[]{:S(2)}, u32[]{:S(2)}) collective-permute-start(bf16[128,2048]{1,0:T(8,128)(2,1)S(1)} %collective-permute-done.3), channel_id=1, source_target_pairs={{2,0},{4,2},{6,4},{7,6},{5,7},{3,5},{1,3},{0,1},{10,8},{12,10},{14... | collective-permute-start | bytes 1572872 | tf_op jit(solution)/shard_map/ppermute | solution.py:73
  168.7 22.8 %collective-permute-start.4 = (bf16[128,2048]{1,0:T(8,128)(2,1)S(1)}, bf16[128,2048]{1,0:T(8,128)(2,1)S(1)}, u32[]{:S(2)}, u32[]{:S(2)}) collective-permute-start(bf16[128,2048]{1,0:T(8,128)(2,1)S(1)} %collective-permute-done.2), channel_id=1, source_target_pairs={{0,2},{2,4},{4,6},{6,7},{7,5},{5,3},{3,1},{1,0},{8,10},{10,12},{12... | collective-permute-start | bytes 1572872 | tf_op jit(solution)/shard_map/ppermute | solution.py:70
  178.1 19.5 %collective-permute-start.14 = (bf16[64,2048]{1,0:T(8,128)(2,1)S(1)}, bf16[64,2048]{1,0:T(8,128)(2,1)S(1)}, u32[]{:S(2)}, u32[]{:S(2)}) collective-permute-start(bf16[64,2048]{1,0:T(8,128)(2,1)S(1)} %slice.177), channel_id=1, source_target_pairs={{0,2},{2,4},{4,6},{6,7},{7,5},{5,3},{3,1},{1,0},{8,10},{10,12},{12... | collective-permute-start | bytes 786440 | tf_op jit(solution)/shard_map/ppermute | solution.py:70
  178.2 20.2 %collective-permute-start.15 = (bf16[64,2048]{1,0:T(8,128)(2,1)S(1)}, bf16[64,2048]{1,0:T(8,128)(2,1)S(1)}, u32[]{:S(2)}, u32[]{:S(2)}) collective-permute-start(bf16[64,2048]{1,0:T(8,128)(2,1)S(1)} %slice.178), channel_id=1, source_target_pairs={{2,0},{4,2},{6,4},{7,6},{5,7},{3,5},{1,3},{0,1},{10,8},{12,10},{14... | collective-permute-start | bytes 786440 | tf_op jit(solution)/shard_map/ppermute | solution.py:73
  443.3 47.4 %collective-permute-start.20 = (bf16[64,2048]{1,0:T(8,128)(2,1)}, bf16[64,2048]{1,0:T(8,128)(2,1)}, u32[]{:S(2)}, u32[]{:S(2)}) collective-permute-start(bf16[64,2048]{1,0:T(8,128)(2,1)} %get-tuple-element.44), channel_id=1, source_target_pairs={{2,0},{4,2},{6,4},{7,6},{5,7},{3,5},{1,3},{0,1},{10,8},{12,10},{14... | collective-permute-start | bytes 786440 | tf_op jit(solution)/shard_map/ppermute | solution.py:73
  443.7 46.0 %collective-permute-start.24 = (bf16[64,2048]{1,0:T(8,128)(2,1)}, bf16[64,2048]{1,0:T(8,128)(2,1)}, u32[]{:S(2)}, u32[]{:S(2)}) collective-permute-start(bf16[64,2048]{1,0:T(8,128)(2,1)} %get-tuple-element.45), channel_id=1, source_target_pairs={{0,2},{2,4},{4,6},{6,7},{7,5},{5,3},{3,1},{1,0},{8,10},{10,12},{12... | collective-permute-start | bytes 786440 | tf_op jit(solution)/shard_map/ppermute | solution.py:70
  445.8 50.7 %collective-permute-start.38 = (bf16[2,64,2048]{2,1,0:T(8,128)(2,1)S(1)}, bf16[2,64,2048]{2,1,0:T(8,128)(2,1)}, u32[]{:S(2)}, u32[]{:S(2)}) collective-permute-start(bf16[2,64,2048]{2,1,0:T(8,128)(2,1)S(1)} %fusion.25), channel_id=1, source_target_pairs={{0,8},{8,0},{16,24},{24,16},{1,9},{9,1},{17,25},{25,17},{2,10},{10... | collective-permute-start | bytes 1572872 | tf_op jit(solution)/shard_map/ppermute | solution.py:122
  450.4 43.8 %collective-permute-start.28 = (bf16[64,2048]{1,0:T(8,128)(2,1)}, bf16[64,2048]{1,0:T(8,128)(2,1)}, u32[]{:S(2)}, u32[]{:S(2)}) collective-permute-start(bf16[64,2048]{1,0:T(8,128)(2,1)} %get-tuple-element.42), channel_id=1, source_target_pairs={{2,0},{4,2},{6,4},{7,6},{5,7},{3,5},{1,3},{0,1},{10,8},{12,10},{14... | collective-permute-start | bytes 786440 | tf_op jit(solution)/shard_map/ppermute | solution.py:73
  450.8 41.6 %collective-permute-start.32 = (bf16[64,2048]{1,0:T(8,128)(2,1)}, bf16[64,2048]{1,0:T(8,128)(2,1)}, u32[]{:S(2)}, u32[]{:S(2)}) collective-permute-start(bf16[64,2048]{1,0:T(8,128)(2,1)} %get-tuple-element.43), channel_id=1, source_target_pairs={{0,2},{2,4},{4,6},{6,7},{7,5},{5,3},{3,1},{1,0},{8,10},{10,12},{12... | collective-permute-start | bytes 786440 | tf_op jit(solution)/shard_map/ppermute | solution.py:70
  489.7 63.9 %collective-permute-start.36 = (bf16[2,512,1024]{2,1,0:T(8,128)(2,1)}, bf16[2,512,1024]{2,1,0:T(8,128)(2,1)S(1)}, u32[]{:S(2)}, u32[]{:S(2)}) collective-permute-start(bf16[2,512,1024]{2,1,0:T(8,128)(2,1)} %fusion.6), channel_id=1, source_target_pairs={{0,8},{8,0},{16,24},{24,16},{1,9},{9,1},{17,25},{25,17},{2,10},{10... | collective-permute-start | bytes 6291464 | tf_op jit(solution)/shard_map/ppermute | solution.py:122
  490.7 100.4 %collective-permute-start.41 = (bf16[2,512,1408]{2,1,0:T(8,128)(2,1)S(1)}, bf16[2,512,1408]{2,1,0:T(8,128)(2,1)S(1)}, u32[]{:S(2)}, u32[]{:S(2)}) collective-permute-start(bf16[2,512,1408]{2,1,0:T(8,128)(2,1)S(1)} %copy-done.17), channel_id=1, source_target_pairs={{0,8},{8,0},{16,24},{24,16},{1,9},{9,1},{17,25},{25,17},{2,10},{10... | collective-permute-start | bytes 8650760 | tf_op jit(solution)/shard_map/ppermute | solution.py:122
  492.4 36.9 %collective-permute-start.25 = (bf16[128,2048]{1,0:T(8,128)(2,1)S(1)}, bf16[128,2048]{1,0:T(8,128)(2,1)S(1)}, u32[]{:S(2)}, u32[]{:S(2)}) collective-permute-start(bf16[128,2048]{1,0:T(8,128)(2,1)S(1)} %pad_maximum_fusion.6), channel_id=1, source_target_pairs={{0,2},{2,4},{4,6},{6,7},{7,5},{5,3},{3,1},{1,0},{8,10},{10,12},{12... | collective-permute-start | bytes 1572872 | tf_op jit(solution)/shard_map/ppermute | solution.py:70
  494.2 23.3 %collective-permute-start.33 = (bf16[128,2048]{1,0:T(8,128)(2,1)S(1)}, bf16[128,2048]{1,0:T(8,128)(2,1)S(1)}, u32[]{:S(2)}, u32[]{:S(2)}) collective-permute-start(bf16[128,2048]{1,0:T(8,128)(2,1)S(1)} %pad_maximum_fusion.8), channel_id=1, source_target_pairs={{0,2},{2,4},{4,6},{6,7},{7,5},{5,3},{3,1},{1,0},{8,10},{10,12},{12... | collective-permute-start | bytes 1572872 | tf_op jit(solution)/shard_map/ppermute | solution.py:70
  496.5 21.5 %collective-permute-start.29 = (bf16[128,2048]{1,0:T(8,128)(2,1)S(1)}, bf16[128,2048]{1,0:T(8,128)(2,1)S(1)}, u32[]{:S(2)}, u32[]{:S(2)}) collective-permute-start(bf16[128,2048]{1,0:T(8,128)(2,1)S(1)} %pad_maximum_fusion.7), channel_id=1, source_target_pairs={{2,0},{4,2},{6,4},{7,6},{5,7},{3,5},{1,3},{0,1},{10,8},{12,10},{14... | collective-permute-start | bytes 1572872 | tf_op jit(solution)/shard_map/ppermute | solution.py:73
  517.5 13.0 %collective-permute-start.21 = (bf16[128,2048]{1,0:T(8,128)(2,1)S(1)}, bf16[128,2048]{1,0:T(8,128)(2,1)S(1)}, u32[]{:S(2)}, u32[]{:S(2)}) collective-permute-start(bf16[128,2048]{1,0:T(8,128)(2,1)S(1)} %pad_maximum_fusion.5), channel_id=1, source_target_pairs={{2,0},{4,2},{6,4},{7,6},{5,7},{3,5},{1,3},{0,1},{10,8},{12,10},{14... | collective-permute-start | bytes 1572872 | tf_op jit(solution)/shard_map/ppermute | solution.py:73
  527.5 14.9 %collective-permute-start.34 = (bf16[128,2048]{1,0:T(8,128)(2,1)S(1)}, bf16[128,2048]{1,0:T(8,128)(2,1)S(1)}, u32[]{:S(2)}, u32[]{:S(2)}) collective-permute-start(bf16[128,2048]{1,0:T(8,128)(2,1)S(1)} %add_convert_fusion.3), channel_id=1, source_target_pairs={{0,2},{2,4},{4,6},{6,7},{7,5},{5,3},{3,1},{1,0},{8,10},{10,12},{12... | collective-permute-start | bytes 1572872 | tf_op jit(solution)/shard_map/ppermute | solution.py:70
  529.3 94.0 %collective-permute-start.43 = (bf16[2,176,2048]{2,1,0:T(8,128)(2,1)}, bf16[2,176,2048]{2,1,0:T(8,128)(2,1)}, u32[]{:S(2)}, u32[]{:S(2)}) collective-permute-start(bf16[2,176,2048]{2,1,0:T(8,128)(2,1)} %fusion.10), channel_id=1, source_target_pairs={{0,8},{8,0},{16,24},{24,16},{1,9},{9,1},{17,25},{25,17},{2,10},{10... | collective-permute-start | bytes 4325384 | tf_op jit(solution)/shard_map/ppermute | solution.py:122
  530.5 20.3 %collective-permute-start.26 = (bf16[128,2048]{1,0:T(8,128)(2,1)S(1)}, bf16[128,2048]{1,0:T(8,128)(2,1)S(1)}, u32[]{:S(2)}, u32[]{:S(2)}) collective-permute-start(bf16[128,2048]{1,0:T(8,128)(2,1)S(1)} %fusion.5), channel_id=1, source_target_pairs={{0,2},{2,4},{4,6},{6,7},{7,5},{5,3},{3,1},{1,0},{8,10},{10,12},{12... | collective-permute-start | bytes 1572872 | tf_op jit(solution)/shard_map/ppermute | solution.py:70
  542.4 48.8 %collective-permute-start.40 = (f32[64,2048]{1,0:T(8,128)S(1)}, f32[64,2048]{1,0:T(8,128)S(1)}, u32[]{:S(2)}, u32[]{:S(2)}) collective-permute-start(f32[64,2048]{1,0:T(8,128)S(1)} %add_bitcast_fusion.1), channel_id=1, source_target_pairs={{0,0},{1,4},{2,8},{3,12},{4,16},{5,20},{6,24},{7,28},{8,1},{9,5},{... | collective-permute-start | bytes 1572872 | tf_op jit(solution)/shard_map/ppermute | solution.py:156
  550.8 39.0 %collective-permute-start.22 = (bf16[128,2048]{1,0:T(8,128)(2,1)S(1)}, bf16[128,2048]{1,0:T(8,128)(2,1)S(1)}, u32[]{:S(2)}, u32[]{:S(2)}) collective-permute-start(bf16[128,2048]{1,0:T(8,128)(2,1)S(1)} %fusion.3), channel_id=1, source_target_pairs={{2,0},{4,2},{6,4},{7,6},{5,7},{3,5},{1,3},{0,1},{10,8},{12,10},{14... | collective-permute-start | bytes 1572872 | tf_op jit(solution)/shard_map/ppermute | solution.py:73
  553.7 65.2 %collective-permute-start.30 = (bf16[128,2048]{1,0:T(8,128)(2,1)S(1)}, bf16[128,2048]{1,0:T(8,128)(2,1)}, u32[]{:S(2)}, u32[]{:S(2)}) collective-permute-start(bf16[128,2048]{1,0:T(8,128)(2,1)S(1)} %add_convert_fusion.5), channel_id=1, source_target_pairs={{2,0},{4,2},{6,4},{7,6},{5,7},{3,5},{1,3},{0,1},{10,8},{12,10},{14... | collective-permute-start | bytes 1572872 | tf_op jit(solution)/shard_map/ppermute | solution.py:73
  589.8 23.0 %collective-permute-start.37 = (bf16[1,512,1024]{2,1,0:T(8,128)(2,1)S(1)}, bf16[1,512,1024]{2,1,0:T(8,128)(2,1)S(1)}, u32[]{:S(2)}, u32[]{:S(2)}) collective-permute-start(bf16[1,512,1024]{2,1,0:T(8,128)(2,1)S(1)} %dynamic-slice_convert_fusion.3), channel_id=1, source_target_pairs={{0,16},{8,24},{16,0},{24,8},{1,17},{9,25},{17,1},{25,9},{2,18},{10... | collective-permute-start | bytes 3145736 | tf_op jit(solution)/shard_map/ppermute | solution.py:122
  591.2 62.2 %collective-permute-start.27 = (bf16[128,2048]{1,0:T(8,128)(2,1)}, bf16[128,2048]{1,0:T(8,128)(2,1)}, u32[]{:S(2)}, u32[]{:S(2)}) collective-permute-start(bf16[128,2048]{1,0:T(8,128)(2,1)} %fusion.4), channel_id=1, source_target_pairs={{0,2},{2,4},{4,6},{6,7},{7,5},{5,3},{3,1},{1,0},{8,10},{10,12},{12... | collective-permute-start | bytes 1572872 | tf_op jit(solution)/shard_map/ppermute | solution.py:70
  593.5 59.8 %collective-permute-start.23 = (bf16[128,2048]{1,0:T(8,128)(2,1)}, bf16[128,2048]{1,0:T(8,128)(2,1)}, u32[]{:S(2)}, u32[]{:S(2)}) collective-permute-start(bf16[128,2048]{1,0:T(8,128)(2,1)} %fusion.2), channel_id=1, source_target_pairs={{2,0},{4,2},{6,4},{7,6},{5,7},{3,5},{1,3},{0,1},{10,8},{12,10},{14... | collective-permute-start | bytes 1572872 | tf_op jit(solution)/shard_map/ppermute | solution.py:73
  612.8 31.8 %collective-permute-start.42 = (bf16[1,512,1408]{2,1,0:T(8,128)(2,1)}, bf16[1,512,1408]{2,1,0:T(8,128)(2,1)}, u32[]{:S(2)}, u32[]{:S(2)}) collective-permute-start(bf16[1,512,1408]{2,1,0:T(8,128)(2,1)} %dynamic-slice_convert_fusion.2), channel_id=1, source_target_pairs={{0,16},{8,24},{16,0},{24,8},{1,17},{9,25},{17,1},{25,9},{2,18},{10... | collective-permute-start | bytes 4325384 | tf_op jit(solution)/shard_map/ppermute | solution.py:122
  614.1 33.3 %all-to-all-start.2 = ((bf16[8,64,1024]{2,1,0:T(8,128)(2,1)}), bf16[8,64,1024]{2,1,0:T(8,128)(2,1)}, u32[]{:S(2)}, u32[]{:S(2)}) async-start(bf16[8,64,1024]{2,1,0:T(8,128)(2,1)} %bitcast.205), calls=%async_computation.2 | async-start | bytes 2097152 | tf_op jit(solution)/shard_map/all_to_all | solution.py:133
  618.9 36.6 %collective-permute-start.35 = (bf16[128,2048]{1,0:T(8,128)(2,1)}, bf16[128,2048]{1,0:T(8,128)(2,1)}, u32[]{:S(2)}, u32[]{:S(2)}) collective-permute-start(bf16[128,2048]{1,0:T(8,128)(2,1)} %add_convert_fusion.2), channel_id=1, source_target_pairs={{0,2},{2,4},{4,6},{6,7},{7,5},{5,3},{3,1},{1,0},{8,10},{10,12},{12... | collective-permute-start | bytes 1572872 | tf_op jit(solution)/shard_map/ppermute | solution.py:70
  623.3 32.1 %collective-permute-start.31 = (bf16[128,2048]{1,0:T(8,128)(2,1)}, bf16[128,2048]{1,0:T(8,128)(2,1)}, u32[]{:S(2)}, u32[]{:S(2)}) collective-permute-start(bf16[128,2048]{1,0:T(8,128)(2,1)} %add_convert_fusion.4), channel_id=1, source_target_pairs={{2,0},{4,2},{6,4},{7,6},{5,7},{3,5},{1,3},{0,1},{10,8},{12,10},{14... | collective-permute-start | bytes 1572872 | tf_op jit(solution)/shard_map/ppermute | solution.py:73
  644.6 18.1 %collective-permute-start.44 = (bf16[1,176,2048]{2,1,0:T(8,128)(2,1)}, bf16[1,176,2048]{2,1,0:T(8,128)(2,1)}, u32[]{:S(2)}, u32[]{:S(2)}) collective-permute-start(bf16[1,176,2048]{2,1,0:T(8,128)(2,1)} %dynamic-slice_convert_fusion.4), channel_id=1, source_target_pairs={{0,16},{8,24},{16,0},{24,8},{1,17},{9,25},{17,1},{25,9},{2,18},{10... | collective-permute-start | bytes 2162696 | tf_op jit(solution)/shard_map/ppermute | solution.py:122
  647.4 39.3 %all-to-all-start.3 = ((bf16[8,64,1408]{2,1,0:T(8,128)(2,1)}), bf16[8,64,1408]{2,1,0:T(8,128)(2,1)}, u32[]{:S(2)}, u32[]{:S(2)}) async-start(bf16[8,64,1408]{2,1,0:T(8,128)(2,1)} %bitcast.202), calls=%async_computation.3 | async-start | bytes 2883584 | tf_op jit(solution)/shard_map/all_to_all | solution.py:133
  (56 other events, 538.2 us)
Sparse Core Ops, SparseCore 0:
  9.6 29.7 all-gather.7
  45.9 48.6 all-gather.3
  129.8 51.4 all-gather.5

commit v3 on v2

--- a/solution.py
+++ b/solution.py
@@ -60,6 +60,7 @@
         self.seq = mesh.shape["seq"]
         self.subs = self.seq // TEAM
         self.groups = self.dp * self.subs
+        self.fused = self.subs == 1 and self.dp == 4
         teams = [[sub * TEAM + i for i in range(TEAM)] for sub in range(self.subs)]
         self.team_groups = None if self.subs == 1 else teams
         self.sub_groups = [[sub * TEAM + i for sub in range(self.subs)] for i in range(TEAM)]
@@ -154,6 +155,335 @@
         count = self.groups
         pairs = [(g * TEAM + s, count * s + g) for g in range(count) for s in range(TEAM)]
         return lax.ppermute(x, ("dp", "seq"), pairs)
+
+
+def remote(src, dst, send, recv, target):
+    return pltpu.make_async_remote_copy(
+        src, dst, send, recv, device_id=target, device_id_type=MESH
+    )
+
+
+class Site:
+    def __init__(self):
+        self.dp, self.seq = lax.axis_index("dp"), lax.axis_index("seq")
+        self.place = self.seq % TEAM
+        self.base = self.seq - self.place
+        self.spot = self.place // 2 + (self.place % 2) * (TEAM - 1 - 2 * (self.place // 2))
+        self.ahead, self.behind = self.device(1), self.device(-1)
+        core, side = self.dp % 2, self.dp // 2
+        self.core_dp = 2 * side + 1 - core
+        self.side_dp = 2 * (1 - side) + core
+        self.cross_dp = 2 * (1 - side) + 1 - core
+
+    def device(self, steps):
+        at = (self.spot + TEAM + steps) % TEAM
+        side = at // (TEAM // 2)
+        return (self.dp, self.base + 2 * (at + side * (TEAM - 1 - 2 * at)) + side)
+
+    def member(self, place):
+        return (self.dp, self.base + place)
+
+    def meet(self, mates=()):
+        barrier = pltpu.get_barrier_semaphore()
+        others = [self.device(k) for k in range(1, TEAM)] + [(dp, self.seq) for dp in mates]
+        for other in others:
+            pl.semaphore_signal(barrier, inc=1, device_id=other, device_id_type=MESH)
+        pl.semaphore_wait(barrier, len(others))
+
+
+class RingSum:
+    def __init__(self, site, rows, part, stage, landed, send, recv):
+        self.site, self.rows, self.part = site, rows, part
+        self.stage, self.landed, self.send, self.recv = stage, landed, send, recv
+
+    def copy(self, way, step, chunk):
+        return remote(
+            self.stage.at[way, step, chunk],
+            self.landed.at[way, step, chunk],
+            self.send.at[way, step, chunk],
+            self.recv.at[way, step, chunk],
+            self.site.ahead if way else self.site.behind,
+        )
+
+    def run(self, fill, between=lambda step: None):
+        part, stage, landed, rows = self.part, self.stage, self.landed, self.rows
+        last = TEAM // 2 - 1
+        fill(TEAM - 1, 1)
+        for way in range(2):
+            stage[way, 0, way] = part[way * CHUNK : (way + 1) * CHUNK].astype(low)
+            self.copy(way, 0, way).start()
+        between(0)
+        for step in range(1, last + 1):
+            fill(2 * (last - step) + 1, 2)
+            for turn in range(2):
+                for way in range(2):
+                    chunk = 1 - way if turn == 0 else way
+                    start = way * rows + chunk * CHUNK
+                    value = part[start : start + CHUNK]
+                    if step > 1 or chunk == way:
+                        self.copy(way, step - 1, chunk).wait_recv()
+                        value = value + landed[way, step - 1, chunk].astype(wide)
+                    stage[way, step, chunk] = value.astype(low)
+                    self.copy(way, step, chunk).start()
+            between(step)
+        fill(0, 1)
+        for chunk in range(2):
+            at = pl.ds(chunk * CHUNK, CHUNK)
+            for way in range(2):
+                self.copy(way, last, chunk).wait_recv()
+            part[at] = (
+                part[at]
+                + landed[0, last, chunk].astype(wide)
+                + landed[1, last, chunk].astype(wide)
+            )
+        for way in range(2):
+            self.copy(way, 0, way).wait_send()
+            for step in range(1, last + 1):
+                for chunk in range(2):
+                    self.copy(way, step, chunk).wait_send()
+
+
+def ring_sum_scratch(rows, width):
+    steps = TEAM // 2
+    return [
+        pltpu.VMEM((2 * rows, width), wide),
+        pltpu.VMEM((2, steps, 2, CHUNK, width), low),
+        pltpu.VMEM((2, steps, 2, CHUNK, width), low),
+        pltpu.SemaphoreType.DMA((2, steps, 2)),
+        pltpu.SemaphoreType.DMA((2, steps, 2)),
+    ]
+
+
+def fill_tiles(part, width, rows, left, product):
+    tile = 512
+
+    def fill(slot, count):
+        value = left(slot * rows, count * rows)
+
+        @pl.loop(0, width // tile)
+        def _(i):
+            at = pl.ds(pl.multiple_of(i * tile, tile), tile)
+            part[: count * rows, at] = product(value, at)
+
+    return fill
+
+
+class Exchange:
+    def __init__(self, site, pieces, source, result, keep, core_in, side_in, sems):
+        self.site, self.pieces, self.source, self.result = site, pieces, source, result
+        self.keep, self.core_in, self.side_in = keep, core_in, side_in
+        (
+            self.load_sem,
+            self.core_send,
+            self.core_recv,
+            self.side_send,
+            self.side_recv,
+            self.piece_send,
+            self.piece_recv,
+        ) = sems
+        self.quarter = keep.shape[1]
+        self.size = self.quarter // pieces
+
+    @staticmethod
+    def scratch(pieces, quarter, width):
+        return [
+            pltpu.VMEM((2, quarter, width), low),
+            pltpu.VMEM((2, quarter, width), low),
+            pltpu.VMEM((quarter, width), low),
+        ] + [pltpu.SemaphoreType.DMA((n,)) for n in (2, 2, 2, pieces, pieces, pieces, pieces)]
+
+    def part(self, dp):
+        return self.source.at[pl.ds(pl.multiple_of(dp * self.quarter, 16), self.quarter)]
+
+    def loads(self, i):
+        dp = self.site.side_dp if i else self.site.dp
+        return pltpu.make_async_copy(self.part(dp), self.keep.at[i], self.load_sem.at[i])
+
+    def core_copy(self, i):
+        dp = self.site.cross_dp if i else self.site.core_dp
+        return remote(
+            self.part(dp),
+            self.core_in.at[i],
+            self.core_send.at[i],
+            self.core_recv.at[i],
+            (self.site.core_dp, self.site.seq),
+        )
+
+    def rows_of(self, piece):
+        return pl.ds(pl.multiple_of(piece * self.size, 16), self.size)
+
+    def side_copy(self, piece):
+        at = self.rows_of(piece)
+        return remote(
+            self.keep.at[1, at],
+            self.side_in.at[at],
+            self.side_send.at[piece],
+            self.side_recv.at[piece],
+            (self.site.side_dp, self.site.seq),
+        )
+
+    def piece_copy(self, piece, source):
+        return remote(
+            self.keep.at[0, self.rows_of(piece)],
+            self.result.at[source],
+            self.piece_send.at[piece],
+            self.piece_recv.at[source],
+            self.site.member(piece),
+        )
+
+    def start(self):
+        for i in (1, 0):
+            self.core_copy(i).start()
+            self.loads(i).start()
+
+    def to_side(self):
+        self.loads(1).wait()
+        self.core_copy(1).wait_recv()
+
+        @pl.loop(0, self.pieces)
+        def _(j):
+            piece = (self.site.place + 1 + j) % self.pieces
+            start = piece * self.size
+
+            @pl.loop(0, self.size // 16)
+            def _(i):
+                at = pl.ds(pl.multiple_of(start + i * 16, 16), 16)
+                total = self.keep[1, at].astype(wide) + self.core_in[1, at].astype(wide)
+                self.keep[1, at] = total.astype(low)
+
+            self.side_copy(piece).start()
+
+    def total(self, piece):
+        self.side_copy(piece).wait_recv()
+
+        def rows(i):
+            at = pl.ds(pl.multiple_of(piece * self.size + i * 16, 16), 16)
+            return (
+                self.keep[0, at].astype(wide)
+                + self.core_in[0, at].astype(wide)
+                + self.side_in[at].astype(wide)
+            )
+
+        return rows
+
+    def settle(self):
+        self.loads(0).wait()
+        self.core_copy(0).wait_recv()
+
+    def pass_on(self, first, last):
+        @pl.loop(first, last)
+        def _(j):
+            piece = (self.site.place + j) % self.pieces
+            rows = self.total(piece)
+
+            @pl.loop(0, self.size // 16)
+            def _(i):
+                at = pl.ds(pl.multiple_of(piece * self.size + i * 16, 16), 16)
+                self.keep[0, at] = rows(i).astype(low)
+
+            self.piece_copy(piece, self.site.place).start()
+
+    def keep_own(self):
+        piece = self.site.place % self.pieces
+        rows = self.total(piece)
+
+        @pl.loop(0, self.size // 16)
+        def _(i):
+            at = pl.ds(pl.multiple_of(i * 16, 16), 16)
+            if self.pieces > 1:
+                self.result[piece, at] = rows(i).astype(low)
+            else:
+                self.result[at] = rows(i)
+
+    def finish(self):
+        for i in range(2):
+            self.core_copy(i).wait_send()
+
+        @pl.loop(0, self.pieces)
+        def _(piece):
+            self.side_copy(piece).wait_send()
+
+        if self.pieces > 1:
+
+            @pl.loop(1, self.pieces)
+            def _(j):
+                piece = (self.site.place + j) % self.pieces
+                self.piece_copy(piece, piece).wait_recv()
+                self.piece_copy(piece, self.site.place).wait_send()
+
+
+def back_kernel(width, rows, transposed, pieces, *refs):
+    count = len(pieces)
+    left_ref, right_ref, *refs = refs
+    sources, refs = refs[:count], refs[count:]
+    sum_ref, refs = refs[0], refs[1:]
+    results, refs = refs[:count], refs[count:]
+    part, stage, landed, send, recv, *refs = refs
+    site = Site()
+    exchanges = []
+    for i in range(count):
+        keep, core_in, side_in, *sems = refs[10 * i : 10 * i + 10]
+        exchanges.append(
+            Exchange(site, pieces[i], sources[i], results[i], keep, core_in, side_in, sems)
+        )
+    site.meet((site.core_dp, site.side_dp))
+    for exchange in exchanges:
+        exchange.start()
+
+    def product(value, at):
+        return dot_t(value, right_ref[at]) if transposed else dot(value, right_ref[:, at])
+
+    fill = fill_tiles(part, width, rows, lambda start, size: left_ref[start : start + size], product)
+
+    def between(step):
+        if step == 0:
+            for exchange in exchanges:
+                exchange.to_side()
+        if step == 1:
+            for exchange in exchanges:
+                exchange.settle()
+        if step >= 1:
+            for exchange in exchanges:
+                if exchange.pieces > 1:
+                    exchange.pass_on(2 * step - 1, 2 * step + 1)
+
+    RingSum(site, rows, part, stage, landed, send, recv).run(fill, between)
+    sum_ref[...] = part[:rows]
+    for exchange in exchanges:
+        if exchange.pieces > 1:
+            exchange.pass_on(TEAM - 1, TEAM)
+        exchange.keep_own()
+    for exchange in exchanges:
+        exchange.finish()
+
+
+def back_call(number, rows, left, right, transposed, gradients):
+    width = right.shape[0] if transposed else right.shape[1]
+    vmem, anywhere = pl.BlockSpec(memory_space=pltpu.VMEM), pl.BlockSpec(memory_space=pl.ANY)
+    shapes, scratch = [jax.ShapeDtypeStruct((rows, width), wide)], ring_sum_scratch(rows, width)
+    for terms, pieces, quarter in gradients:
+        columns = terms.shape[1]
+        if pieces > 1:
+            shapes.append(jax.ShapeDtypeStruct((pieces, quarter // pieces, columns), low))
+        else:
+            shapes.append(jax.ShapeDtypeStruct((quarter, columns), wide))
+        scratch += Exchange.scratch(pieces, quarter, columns)
+    pieces = tuple(pieces for _, pieces, _ in gradients)
+    return pl.pallas_call(
+        functools.partial(back_kernel, width, rows, transposed, pieces),
+        out_shape=tuple(shapes),
+        in_specs=[vmem, vmem] + [anywhere] * len(gradients),
+        out_specs=(vmem,) * len(shapes),
+        scratch_shapes=scratch,
+        compiler_params=pltpu.CompilerParams(
+            collective_id=number, has_side_effects=True, vmem_limit_bytes=60 * 2**20
+        ),
+        cost_estimate=pl.CostEstimate(
+            flops=2 * left.shape[0] * left.shape[1] * width,
+            bytes_accessed=60 * 2**20,
+            transcendentals=0,
+        ),
+    )(left, right, *[terms for terms, _, _ in gradients])
 
 
 def middle_kernel(
@@ -180,43 +510,25 @@
     hiddens,
     pairs,
     gathered,
-    part,
     proj,
     own_squares,
+    part,
     stage,
     landed,
+    reduce_send,
+    reduce_recv,
     load_sems,
     store_sems,
     gather_send,
     gather_recv,
-    reduce_send,
-    reduce_recv,
     square_send,
     square_recv,
     coef_send,
     coef_recv,
 ):
-    dp, seq = lax.axis_index("dp"), lax.axis_index("seq")
-    place = seq % TEAM
-    base = seq - place
-    spot = place // 2 + (place % 2) * (TEAM - 1 - 2 * (place // 2))
+    site = Site()
     rows = tokens_ref.shape[0]
-
-    def device(steps):
-        at = (spot + TEAM + steps) % TEAM
-        side = at // (TEAM // 2)
-        return (dp, base + 2 * (at + side * (TEAM - 1 - 2 * at)) + side)
-
-    ahead, behind = device(1), device(-1)
-    barrier = pltpu.get_barrier_semaphore()
-    for k in range(1, TEAM):
-        pl.semaphore_signal(barrier, inc=1, device_id=device(k), device_id_type=MESH)
-    pl.semaphore_wait(barrier, TEAM - 1)
-
-    def remote(src, dst, send, recv, target):
-        return pltpu.make_async_remote_copy(
-            src, dst, send, recv, device_id=target, device_id_type=MESH
-        )
+    site.meet()
 
     def slab(ref, slot, chunk):
         return ref.at[pl.ds(slot * rows + chunk * CHUNK, CHUNK)]
@@ -236,7 +548,7 @@
             own_squares.at[k],
             square_send.at[k],
             square_recv.at[k],
-            device(-k),
+            site.device(-k),
         )
         for k in range(1, TEAM)
     ]
@@ -251,7 +563,7 @@
             slab(buffer, target, chunk),
             gather_send.at[way, step - 1, chunk],
             gather_recv.at[way, step - 1, chunk],
-            behind if way else ahead,
+            site.behind if way else site.ahead,
         )
 
     def gather_chunks(way, step):
@@ -276,68 +588,21 @@
                 for chunk in gather_chunks(way, step):
                     gather_copy(buffer, way, step, chunk).wait_send()
 
-    def reduce_copy(way, step, chunk):
-        return remote(
-            stage.at[way, step, chunk],
-            landed.at[way, step, chunk],
-            reduce_send.at[way, step, chunk],
-            reduce_recv.at[way, step, chunk],
-            ahead if way else behind,
-        )
-
-    def ring_sum(fill):
-        last = TEAM // 2 - 1
-        fill(TEAM - 1, 1)
-        for way in range(2):
-            stage[way, 0, way] = part[way * CHUNK : (way + 1) * CHUNK].astype(low)
-            reduce_copy(way, 0, way).start()
-        for step in range(1, last + 1):
-            slot = 2 * (last - step) + 1
-            fill(slot, 2)
-            for turn in range(2):
-                for way in range(2):
-                    chunk = 1 - way if turn == 0 else way
-                    start = way * rows + chunk * CHUNK
-                    value = part[start : start + CHUNK]
-                    if step > 1 or chunk == way:
-                        reduce_copy(way, step - 1, chunk).wait_recv()
-                        value = value + landed[way, step - 1, chunk].astype(wide)
-                    stage[way, step, chunk] = value.astype(low)
-                    reduce_copy(way, step, chunk).start()
-        fill(0, 1)
-        for chunk in range(2):
-            at = pl.ds(chunk * CHUNK, CHUNK)
-            for way in range(2):
-                reduce_copy(way, last, chunk).wait_recv()
-            part[at] = (
-                part[at]
-                + landed[0, last, chunk].astype(wide)
-                + landed[1, last, chunk].astype(wide)
-            )
-        for way in range(2):
-            reduce_copy(way, 0, way).wait_send()
-            for step in range(1, last + 1):
-                for chunk in range(2):
-                    reduce_copy(way, step, chunk).wait_send()
-
-    tile = 512
-
-    def fill_output(slot, count):
-        left = raw_ref[slot * rows : (slot + count) * rows]
-
-        @pl.loop(0, model_width // tile)
-        def _(i):
-            at = pl.ds(pl.multiple_of(i * tile, tile), tile)
-            part[: count * rows, at] = dot(left, output_ref[:, at])
-
-    def fill_pairs(slot, count):
-        left = pairs[slot * rows : (slot + count) * rows]
-
-        @pl.loop(0, model_width // tile)
-        def _(i):
-            at = pl.ds(pl.multiple_of(i * tile, tile), tile)
-            part[: count * rows, at] = dot_t(left, mlp[at])
-
+    ring = RingSum(site, rows, part, stage, landed, reduce_send, reduce_recv)
+    fill_output = fill_tiles(
+        part,
+        model_width,
+        rows,
+        lambda start, size: raw_ref[start : start + size],
+        lambda value, at: dot(value, output_ref[:, at]),
+    )
+    fill_pairs = fill_tiles(
+        part,
+        model_width,
+        rows,
+        lambda start, size: pairs[start : start + size],
+        lambda value, at: dot_t(value, mlp[at]),
+    )
     eye = lax.broadcasted_iota(jnp.int32, (rows, rows), 0) == lax.broadcasted_iota(
         jnp.int32, (rows, rows), 1
     )
@@ -348,7 +613,7 @@
     def row_of(column):
         return jnp.sum(jnp.where(eye, jnp.broadcast_to(column, (rows, rows)), 0.0), axis=0, keepdims=True)
 
-    ring_sum(fill_output)
+    ring.run(fill_output)
     total = squares_ref[0, 0:1]
     for copy in square_copies:
         copy.wait_recv()
@@ -393,7 +658,7 @@
     for store in stores[:3]:
         store.start()
 
-    ring_sum(fill_pairs)
+    ring.run(fill_pairs)
     middle_grad_ref[...] = cotangents[:rows].astype(wide) + norm_back(middle_ref[...], part[:rows])
     middle_low = middle_grad_ref[...].astype(low)
     gathered[:rows] = middle_low
@@ -408,7 +673,7 @@
             coefficients_ref.at[ORDER.index(k)],
             coef_send.at[k],
             coef_recv.at[k],
-            device(k),
+            site.device(k),
         )
         for k in range(1, TEAM)
     ]
@@ -456,15 +721,11 @@
             pltpu.VMEM((team_rows, padded), low),
             pltpu.VMEM((team_rows, 2 * hidden), low),
             pltpu.VMEM((team_rows, width), low),
-            pltpu.VMEM((2 * rows, width), wide),
             pltpu.VMEM((rows, width), wide),
             pltpu.VMEM((TEAM, 8, rows), wide),
-            pltpu.VMEM((2, steps, 2, CHUNK, width), low),
-            pltpu.VMEM((2, steps, 2, CHUNK, width), low),
+            *ring_sum_scratch(rows, width),
             pltpu.SemaphoreType.DMA((3,)),
             pltpu.SemaphoreType.DMA((4,)),
-            pltpu.SemaphoreType.DMA((2, steps, 2)),
-            pltpu.SemaphoreType.DMA((2, steps, 2)),
             pltpu.SemaphoreType.DMA((2, steps, 2)),
             pltpu.SemaphoreType.DMA((2, steps, 2)),
             pltpu.SemaphoreType.DMA((TEAM,)),
@@ -623,23 +884,35 @@
     )
     scale_rows = coefficients[:, 0].reshape(team_tokens, 1)
     inner_rows = coefficients[:, 1].reshape(team_tokens, 1)
-    mixed = (middle + plan.ring_reduce(lambda i: dot(rows(hidden_low, i), down_w))).astype(low)
-    grad_down = plan.across_sum(outer(hidden_low, cotangents)[:hidden])
-    grad_pair = plan.across_sum(outer(second, pair_grads))
+    down_terms = outer(hidden_low, cotangents)
+    pair_terms = outer(second, pair_grads)
+    if plan.fused:
+        down_sum, grad_pair, grad_down = back_call(
+            1,
+            row_count,
+            hidden_low,
+            down_w,
+            False,
+            [(pair_terms.astype(low), TEAM, TEAM * weight_rows), (down_terms.astype(low), 1, piece)],
+        )
+    else:
+        down_sum = plan.ring_reduce(lambda i: dot(rows(hidden_low, i), down_w))
+        grad_down = plan.across_sum(down_terms[:hidden])
+        grad_pair = plan.across_sum(pair_terms).astype(low)
+        grad_pair = plan.swap(grad_pair.reshape(TEAM, weight_rows, 2 * hidden))
+    mixed = (middle + down_sum).astype(low)
 
     def from_units(x):
         x = x.reshape(TEAM, weight_rows, groups, piece).transpose(1, 2, 0, 3)
         return x.reshape(weight_rows, TEAM * hidden).astype(wide)
 
-    grad_pair = plan.swap(grad_pair.astype(low).reshape(TEAM, weight_rows, 2 * hidden))
     grad_gate = from_units(grad_pair[:, :, :hidden])
     grad_up = from_units(grad_pair[:, :, hidden:])
 
     gated_grad = dot_t(middle_all, output_w)
     normed_heads = heads_out * scale_rows
     gated = (normed_heads * z_unit).astype(low)
-    grad_output = plan.across_sum(outer(gated, middle_all))
-    grad_output = plan.team_rows_back(grad_output)
+    output_terms = outer(gated, middle_all)
     unit_grad = (gated_grad * normed_heads).astype(low)
     heads_grad = to_heads(
         (scale_rows * gated_grad * z_unit - heads_out * inner_rows).astype(low)
@@ -668,9 +941,22 @@
         ],
         axis=1,
     )
-    first_grad = plan.ring_reduce(lambda k: dot_t(rows(z_grads, k), attn_w))
-    grad_four = plan.across_sum(outer(jnp.concatenate(normed, axis=0), z_grads))
-    grad_four = plan.swap(grad_four.astype(low).reshape(TEAM, weight_rows, 4 * head_width))
+    four_terms = outer(jnp.concatenate(normed, axis=0), z_grads)
+    if plan.fused:
+        first_grad, grad_four, grad_output = back_call(
+            2,
+            row_count,
+            z_grads,
+            attn_w,
+            True,
+            [(four_terms.astype(low), TEAM, TEAM * weight_rows), (output_terms.astype(low), 1, weight_rows)],
+        )
+    else:
+        first_grad = plan.ring_reduce(lambda i: dot_t(rows(z_grads, i), attn_w))
+        grad_four = plan.across_sum(four_terms).astype(low)
+        grad_four = plan.swap(grad_four.reshape(TEAM, weight_rows, 4 * head_width))
+        grad_output = plan.across_sum(output_terms)
+    grad_output = plan.team_rows_back(grad_output)
 
     def from_columns(x):
         return x.transpose(1, 0, 2).reshape(weight_rows, TEAM * head_width).astype(wide)

time: 726 us -> 670 us (0.923)
  the two profiles are of different devices: /device:TPU:0 before, /device:TPU:28 now
where the time goes in v3:
time: 670 us; the launch traced here: 661 us
  Pallas kernels  340 us (51%)
  waiting for transfers between devices  76.2 us (11%)
  local copies, waits for them, and re-layouts  69.2 us (10%)
  starting transfers between devices  53.9 us (8%)
  matrix products  48.6 us (7%)
  blocking collectives  29 us (4%)
  other arithmetic  28.2 us (4%)
  between operations  15.9 us (2%)
    pallas_call x1, Pallas kernels, middle_call(): pl.pallas_call(functools.partial(middle_kernel, width, hidden), out_shape...  182 us
    pallas_call x2, Pallas kernels, back_call(): pl.pallas_call(functools.partial(back_kernel, width, rows, transposed, pi...  157 us
    all_to_all x1, waiting for transfers between devices, swap(): lax.all_to_all(x, 'seq', 0, 0, tiled=True, axis_index_groups=self.team_gr...  41.7 us
    all_to_all x1, blocking collectives, swap(): lax.all_to_all(x, 'seq', 0, 0, tiled=True, axis_index_groups=self.team_gr...  29 us
    dot_general x4, matrix products, outer(): lax.dot_general(left, right, (((0,), (0,)), ((), ())), preferred_element_...  28.1 us
    unnamed x98, local copies, waits for them, and re-layouts  24.3 us
    convert_element_type x6, local copies, waits for them, and re-layouts, from_units(): return x.reshape(weight_rows, TEAM * hidden).astype(wide)  18.1 us
    ppermute x8, starting transfers between devices, to_previous(): return lax.ppermute(x, 'seq', self.down)  16.1 us
  transfers between devices with their start and end apart: 25, of which 7 were waited for; matrix products, arithmetic and copies ran while one was open for 16% of the time, Pallas kernels for 14%

profile of v3, /device:TPU:28, one launch (start us, length us, event | category | flops | bytes accessed | tf_op | source)
XLA Modules:
  0.0 660.6 jit_solution(16886298171305817335)
XLA Ops:
  10.3 29.0 %all_to_all.10 = bf16[8,64,1024]{2,1,0:T(8,128)(2,1)} all-to-all(bf16[8,64,1024]{2,1,0:T(8,128)(2,1)S(1)} %pad_maximum_fusion.2), channel_id=1, replica_groups=mesh['dp'=4,'seq'=8] {'seq'}, dimensions={0} | all-to-all | bytes 2097152 | tf_op jit(solution)/shard_map/all_to_all | solution.py:134
  41.2 3.2 collective-permute-start.16
  44.4 5.0 collective-permute-start.19
  51.2 2.0 reshape.249
  54.6 3.0 reshape.251
  60.6 6.7 %all-to-all-start.1 = ((bf16[8,64,1408]{2,1,0:T(8,128)(2,1)}), bf16[8,64,1408]{2,1,0:T(8,128)(2,1)S(1)}, u32[]{:S(2)}, u32[]{:S(2)}) async-start(bf16[8,64,1408]{2,1,0:T(8,128)(2,1)} %pad_maximum_fusion.1), calls=%async_computation.1 | async-start | bytes 2883584 | tf_op jit(solution)/shard_map/all_to_all | solution.py:134
  75.9 9.4 %collective-permute-done.17 = bf16[64,2048]{1,0:T(8,128)(2,1)} collective-permute-done((bf16[64,2048]{1,0:T(8,128)(2,1)}, bf16[64,2048]{1,0:T(8,128)(2,1)}, u32[]{:S(2)}, u32[]{:S(2)}) %collective-permute-start.17) | collective-permute-done | bytes 262176 | tf_op jit(solution)/shard_map/ppermute | solution.py:144
  85.3 2.0 collective-permute-start.9
  87.3 2.0 collective-permute-start
  90.6 41.7 %all-to-all-done.1 = bf16[8,64,1408]{2,1,0:T(8,128)(2,1)S(1)} async-done(((bf16[8,64,1408]{2,1,0:T(8,128)(2,1)}), bf16[8,64,1408]{2,1,0:T(8,128)(2,1)S(1)}, u32[]{:S(2)}, u32[]{:S(2)}) %all-to-all-start.1) | async-done | bytes 1441824 | tf_op jit(solution)/shard_map/all_to_all | solution.py:134
  134.8 2.0 collective-permute-start.11
  136.9 2.0 collective-permute-start.2
  140.8 2.0 constant_dynamic-update-slice_fusion.6
  142.8 2.0 constant_dynamic-update-slice_fusion.16
  145.7 4.2 collective-permute-done.10
  149.9 3.0 collective-permute-start.12
  152.9 2.5 collective-permute-start.13
  155.4 5.8 collective-permute-done.3
  161.2 2.0 collective-permute-start.5
  166.7 5.6 collective-permute-done.12
  172.5 5.5 collective-permute-start.15
  178.0 5.7 collective-permute-done.5
  183.7 2.0 collective-permute-start.7
  190.9 3.0 collective-permute-done.6
  195.3 3.9 pad.5.down_hbm.refs_1_
  199.2 3.1 convolution_dynamic-update-slice_fusion.7
  209.1 2.0 copy-done.2
  211.4 2.3 multiply_convert_fusion.4
  214.2 3.1 multiply_convert_fusion.1
  218.9 2.2 fusion.13
  221.2 2.1 fusion.10.raw_ref
  224.0 182.2 %shard_map.213 = (f32[128,2048]{1,0:T(8,128)}, f32[128,2048]{1,0:T(8,128)}, bf16[1024,2048]{1,0:T(8,128)(2,1)}, bf16[1024,768]{1,0:T(8,128)(2,1)}, bf16[1024,140...) custom-call(f32[8,8,128]{2,1,0:T(8,128)} %broadcast_in_dim.20.squares_ref, ...), custom_call_target="tpu_custom_call" | custom-call | flops 17179869184 | bytes 62914560 | tf_op jit(solution)/shard_map/pallas_call | solution.py:703
  407.1 5.3 convolution_convert_fusion.3.refs_3_
  412.5 3.6 fusion.12
  423.0 5.1 convolution_convert_fusion.2.refs_3_
  432.9 8.7 %convolution_convert_fusion.1.refs_2_ = bf16[2048,1024]{1,0:T(8,128)(2,1)} fusion(bf16[1024,2048]{1,0:T(8,128)(2,1)} %constant_dynamic-update-slice_fusion.9, bf16[1024,256]{1,0:T(8,128)(2,1)S(1)} %copy-done.33, bf16[1024,256]{1,0:T(8,128)(2,1)S(1)} %bitcast.181, bf16[1024,256]{1,0:T(8,128)(2,1)S(1)} %get-tuple-element.39, ...), kind=kOutput, calls=%fused_computation.5 | convolution fusion | flops 4305453056 | bytes 10485760 | tf_op jit(solution)/shard_map/dot_general | solution.py:49
  441.6 65.9 %shard_map.215 = (f32[128,2048]{1,0:T(8,128)}, bf16[8,64,1024]{2,1,0:T(8,128)(2,1)}, f32[64,2048]{1,0:T(8,128)}) custom-call(bf16[1024,1024]{1,0:T(8,128)(2,1)} %pad_maximum_fusion.refs_0_, bf16[2048,1024]{1,0:T(8,128)(2,1)} %all-gather.4.cloned.1.call-done.refs_1_, bf16[2048,1024]{1,0:T(8,128)(2,1)} %convolution_convert_fusion.1.refs_2_, ...), custom_call_target="tpu_custom_call" | custom-call | flops 4294967296 | bytes 62914560 | tf_op jit(solution)/shard_map/pallas_call | solution.py:472
  509.1 11.7 %collective-permute-start.20 = (f32[64,2048]{1,0:T(8,128)}, f32[64,2048]{1,0:T(8,128)S(1)}, u32[]{:S(2)}, u32[]{:S(2)}) collective-permute-start(f32[64,2048]{1,0:T(8,128)} %get-tuple-element.33), channel_id=1, source_target_pairs={{0,0},{1,4},{2,8},{3,12},{4,16},{5,20},{6,24},{7,28},{8,1},{9,5},{... | collective-permute-start | bytes 1572872 | tf_op jit(solution)/shard_map/ppermute | solution.py:157
  525.6 8.9 %convolution_convert_fusion.refs_2_ = bf16[2048,1408]{1,0:T(8,128)(2,1)} fusion(bf16[1024,2048]{1,0:T(8,128)(2,1)S(1)} %copy-done.38, bf16[1024,1408]{1,0:T(8,128)(2,1)S(1)} %copy-done.39), kind=kOutput, calls=%fused_computation.1 | convolution fusion | flops 5908463616 | bytes 12845056 | tf_op jit(solution)/shard_map/dot_general | solution.py:49
  534.6 91.5 %shard_map.214 = (f32[128,2048]{1,0:T(8,128)}, bf16[8,64,1408]{2,1,0:T(8,128)(2,1)}, f32[176,2048]{1,0:T(8,128)}) custom-call(bf16[1024,768]{1,0:T(8,128)(2,1)} %get-tuple-element.24.refs_0_, bf16[768,2048]{1,0:T(8,128)(2,1)} %pad.5.down_hbm.refs_1_, bf16[2048,1408]{1,0:T(8,128)(2,1)} %convolution_convert_fusion.refs_2_, ...), custom_call_target="tpu_custom_call" | custom-call | flops 3221225472 | bytes 62914560 | tf_op jit(solution)/shard_map/pallas_call | solution.py:472
  626.1 3.6 slice_convert_fusion.1
  629.7 3.0 reshape.267
  632.7 2.5 copy.91
  635.3 3.3 reshape.265
  638.6 3.3 reshape.266
  641.9 2.5 copy.90
  644.4 3.4 reshape.264
  647.9 2.6 add_convert_fusion
  (201 shorter events, 67.4 us)
Async XLA Ops:
  7.2 44.1 %copy-start.31 = (bf16[64,5632]{1,0:T(8,128)(2,1)S(1)}, bf16[64,5632]{1,0:T(8,128)(2,1)}, u32[]{:S(2)}) copy-start(bf16[64,5632]{1,0:T(8,128)(2,1)} %param.22) | copy-start | bytes 2162692
  7.2 188.1 %all-gather.8.cloned.1.call-start = ((), (), s32[]{:S(2)}) async-start(), calls=%async_computation.4 | async-start | bytes 3604480 | tf_op jit(solution)/shard_map/all_gather | solution.py:110
  7.9 191.3 %all-gather.4.cloned.1.call-start = ((), (), s32[]{:S(2)}) async-start(), calls=%async_computation.2 | async-start | bytes 5242880 | tf_op jit(solution)/shard_map/all_gather | solution.py:110
  39.3 46.0 %collective-permute-start.17 = (bf16[64,2048]{1,0:T(8,128)(2,1)}, bf16[64,2048]{1,0:T(8,128)(2,1)}, u32[]{:S(2)}, u32[]{:S(2)}) collective-permute-start(bf16[64,2048]{1,0:T(8,128)(2,1)} %param.21), channel_id=1, source_target_pairs={{1,0},{5,1},{9,2},{13,3},{17,4},{21,5},{25,6},{29,7},{2,8},{6,9},{... | collective-permute-start | bytes 786440 | tf_op jit(solution)/shard_map/ppermute | solution.py:144
  41.2 46.0 %collective-permute-start.16 = (bf16[64,2048]{1,0:T(8,128)(2,1)}, bf16[64,2048]{1,0:T(8,128)(2,1)}, u32[]{:S(2)}, u32[]{:S(2)}) collective-permute-start(bf16[64,2048]{1,0:T(8,128)(2,1)} %param.21), channel_id=1, source_target_pairs={{0,0},{4,1},{8,2},{12,3},{16,4},{20,5},{24,6},{28,7},{1,8},{5,9},{... | collective-permute-start | bytes 786440 | tf_op jit(solution)/shard_map/ppermute | solution.py:144
  44.4 42.9 %collective-permute-start.19 = (bf16[64,2048]{1,0:T(8,128)(2,1)}, bf16[64,2048]{1,0:T(8,128)(2,1)}, u32[]{:S(2)}, u32[]{:S(2)}) collective-permute-start(bf16[64,2048]{1,0:T(8,128)(2,1)} %param.21), channel_id=1, source_target_pairs={{3,0},{7,1},{11,2},{15,3},{19,4},{23,5},{27,6},{31,7},{0,8},{4,9},... | collective-permute-start | bytes 786440 | tf_op jit(solution)/shard_map/ppermute | solution.py:144
  49.4 39.9 %collective-permute-start.18 = (bf16[64,2048]{1,0:T(8,128)(2,1)}, bf16[64,2048]{1,0:T(8,128)(2,1)}, u32[]{:S(2)}, u32[]{:S(2)}) collective-permute-start(bf16[64,2048]{1,0:T(8,128)(2,1)} %param.21), channel_id=1, source_target_pairs={{2,0},{6,1},{10,2},{14,3},{18,4},{22,5},{26,6},{30,7},{3,8},{7,9},... | collective-permute-start | bytes 786440 | tf_op jit(solution)/shard_map/ppermute | solution.py:144
  51.2 83.7 %collective-permute-start.8 = (bf16[128,2048]{1,0:T(8,128)(2,1)}, bf16[128,2048]{1,0:T(8,128)(2,1)}, u32[]{:S(2)}, u32[]{:S(2)}) collective-permute-start(bf16[128,2048]{1,0:T(8,128)(2,1)} %param.15), channel_id=1, source_target_pairs={{0,2},{2,4},{4,6},{6,7},{7,5},{5,3},{3,1},{1,0},{8,10},{10,12},{12... | collective-permute-start | bytes 1572872 | tf_op jit(solution)/shard_map/ppermute | solution.py:71
  58.1 9.2 %copy-start.37 = (s32[8]{0:T(128)S(1)}, s32[8]{0:T(128)}, u32[]{:S(2)}) copy-start(s32[8]{0:T(128)} %constant.127.clone) | copy-start | bytes 100
  58.1 10.4 %copy-start.36 = (s32[8]{0:T(128)S(1)}, s32[8]{0:T(128)}, u32[]{:S(2)}) copy-start(s32[8]{0:T(128)} %constant.136) | copy-start | bytes 100
  58.1 10.5 %copy-start = (s32[8]{0:T(128)S(1)}, s32[8]{0:T(128)}, u32[]{:S(2)}) copy-start(s32[8]{0:T(128)} %constant.128.clone) | copy-start | bytes 100
  58.1 11.2 %copy-start.35 = (s32[1,4]{1,0:T(1,128)S(1)}, s32[1,4]{1,0:T(1,128)}, u32[]{:S(2)}) copy-start(s32[1,4]{1,0:T(1,128)} %param.16) | copy-start | bytes 52
  58.1 11.7 %copy-start.4 = (bf16[128,2048]{1,0:T(8,128)(2,1)S(1)}, bf16[128,2048]{1,0:T(8,128)(2,1)}, u32[]{:S(2)}) copy-start(bf16[128,2048]{1,0:T(8,128)(2,1)} %tokens_ref.1) | copy-start | bytes 1572868
  60.6 71.8 %all-to-all-start.1 = ((bf16[8,64,1408]{2,1,0:T(8,128)(2,1)}), bf16[8,64,1408]{2,1,0:T(8,128)(2,1)S(1)}, u32[]{:S(2)}, u32[]{:S(2)}) async-start(bf16[8,64,1408]{2,1,0:T(8,128)(2,1)} %pad_maximum_fusion.1), calls=%async_computation.1 | async-start | bytes 2883584 | tf_op jit(solution)/shard_map/all_to_all | solution.py:134
  67.2 156.1 %all-gather.6.cloned.1.call-start = ((), (), s32[]{:S(2)}) async-start(), calls=%async_computation.3 | async-start | bytes 7208960 | tf_op jit(solution)/shard_map/all_gather | solution.py:110
  85.3 49.6 %collective-permute-start.9 = (bf16[128,2048]{1,0:T(8,128)(2,1)}, bf16[128,2048]{1,0:T(8,128)(2,1)}, u32[]{:S(2)}, u32[]{:S(2)}) collective-permute-start(bf16[128,2048]{1,0:T(8,128)(2,1)} %param.15), channel_id=1, source_target_pairs={{2,0},{4,2},{6,4},{7,6},{5,7},{3,5},{1,3},{0,1},{10,8},{12,10},{14... | collective-permute-start | bytes 1572872 | tf_op jit(solution)/shard_map/ppermute | solution.py:74
  87.3 49.6 %collective-permute-start.1 = (bf16[128,2048]{1,0:T(8,128)(2,1)S(1)}, bf16[128,2048]{1,0:T(8,128)(2,1)S(1)}, u32[]{:S(2)}, u32[]{:S(2)}) collective-permute-start(bf16[128,2048]{1,0:T(8,128)(2,1)S(1)} %get-tuple-element.37), channel_id=1, source_target_pairs={{2,0},{4,2},{6,4},{7,6},{5,7},{3,5},{1,3},{0,1},{10,8},{12,10},{14... | collective-permute-start | bytes 1572872 | tf_op jit(solution)/shard_map/ppermute | solution.py:74
  87.3 49.7 %collective-permute-start = (bf16[128,2048]{1,0:T(8,128)(2,1)S(1)}, bf16[128,2048]{1,0:T(8,128)(2,1)}, u32[]{:S(2)}, u32[]{:S(2)}) collective-permute-start(bf16[128,2048]{1,0:T(8,128)(2,1)S(1)} %get-tuple-element.37), channel_id=1, source_target_pairs={{0,2},{2,4},{4,6},{6,7},{7,5},{5,3},{3,1},{1,0},{8,10},{10,12},{12... | collective-permute-start | bytes 1572872 | tf_op jit(solution)/shard_map/ppermute | solution.py:71
  133.6 12.1 %copy-start.27 = (bf16[64,2048]{1,0:T(8,128)(2,1)}, bf16[64,2048]{1,0:T(8,128)(2,1)S(1)}, u32[]{:S(2)}) copy-start(bf16[64,2048]{1,0:T(8,128)(2,1)S(1)} %get-tuple-element.52) | copy-start | bytes 786436
  133.6 12.1 %copy-start.29 = (bf16[64,2048]{1,0:T(8,128)(2,1)}, bf16[64,2048]{1,0:T(8,128)(2,1)S(1)}, u32[]{:S(2)}) copy-start(bf16[64,2048]{1,0:T(8,128)(2,1)S(1)} %get-tuple-element.53) | copy-start | bytes 786436
  133.6 29.6 %copy-start.23 = (bf16[64,2048]{1,0:T(8,128)(2,1)}, bf16[64,2048]{1,0:T(8,128)(2,1)S(1)}, u32[]{:S(2)}) copy-start(bf16[64,2048]{1,0:T(8,128)(2,1)S(1)} %get-tuple-element.50) | copy-start | bytes 786436
  133.6 29.6 %copy-start.25 = (bf16[64,2048]{1,0:T(8,128)(2,1)}, bf16[64,2048]{1,0:T(8,128)(2,1)S(1)}, u32[]{:S(2)}) copy-start(bf16[64,2048]{1,0:T(8,128)(2,1)S(1)} %get-tuple-element.51) | copy-start | bytes 786436
  134.8 15.1 %collective-permute-start.10 = (bf16[128,2048]{1,0:T(8,128)(2,1)}, bf16[128,2048]{1,0:T(8,128)(2,1)S(1)}, u32[]{:S(2)}, u32[]{:S(2)}) collective-permute-start(bf16[128,2048]{1,0:T(8,128)(2,1)} %collective-permute-done.8), channel_id=1, source_target_pairs={{0,2},{2,4},{4,6},{6,7},{7,5},{5,3},{3,1},{1,0},{8,10},{10,12},{12... | collective-permute-start | bytes 1572872 | tf_op jit(solution)/shard_map/ppermute | solution.py:71
  134.8 18.0 %collective-permute-start.11 = (bf16[128,2048]{1,0:T(8,128)(2,1)}, bf16[128,2048]{1,0:T(8,128)(2,1)S(1)}, u32[]{:S(2)}, u32[]{:S(2)}) collective-permute-start(bf16[128,2048]{1,0:T(8,128)(2,1)} %collective-permute-done.9), channel_id=1, source_target_pairs={{2,0},{4,2},{6,4},{7,6},{5,7},{3,5},{1,3},{0,1},{10,8},{12,10},{14... | collective-permute-start | bytes 1572872 | tf_op jit(solution)/shard_map/ppermute | solution.py:74
  136.9 18.5 %copy-start.9 = (bf16[128,2048]{1,0:T(8,128)(2,1)}, bf16[128,2048]{1,0:T(8,128)(2,1)S(1)}, u32[]{:S(2)}) copy-start(bf16[128,2048]{1,0:T(8,128)(2,1)S(1)} %collective-permute-done.1) | copy-start | bytes 1572868
  136.9 24.3 %collective-permute-start.3 = (bf16[128,2048]{1,0:T(8,128)(2,1)S(1)}, bf16[128,2048]{1,0:T(8,128)(2,1)S(1)}, u32[]{:S(2)}, u32[]{:S(2)}) collective-permute-start(bf16[128,2048]{1,0:T(8,128)(2,1)S(1)} %collective-permute-done.1), channel_id=1, source_target_pairs={{2,0},{4,2},{6,4},{7,6},{5,7},{3,5},{1,3},{0,1},{10,8},{12,10},{14... | collective-permute-start | bytes 1572872 | tf_op jit(solution)/shard_map/ppermute | solution.py:74
  136.9 26.2 %collective-permute-start.2 = (bf16[128,2048]{1,0:T(8,128)(2,1)}, bf16[128,2048]{1,0:T(8,128)(2,1)S(1)}, u32[]{:S(2)}, u32[]{:S(2)}) collective-permute-start(bf16[128,2048]{1,0:T(8,128)(2,1)} %collective-permute-done), channel_id=1, source_target_pairs={{0,2},{2,4},{4,6},{6,7},{7,5},{5,3},{3,1},{1,0},{8,10},{10,12},{12... | collective-permute-start | bytes 1572872 | tf_op jit(solution)/shard_map/ppermute | solution.py:71
  149.9 22.5 %collective-permute-start.12 = (bf16[128,2048]{1,0:T(8,128)(2,1)S(1)}, bf16[128,2048]{1,0:T(8,128)(2,1)S(1)}, u32[]{:S(2)}, u32[]{:S(2)}) collective-permute-start(bf16[128,2048]{1,0:T(8,128)(2,1)S(1)} %collective-permute-done.10), channel_id=1, source_target_pairs={{0,2},{2,4},{4,6},{6,7},{7,5},{5,3},{3,1},{1,0},{8,10},{10,12},{12... | collective-permute-start | bytes 1572872 | tf_op jit(solution)/shard_map/ppermute | solution.py:71
  152.9 19.6 %collective-permute-start.13 = (bf16[128,2048]{1,0:T(8,128)(2,1)S(1)}, bf16[128,2048]{1,0:T(8,128)(2,1)S(1)}, u32[]{:S(2)}, u32[]{:S(2)}) collective-permute-start(bf16[128,2048]{1,0:T(8,128)(2,1)S(1)} %collective-permute-done.11), channel_id=1, source_target_pairs={{2,0},{4,2},{6,4},{7,6},{5,7},{3,5},{1,3},{0,1},{10,8},{12,10},{14... | collective-permute-start | bytes 1572872 | tf_op jit(solution)/shard_map/ppermute | solution.py:74
  161.2 22.5 %collective-permute-start.5 = (bf16[128,2048]{1,0:T(8,128)(2,1)S(1)}, bf16[128,2048]{1,0:T(8,128)(2,1)S(1)}, u32[]{:S(2)}, u32[]{:S(2)}) collective-permute-start(bf16[128,2048]{1,0:T(8,128)(2,1)S(1)} %collective-permute-done.3), channel_id=1, source_target_pairs={{2,0},{4,2},{6,4},{7,6},{5,7},{3,5},{1,3},{0,1},{10,8},{12,10},{14... | collective-permute-start | bytes 1572872 | tf_op jit(solution)/shard_map/ppermute | solution.py:74
  163.2 22.5 %collective-permute-start.4 = (bf16[128,2048]{1,0:T(8,128)(2,1)S(1)}, bf16[128,2048]{1,0:T(8,128)(2,1)S(1)}, u32[]{:S(2)}, u32[]{:S(2)}) collective-permute-start(bf16[128,2048]{1,0:T(8,128)(2,1)S(1)} %collective-permute-done.2), channel_id=1, source_target_pairs={{0,2},{2,4},{4,6},{6,7},{7,5},{5,3},{3,1},{1,0},{8,10},{10,12},{12... | collective-permute-start | bytes 1572872 | tf_op jit(solution)/shard_map/ppermute | solution.py:71
  172.4 17.0 %collective-permute-start.14 = (bf16[64,2048]{1,0:T(8,128)(2,1)S(1)}, bf16[64,2048]{1,0:T(8,128)(2,1)S(1)}, u32[]{:S(2)}, u32[]{:S(2)}) collective-permute-start(bf16[64,2048]{1,0:T(8,128)(2,1)S(1)} %slice.52), channel_id=1, source_target_pairs={{0,2},{2,4},{4,6},{6,7},{7,5},{5,3},{3,1},{1,0},{8,10},{10,12},{12... | collective-permute-start | bytes 786440 | tf_op jit(solution)/shard_map/ppermute | solution.py:71
  172.5 17.6 %collective-permute-start.15 = (bf16[64,2048]{1,0:T(8,128)(2,1)S(1)}, bf16[64,2048]{1,0:T(8,128)(2,1)S(1)}, u32[]{:S(2)}, u32[]{:S(2)}) collective-permute-start(bf16[64,2048]{1,0:T(8,128)(2,1)S(1)} %slice.53), channel_id=1, source_target_pairs={{2,0},{4,2},{6,4},{7,6},{5,7},{3,5},{1,3},{0,1},{10,8},{12,10},{14... | collective-permute-start | bytes 786440 | tf_op jit(solution)/shard_map/ppermute | solution.py:74
  183.7 10.9 %collective-permute-start.7 = (bf16[64,2048]{1,0:T(8,128)(2,1)S(1)}, bf16[64,2048]{1,0:T(8,128)(2,1)S(1)}, u32[]{:S(2)}, u32[]{:S(2)}) collective-permute-start(bf16[64,2048]{1,0:T(8,128)(2,1)S(1)} %slice.51), channel_id=1, source_target_pairs={{2,0},{4,2},{6,4},{7,6},{5,7},{3,5},{1,3},{0,1},{10,8},{12,10},{14... | collective-permute-start | bytes 786440 | tf_op jit(solution)/shard_map/ppermute | solution.py:74
  185.7 8.1 %collective-permute-start.6 = (bf16[64,2048]{1,0:T(8,128)(2,1)S(1)}, bf16[64,2048]{1,0:T(8,128)(2,1)S(1)}, u32[]{:S(2)}, u32[]{:S(2)}) collective-permute-start(bf16[64,2048]{1,0:T(8,128)(2,1)S(1)} %slice.50), channel_id=1, source_target_pairs={{0,2},{2,4},{4,6},{6,7},{7,5},{5,3},{3,1},{1,0},{8,10},{10,12},{12... | collective-permute-start | bytes 786440 | tf_op jit(solution)/shard_map/ppermute | solution.py:71
  199.2 5.3 copy-start.10
  211.4 5.9 copy-start.11
  406.1 6.3 copy-start.7
  406.2 6.3 copy-start.24
  406.2 6.3 copy-start.26
  406.2 6.3 copy-start.28
  406.2 6.3 copy-start.30
  441.6 65.9 %copy-start.5 = (bf16[128,2048]{1,0:T(8,128)(2,1)S(1)}, bf16[128,2048]{1,0:T(8,128)(2,1)}, u32[]{:S(2)}) copy-start(bf16[128,2048]{1,0:T(8,128)(2,1)} %tokens_ref.1) | copy-start | bytes 1572868
  507.5 18.1 %copy-start.38 = (bf16[1024,2048]{1,0:T(8,128)(2,1)S(1)}, bf16[1024,2048]{1,0:T(8,128)(2,1)}, u32[]{:S(2)}) copy-start(bf16[1024,2048]{1,0:T(8,128)(2,1)} %get-tuple-element.25) | copy-start | bytes 12582916
  507.5 18.1 %copy-start.39 = (bf16[1024,1408]{1,0:T(8,128)(2,1)S(1)}, bf16[1024,1408]{1,0:T(8,128)(2,1)}, u32[]{:S(2)}) copy-start(bf16[1024,1408]{1,0:T(8,128)(2,1)} %get-tuple-element.26) | copy-start | bytes 8650756
  509.1 142.5 %collective-permute-start.20 = (f32[64,2048]{1,0:T(8,128)}, f32[64,2048]{1,0:T(8,128)S(1)}, u32[]{:S(2)}, u32[]{:S(2)}) collective-permute-start(f32[64,2048]{1,0:T(8,128)} %get-tuple-element.33), channel_id=1, source_target_pairs={{0,0},{1,4},{2,8},{3,12},{4,16},{5,20},{6,24},{7,28},{8,1},{9,5},{... | collective-permute-start | bytes 1572872 | tf_op jit(solution)/shard_map/ppermute | solution.py:157
  644.4 6.0 copy-start.8
  644.4 6.0 copy-start.22
  (17 other events, 38.1 us)
Sparse Core Ops, SparseCore 0:
  9.6 27.0 all-gather.7
  39.4 43.5 all-gather.3
  133.6 42.4 all-gather.5

commit v4 on v3

v4 whole, which is shorter than its diff:
```python
import functools
import math

import jax
import jax.numpy as jnp
from jax import lax
from jax.experimental import pallas as pl
from jax.experimental.pallas import tpu as pltpu
from jax.sharding import PartitionSpec as P

H = 16
DH = 128
LONG_DEV = 64
SHORT_DEV = 64
HEADS_DEV = 4
TEAM = H // HEADS_DEV
RING = (0, 2, 3, 1)
PLACE = tuple(RING.index(i) for i in range(TEAM))
ORDER = (0, 1, 3, 2)
CHUNK = 64
ATTN_SPLIT = 2
MLP_SPLIT = 2
MESH = pl.DeviceIdType.MESH

epsilon = 1e-06
layer_number = 14
total_layers = 16
low = jnp.bfloat16
wide = jnp.float32


def normalize(values):
    return values * lax.rsqrt(jnp.mean(values * values, axis=-1, keepdims=True) + epsilon)


def norm_back(values, upstream):
    scale = lax.rsqrt(jnp.mean(values * values, axis=-1, keepdims=True) + epsilon)
    inner = jnp.mean(upstream * values, axis=-1, keepdims=True)
    return scale * upstream - values * (scale * scale * scale) * inner


def dot(left, right):
    return jnp.dot(left, right, preferred_element_type=wide)


def dot_t(left, right):
    return lax.dot_general(left, right, (((1,), (1,)), ((), ())), preferred_element_type=wide)


def outer(left, right):
    return lax.dot_general(left, right, (((0,), (0,)), ((), ())), preferred_element_type=wide)


def head_rates(order):
    factor = 1.0 - layer_number / (total_layers - 1.0) + 1e-05
    return jnp.exp(-(order + 1.0) * (8.0 / H) * math.log(2.0)) * factor


class Plan:
    def __init__(self, mesh):
        self.dp = mesh.shape["dp"]
        self.seq = mesh.shape["seq"]
        self.subs = self.seq // TEAM
        self.groups = self.dp * self.subs
        self.fused = self.subs == 2 and self.dp == 4
        teams = [[sub * TEAM + i for i in range(TEAM)] for sub in range(self.subs)]
        self.team_groups = None if self.subs == 1 else teams
        self.sub_groups = [[sub * TEAM + i for sub in range(self.subs)] for i in range(TEAM)]
        self.up = [(t[RING[i]], t[RING[(i + 1) % TEAM]]) for t in teams for i in range(TEAM)]
        self.down = [(b, a) for a, b in self.up]

    def to_next(self, x):
        return lax.ppermute(x, "seq", self.up)

    def to_previous(self, x):
        return lax.ppermute(x, "seq", self.down)

    def ring_gather(self, x):
        half = x.shape[0] // 2
        blocks = [x] + [None] * (TEAM - 1)
        forth = back = x
        for k in range(1, TEAM // 2):
            forth, back = self.to_next(forth), self.to_previous(back)
            blocks[k], blocks[TEAM - k] = forth, back
        blocks[TEAM // 2] = jnp.concatenate(
            [self.to_next(forth[:half]), self.to_previous(back[half:])], axis=0
        )
        return [blocks[k] for k in ORDER]

    def ring_reduce(self, slot_part):
        def part(k):
            return slot_part(ORDER.index(k))

        middle = part(TEAM // 2)
        half = middle.shape[0] // 2
        back = self.to_previous(middle[:half].astype(low))
        forth = self.to_next(middle[half:].astype(low))
        for k in range(TEAM // 2 - 1, 0, -1):
            a, b = part(k), part(TEAM - k)
            if k == TEAM // 2 - 1:
                a = jnp.concatenate([a[:half] + back.astype(wide), a[half:]], axis=0)
                b = jnp.concatenate([b[:half], b[half:] + forth.astype(wide)], axis=0)
            else:
                a, b = a + back.astype(wide), b + forth.astype(wide)
            back = self.to_previous(a.astype(low))
            forth = self.to_next(b.astype(low))
        return part(0) + back.astype(wide) + forth.astype(wide)

    def across(self, x):
        if self.subs > 1:
            x = lax.all_gather(x, "seq", axis=0, tiled=True, axis_index_groups=self.sub_groups)
        return lax.all_gather(x, "dp", axis=0, tiled=True)

    def across_sum(self, x):
        rows = x.shape[0] // self.groups
        count = self.dp
        mine = lax.axis_index("dp")
        x = x.reshape((self.dp, self.subs * rows) + x.shape[1:])
        bit = 1
        while bit < count:
            pairs = x.reshape((x.shape[0] // 2, 2) + x.shape[1:])
            own = (mine // bit) % 2
            keep = lax.dynamic_index_in_dim(pairs, own, 1, False)
            send = lax.dynamic_index_in_dim(pairs, 1 - own, 1, False)
            got = lax.ppermute(send.astype(low), "dp", [(i, i ^ bit) for i in range(count)])
            x = keep.astype(wide) + got.astype(wide)
            bit *= 2
        x = x[0]
        if self.subs > 1:
            x = lax.psum_scatter(
                x, "seq", scatter_dimension=0, tiled=True, axis_index_groups=self.sub_groups
            )
        return x

    def swap(self, x):
        return lax.all_to_all(x, "seq", 0, 0, tiled=True, axis_index_groups=self.team_groups)

    def team_rows(self, x):
        count = self.groups
        spot = lax.axis_index("dp") * self.subs + lax.axis_index("seq") // TEAM
        got = []
        for i in range(count):
            pairs = [
                (count * s + (g + i) % count, g * TEAM + s) for g in range(count) for s in range(TEAM)
            ]
            got.append(lax.ppermute(x, ("dp", "seq"), pairs))
        got = jnp.stack(got)
        return jnp.concatenate(
            [
                lax.dynamic_index_in_dim(got, (j - spot + count) % count, 0, False)
                for j in range(count)
            ],
            axis=0,
        )

    def team_rows_back(self, x):
        count = self.groups
        pairs = [(g * TEAM + s, count * s + g) for g in range(count) for s in range(TEAM)]
        return lax.ppermute(x, ("dp", "seq"), pairs)


def remote(src, dst, send, recv, target):
    return pltpu.make_async_remote_copy(
        src, dst, send, recv, device_id=target, device_id_type=MESH
    )


class Site:
    def __init__(self):
        self.dp, self.seq = lax.axis_index("dp"), lax.axis_index("seq")
        self.place = self.seq % TEAM
        self.base = self.seq - self.place
        self.spot = self.place // 2 + (self.place % 2) * (TEAM - 1 - 2 * (self.place // 2))
        self.ahead, self.behind = self.device(1), self.device(-1)
        self.sub = self.seq // TEAM
        self.core_mate = (self.dp + 1 - 2 * (self.dp % 2), self.seq)
        self.side_mate = (self.dp + 2 - 4 * (self.dp // 2), self.seq)
        self.far_mate = (self.dp, (self.seq + TEAM) % (2 * TEAM))

    def device(self, steps):
        at = (self.spot + TEAM + steps) % TEAM
        side = at // (TEAM // 2)
        return (self.dp, self.base + 2 * (at + side * (TEAM - 1 - 2 * at)) + side)

    def member(self, place):
        return (self.dp, self.base + place)

    def group(self, core=0, side=0, far=0):
        own_core, own_side = self.dp % 2, self.dp // 2
        dp = 2 * (own_side + side * (1 - 2 * own_side)) + own_core + core * (1 - 2 * own_core)
        return 2 * dp + self.sub + far * (1 - 2 * self.sub)

    def meet(self, mates=(), more=None, other=None):
        barrier = pltpu.get_barrier_semaphore()
        others = [self.device(k) for k in range(1, TEAM)] + list(mates)
        for device in others:
            pl.semaphore_signal(barrier, inc=1, device_id=device, device_id_type=MESH)
        if more is None:
            pl.semaphore_wait(barrier, len(others))
            return

        @pl.when(more != 0)
        def _():
            pl.semaphore_signal(barrier, inc=1, device_id=other, device_id_type=MESH)
            pl.semaphore_wait(barrier, len(others) + 1)

        @pl.when(more == 0)
        def _():
            pl.semaphore_wait(barrier, len(others))


class RingSum:
    def __init__(self, site, rows, part, stage, landed, send, recv):
        self.site, self.rows, self.part = site, rows, part
        self.stage, self.landed, self.send, self.recv = stage, landed, send, recv

    def copy(self, way, step, chunk):
        return remote(
            self.stage.at[way, step, chunk],
            self.landed.at[way, step, chunk],
            self.send.at[way, step, chunk],
            self.recv.at[way, step, chunk],
            self.site.ahead if way else self.site.behind,
        )

    def run(self, fill, between=lambda step: None):
        part, stage, landed, rows = self.part, self.stage, self.landed, self.rows
        last = TEAM // 2 - 1
        fill(TEAM - 1, 1)
        for way in range(2):
            stage[way, 0, way] = part[way * CHUNK : (way + 1) * CHUNK].astype(low)
            self.copy(way, 0, way).start()
        between(0)
        for step in range(1, last + 1):
            fill(2 * (last - step) + 1, 2)
            for turn in range(2):
                for way in range(2):
                    chunk = 1 - way if turn == 0 else way
                    start = way * rows + chunk * CHUNK
                    value = part[start : start + CHUNK]
                    if step > 1 or chunk == way:
                        self.copy(way, step - 1, chunk).wait_recv()
                        value = value + landed[way, step - 1, chunk].astype(wide)
                    stage[way, step, chunk] = value.astype(low)
                    self.copy(way, step, chunk).start()
            between(step)
        fill(0, 1)
        for chunk in range(2):
            at = pl.ds(chunk * CHUNK, CHUNK)
            for way in range(2):
                self.copy(way, last, chunk).wait_recv()
            part[at] = (
                part[at]
                + landed[0, last, chunk].astype(wide)
                + landed[1, last, chunk].astype(wide)
            )
        for way in range(2):
            self.copy(way, 0, way).wait_send()
            for step in range(1, last + 1):
                for chunk in range(2):
                    self.copy(way, step, chunk).wait_send()


def ring_sum_scratch(rows, width):
    steps = TEAM // 2
    return [
        pltpu.VMEM((2 * rows, width), wide),
        pltpu.VMEM((2, steps, 2, CHUNK, width), low),
        pltpu.VMEM((2, steps, 2, CHUNK, width), low),
        pltpu.SemaphoreType.DMA((2, steps, 2)),
        pltpu.SemaphoreType.DMA((2, steps, 2)),
    ]


def fill_tiles(part, width, rows, left, product):
    tile = 512

    def fill(slot, count):
        value = left(slot * rows, count * rows)

        @pl.loop(0, width // tile)
        def _(i):
            at = pl.ds(pl.multiple_of(i * tile, tile), tile)
            part[: count * rows, at] = product(value, at)

    return fill


class Exchange:
    def __init__(self, site, pieces, split, source, result, keep, core_in, side_in, far_in, sems):
        self.site, self.pieces, self.split = site, pieces, split
        self.source, self.result = source, result
        self.keep, self.core_in, self.side_in, self.far_in = keep, core_in, side_in, far_in
        (
            self.load_sem,
            self.core_send,
            self.core_recv,
            self.side_send,
            self.side_recv,
            self.far_send,
            self.far_recv,
            self.piece_send,
            self.piece_recv,
        ) = sems
        self.block = keep.shape[1]
        self.count = pieces * split
        self.size = self.block // self.count

    SCRATCH = 13

    @staticmethod
    def scratch(pieces, split, block, width):
        count = pieces * split
        return [
            pltpu.VMEM((4, block, width), low),
            pltpu.VMEM((4, block, width), low),
            pltpu.VMEM((2, block, width), low),
            pltpu.VMEM((block, width), low),
            pltpu.SemaphoreType.DMA((4,)),
            pltpu.SemaphoreType.DMA((4,)),
            pltpu.SemaphoreType.DMA((4,)),
            pltpu.SemaphoreType.DMA((2, count)),
            pltpu.SemaphoreType.DMA((2, count)),
            pltpu.SemaphoreType.DMA((count,)),
            pltpu.SemaphoreType.DMA((count,)),
            pltpu.SemaphoreType.DMA((pieces, split)),
            pltpu.SemaphoreType.DMA((pieces, split)),
        ]

    def terms(self, core, i):
        group = self.site.group(core, i // 2, i % 2)
        return self.source.at[pl.ds(pl.multiple_of(group * self.block, 16), self.block)]

    def load(self, i):
        return pltpu.make_async_copy(self.terms(0, i), self.keep.at[i], self.load_sem.at[i])

    def core_copy(self, i):
        return remote(
            self.terms(1, i),
            self.core_in.at[i],
            self.core_send.at[i],
            self.core_recv.at[i],
            self.site.core_mate,
        )

    def piece(self, j):
        return (self.site.place + 1 + j // self.split) % self.pieces

    def start_of(self, j):
        return (self.piece(j) * self.split + j % self.split) * self.size

    def at(self, j):
        return pl.ds(pl.multiple_of(self.start_of(j), 16), self.size)

    def side_copy(self, far, j):
        return remote(
            self.keep.at[2 + far, self.at(j)],
            self.side_in.at[far, self.at(j)],
            self.side_send.at[far, j],
            self.side_recv.at[far, j],
            self.site.side_mate,
        )

    def far_copy(self, j):
        return remote(
            self.keep.at[1, self.at(j)],
            self.far_in.at[self.at(j)],
            self.far_send.at[j],
            self.far_recv.at[j],
            self.site.far_mate,
        )

    def piece_copy(self, j, target, source):
        sub = j % self.split
        return remote(
            self.keep.at[0, self.at(j)],
            self.result.at[source, pl.ds(sub * self.size, self.size)],
            self.piece_send.at[target, sub],
            self.piece_recv.at[source, sub],
            self.site.member(target),
        )

    def add(self, j, into, terms):
        start = self.start_of(j)

        @pl.loop(0, self.size // 16)
        def _(i):
            at = pl.ds(pl.multiple_of(start + i * 16, 16), 16)
            total = terms[0][at].astype(wide)
            for term in terms[1:]:
                total = total + term[at].astype(wide)
            into[at] = total.astype(into.dtype)

    def start(self):
        for i in (3, 2, 1, 0):
            self.core_copy(i).start()
            self.load(i).start()

    def to_side(self, far, j):
        if j == 0:
            self.load(2 + far).wait()
            self.core_copy(2 + far).wait_recv()
        into = self.keep.at[2 + far]
        self.add(j, into, (into, self.core_in.at[2 + far]))
        self.side_copy(far, j).start()

    def to_far(self, j):
        if j == 0:
            self.load(1).wait()
            self.core_copy(1).wait_recv()
        self.side_copy(1, j).wait_recv()
        into = self.keep.at[1]
        self.add(j, into, (into, self.core_in.at[1], self.side_in.at[1]))
        self.far_copy(j).start()

    def to_owner(self, j):
        if j == 0:
            self.load(0).wait()
            self.core_copy(0).wait_recv()
        self.side_copy(0, j).wait_recv()
        self.far_copy(j).wait_recv()
        own = self.keep.at[0]
        terms = (own, self.core_in.at[0], self.side_in.at[0], self.far_in)
        if self.pieces == 1:
            self.add(j, self.result, terms)
            return
        self.add(j, own, terms)
        if j < self.count - self.split:
            self.piece_copy(j, self.piece(j), self.site.place).start()
        else:
            sub = pl.ds((j % self.split) * self.size, self.size)
            self.result[self.site.place, sub] = own[self.at(j)]

    def finish(self):
        for i in range(4):
            self.core_copy(i).wait_send()

        @pl.loop(0, self.count)
        def _(j):
            self.side_copy(0, j).wait_send()
            self.side_copy(1, j).wait_send()
            self.far_copy(j).wait_send()

        if self.pieces > 1:

            @pl.loop(0, self.count - self.split)
            def _(j):
                self.piece_copy(j, self.piece(j), self.piece(j)).wait_recv()
                self.piece_copy(j, self.piece(j), self.site.place).wait_send()


class Exchanges:
    def __init__(self, exchanges):
        self.exchanges = exchanges
        self.parts = [(exchange, j) for exchange in exchanges for j in range(exchange.count)]
        self.sides = [(1, part) for part in self.parts] + [(0, part) for part in self.parts]
        self.sent = self.done = 0

    def start(self, depth=3):
        for exchange in self.exchanges:
            exchange.start()
        for _ in range(depth):
            self.next_side()

    def next_side(self):
        if self.sent < len(self.sides):
            far, (exchange, j) = self.sides[self.sent]
            exchange.to_side(far, j)
            self.sent += 1

    def step(self, count=1):
        for _ in range(count):
            if self.done < len(self.parts):
                exchange, j = self.parts[self.done]
                exchange.to_far(j)
                self.next_side()
                self.done += 1

    def finish(self):
        self.step(len(self.parts))
        while self.sent < len(self.sides):
            self.next_side()
        for exchange, j in self.parts:
            exchange.to_owner(j)
        for exchange in self.exchanges:
            exchange.finish()


class WeightStream:
    def __init__(self, site, pieces, split, source, result, sems):
        self.site, self.pieces, self.split = site, pieces, split
        self.source, self.result = source, result
        self.own_sem, self.swap_send, self.swap_recv, self.send, self.recv = sems
        self.count = pieces * split
        self.size = result.shape[0] // (8 * self.count)

    SCRATCH = 5

    @staticmethod
    def scratch(pieces, split):
        return [
            pltpu.SemaphoreType.DMA((1,)),
            pltpu.SemaphoreType.DMA((pieces,)),
            pltpu.SemaphoreType.DMA((pieces,)),
            pltpu.SemaphoreType.DMA((7, pieces * split)),
            pltpu.SemaphoreType.DMA((7, pieces * split)),
        ]

    def piece(self, j):
        return (self.site.place + j // self.split) % self.pieces

    def at(self, group, j):
        start = ((group * self.pieces + self.piece(j)) * self.split + j % self.split) * self.size
        return self.result.at[pl.ds(pl.multiple_of(start, 16), self.size)]

    def whole(self, place):
        size = self.size * self.split
        start = (self.site.group() * self.pieces + place) * size
        return self.result.at[pl.ds(pl.multiple_of(start, 16), size)]

    def own_copy(self):
        place = self.site.place % self.pieces
        source = self.source.at[place] if self.pieces > 1 else self.source
        return pltpu.make_async_copy(source, self.whole(place), self.own_sem.at[0])

    def swap_copy(self, target, source):
        return remote(
            self.source.at[target],
            self.whole(source),
            self.swap_send.at[target],
            self.swap_recv.at[source],
            self.site.member(target),
        )

    def hop(self, kind, j, arriving=False):
        site = self.site
        mate = site.far_mate if kind == 0 else site.side_mate if kind < 3 else site.core_mate
        side, far = ((0, 0), (0, 0), (0, 1), (0, 0), (0, 1), (1, 0), (1, 1))[kind]
        if arriving:
            if kind == 0:
                far = 1
            elif kind < 3:
                side = 1
        at = self.at(site.group(int(arriving and kind >= 3), side, far), j)
        return remote(at, at, self.send.at[kind, j], self.recv.at[kind, j], mate)

    def start(self):
        self.own_copy().start()

        @pl.loop(1, self.pieces)
        def _(j):
            target = (self.site.place + j) % self.pieces
            self.swap_copy(target, self.site.place).start()

    def launch(self, j):
        if j == 0:
            self.own_copy().wait()
        elif j % self.split == 0 and self.pieces > 1:
            self.swap_copy(self.piece(j), self.piece(j)).wait_recv()
        for kind in (0, 1, 3):
            self.hop(kind, j).start()

    def land(self, j):
        self.hop(0, j, True).wait_recv()
        for kind in (2, 4):
            self.hop(kind, j).start()
        self.hop(1, j, True).wait_recv()
        self.hop(5, j).start()

    def cross(self, j):
        self.hop(2, j, True).wait_recv()
        self.hop(6, j).start()

    def finish(self):
        @pl.loop(0, self.count)
        def _(j):
            for kind in range(3, 7):
                self.hop(kind, j, True).wait_recv()
            for kind in range(7):
                self.hop(kind, j).wait_send()

        @pl.loop(1, self.pieces)
        def _(j):
            self.swap_copy((self.site.place + j) % self.pieces, self.site.place).wait_send()


class WeightStreams:
    def __init__(self, streams, depth=2):
        self.streams, self.depth = streams, depth
        self.parts = [(stream, j) for stream in streams for j in range(stream.count)]
        self.done = 0

    def start(self):
        for stream in self.streams:
            stream.start()

    def launch(self):
        for stream, j in self.parts[: self.depth]:
            stream.launch(j)

    def step(self, count=1):
        for _ in range(count):
            if self.done == len(self.parts):
                return
            stream, j = self.parts[self.done]
            stream.land(j)
            if self.done + self.depth < len(self.parts):
                stream, j = self.parts[self.done + self.depth]
                stream.launch(j)
            if self.done >= self.depth:
                stream, j = self.parts[self.done - self.depth]
                stream.cross(j)
            self.done += 1

    def finish(self):
        self.step(len(self.parts))
        for stream, j in self.parts[len(self.parts) - self.depth :]:
            stream.cross(j)
        for stream in self.streams:
            stream.finish()


class SpreadStream(WeightStream):
    def __init__(self, site, split, source, result, sems):
        super().__init__(site, 1, split, source, result, sems)
        index = TEAM * site.sub + site.place
        self.target = (index // 2, (index % 2) * TEAM + site.dp)
        group = site.group()
        self.origin = (site.place, (group // TEAM) * TEAM + group % TEAM)
        self.rows = result.at[pl.ds(pl.multiple_of(index * source.shape[0], 16), source.shape[0])]
        self.elsewhere = (self.target[0] - site.dp) * (self.target[0] - site.dp) + (
            self.target[1] - site.seq
        ) * (self.target[1] - site.seq)

    def first_copy(self):
        return remote(
            self.source, self.rows, self.swap_send.at[0], self.swap_recv.at[0], self.target
        )

    def start(self):
        @pl.when(self.elsewhere != 0)
        def _():
            self.first_copy().start()

        @pl.when(self.elsewhere == 0)
        def _():
            self.own_copy().start()

    def launch(self, j):
        if j == 0:

            @pl.when(self.elsewhere != 0)
            def _():
                self.first_copy().wait_recv()

            @pl.when(self.elsewhere == 0)
            def _():
                self.own_copy().wait()

        for kind in (0, 1, 3):
            self.hop(kind, j).start()

    def finish(self):
        super().finish()

        @pl.when(self.elsewhere != 0)
        def _():
            self.first_copy().wait_send()


class RingGather:
    def __init__(self, site, rows, own, buffer, send, recv):
        self.site, self.rows, self.own, self.buffer = site, rows, own, buffer
        self.send, self.recv = send, recv

    @staticmethod
    def scratch():
        return [pltpu.SemaphoreType.DMA((2, TEAM // 2, 2))] * 2

    def slab(self, slot, chunk):
        return self.buffer.at[pl.ds(slot * self.rows + chunk * CHUNK, CHUNK)]

    def copy(self, way, step, chunk):
        source = self.own.at[pl.ds(chunk * CHUNK, CHUNK)]
        if step > 1:
            source = self.slab(2 * (step - 1) - 1 + way, chunk)
        target = 2 * step - 1 + way if step < TEAM // 2 else TEAM - 1
        return remote(
            source,
            self.slab(target, chunk),
            self.send.at[way, step - 1, chunk],
            self.recv.at[way, step - 1, chunk],
            self.site.behind if way else self.site.ahead,
        )

    def chunks(self, way, step):
        return (0, 1) if step < TEAM // 2 else (way,)

    def start(self):
        for chunk in range(2):
            for way in range(2):
                self.copy(way, 1, chunk).start()

    def step(self, step):
        for chunk in range(2):
            for way in range(2):
                if chunk in self.chunks(way, step):
                    self.copy(way, step, chunk).wait_recv()
                    if step < TEAM // 2 and chunk in self.chunks(way, step + 1):
                        self.copy(way, step + 1, chunk).start()

    def finish(self):
        for step in range(1, TEAM // 2 + 1):
            for way in range(2):
                for chunk in self.chunks(way, step):
                    self.copy(way, step, chunk).wait_send()


def front_kernel(
    normed_ref,
    cotangent_ref,
    pieces_ref,
    output_rows_ref,
    normed_out,
    cotangents_out,
    weight_out,
    output_out,
    own_sems,
    *sems,
):
    site = Site()
    rows = normed_ref.shape[0]
    normed_ring = RingGather(site, rows, normed_ref, normed_out, *sems[:2])
    cotangent_ring = RingGather(site, rows, cotangent_ref, cotangents_out, *sems[2:4])
    attention = WeightStream(site, TEAM, ATTN_SPLIT, pieces_ref, weight_out, sems[4:9])
    output = SpreadStream(site, 2, output_rows_ref, output_out, sems[9:])
    streams = WeightStreams([attention, output], 4)
    own = [
        pltpu.make_async_copy(ref, out.at[pl.ds(0, rows)], own_sems.at[i])
        for i, (ref, out) in enumerate(
            ((normed_ref, normed_out), (cotangent_ref, cotangents_out))
        )
    ]
    site.meet([site.core_mate, site.side_mate, site.far_mate], output.elsewhere, output.origin)
    streams.start()
    for copy in own:
        copy.start()
    streams.launch()
    streams.step(2)
    normed_ring.start()
    streams.step(4)
    normed_ring.step(1)
    cotangent_ring.start()
    streams.step(3)
    normed_ring.step(2)
    streams.step(1)
    cotangent_ring.step(1)
    streams.finish()
    cotangent_ring.step(2)
    normed_ring.finish()
    cotangent_ring.finish()
    for copy in own:
        copy.wait()


def front_call(normed, cotangent, pieces, output_rows):
    rows, width = normed.shape
    anywhere = pl.BlockSpec(memory_space=pl.ANY)
    return pl.pallas_call(
        front_kernel,
        out_shape=(
            jax.ShapeDtypeStruct((TEAM * rows, width), low),
            jax.ShapeDtypeStruct((TEAM * rows, width), low),
            jax.ShapeDtypeStruct((8 * TEAM * pieces.shape[1], pieces.shape[2]), low),
            jax.ShapeDtypeStruct((8 * output_rows.shape[0], output_rows.shape[1]), low),
        ),
        in_specs=[pl.BlockSpec(memory_space=pltpu.VMEM)] * 4,
        out_specs=(anywhere,) * 4,
        scratch_shapes=[
            pltpu.SemaphoreType.DMA((2,)),
            *RingGather.scratch(),
            *RingGather.scratch(),
            *WeightStream.scratch(TEAM, ATTN_SPLIT),
            *WeightStream.scratch(1, 2),
        ],
        compiler_params=pltpu.CompilerParams(collective_id=3, has_side_effects=True),
        cost_estimate=pl.CostEstimate(flops=0, bytes_accessed=60 * 2**20, transcendentals=0),
    )(normed, cotangent, pieces, output_rows)


def back_kernel(width, rows, transposed, kinds, *refs):
    count = len(kinds)
    left_ref, right_ref, *refs = refs
    sources, refs = refs[:count], refs[count:]
    sum_ref, refs = refs[0], refs[1:]
    results, refs = refs[:count], refs[count:]
    part, stage, landed, send, recv, *refs = refs
    site = Site()
    exchanges = []
    for i, (pieces, split) in enumerate(kinds):
        keep, core_in, side_in, far_in, *sems = refs[: Exchange.SCRATCH]
        refs = refs[Exchange.SCRATCH :]
        exchanges.append(
            Exchange(
                site, pieces, split, sources[i], results[i], keep, core_in, side_in, far_in, sems
            )
        )
    exchanges = Exchanges(exchanges)
    site.meet([site.core_mate, site.side_mate, site.far_mate])
    exchanges.start()

    def product(value, at):
        return dot_t(value, right_ref[at]) if transposed else dot(value, right_ref[:, at])

    fill = fill_tiles(part, width, rows, lambda start, size: left_ref[start : start + size], product)
    ring = RingSum(site, rows, part, stage, landed, send, recv)
    ring.run(fill, lambda step: exchanges.step(2))
    sum_ref[...] = part[:rows]
    exchanges.finish()


def back_call(number, rows, left, right, transposed, gradients):
    width = right.shape[0] if transposed else right.shape[1]
    vmem, anywhere = pl.BlockSpec(memory_space=pltpu.VMEM), pl.BlockSpec(memory_space=pl.ANY)
    shapes, scratch = [jax.ShapeDtypeStruct((rows, width), wide)], ring_sum_scratch(rows, width)
    for terms, pieces, split, block in gradients:
        columns = terms.shape[1]
        if pieces > 1:
            shapes.append(jax.ShapeDtypeStruct((pieces, block // pieces, columns), low))
        else:
            shapes.append(jax.ShapeDtypeStruct((block, columns), wide))
        scratch += Exchange.scratch(pieces, split, block, columns)
    kinds = tuple((pieces, split) for _, pieces, split, _ in gradients)
    return pl.pallas_call(
        functools.partial(back_kernel, width, rows, transposed, kinds),
        out_shape=tuple(shapes),
        in_specs=[vmem, vmem] + [anywhere] * len(gradients),
        out_specs=(vmem,) * len(shapes),
        scratch_shapes=scratch,
        compiler_params=pltpu.CompilerParams(
            collective_id=number, has_side_effects=True, vmem_limit_bytes=60 * 2**20
        ),
        cost_estimate=pl.CostEstimate(
            flops=2 * left.shape[0] * left.shape[1] * width,
            bytes_accessed=60 * 2**20,
            transcendentals=0,
        ),
    )(left, right, *[gradient[0] for gradient in gradients])


def attention_tables(plan, lengths, rates):
    place, segments, enter, leave = team_places(plan, lengths, LONG_DEV, SHORT_DEV)
    sub = lax.axis_index("seq") // TEAM

    def by_rows(long, short):
        parts = jnp.stack([long.reshape(TEAM, LONG_DEV), short.reshape(TEAM, SHORT_DEV)], axis=1)
        return parts.astype(wide).reshape(-1)

    ones = jnp.ones_like(enter)
    kinds = [
        by_rows(place[0], place[1]),
        by_rows(segments[0], segments[1]),
        by_rows(ones, enter) * (sub > 0).astype(wide),
        by_rows(ones, leave),
        by_rows(ones, jnp.zeros_like(ones)),
    ]
    table = jnp.stack(kinds + [jnp.zeros_like(kinds[0])] * 3)
    return table.T, table, jnp.broadcast_to(jnp.pad(rates, (0, 8 - HEADS_DEV))[:, None], (8, 128))


def head_lanes(part, head):
    return pl.ds(pl.multiple_of(part * HEADS_DEV * DH + head * DH, DH), DH)


class Heads:
    def __init__(self, columns_ref, rows_ref, rates_ref):
        self.columns, self.rows, self.rates = columns_ref, rows_ref, rates_ref
        self.count = columns_ref.shape[0]
        self.length = self.count // 2

    def rate(self, head):
        return self.rates[pl.ds(head, 1), 0:1]

    def decay(self, head):
        spacing = self.columns[:, 0:1] - self.rows[0:1, :]
        linked = (self.columns[:, 1:2] == self.rows[1:2, :]) & (spacing >= 0.0)
        return jnp.where(linked, jnp.exp(-self.rate(head) * jnp.where(linked, spacing, 0.0)), 0.0)

    def into(self, head):
        return jnp.exp(-self.rate(head) * (self.columns[:, 0:1] + 1.0)) * self.columns[:, 2:3]

    def out(self, head):
        left = self.length - 1.0 - self.columns[:, 0:1]
        return jnp.exp(-self.rate(head) * left) * self.columns[:, 3:4]

    def is_long(self):
        return self.columns[:, 4:5] > 0.5

    def split(self, x):
        long = self.columns[:, 4:5]
        return (x.astype(wide) * long).astype(low), (x.astype(wide) * (1.0 - long)).astype(low)


class Attention:
    def __init__(self, site, heads, mix, unit, out, increment, state, send, recv):
        self.site, self.heads = site, heads
        self.mix, self.unit, self.out = mix, unit, out
        self.increment, self.state, self.send, self.recv = increment, state, send, recv

    def project(self, normed, weight_hbm, z_hbm, tiles, staging, tile_sems, z_sems, pump):
        width = HEADS_DEV * DH

        def tile_copy(i):
            source = weight_hbm.at[:, pl.ds(i * width, width)]
            return pltpu.make_async_copy(source, tiles.at[i % 2], tile_sems.at[i % 2])

        def z_copy(i):
            target = z_hbm.at[:, pl.ds(i * width, width)]
            return pltpu.make_async_copy(staging.at[i % 2], target, z_sems.at[i % 2])

        tile_copy(0).start()
        for i in range(4):
            if i < 3:
                tile_copy(i + 1).start()
            tile_copy(i).wait()
            if i >= 2:
                z_copy(i - 2).wait()

            @pl.loop(0, TEAM)
            def _(r, i=i):
                rows = self.heads.count // TEAM
                at = pl.ds(pl.multiple_of(r * rows, rows), rows)
                z = dot(normed[at], tiles[i % 2])
                staging[i % 2, at] = z
                if i < 3:
                    value = z * jax.nn.sigmoid(z) if i < 2 else z
                    self.mix[at, i * width : (i + 1) * width] = value.astype(low)
                else:
                    self.unit[at] = z

            z_copy(i).start()
            pump()
        for i in (2, 3):
            z_copy(i).wait()

    def state_copy(self):
        return remote(
            self.increment, self.state, self.send.at[0], self.recv.at[0], self.site.far_mate
        )

    def run(self, pump):
        heads, mix = self.heads, self.mix

        @pl.loop(0, HEADS_DEV)
        def _(h):
            key_out = (mix[:, head_lanes(1, h)].astype(wide) * heads.out(h)).astype(low)
            mix[:, head_lanes(3, h)] = key_out
            for i, part in enumerate(heads.split(key_out)):
                self.increment[h, i] = outer(part, mix[:, head_lanes(2, h)]).astype(low)

        self.state_copy().start()
        pump()

        @pl.loop(0, HEADS_DEV)
        def _(h):
            scores = dot_t(mix[:, head_lanes(0, h)], mix[:, head_lanes(1, h)])
            weights = (scores * heads.decay(h)).astype(low)
            self.out[:, head_lanes(0, h)] = dot(weights, mix[:, head_lanes(2, h)])

        pump()
        self.state_copy().wait()

        @pl.loop(0, HEADS_DEV)
        def _(h):
            query = mix[:, head_lanes(0, h)]
            carried = jnp.where(
                heads.is_long(), dot(query, self.state[h, 0]), dot(query, self.state[h, 1])
            )
            self.out[:, head_lanes(0, h)] += carried * heads.into(h)

        pump()


def middle_kernel(model_width, hidden, streamed, *refs):
    refs = iter(refs)

    def take(count):
        return [next(refs) for _ in range(count)]

    if streamed:
        normed_hbm, attn_hbm, columns_ref, rows_ref, rates_ref = take(5)
    else:
        squares_ref, raw_ref = take(2)
    tokens_ref, cotangents_hbm, output_ref, mlp_hbm, down_hbm = take(5)
    middle_ref, middle_grad_ref, second_hbm, hidden_hbm, pairs_hbm, gathered_hbm = take(6)
    coefficients_ref, down_out = take(2)
    if streamed:
        z_hbm, out_hbm, state_ref = take(3)
    cotangents, mlp, down, second, hiddens, pairs, gathered, proj, own_squares = take(9)
    part, stage, landed, reduce_send, reduce_recv, load_sems, store_sems = take(7)
    gather_send, gather_recv, square_send, square_recv, coef_send, coef_recv = take(6)
    if streamed:
        stream_sems = take(10)
        squares_ref, raw_ref, tiles, staging, unit, heads_out, increment = take(7)
        tile_sems, z_sems, state_send, state_recv, out_sem, normed_sem = take(6)
    site = Site()
    rows = tokens_ref.shape[0]
    if streamed:
        site.meet([site.core_mate, site.side_mate, site.far_mate])
        streams = WeightStreams(
            [
                WeightStream(site, TEAM, MLP_SPLIT, mlp_hbm, mlp, stream_sems[:5]),
                WeightStream(site, 1, down_hbm.shape[0] // 16, down_hbm, down, stream_sems[5:]),
            ],
            4,
        )
        streams.start()
        streams.launch()
    else:
        site.meet()

    loads = [
        pltpu.make_async_copy(src, dst, load_sems.at[i])
        for i, (src, dst) in enumerate(
            ((cotangents_hbm, cotangents), (mlp_hbm, mlp), (down_hbm, down))
        )
    ][: 1 if streamed else 3]
    for load in loads:
        load.start()
    eye = lax.broadcasted_iota(jnp.int32, (rows, rows), 0) == lax.broadcasted_iota(
        jnp.int32, (rows, rows), 1
    )

    def column(row):
        return jnp.sum(jnp.where(eye, jnp.broadcast_to(row, (rows, rows)), 0.0), axis=1, keepdims=True)

    def row_of(column):
        return jnp.sum(jnp.where(eye, jnp.broadcast_to(column, (rows, rows)), 0.0), axis=0, keepdims=True)

    if streamed:
        normed_load = pltpu.make_async_copy(normed_hbm, gathered, normed_sem.at[0])
        normed_load.start()
        heads = Heads(columns_ref, rows_ref, rates_ref)
        attention = Attention(
            site, heads, second, unit, heads_out, increment, state_ref, state_send, state_recv
        )
        normed_load.wait()
        attention.project(
            gathered, attn_hbm, z_hbm, tiles, staging, tile_sems, z_sems, lambda: None
        )
        attention.run(streams.step)
        out_copy = pltpu.make_async_copy(heads_out, out_hbm, out_sem.at[0])
        out_copy.start()
        for slot in range(TEAM):
            at = pl.ds(slot * rows, rows)
            out = heads_out[at]
            squares = row_of(jnp.sum(out * out, axis=1, keepdims=True))
            squares_ref[slot] = jnp.broadcast_to(squares, (8, rows))
            raw_ref[at] = (out * unit[at]).astype(low)

    square_copies = [
        remote(
            squares_ref.at[ORDER.index(k)],
            own_squares.at[k],
            square_send.at[k],
            square_recv.at[k],
            site.device(-k),
        )
        for k in range(1, TEAM)
    ]
    for copy in square_copies:
        copy.start()

    second_ring, gathered_ring = (
        RingGather(site, rows, buffer.at[pl.ds(0, rows)], buffer, gather_send, gather_recv)
        for buffer in (second, gathered)
    )
    ring = RingSum(site, rows, part, stage, landed, reduce_send, reduce_recv)
    fill_output = fill_tiles(
        part,
        model_width,
        rows,
        lambda start, size: raw_ref[start : start + size],
        lambda value, at: dot(value, output_ref[:, at]),
    )
    fill_pairs = fill_tiles(
        part,
        model_width,
        rows,
        lambda start, size: pairs[start : start + size],
        lambda value, at: dot_t(value, mlp[at]),
    )

    def between(step):
        if streamed:
            streams.step(2)

    ring.run(fill_output, between)
    total = squares_ref[0, 0:1]
    for copy in square_copies:
        copy.wait_recv()
    for k in range(1, TEAM):
        total = total + own_squares[k, 0:1]
    scale = lax.rsqrt(column(total) / model_width + epsilon)
    proj[...] = part[:rows] * scale
    middle_ref[...] = tokens_ref[...].astype(wide) + proj[...]
    second[:rows] = normalize(middle_ref[...]).astype(low)
    second_ring.start()

    def units(slot, count):
        at = pl.ds(slot * rows, count * rows)
        pair = dot(second[at], mlp[...])
        turned = pltpu.roll(pair, hidden, 1)
        hiddens[at] = (pair * turned)[:, : hiddens.shape[1]].astype(low)
        above = dot_t(cotangents[at], down[...])
        above = jnp.concatenate(
            [above, jnp.zeros((count * rows, 2 * hidden - above.shape[1]), wide)], axis=1
        )
        pairs[at] = ((above + pltpu.roll(above, hidden, 1)) * turned).astype(low)

    for load in loads:
        load.wait()
    if streamed:
        for step in range(1, TEAM // 2 + 1):
            streams.step(2)
            second_ring.step(step)
        streams.finish()
        units(0, 2)
        units(2, 2)
    else:
        units(0, 1)
        for step in range(1, TEAM // 2):
            second_ring.step(step)
            units(2 * step - 1, 2)
        second_ring.step(TEAM // 2)
        units(TEAM - 1, 1)
    stores = [
        pltpu.make_async_copy(src, dst, store_sems.at[i])
        for i, (src, dst) in enumerate(
            (
                (second, second_hbm),
                (hiddens, hidden_hbm),
                (pairs, pairs_hbm),
                (down, down_out),
                (gathered, gathered_hbm),
            )
        )
    ]
    for store in stores[:4]:
        store.start()

    ring.run(fill_pairs)
    middle_grad_ref[...] = cotangents[:rows].astype(wide) + norm_back(middle_ref[...], part[:rows])
    middle_low = middle_grad_ref[...].astype(low)
    gathered[:rows] = middle_low
    second_ring.finish()
    gathered_ring.start()
    inner = jnp.sum(middle_low.astype(wide) * proj[...], axis=1, keepdims=True) / model_width
    coefficients_ref[0, 0:1] = row_of(scale)
    coefficients_ref[0, 1:2] = row_of(scale * scale * inner)
    coefficients_ref[0, 2:8] = jnp.zeros((6, rows), wide)
    coef_copies = [
        remote(
            coefficients_ref.at[0],
            coefficients_ref.at[ORDER.index(k)],
            coef_send.at[k],
            coef_recv.at[k],
            site.device(k),
        )
        for k in range(1, TEAM)
    ]
    for copy in coef_copies:
        copy.start()
    for step in range(1, TEAM // 2 + 1):
        gathered_ring.step(step)
    stores[4].start()
    gathered_ring.finish()
    for copy in coef_copies:
        copy.wait()
    for copy in square_copies:
        copy.wait_send()
    for store in stores:
        store.wait()
    if streamed:
        out_copy.wait()


def middle_call(plan, attention, tokens, cotangents, output_w, mlp_w, down_w):
    rows, width = tokens.shape
    team_rows = rows * TEAM
    streamed = plan.fused
    hidden = mlp_w.shape[-1] // 2
    padded = 8 * down_w.shape[0] if streamed else down_w.shape[0]
    head_width = HEADS_DEV * DH
    vmem, anywhere = pl.BlockSpec(memory_space=pltpu.VMEM), pl.BlockSpec(memory_space=pl.ANY)
    flops = 2 * team_rows * width * (2 * head_width + 4 * hidden + padded)
    shapes = [
        jax.ShapeDtypeStruct((rows, width), wide),
        jax.ShapeDtypeStruct((rows, width), wide),
        jax.ShapeDtypeStruct((team_rows, width), low),
        jax.ShapeDtypeStruct((team_rows, padded), low),
        jax.ShapeDtypeStruct((team_rows, 2 * hidden), low),
        jax.ShapeDtypeStruct((team_rows, width), low),
        jax.ShapeDtypeStruct((TEAM, 8, rows), wide),
        jax.ShapeDtypeStruct((padded, width), low),
    ]
    out_specs = [vmem, vmem] + [anywhere] * 4 + [vmem, anywhere]
    scratch = [
        pltpu.VMEM((team_rows, width), low),
        pltpu.VMEM((width, 2 * hidden), low),
        pltpu.VMEM((padded, width), low),
        pltpu.VMEM((team_rows, width), low),
        pltpu.VMEM((team_rows, padded), low),
        pltpu.VMEM((team_rows, 2 * hidden), low),
        pltpu.VMEM((team_rows, width), low),
        pltpu.VMEM((rows, width), wide),
        pltpu.VMEM((TEAM, 8, rows), wide),
        *ring_sum_scratch(rows, width),
        pltpu.SemaphoreType.DMA((3,)),
        pltpu.SemaphoreType.DMA((5,)),
        *RingGather.scratch(),
        *[pltpu.SemaphoreType.DMA((TEAM,))] * 4,
    ]
    if streamed:
        state = (HEADS_DEV, 2, DH, DH)
        shapes += [
            jax.ShapeDtypeStruct((team_rows, 4 * head_width), wide),
            jax.ShapeDtypeStruct((team_rows, head_width), wide),
            jax.ShapeDtypeStruct(state, low),
        ]
        out_specs += [anywhere, anywhere, vmem]
        scratch += [
            *WeightStream.scratch(TEAM, MLP_SPLIT),
            *WeightStream.scratch(1, down_w.shape[0] // 16),
            pltpu.VMEM((TEAM, 8, rows), wide),
            pltpu.VMEM((team_rows, head_width), low),
            pltpu.VMEM((2, width, head_width), low),
            pltpu.VMEM((2, team_rows, head_width), wide),
            pltpu.VMEM((team_rows, head_width), wide),
            pltpu.VMEM((team_rows, head_width), wide),
            pltpu.VMEM(state, low),
            *[pltpu.SemaphoreType.DMA((n,)) for n in (2, 2, 1, 1, 1, 1)],
        ]
    first = [anywhere, anywhere, vmem, vmem, vmem] if streamed else [vmem, vmem]
    return pl.pallas_call(
        functools.partial(middle_kernel, width, hidden, streamed),
        out_shape=tuple(shapes),
        in_specs=first + [vmem, anywhere, vmem, anywhere, anywhere],
        out_specs=tuple(out_specs),
        scratch_shapes=scratch,
        compiler_params=pltpu.CompilerParams(
            collective_id=0, has_side_effects=True, vmem_limit_bytes=62 * 2**20
        ),
        cost_estimate=pl.CostEstimate(flops=flops, bytes_accessed=60 * 2**20, transcendentals=0),
    )(*attention, tokens, cotangents, output_w, mlp_w, down_w)


def team_rates():
    place = lax.axis_index("seq") % TEAM
    return head_rates((place * HEADS_DEV + jnp.arange(HEADS_DEV)).astype(wide))


def team_places(plan, lengths, long_rows, short_rows):
    sub = lax.axis_index("seq") // TEAM
    spot = jnp.asarray(PLACE, jnp.int32)[lax.axis_index("seq") % TEAM]
    blocks = jnp.asarray(RING, jnp.int32)[(spot + TEAM - jnp.asarray(ORDER)) % TEAM]
    ends = jnp.cumsum(lengths)
    starts = ends - lengths

    def places(rows):
        return (blocks[:, None] * rows + jnp.arange(rows, dtype=jnp.int32)[None]).reshape(-1)

    def segment_of(place):
        return jnp.sum((place[..., None] >= ends).astype(jnp.int32), axis=-1)

    long_place, short_place = places(long_rows), places(short_rows)
    first = sub * short_rows * TEAM
    last = first + short_rows * TEAM - 1
    segment = segment_of(first + short_place)
    enter = (segment == segment_of(first)) & (jnp.sum((starts == first).astype(jnp.int32)) == 0)
    leave = segment == segment_of(last)
    place = jnp.stack([long_place, short_place])
    return place, jnp.stack([jnp.full_like(long_place, -1), segment]), enter, leave


def decay_tables(plan, lengths, long_rows, short_rows):
    rates = team_rates()
    place, segments, enter, leave = team_places(plan, lengths, long_rows, short_rows)
    spacing = (place[:, :, None] - place[:, None, :]).astype(wide)
    linked = (segments[:, :, None] == segments[:, None, :]) & (spacing >= 0.0)
    decay = jnp.where(
        linked[:, None],
        jnp.exp(-rates[None, :, None, None] * jnp.where(linked, spacing, 0.0)[:, None]),
        0.0,
    )
    if plan.subs == 1:
        return decay, None
    sub = lax.axis_index("seq") // TEAM
    first = sub * short_rows * TEAM
    last = first + short_rows * TEAM - 1
    ends = jnp.cumsum(lengths)
    starts = ends - lengths
    masks_in = jnp.stack([jnp.ones_like(enter), enter]).astype(wide)
    masks_out = jnp.stack([jnp.ones_like(leave), leave]).astype(wide)
    size = jnp.asarray((long_rows * TEAM, short_rows * TEAM), wide)[:, None]
    into = jnp.exp(-rates[None, :, None] * (place.astype(wide) + 1.0)[:, None]) * masks_in[:, None]
    out = (
        jnp.exp(-rates[None, :, None] * (size - 1.0 - place.astype(wide))[:, None])
        * masks_out[:, None]
    )
    broken = jnp.sum(((starts >= first) & (starts <= last)).astype(jnp.int32)) > 0
    unbroken = jnp.stack([jnp.ones((), bool), ~broken]).astype(wide)
    carry = jnp.exp(-rates[None, :] * size) * unbroken[:, None]
    return decay, (into[..., None], out[..., None], carry[..., None, None])


def carried(plan, carry, increment, backward):
    sub = lax.axis_index("seq") // TEAM
    if plan.subs == 2:
        pairs = [(i, (i + TEAM) % plan.seq) for i in range(plan.seq)]
        got = lax.ppermute(increment.astype(low), "seq", pairs)
        return jnp.where(sub == (0 if backward else 1), got, jnp.zeros_like(got))
    groups = plan.sub_groups
    all_carry = lax.all_gather(carry, "seq", axis_index_groups=groups)
    all_increment = lax.all_gather(increment.astype(low), "seq", axis_index_groups=groups)
    state = jnp.zeros_like(increment)
    for hop in range(plan.subs):
        source = plan.subs - 1 - hop if backward else hop
        ahead = source > sub if backward else source < sub
        update = all_carry[source] * state + all_increment[source].astype(wide)
        state = jnp.where(ahead, update, state)
    return state.astype(low)


def bmm(left, right, left_dim, right_dim):
    return lax.dot_general(
        left,
        right,
        (((left_dim,), (right_dim,)), ((0, 1), (0, 1))),
        preferred_element_type=wide,
    )


def local(
    plan,
    tokens,
    cotangent,
    short_lengths,
    w_query,
    w_key,
    w_value,
    w_unit,
    w_output,
    w_gate,
    w_up,
    w_down,
):
    row_count, model_width = tokens.shape
    weight_rows = w_query.shape[0]
    groups = plan.groups
    piece = w_down.shape[0]
    hidden = piece * groups
    head_width = HEADS_DEV * DH
    team_tokens = row_count * TEAM

    def by_heads(w):
        return w.reshape(weight_rows, TEAM, head_width).transpose(1, 0, 2)

    def by_units(w):
        return w.reshape(weight_rows, groups, TEAM, piece).transpose(2, 0, 1, 3).reshape(TEAM, weight_rows, hidden)

    inputs = tokens.astype(wide)
    attn_pieces = jnp.concatenate([by_heads(w) for w in (w_query, w_key, w_value, w_unit)], axis=2)
    mlp_pieces = jnp.concatenate([by_units(w_gate), by_units(w_up)], axis=2)
    normed_own = normalize(inputs).astype(low)
    if plan.fused:
        normed, cotangents, attn_w, output_w = front_call(normed_own, cotangent, attn_pieces, w_output)
        mlp_w, down_w = mlp_pieces, w_down
    else:
        output_w = plan.team_rows(w_output)
        attn_w = plan.across(plan.swap(attn_pieces).reshape(TEAM * weight_rows, 4 * head_width))
        mlp_w = plan.across(plan.swap(mlp_pieces).reshape(TEAM * weight_rows, 2 * hidden))
        down_w = plan.across(w_down)
        normed = jnp.concatenate(plan.ring_gather(normed_own), axis=0)
        cotangents = jnp.concatenate(plan.ring_gather(cotangent), axis=0)

    def to_heads(x):
        x = x.reshape(TEAM, 2, LONG_DEV, HEADS_DEV, DH).transpose(1, 3, 0, 2, 4)
        return x.reshape(2, HEADS_DEV, TEAM * LONG_DEV, DH)

    def from_heads(x):
        x = x.reshape(2, HEADS_DEV, TEAM, LONG_DEV, DH).transpose(2, 0, 3, 1, 4)
        return x.reshape(team_tokens, head_width)

    def heads_of(z_all):
        z_query, z_key, z_value, _ = jnp.split(z_all, 4, axis=1)
        query = to_heads(jax.nn.silu(z_query).astype(low))
        key = to_heads(jax.nn.silu(z_key).astype(low))
        value = to_heads(z_value.astype(low))
        weights = (bmm(query, key, 3, 3) * decay).astype(low)
        return query, key, value, weights

    def rows(x, k):
        return x[k * row_count : (k + 1) * row_count]

    decay, passing = decay_tables(plan, short_lengths[0], LONG_DEV, SHORT_DEV)
    into, out, carry = passing or (None, None, None)
    if plan.fused:
        tables = attention_tables(plan, short_lengths[0], team_rates())
        *results, z_all, heads_out, got = middle_call(
            plan, (normed, attn_w, *tables), tokens, cotangents, output_w, mlp_w, down_w
        )
        query, key, value, weights = heads_of(z_all)
        key_out = (key.astype(wide) * out).astype(low)
        ahead = lax.axis_index("seq") >= TEAM
        state = jnp.where(ahead, got, jnp.zeros_like(got)).transpose(1, 0, 2, 3)
    else:
        z_all = dot(normed, attn_w)
        query, key, value, weights = heads_of(z_all)
        heads_out = bmm(weights, value, 3, 2)
        if passing is not None:
            key_out = (key.astype(wide) * out).astype(low)
            state = carried(plan, carry, bmm(key_out, value, 2, 2), False)
            heads_out = heads_out + bmm(query, state, 3, 2) * into
        heads_out = from_heads(heads_out)
        squares = jnp.sum(heads_out * heads_out, axis=1).reshape(TEAM, 1, row_count)
        squares = jnp.broadcast_to(squares, (TEAM, 8, row_count))
        gated_raw = (heads_out * z_all[:, 3 * head_width :]).astype(low)
        results = middle_call(
            plan, (squares, gated_raw), tokens, cotangents, output_w, mlp_w, down_w
        )
    middle, middle_grad, second, hidden_low, pair_grads, middle_all, coefficients, down_w = results
    z_query, z_key, _, z_unit = jnp.split(z_all, 4, axis=1)
    scale_rows = coefficients[:, 0].reshape(team_tokens, 1)
    inner_rows = coefficients[:, 1].reshape(team_tokens, 1)
    down_terms = outer(hidden_low, cotangents)
    pair_terms = outer(second, pair_grads)
    if plan.fused:
        down_sum, grad_pair, grad_down = back_call(
            1,
            row_count,
            hidden_low,
            down_w,
            False,
            [
                (pair_terms.astype(low), TEAM, MLP_SPLIT, TEAM * weight_rows),
                (down_terms.astype(low), 1, piece // 16, piece),
            ],
        )
    else:
        down_sum = plan.ring_reduce(lambda i: dot(rows(hidden_low, i), down_w))
        grad_down = plan.across_sum(down_terms)
        grad_pair = plan.across_sum(pair_terms).astype(low)
        grad_pair = plan.swap(grad_pair.reshape(TEAM, weight_rows, 2 * hidden))
    mixed = (middle + down_sum).astype(low)

    def from_units(x):
        x = x.reshape(TEAM, weight_rows, groups, piece).transpose(1, 2, 0, 3)
        return x.reshape(weight_rows, TEAM * hidden).astype(wide)

    grad_gate = from_units(grad_pair[:, :, :hidden])
    grad_up = from_units(grad_pair[:, :, hidden:])

    gated_grad = dot_t(middle_all, output_w)
    normed_heads = heads_out * scale_rows
    gated = (normed_heads * z_unit).astype(low)
    output_terms = outer(gated, middle_all)
    unit_grad = (gated_grad * normed_heads).astype(low)
    heads_grad = to_heads(
        (scale_rows * gated_grad * z_unit - heads_out * inner_rows).astype(low)
    )
    scores = (bmm(heads_grad, value, 3, 3) * decay).astype(low)
    query_grad = bmm(scores, key, 3, 2)
    key_grad = bmm(scores, query, 2, 2)
    value_grad = bmm(weights, heads_grad, 2, 2)
    if passing is not None:
        query_grad = query_grad + bmm(heads_grad, state, 3, 3) * into
        local_state = bmm(query, (heads_grad.astype(wide) * into).astype(low), 2, 2)
        state_grad = carried(plan, carry, local_state, True)
        key_grad = key_grad + bmm(value, state_grad, 3, 3) * out
        value_grad = value_grad + bmm(key_out, state_grad, 3, 2)

    def silu_slope(z):
        sigma = jax.nn.sigmoid(z)
        return sigma * (1.0 + z * (1.0 - sigma))

    z_grads = jnp.concatenate(
        [
            (from_heads(query_grad) * silu_slope(z_query)).astype(low),
            (from_heads(key_grad) * silu_slope(z_key)).astype(low),
            from_heads(value_grad).astype(low),
            unit_grad,
        ],
        axis=1,
    )
    four_terms = outer(normed, z_grads)
    if plan.fused:
        first_grad, grad_four, grad_output = back_call(
            2,
            row_count,
            z_grads,
            attn_w,
            True,
            [
                (four_terms.astype(low), TEAM, ATTN_SPLIT, TEAM * weight_rows),
                (output_terms.astype(low), 1, 2, weight_rows),
            ],
        )
    else:
        first_grad = plan.ring_reduce(lambda i: dot_t(rows(z_grads, i), attn_w))
        grad_four = plan.across_sum(four_terms).astype(low)
        grad_four = plan.swap(grad_four.reshape(TEAM, weight_rows, 4 * head_width))
        grad_output = plan.across_sum(output_terms)
    grad_output = plan.team_rows_back(grad_output)

    def from_columns(x):
        return x.transpose(1, 0, 2).reshape(weight_rows, TEAM * head_width).astype(wide)

    grad_query, grad_key, grad_value, grad_unit = (
        from_columns(grad_four[:, :, i * head_width : (i + 1) * head_width]) for i in range(4)
    )
    tokens_grad = (middle_grad + norm_back(inputs, first_grad)).astype(low)
    return (
        mixed,
        tokens_grad,
        grad_query,
        grad_key,
        grad_value,
        grad_unit,
        grad_output,
        grad_gate,
        grad_up,
        grad_down,
    )


def solution(mesh):
    plan = Plan(mesh)
    rows = P(("dp", "seq"), None)
    in_specs = (rows, rows, P("dp", None)) + (rows,) * 8

    def layer(*args):
        return local(plan, *args)

    return jax.shard_map(layer, mesh=mesh, in_specs=in_specs, out_specs=(rows,) * 10, check_vma=False)
```

time: 670 us -> 665 us (level)
  the two profiles are of different devices: /device:TPU:28 before, /device:TPU:2 now
where the time goes in v4:
time: 665 us; the launch traced here: 658 us
  Pallas kernels  517 us (78%)
  local copies, waits for them, and re-layouts  43.8 us (7%)
  matrix products  42.7 us (6%)
  other arithmetic  26.6 us (4%)
  waiting for transfers between devices  21.9 us (3%)
    pallas_call x2, Pallas kernels, back_call(): pl.pallas_call(functools.partial(back_kernel, width, rows, transposed, ki...  214 us
    pallas_call x1, Pallas kernels, middle_call(): pl.pallas_call(functools.partial(middle_kernel, width, hidden, streamed),...  204 us
    pallas_call x1, Pallas kernels, front_call(): pl.pallas_call(front_kernel, out_shape=(jax.ShapeDtypeStruct((TEAM * rows...  98.8 us
    dot_general x4, matrix products, outer(): lax.dot_general(left, right, (((0,), (0,)), ((), ())), preferred_element_...  28.4 us
    ppermute x1, waiting for transfers between devices, team_rows_back(): return lax.ppermute(x, ('dp', 'seq'), pairs)  21.9 us
    convert_element_type x6, local copies, waits for them, and re-layouts, from_units(): return x.reshape(weight_rows, TEAM * hidden).astype(wide)  17.8 us
  transfers between devices with their start and end apart: 2, of which 1 were waited for; matrix products, arithmetic and copies ran while one was open for 7% of the time, Pallas kernels for 19%

profile of v4, /device:TPU:2, one launch (start us, length us, event | category | flops | bytes accessed | tf_op | source)
XLA Modules:
  0.0 658.1 jit_solution(10686113579490257678)
XLA Ops:
  0.7 1.3 dynamic_slice.6
  3.4 1.3 gather_fusion
  6.0 1.0 convert_select_fusion
  7.0 0.9 fusion.20
  7.9 1.3 fusion.27
  9.8 1.3 broadcast_compare_fusion
  11.2 1.8 compare_and_fusion.1
  14.7 0.8 copy.78.refs_2_
  16.6 1.2 fusion.4
  18.4 0.9 fusion.5.normed_ref
  19.4 2.1 reshape.399
  21.6 1.2 reshape.400
  22.8 2.1 reshape.401
  25.0 1.2 reshape.402
  26.2 1.1 bitcast_bitcast_fusion
  27.3 1.2 pad_maximum_fusion.1.refs_8_
  28.5 1.1 pad_maximum_fusion.2.pieces_ref
  29.7 98.8 %shard_map.249 = (bf16[512,2048]{1,0:T(8,128)(2,1)}, bf16[512,2048]{1,0:T(8,128)(2,1)}, bf16[2048,2048]{1,0:T(8,128)(2,1)}, bf16[512,2048]{1,0:T(8,128)(2,1)}) custom-call(bf16[128,2048]{1,0:T(8,128)(2,1)} %fusion.5.normed_ref, bf16[128,2048]{1,0:T(8,128)(2,1)} %cotangent_ref.1, bf16[4,64,2048]{2,1,0:T(8,128)(2,1)} %pad_maximum_fusion.2.pieces_ref, ...), custom_call_target="tpu_custom_call" | custom-call | bytes 62914560 | tf_op jit(solution)/shard_map/pallas_call | solution.py:769
  129.1 204.0 %shard_map.250 = (f32[128,2048]{1,0:T(8,128)}, f32[128,2048]{1,0:T(8,128)}, bf16[512,2048]{1,0:T(8,128)(2,1)}, bf16[512,1408]{1,0:T(8,128)(2,1)}, bf16[512,2816]...) custom-call(bf16[512,2048]{1,0:T(8,128)(2,1)} %get-tuple-element.31., ...), custom_call_target="tpu_custom_call" | custom-call | flops 16911433728 | bytes 62914560 | tf_op jit(solution)/shard_map/pallas_call | solution.py:1245
  333.9 1.3 split.28
  335.2 5.3 multiply_convert_fusion.7
  344.8 2.5 fusion.12
  347.5 1.3 convolution_convert_fusion.4
  348.8 1.5 collective-permute-start
  350.3 4.3 convolution_convert_fusion.3.refs_3_
  354.7 2.9 fusion
  357.6 7.7 %convolution_convert_fusion.2.refs_3_ = bf16[1408,2048]{1,0:T(8,128)(2,1)} fusion(bf16[512,1408]{1,0:T(8,128)(2,1)S(1)} %copy-done.13, bf16[512,2048]{1,0:T(8,128)(2,1)} %get-tuple-element.33.refs_6_), kind=kOutput, calls=%fused_computation.3 | convolution fusion | flops 2955673600 | bytes 9306112 | tf_op jit(solution)/shard_map/dot_general | solution.py:51
  365.3 8.9 %convolution_convert_fusion.refs_2_ = bf16[2048,2816]{1,0:T(8,128)(2,1)} fusion(bf16[512,2048]{1,0:T(8,128)(2,1)S(1)} %copy-done.40, bf16[512,2816]{1,0:T(8,128)(2,1)S(1)} %copy-done.39), kind=kOutput, calls=%fused_computation.1 | convolution fusion | flops 5911347200 | bytes 16515072 | tf_op jit(solution)/shard_map/dot_general | solution.py:51
  374.2 123.4 %shard_map.251 = (f32[128,2048]{1,0:T(8,128)}, bf16[4,64,2816]{2,1,0:T(8,128)(2,1)}, f32[176,2048]{1,0:T(8,128)}) custom-call(bf16[512,1408]{1,0:T(8,128)(2,1)} %get-tuple-element.36.refs_0_, bf16[1408,2048]{1,0:T(8,128)(2,1)} %get-tuple-element.37.refs_1_, bf16[2048,2816]{1,0:T(8,128)(2,1)} %convolution_convert_fusion.refs_2_, ...), custom_call_target="tpu_custom_call" | custom-call | flops 2952790016 | bytes 62914560 | tf_op jit(solution)/shard_map/pallas_call | solution.py:834
  497.6 2.7 slice_convert_fusion.1
  500.2 2.6 reshape.422
  502.9 2.7 copy.96
  505.6 4.2 reshape.420
  509.8 1.4 reshape.423
  511.2 2.7 copy.97
  513.9 4.2 reshape.421
  518.1 0.9 add_convert_fusion
  520.2 1.3 fusion.1
  522.2 1.6 fusion.11
  523.9 1.6 fusion.3
  526.0 7.5 %convolution_convert_fusion.1.refs_2_ = bf16[2048,2048]{1,0:T(8,128)(2,1)} fusion(bf16[512,2048]{1,0:T(8,128)(2,1)S(1)} %copy-done.36, bf16[512,512]{1,0:T(8,128)(2,1)S(1)} %copy-done.21, bf16[512,512]{1,0:T(8,128)(2,1)S(1)} %bitcast.143, bf16[512,512]{1,0:T(8,128)(2,1)S(1)} %fusion.11, bf16[512,512]{1,0:T(8,128)(2,1)S(1)} %copy-done.11), kind=kOutput, calls=%fused_computation.2 | convolution fusion | flops 4307550208 | bytes 12582912 | tf_op jit(solution)/shard_map/dot_general | solution.py:51
  533.5 1.7 pad_maximum_fusion.refs_0_
  535.2 90.7 %shard_map.252 = (f32[128,2048]{1,0:T(8,128)}, bf16[4,64,2048]{2,1,0:T(8,128)(2,1)}, f32[64,2048]{1,0:T(8,128)}) custom-call(bf16[512,2048]{1,0:T(8,128)(2,1)} %pad_maximum_fusion.refs_0_, bf16[2048,2048]{1,0:T(8,128)(2,1)} %get-tuple-element.32.refs_1_, bf16[2048,2048]{1,0:T(8,128)(2,1)} %convolution_convert_fusion.1.refs_2_, ...), custom_call_target="tpu_custom_call" | custom-call | flops 4294967296 | bytes 62914560 | tf_op jit(solution)/shard_map/pallas_call | solution.py:834
  625.8 1.4 convert_bitcast_fusion
  630.7 1.9 collective-permute-start.1
  632.8 1.2 fusion.9
  634.1 21.9 %collective-permute-done.1 = f32[64,2048]{1,0:T(8,128)S(1)} collective-permute-done((f32[64,2048]{1,0:T(8,128)S(1)}, f32[64,2048]{1,0:T(8,128)S(1)}, u32[]{:S(2)}, u32[]{:S(2)}) %collective-permute-start.1) | collective-permute-done | bytes 524320 | tf_op jit(solution)/shard_map/ppermute | solution.py:159
  656.8 1.1 copy.130
  (140 shorter events, 18.2 us)
Async XLA Ops:
  0.6 17.8 %copy-start = (bf16[128,2048]{1,0:T(8,128)(2,1)S(1)}, bf16[128,2048]{1,0:T(8,128)(2,1)}, u32[]{:S(2)}) copy-start(bf16[128,2048]{1,0:T(8,128)(2,1)} %refs_5_.1) | copy-start | bytes 1572868
  0.7 18.7 %copy-start.18 = (bf16[64,5632]{1,0:T(8,128)(2,1)S(1)}, bf16[64,5632]{1,0:T(8,128)(2,1)}, u32[]{:S(2)}) copy-start(bf16[64,5632]{1,0:T(8,128)(2,1)} %param.26) | copy-start | bytes 2162692
  14.7 6.9 %copy-start.26 = (f32[8,512]{1,0:T(8,128)}, f32[8,512]{1,0:T(8,128)S(1)}, u32[]{:S(2)}) copy-start(f32[8,512]{1,0:T(8,128)S(1)} %stack.41.refs_3_) | copy-start | bytes 49156
  18.4 1.0 copy-start.31
  21.6 1.2 copy-start.19
  25.0 2.3 copy-start.23
  25.0 2.3 copy-start.24
  28.5 99.9 %copy-start.35 = (f32[8]{0:T(128)S(1)}, f32[8]{0:T(128)}, u32[]{:S(2)}) copy-start(f32[8]{0:T(128)} %pad.10) | copy-start | bytes 100
  340.8 1.0 copy-start.20
  340.8 1.1 copy-start.25
  340.8 1.0 copy-start.34
  341.0 1.4 copy-start.9
  341.3 13.4 %copy-start.4 = (bf16[2,4,4,64,128]{4,3,2,1,0:T(8,128)(2,1)}, bf16[2,4,4,64,128]{4,3,2,1,0:T(8,128)(2,1)S(1)}, u32[]{:S(2)}) copy-start(bf16[2,4,4,64,128]{4,3,2,1,0:T(8,128)(2,1)S(1)} %copy.82) | copy-start | bytes 1572868
  342.4 1.0 copy-start.6
  342.4 0.6 copy-start.29
  342.4 0.7 copy-start.30
  342.4 0.7 copy-start.27
  342.5 0.8 copy-start.28
  342.5 1.2 copy-start.22
  347.3 3.0 copy-start.38
  347.5 7.2 %copy-start.2 = (bf16[4,2,64,4,128]{4,2,0,3,1:T(8,128)(2,1)}, bf16[4,2,64,4,128]{4,2,0,3,1:T(8,128)(2,1)S(1)}, u32[]{:S(2)}) copy-start(bf16[4,2,64,4,128]{4,2,0,3,1:T(8,128)(2,1)S(1)} %copy.85) | copy-start | bytes 1572868
  348.8 171.3 %collective-permute-start = (bf16[2,4,128,128]{3,2,1,0:T(8,128)(2,1)}, bf16[2,4,128,128]{3,2,1,0:T(8,128)(2,1)}, u32[]{:S(2)}, u32[]{:S(2)}) collective-permute-start(bf16[2,4,128,128]{3,2,1,0:T(8,128)(2,1)} %convolution_convert_fusion.4), channel_id=1, source_target_pairs={{0,4},{1,5},{2,6},{3,7},{4,0},{5,1},{6,2},{7,3},{8,12},{9,13},{10,... | collective-permute-start | bytes 786440 | tf_op jit(solution)/shard_map/ppermute | solution.py:1321
  354.7 2.9 copy-start.13
  357.6 7.7 %copy-start.39 = (bf16[512,2816]{1,0:T(8,128)(2,1)S(1)}, bf16[512,2816]{1,0:T(8,128)(2,1)}, u32[]{:S(2)}) copy-start(bf16[512,2816]{1,0:T(8,128)(2,1)} %get-tuple-element.39) | copy-start | bytes 8650756
  357.6 7.7 %copy-start.40 = (bf16[512,2048]{1,0:T(8,128)(2,1)S(1)}, bf16[512,2048]{1,0:T(8,128)(2,1)}, u32[]{:S(2)}) copy-start(bf16[512,2048]{1,0:T(8,128)(2,1)} %get-tuple-element.38) | copy-start | bytes 6291460
  513.9 4.2 copy-start.15
  513.9 4.2 copy-start.16
  518.1 1.0 copy-start.3
  518.1 1.6 copy-start.7
  518.1 2.1 copy-start.10
  521.5 2.3 copy-start.5
  521.5 2.3 copy-start.17
  523.8 2.1 copy-start.11
  523.9 2.1 copy-start.21
  523.9 2.1 copy-start.36
  627.3 3.4 copy-start.37
  627.3 5.3 copy-start.1
  627.3 5.3 copy-start.8
  629.0 3.8 copy-start.14
  629.0 3.8 copy-start.32
  629.0 3.8 copy-start.33
  630.7 25.3 %collective-permute-start.1 = (f32[64,2048]{1,0:T(8,128)S(1)}, f32[64,2048]{1,0:T(8,128)S(1)}, u32[]{:S(2)}, u32[]{:S(2)}) collective-permute-start(f32[64,2048]{1,0:T(8,128)S(1)} %copy-done.37), channel_id=1, source_target_pairs={{0,0},{1,8},{2,16},{3,24},{4,1},{5,9},{6,17},{7,25},{8,2},{9,10},{... | collective-permute-start | bytes 1572872 | tf_op jit(solution)/shard_map/ppermute | solution.py:159
  632.8 23.9 %copy-start.12 = (f32[176,2048]{1,0:T(8,128)S(1)}, f32[176,2048]{1,0:T(8,128)}, u32[]{:S(2)}) copy-start(f32[176,2048]{1,0:T(8,128)} %get-tuple-element.107) | copy-start | bytes 4325380

commit v5 on v4

--- a/solution.py
+++ b/solution.py
@@ -182,6 +182,11 @@
         side = at // (TEAM // 2)
         return (self.dp, self.base + 2 * (at + side * (TEAM - 1 - 2 * at)) + side)
 
+    def block(self, slot):
+        at = (self.spot + TEAM - ORDER[slot]) % TEAM
+        side = at // (TEAM // 2)
+        return 2 * (at + side * (TEAM - 1 - 2 * at)) + side
+
     def member(self, place):
         return (self.dp, self.base + place)
 
@@ -190,18 +195,24 @@
         dp = 2 * (own_side + side * (1 - 2 * own_side)) + own_core + core * (1 - 2 * own_core)
         return 2 * dp + self.sub + far * (1 - 2 * self.sub)
 
-    def meet(self, mates=(), more=None, other=None):
+    def meet(self, mates=(), more=None, other=None, meanwhile=lambda: None):
         barrier = pltpu.get_barrier_semaphore()
         others = [self.device(k) for k in range(1, TEAM)] + list(mates)
         for device in others:
             pl.semaphore_signal(barrier, inc=1, device_id=device, device_id_type=MESH)
         if more is None:
+            meanwhile()
             pl.semaphore_wait(barrier, len(others))
             return
 
         @pl.when(more != 0)
         def _():
             pl.semaphore_signal(barrier, inc=1, device_id=other, device_id_type=MESH)
+
+        meanwhile()
+
+        @pl.when(more != 0)
+        def _():
             pl.semaphore_wait(barrier, len(others) + 1)
 
         @pl.when(more == 0)
@@ -716,39 +727,98 @@
                     self.copy(way, step, chunk).wait_send()
 
 
+def unit_pieces(groups, piece, ref, put):
+    @pl.loop(0, ref.shape[0] // 16)
+    def _(i):
+        at = pl.ds(pl.multiple_of(i * 16, 16), 16)
+        value = ref[at].astype(wide)
+        for place in range(TEAM):
+            starts = [(group * TEAM + place) * piece for group in range(groups)]
+            columns = [value[:, start : start + piece] for start in starts]
+            put(place, at, jnp.concatenate(columns, axis=1))
+
+
+def unit_columns(groups, piece, get, out_ref):
+    @pl.loop(0, out_ref.shape[0] // 16)
+    def _(i):
+        at = pl.ds(pl.multiple_of(i * 16, 16), 16)
+        places = [get(place, at).astype(wide) for place in range(TEAM)]
+        columns = [
+            places[place][:, group * piece : (group + 1) * piece]
+            for group in range(groups)
+            for place in range(TEAM)
+        ]
+        out_ref[at] = jnp.concatenate(columns, axis=1)
+
+
 def front_kernel(
-    normed_ref,
+    tokens_ref,
     cotangent_ref,
-    pieces_ref,
+    lengths_ref,
+    query_ref,
+    key_ref,
+    value_ref,
+    unit_ref,
     output_rows_ref,
+    gate_ref,
+    up_ref,
     normed_out,
     cotangents_out,
     weight_out,
     output_out,
+    mlp_pieces_ref,
+    columns_ref,
+    rows_ref,
+    rates_ref,
+    normed,
+    pieces,
     own_sems,
     *sems,
 ):
     site = Site()
-    rows = normed_ref.shape[0]
-    normed_ring = RingGather(site, rows, normed_ref, normed_out, *sems[:2])
+    rows = tokens_ref.shape[0]
+    width = HEADS_DEV * DH
+    groups = 8
+    piece = gate_ref.shape[1] // (groups * TEAM)
+    normed_ring = RingGather(site, rows, normed, normed_out, *sems[:2])
     cotangent_ring = RingGather(site, rows, cotangent_ref, cotangents_out, *sems[2:4])
-    attention = WeightStream(site, TEAM, ATTN_SPLIT, pieces_ref, weight_out, sems[4:9])
+    attention = WeightStream(site, TEAM, ATTN_SPLIT, pieces, weight_out, sems[4:9])
     output = SpreadStream(site, 2, output_rows_ref, output_out, sems[9:])
     streams = WeightStreams([attention, output], 4)
     own = [
         pltpu.make_async_copy(ref, out.at[pl.ds(0, rows)], own_sems.at[i])
-        for i, (ref, out) in enumerate(
-            ((normed_ref, normed_out), (cotangent_ref, cotangents_out))
-        )
+        for i, (ref, out) in enumerate(((normed, normed_out), (cotangent_ref, cotangents_out)))
     ]
-    site.meet([site.core_mate, site.side_mate, site.far_mate], output.elsewhere, output.origin)
+
+    def cut():
+        for i, ref in enumerate((query_ref, key_ref, value_ref, unit_ref)):
+            for place in range(TEAM):
+                columns = ref[:, place * width : (place + 1) * width]
+                pieces[place, :, i * width : (i + 1) * width] = columns
+
+    mates = [site.core_mate, site.side_mate, site.far_mate]
+    site.meet(mates, output.elsewhere, output.origin, cut)
     streams.start()
+    streams.launch()
+    normed[...] = normalize(tokens_ref[...].astype(wide)).astype(low)
     for copy in own:
         copy.start()
-    streams.launch()
+    streams.step(1)
+    normed_ring.start()
+    columns_ref[...] = attention_table(site, lengths_ref, columns_ref.shape, 0)
+    rows_ref[...] = attention_table(site, lengths_ref, rows_ref.shape, 1)
+    heads = lax.broadcasted_iota(jnp.int32, rates_ref.shape, 0)
+    rates_ref[...] = head_rates((site.place * HEADS_DEV + heads).astype(wide))
     streams.step(2)
-    normed_ring.start()
-    streams.step(4)
+    hidden = groups * piece
+    for i, ref in enumerate((gate_ref, up_ref)):
+
+        def put(place, at, columns, start=i * hidden):
+            mlp_pieces_ref[place, at, start : start + hidden] = columns.astype(low)
+
+        unit_pieces(groups, piece, ref, put)
+        streams.step(1)
+    streams.step(1)
     normed_ring.step(1)
     cotangent_ring.start()
     streams.step(3)
@@ -763,109 +833,70 @@
         copy.wait()
 
 
-def front_call(normed, cotangent, pieces, output_rows):
-    rows, width = normed.shape
+def front_call(tokens, cotangent, lengths, attention, output_rows, gate, up):
+    rows, width = tokens.shape
+    weight_rows = gate.shape[0]
     anywhere = pl.BlockSpec(memory_space=pl.ANY)
+    vmem = pl.BlockSpec(memory_space=pltpu.VMEM)
+    head_width = HEADS_DEV * DH
+    piece_width = 2 * gate.shape[1] // TEAM
     return pl.pallas_call(
         front_kernel,
         out_shape=(
             jax.ShapeDtypeStruct((TEAM * rows, width), low),
             jax.ShapeDtypeStruct((TEAM * rows, width), low),
-            jax.ShapeDtypeStruct((8 * TEAM * pieces.shape[1], pieces.shape[2]), low),
+            jax.ShapeDtypeStruct((8 * TEAM * weight_rows, 4 * head_width), low),
             jax.ShapeDtypeStruct((8 * output_rows.shape[0], output_rows.shape[1]), low),
+            jax.ShapeDtypeStruct((TEAM, weight_rows, piece_width), low),
+            jax.ShapeDtypeStruct((TEAM * rows, 8), wide),
+            jax.ShapeDtypeStruct((8, TEAM * rows), wide),
+            jax.ShapeDtypeStruct((8, 128), wide),
         ),
-        in_specs=[pl.BlockSpec(memory_space=pltpu.VMEM)] * 4,
-        out_specs=(anywhere,) * 4,
+        in_specs=[vmem, vmem, pl.BlockSpec(memory_space=pltpu.SMEM)] + [vmem] * 7,
+        out_specs=(anywhere,) * 4 + (vmem,) * 4,
         scratch_shapes=[
+            pltpu.VMEM((rows, width), low),
+            pltpu.VMEM((TEAM, weight_rows, 4 * head_width), low),
             pltpu.SemaphoreType.DMA((2,)),
             *RingGather.scratch(),
             *RingGather.scratch(),
             *WeightStream.scratch(TEAM, ATTN_SPLIT),
             *WeightStream.scratch(1, 2),
         ],
-        compiler_params=pltpu.CompilerParams(collective_id=3, has_side_effects=True),
+        compiler_params=pltpu.CompilerParams(
+            collective_id=3, has_side_effects=True, vmem_limit_bytes=32 * 2**20
+        ),
         cost_estimate=pl.CostEstimate(flops=0, bytes_accessed=60 * 2**20, transcendentals=0),
-    )(normed, cotangent, pieces, output_rows)
-
-
-def back_kernel(width, rows, transposed, kinds, *refs):
-    count = len(kinds)
-    left_ref, right_ref, *refs = refs
-    sources, refs = refs[:count], refs[count:]
-    sum_ref, refs = refs[0], refs[1:]
-    results, refs = refs[:count], refs[count:]
-    part, stage, landed, send, recv, *refs = refs
-    site = Site()
-    exchanges = []
-    for i, (pieces, split) in enumerate(kinds):
-        keep, core_in, side_in, far_in, *sems = refs[: Exchange.SCRATCH]
-        refs = refs[Exchange.SCRATCH :]
-        exchanges.append(
-            Exchange(
-                site, pieces, split, sources[i], results[i], keep, core_in, side_in, far_in, sems
-            )
-        )
-    exchanges = Exchanges(exchanges)
-    site.meet([site.core_mate, site.side_mate, site.far_mate])
-    exchanges.start()
-
-    def product(value, at):
-        return dot_t(value, right_ref[at]) if transposed else dot(value, right_ref[:, at])
-
-    fill = fill_tiles(part, width, rows, lambda start, size: left_ref[start : start + size], product)
-    ring = RingSum(site, rows, part, stage, landed, send, recv)
-    ring.run(fill, lambda step: exchanges.step(2))
-    sum_ref[...] = part[:rows]
-    exchanges.finish()
-
-
-def back_call(number, rows, left, right, transposed, gradients):
-    width = right.shape[0] if transposed else right.shape[1]
-    vmem, anywhere = pl.BlockSpec(memory_space=pltpu.VMEM), pl.BlockSpec(memory_space=pl.ANY)
-    shapes, scratch = [jax.ShapeDtypeStruct((rows, width), wide)], ring_sum_scratch(rows, width)
-    for terms, pieces, split, block in gradients:
-        columns = terms.shape[1]
-        if pieces > 1:
-            shapes.append(jax.ShapeDtypeStruct((pieces, block // pieces, columns), low))
-        else:
-            shapes.append(jax.ShapeDtypeStruct((block, columns), wide))
-        scratch += Exchange.scratch(pieces, split, block, columns)
-    kinds = tuple((pieces, split) for _, pieces, split, _ in gradients)
-    return pl.pallas_call(
-        functools.partial(back_kernel, width, rows, transposed, kinds),
-        out_shape=tuple(shapes),
-        in_specs=[vmem, vmem] + [anywhere] * len(gradients),
-        out_specs=(vmem,) * len(shapes),
-        scratch_shapes=scratch,
-        compiler_params=pltpu.CompilerParams(
-            collective_id=number, has_side_effects=True, vmem_limit_bytes=60 * 2**20
-        ),
-        cost_estimate=pl.CostEstimate(
-            flops=2 * left.shape[0] * left.shape[1] * width,
-            bytes_accessed=60 * 2**20,
-            transcendentals=0,
-        ),
-    )(left, right, *[gradient[0] for gradient in gradients])
-
-
-def attention_tables(plan, lengths, rates):
-    place, segments, enter, leave = team_places(plan, lengths, LONG_DEV, SHORT_DEV)
-    sub = lax.axis_index("seq") // TEAM
-
-    def by_rows(long, short):
-        parts = jnp.stack([long.reshape(TEAM, LONG_DEV), short.reshape(TEAM, SHORT_DEV)], axis=1)
-        return parts.astype(wide).reshape(-1)
-
-    ones = jnp.ones_like(enter)
-    kinds = [
-        by_rows(place[0], place[1]),
-        by_rows(segments[0], segments[1]),
-        by_rows(ones, enter) * (sub > 0).astype(wide),
-        by_rows(ones, leave),
-        by_rows(ones, jnp.zeros_like(ones)),
-    ]
-    table = jnp.stack(kinds + [jnp.zeros_like(kinds[0])] * 3)
-    return table.T, table, jnp.broadcast_to(jnp.pad(rates, (0, 8 - HEADS_DEV))[:, None], (8, 128))
+    )(tokens, cotangent, lengths, *attention, output_rows, gate, up)
+
+
+def attention_table(site, lengths_ref, shape, axis):
+    row = lax.broadcasted_iota(jnp.int32, shape, axis)
+    kind = lax.broadcasted_iota(jnp.int32, shape, 1 - axis)
+    block_rows = LONG_DEV + SHORT_DEV
+    slot, local = row // block_rows, row % block_rows
+    long = local < LONG_DEV
+    block = jnp.zeros(shape, jnp.int32)
+    for i in range(TEAM):
+        block = jnp.where(slot == i, site.block(i), block)
+    place = jnp.where(long, block * LONG_DEV + local, block * SHORT_DEV + local - LONG_DEV)
+    lengths = [lengths_ref[0, i] for i in range(lengths_ref.shape[1])]
+    ends = [sum(lengths[1 : i + 1], lengths[0]) for i in range(len(lengths))]
+    starts = [end - length for end, length in zip(ends, lengths)]
+
+    def segment_of(at):
+        return sum(jnp.where(at >= end, 1, 0) for end in ends)
+
+    first = site.sub * SHORT_DEV * TEAM
+    segment = segment_of(place + first)
+    opened = sum(jnp.where(start == first, 1, 0) for start in starts)
+    same_first = segment == segment_of(first)
+    same_last = segment == segment_of(first + SHORT_DEV * TEAM - 1)
+    enter = jnp.where(long, 1, jnp.where(same_first, jnp.where(opened == 0, 1, 0), 0)) * site.sub
+    leave = jnp.where(long | same_last, 1, 0)
+    table = jnp.where(kind == 0, place, jnp.where(kind == 1, jnp.where(long, -1, segment), 0))
+    table = jnp.where(kind == 2, enter, jnp.where(kind == 3, leave, table))
+    return jnp.where(kind == 4, jnp.where(long, 1, 0), table).astype(wide)
 
 
 def head_lanes(part, head):
@@ -1255,6 +1286,272 @@
     )(*attention, tokens, cotangents, output_w, mlp_w, down_w)
 
 
+class AttentionBack:
+    def __init__(self, site, heads, z, mix, out_grad, grads, state, increment, landed, send, recv):
+        self.site, self.heads, self.z, self.mix = site, heads, z, mix
+        self.out_grad, self.grads, self.state = out_grad, grads, state
+        self.increment, self.landed, self.send, self.recv = increment, landed, send, recv
+
+    def state_copy(self):
+        return remote(
+            self.increment, self.landed, self.send.at[0], self.recv.at[0], self.site.far_mate
+        )
+
+    def gate(self, gathered, output, out, coefficients, column):
+        width = HEADS_DEV * DH
+        rows = self.heads.count // TEAM
+        for slot in range(TEAM):
+            at = pl.ds(slot * rows, rows)
+            scale = column(coefficients[slot, 0:1])
+            inner = column(coefficients[slot, 1:2])
+            gated = dot_t(gathered[at], output[...])
+            value = out[at]
+            self.grads[at, 3 * width :] = (gated * (value * scale)).astype(low)
+            unit = self.z[at, 3 * width :]
+            self.out_grad[at] = (scale * gated * unit - value * inner).astype(low)
+            for i in range(2):
+                z = self.z[at, i * width : (i + 1) * width]
+                self.mix[at, i * width : (i + 1) * width] = (z * jax.nn.sigmoid(z)).astype(low)
+            self.mix[at, 2 * width : 3 * width] = self.z[at, 2 * width : 3 * width].astype(low)
+
+    def feed(self):
+        heads, mix = self.heads, self.mix
+
+        @pl.loop(0, HEADS_DEV)
+        def _(h):
+            grad = (self.out_grad[:, head_lanes(0, h)].astype(wide) * heads.into(h)).astype(low)
+            for i, part in enumerate(heads.split(mix[:, head_lanes(0, h)])):
+                self.increment[h, i] = outer(part, grad).astype(low)
+            key_out = (mix[:, head_lanes(1, h)].astype(wide) * heads.out(h)).astype(low)
+            mix[:, head_lanes(3, h)] = key_out
+
+        self.state_copy().start()
+
+    def run(self, pump):
+        heads, mix, grads = self.heads, self.mix, self.grads
+        self.state_copy().wait()
+        carried_on = (1 - self.site.sub).astype(wide)
+
+        def by_part(product, h, left, right):
+            return jnp.where(
+                heads.is_long(), product(left, right[h, 0]), product(left, right[h, 1])
+            )
+
+        def slope(z):
+            sigma = jax.nn.sigmoid(z)
+            return sigma * (1.0 + z * (1.0 - sigma))
+
+        @pl.loop(0, HEADS_DEV)
+        def _(h):
+            query, key = mix[:, head_lanes(0, h)], mix[:, head_lanes(1, h)]
+            value, key_out = mix[:, head_lanes(2, h)], mix[:, head_lanes(3, h)]
+            grad = self.out_grad[:, head_lanes(0, h)]
+            decay = heads.decay(h)
+            weights = (dot_t(query, key) * decay).astype(low)
+            value_grad = outer(weights, grad)
+            value_grad += by_part(dot, h, key_out, self.landed) * carried_on
+            grads[:, head_lanes(2, h)] = value_grad.astype(low)
+            scores = (dot_t(grad, value) * decay).astype(low)
+            query_grad = dot(scores, key)
+            query_grad += by_part(dot_t, h, grad, self.state) * heads.into(h)
+            query_grad *= slope(self.z[:, head_lanes(0, h)])
+            grads[:, head_lanes(0, h)] = query_grad.astype(low)
+            key_grad = outer(scores, query)
+            key_grad += by_part(dot_t, h, value, self.landed) * (heads.out(h) * carried_on)
+            key_grad *= slope(self.z[:, head_lanes(1, h)])
+            grads[:, head_lanes(1, h)] = key_grad.astype(low)
+
+        pump()
+
+
+def exchange_scratch(gradients):
+    scratch = []
+    for terms, pieces, split, block in gradients:
+        scratch += Exchange.scratch(pieces, split, block, terms.shape[1])
+    return scratch
+
+
+def exchanges_of(site, kinds, sources, results, refs):
+    exchanges = []
+    for i, (pieces, split) in enumerate(kinds):
+        at = i * Exchange.SCRATCH
+        keep, core_in, side_in, far_in, *sems = refs[at : at + Exchange.SCRATCH]
+        exchanges.append(
+            Exchange(
+                site, pieces, split, sources[i], results[i], keep, core_in, side_in, far_in, sems
+            )
+        )
+    return Exchanges(exchanges)
+
+
+def turn_kernel(width, rows, kinds, *refs):
+    refs = iter(refs)
+
+    def take(count):
+        return [next(refs) for _ in range(count)]
+
+    count = len(kinds)
+    left_ref, right_ref, gathered, output, z_hbm, out, state, coefficients = take(8)
+    columns_ref, rows_ref, rates_ref = take(3)
+    sources = take(count)
+    sum_ref, grads_hbm = take(2)
+    results = take(count)
+    part, stage, landed, send, recv = take(5)
+    z, mix, out_grad, grads, increment, state_in, z_sem, grads_sem, state_send, state_recv = take(10)
+    site = Site()
+    exchanges = exchanges_of(site, kinds, sources, results, list(refs))
+    z_load = pltpu.make_async_copy(z_hbm, z, z_sem.at[0])
+    z_load.start()
+    site.meet([site.core_mate, site.side_mate, site.far_mate])
+    exchanges.start()
+    fill = fill_tiles(
+        part,
+        width,
+        rows,
+        lambda start, size: left_ref[start : start + size],
+        lambda value, at: dot(value, right_ref[:, at]),
+    )
+    ring = RingSum(site, rows, part, stage, landed, send, recv)
+    eye = lax.broadcasted_iota(jnp.int32, (rows, rows), 0) == lax.broadcasted_iota(
+        jnp.int32, (rows, rows), 1
+    )
+
+    def column(row):
+        return jnp.sum(jnp.where(eye, jnp.broadcast_to(row, (rows, rows)), 0.0), axis=1, keepdims=True)
+
+    back = AttentionBack(
+        site,
+        Heads(columns_ref, rows_ref, rates_ref),
+        z,
+        mix,
+        out_grad,
+        grads,
+        state,
+        increment,
+        state_in,
+        state_send,
+        state_recv,
+    )
+    z_load.wait()
+    back.gate(gathered, output, out, coefficients, column)
+    back.feed()
+    exchanges.step(1)
+    ring.run(fill, lambda step: exchanges.step(2))
+    sum_ref[...] = part[:rows]
+    back.run(lambda: exchanges.step(2))
+    store = pltpu.make_async_copy(grads, grads_hbm, grads_sem.at[0])
+    store.start()
+    exchanges.finish()
+    store.wait()
+
+
+def turn_call(left, right, rows, attention, tables, gradients):
+    width = right.shape[1]
+    team_rows = left.shape[0]
+    head_width = HEADS_DEV * DH
+    vmem, anywhere = pl.BlockSpec(memory_space=pltpu.VMEM), pl.BlockSpec(memory_space=pl.ANY)
+    shapes = [
+        jax.ShapeDtypeStruct((rows, width), wide),
+        jax.ShapeDtypeStruct((team_rows, 4 * head_width), low),
+    ]
+    for terms, pieces, _, block in gradients:
+        columns = terms.shape[1]
+        if pieces > 1:
+            shapes.append(jax.ShapeDtypeStruct((pieces, block // pieces, columns), low))
+        else:
+            shapes.append(jax.ShapeDtypeStruct((block, columns), wide))
+    state = (HEADS_DEV, 2, DH, DH)
+    kinds = tuple((pieces, split) for _, pieces, split, _ in gradients)
+    return pl.pallas_call(
+        functools.partial(turn_kernel, width, rows, kinds),
+        out_shape=tuple(shapes),
+        in_specs=[vmem] * 4 + [anywhere] + [vmem] * 6 + [anywhere] * len(gradients),
+        out_specs=(vmem, anywhere) + (vmem,) * len(gradients),
+        scratch_shapes=[
+            *ring_sum_scratch(rows, width),
+            pltpu.VMEM((team_rows, 4 * head_width), wide),
+            pltpu.VMEM((team_rows, 4 * head_width), low),
+            pltpu.VMEM((team_rows, head_width), low),
+            pltpu.VMEM((team_rows, 4 * head_width), low),
+            pltpu.VMEM(state, low),
+            pltpu.VMEM(state, low),
+            *[pltpu.SemaphoreType.DMA((1,))] * 4,
+            *exchange_scratch(gradients),
+        ],
+        compiler_params=pltpu.CompilerParams(
+            collective_id=1, has_side_effects=True, vmem_limit_bytes=62 * 2**20
+        ),
+        cost_estimate=pl.CostEstimate(
+            flops=2 * team_rows * left.shape[1] * width,
+            bytes_accessed=60 * 2**20,
+            transcendentals=0,
+        ),
+    )(left, right, *attention, *tables, *[gradient[0] for gradient in gradients])
+
+
+def last_kernel(width, rows, split, *refs):
+    left_ref, right_ref, pair_ref, source, sum_ref, *refs = refs
+    outs, gate_out, up_out, refs = refs[:4], refs[4], refs[5], refs[6:]
+    part, stage, landed, send, recv, result, *refs = refs
+    site = Site()
+    exchanges = exchanges_of(site, ((TEAM, split),), [source], [result], refs)
+    site.meet([site.core_mate, site.side_mate, site.far_mate])
+    exchanges.start()
+    fill = fill_tiles(
+        part,
+        width,
+        rows,
+        lambda start, size: left_ref[start : start + size],
+        lambda value, at: dot_t(value, right_ref[at]),
+    )
+    RingSum(site, rows, part, stage, landed, send, recv).run(fill, lambda step: exchanges.step(1))
+    sum_ref[...] = part[:rows]
+    groups = 8
+    hidden = pair_ref.shape[2] // 2
+    for i, out in enumerate((gate_out, up_out)):
+
+        def get(place, at, start=i * hidden):
+            return pair_ref[place, at, start : start + hidden]
+
+        unit_columns(groups, hidden // groups, get, out)
+        exchanges.step(1)
+    exchanges.finish()
+    head_width = HEADS_DEV * DH
+    for i, out in enumerate(outs):
+        for place in range(TEAM):
+            columns = result[place, :, i * head_width : (i + 1) * head_width]
+            out[:, place * head_width : (place + 1) * head_width] = columns.astype(wide)
+
+
+def last_call(left, right, rows, pair, terms, split):
+    width = right.shape[0]
+    weight_rows = pair.shape[1]
+    vmem, anywhere = pl.BlockSpec(memory_space=pltpu.VMEM), pl.BlockSpec(memory_space=pl.ANY)
+    shapes = [jax.ShapeDtypeStruct((rows, width), wide)]
+    shapes += [jax.ShapeDtypeStruct((weight_rows, width), wide)] * 4
+    shapes += [jax.ShapeDtypeStruct((weight_rows, TEAM * pair.shape[2] // 2), wide)] * 2
+    gradients = [(terms, TEAM, split, TEAM * weight_rows)]
+    return pl.pallas_call(
+        functools.partial(last_kernel, width, rows, split),
+        out_shape=tuple(shapes),
+        in_specs=[vmem] * 3 + [anywhere],
+        out_specs=(vmem,) * len(shapes),
+        scratch_shapes=[
+            *ring_sum_scratch(rows, width),
+            pltpu.VMEM((TEAM, weight_rows, terms.shape[1]), low),
+            *exchange_scratch(gradients),
+        ],
+        compiler_params=pltpu.CompilerParams(
+            collective_id=2, has_side_effects=True, vmem_limit_bytes=60 * 2**20
+        ),
+        cost_estimate=pl.CostEstimate(
+            flops=2 * left.shape[0] * left.shape[1] * width,
+            bytes_accessed=60 * 2**20,
+            transcendentals=0,
+        ),
+    )(left, right, pair, terms)
+
+
 def team_rates():
     place = lax.axis_index("seq") % TEAM
     return head_rates((place * HEADS_DEV + jnp.arange(HEADS_DEV)).astype(wide))
@@ -1316,10 +1613,6 @@
 
 def carried(plan, carry, increment, backward):
     sub = lax.axis_index("seq") // TEAM
-    if plan.subs == 2:
-        pairs = [(i, (i + TEAM) % plan.seq) for i in range(plan.seq)]
-        got = lax.ppermute(increment.astype(low), "seq", pairs)
-        return jnp.where(sub == (0 if backward else 1), got, jnp.zeros_like(got))
     groups = plan.sub_groups
     all_carry = lax.all_gather(carry, "seq", axis_index_groups=groups)
     all_increment = lax.all_gather(increment.astype(low), "seq", axis_index_groups=groups)
@@ -1341,7 +1634,7 @@
     )
 
 
-def local(
+def fused_layer(
     plan,
     tokens,
     cotangent,
@@ -1355,7 +1648,77 @@
     w_up,
     w_down,
 ):
-    row_count, model_width = tokens.shape
+    row_count = tokens.shape[0]
+    weight_rows = w_query.shape[0]
+    piece = w_down.shape[0]
+    head_width = HEADS_DEV * DH
+    team_tokens = row_count * TEAM
+    normed, cotangents, attn_w, output_w, mlp_pieces, *tables = front_call(
+        tokens,
+        cotangent,
+        short_lengths,
+        (w_query, w_key, w_value, w_unit),
+        w_output,
+        w_gate,
+        w_up,
+    )
+    *results, z_all, heads_out, state = middle_call(
+        plan, (normed, attn_w, *tables), tokens, cotangents, output_w, mlp_pieces, w_down
+    )
+    middle, middle_grad, second, hidden_low, pair_grads, middle_all, coefficients, down_w = results
+    scale_rows = coefficients[:, 0].reshape(team_tokens, 1)
+    gated = (heads_out * scale_rows * z_all[:, 3 * head_width :]).astype(low)
+    output_terms = outer(gated, middle_all).astype(low)
+    down_terms = outer(hidden_low, cotangents).astype(low)
+    pair_terms = outer(second, pair_grads).astype(low)
+    down_sum, z_grads, grad_pair, grad_down, grad_output = turn_call(
+        hidden_low,
+        down_w,
+        row_count,
+        (middle_all, output_w, z_all, heads_out, state, coefficients),
+        tables,
+        [
+            (pair_terms, TEAM, MLP_SPLIT, TEAM * weight_rows),
+            (down_terms, 1, piece // 16, piece),
+            (output_terms, 1, 2, weight_rows),
+        ],
+    )
+    grad_output = plan.team_rows_back(grad_output)
+    mixed = (middle + down_sum).astype(low)
+    four_terms = outer(normed, z_grads).astype(low)
+    first_grad, grad_query, grad_key, grad_value, grad_unit, grad_gate, grad_up = last_call(
+        z_grads, attn_w, row_count, grad_pair, four_terms, ATTN_SPLIT
+    )
+    tokens_grad = (middle_grad + norm_back(tokens.astype(wide), first_grad)).astype(low)
+    return (
+        mixed,
+        tokens_grad,
+        grad_query,
+        grad_key,
+        grad_value,
+        grad_unit,
+        grad_output,
+        grad_gate,
+        grad_up,
+        grad_down,
+    )
+
+
+def plain_layer(
+    plan,
+    tokens,
+    cotangent,
+    short_lengths,
+    w_query,
+    w_key,
+    w_value,
+    w_unit,
+    w_output,
+    w_gate,
+    w_up,
+    w_down,
+):
+    row_count = tokens.shape[0]
     weight_rows = w_query.shape[0]
     groups = plan.groups
     piece = w_down.shape[0]
@@ -1373,16 +1736,12 @@
     attn_pieces = jnp.concatenate([by_heads(w) for w in (w_query, w_key, w_value, w_unit)], axis=2)
     mlp_pieces = jnp.concatenate([by_units(w_gate), by_units(w_up)], axis=2)
     normed_own = normalize(inputs).astype(low)
-    if plan.fused:
-        normed, cotangents, attn_w, output_w = front_call(normed_own, cotangent, attn_pieces, w_output)
-        mlp_w, down_w = mlp_pieces, w_down
-    else:
-        output_w = plan.team_rows(w_output)
-        attn_w = plan.across(plan.swap(attn_pieces).reshape(TEAM * weight_rows, 4 * head_width))
-        mlp_w = plan.across(plan.swap(mlp_pieces).reshape(TEAM * weight_rows, 2 * hidden))
-        down_w = plan.across(w_down)
-        normed = jnp.concatenate(plan.ring_gather(normed_own), axis=0)
-        cotangents = jnp.concatenate(plan.ring_gather(cotangent), axis=0)
+    output_w = plan.team_rows(w_output)
+    attn_w = plan.across(plan.swap(attn_pieces).reshape(TEAM * weight_rows, 4 * head_width))
+    mlp_w = plan.across(plan.swap(mlp_pieces).reshape(TEAM * weight_rows, 2 * hidden))
+    down_w = plan.across(w_down)
+    normed = jnp.concatenate(plan.ring_gather(normed_own), axis=0)
+    cotangents = jnp.concatenate(plan.ring_gather(cotangent), axis=0)
 
     def to_heads(x):
         x = x.reshape(TEAM, 2, LONG_DEV, HEADS_DEV, DH).transpose(1, 3, 0, 2, 4)
@@ -1405,53 +1764,28 @@
 
     decay, passing = decay_tables(plan, short_lengths[0], LONG_DEV, SHORT_DEV)
     into, out, carry = passing or (None, None, None)
-    if plan.fused:
-        tables = attention_tables(plan, short_lengths[0], team_rates())
-        *results, z_all, heads_out, got = middle_call(
-            plan, (normed, attn_w, *tables), tokens, cotangents, output_w, mlp_w, down_w
-        )
-        query, key, value, weights = heads_of(z_all)
+    z_all = dot(normed, attn_w)
+    query, key, value, weights = heads_of(z_all)
+    heads_out = bmm(weights, value, 3, 2)
+    if passing is not None:
         key_out = (key.astype(wide) * out).astype(low)
-        ahead = lax.axis_index("seq") >= TEAM
-        state = jnp.where(ahead, got, jnp.zeros_like(got)).transpose(1, 0, 2, 3)
-    else:
-        z_all = dot(normed, attn_w)
-        query, key, value, weights = heads_of(z_all)
-        heads_out = bmm(weights, value, 3, 2)
-        if passing is not None:
-            key_out = (key.astype(wide) * out).astype(low)
-            state = carried(plan, carry, bmm(key_out, value, 2, 2), False)
-            heads_out = heads_out + bmm(query, state, 3, 2) * into
-        heads_out = from_heads(heads_out)
-        squares = jnp.sum(heads_out * heads_out, axis=1).reshape(TEAM, 1, row_count)
-        squares = jnp.broadcast_to(squares, (TEAM, 8, row_count))
-        gated_raw = (heads_out * z_all[:, 3 * head_width :]).astype(low)
-        results = middle_call(
-            plan, (squares, gated_raw), tokens, cotangents, output_w, mlp_w, down_w
-        )
+        state = carried(plan, carry, bmm(key_out, value, 2, 2), False)
+        heads_out = heads_out + bmm(query, state, 3, 2) * into
+    heads_out = from_heads(heads_out)
+    squares = jnp.sum(heads_out * heads_out, axis=1).reshape(TEAM, 1, row_count)
+    squares = jnp.broadcast_to(squares, (TEAM, 8, row_count))
+    gated_raw = (heads_out * z_all[:, 3 * head_width :]).astype(low)
+    results = middle_call(plan, (squares, gated_raw), tokens, cotangents, output_w, mlp_w, down_w)
     middle, middle_grad, second, hidden_low, pair_grads, middle_all, coefficients, down_w = results
     z_query, z_key, _, z_unit = jnp.split(z_all, 4, axis=1)
     scale_rows = coefficients[:, 0].reshape(team_tokens, 1)
     inner_rows = coefficients[:, 1].reshape(team_tokens, 1)
     down_terms = outer(hidden_low, cotangents)
     pair_terms = outer(second, pair_grads)
-    if plan.fused:
-        down_sum, grad_pair, grad_down = back_call(
-            1,
-            row_count,
-            hidden_low,
-            down_w,
-            False,
-            [
-                (pair_terms.astype(low), TEAM, MLP_SPLIT, TEAM * weight_rows),
-                (down_terms.astype(low), 1, piece // 16, piece),
-            ],
-        )
-    else:
-        down_sum = plan.ring_reduce(lambda i: dot(rows(hidden_low, i), down_w))
-        grad_down = plan.across_sum(down_terms)
-        grad_pair = plan.across_sum(pair_terms).astype(low)
-        grad_pair = plan.swap(grad_pair.reshape(TEAM, weight_rows, 2 * hidden))
+    down_sum = plan.ring_reduce(lambda i: dot(rows(hidden_low, i), down_w))
+    grad_down = plan.across_sum(down_terms)
+    grad_pair = plan.across_sum(pair_terms).astype(low)
+    grad_pair = plan.swap(grad_pair.reshape(TEAM, weight_rows, 2 * hidden))
     mixed = (middle + down_sum).astype(low)
 
     def from_units(x):
@@ -1494,23 +1828,10 @@
         axis=1,
     )
     four_terms = outer(normed, z_grads)
-    if plan.fused:
-        first_grad, grad_four, grad_output = back_call(
-            2,
-            row_count,
-            z_grads,
-            attn_w,
-            True,
-            [
-                (four_terms.astype(low), TEAM, ATTN_SPLIT, TEAM * weight_rows),
-                (output_terms.astype(low), 1, 2, weight_rows),
-            ],
-        )
-    else:
-        first_grad = plan.ring_reduce(lambda i: dot_t(rows(z_grads, i), attn_w))
-        grad_four = plan.across_sum(four_terms).astype(low)
-        grad_four = plan.swap(grad_four.reshape(TEAM, weight_rows, 4 * head_width))
-        grad_output = plan.across_sum(output_terms)
+    first_grad = plan.ring_reduce(lambda i: dot_t(rows(z_grads, i), attn_w))
+    grad_four = plan.across_sum(four_terms).astype(low)
+    grad_four = plan.swap(grad_four.reshape(TEAM, weight_rows, 4 * head_width))
+    grad_output = plan.across_sum(output_terms)
     grad_output = plan.team_rows_back(grad_output)
 
     def from_columns(x):
@@ -1540,6 +1861,6 @@
     in_specs = (rows, rows, P("dp", None)) + (rows,) * 8
 
     def layer(*args):
-        return local(plan, *args)
+        return (fused_layer if plan.fused else plain_layer)(plan, *args)
 
     return jax.shard_map(layer, mesh=mesh, in_specs=in_specs, out_specs=(rows,) * 10, check_vma=False)

time: 665 us -> 614 us (0.923)
  the two profiles are of different devices: /device:TPU:2 before, /device:TPU:0 now
where the time goes in v5:
time: 614 us; the launch traced here: 605 us
  Pallas kernels  534 us (87%)
  matrix products  31 us (5%)
  local copies, waits for them, and re-layouts  29.9 us (5%)
    pallas_call x1, Pallas kernels, middle_call(): pl.pallas_call(functools.partial(middle_kernel, width, hidden, streamed),...  206 us
    pallas_call x1, Pallas kernels, turn_call(): pl.pallas_call(functools.partial(turn_kernel, width, rows, kinds), out_sh...  144 us
    pallas_call x1, Pallas kernels, front_call(): pl.pallas_call(front_kernel, out_shape=(jax.ShapeDtypeStruct((TEAM * rows...  98.3 us
    pallas_call x1, Pallas kernels, last_call(): pl.pallas_call(functools.partial(last_kernel, width, rows, split), out_sh...  86.3 us
    dot_general x4, matrix products, outer(): lax.dot_general(left, right, (((0,), (0,)), ((), ())), preferred_element_...  31 us
    unnamed x76, local copies, waits for them, and re-layouts  29.2 us
  transfers between devices with their start and end apart: 1, of which 0 were waited for; matrix products, arithmetic and copies ran while one was open for 2% of the time, Pallas kernels for 14%

profile of v5, /device:TPU:0, one launch (start us, length us, event | category | flops | bytes accessed | tf_op | source)
XLA Modules:
  0.0 604.5 jit_solution(15208071394021682819)
XLA Ops:
  0.6 0.0 copy-start.1
  0.7 1.0 copy-done.1
  1.7 1.1 copy-done.4
  2.8 1.1 copy-done.5
  3.9 1.0 copy-done.6
  5.0 0.9 copy-done.8
  5.9 0.9 copy-done.9
  6.9 0.9 copy-done.10
  7.8 0.9 copy-done.11
  8.8 0.9 copy-done.12
  9.7 0.7 copy-done.15
  10.4 98.3 %shard_map.186 = (bf16[512,2048]{1,0:T(8,128)(2,1)S(1)}, bf16[512,2048]{1,0:T(8,128)(2,1)S(1)}, bf16[2048,2048]{1,0:T(8,128)(2,1)S(1)}, bf16[512,2048]{1,0:T(8,1...) custom-call(bf16[128,2048]{1,0:T(8,128)(2,1)S(1)} %copy-done.1, ...), custom_call_target="tpu_custom_call" | custom-call | bytes 62914560 | tf_op jit(solution)/shard_map/pallas_call | solution.py:843
  108.7 0.0 copy-start
  108.7 3.2 copy-done
  111.9 1.4 copy-done.3
  113.3 0.7 copy-done.7
  114.0 0.6 copy-done.13
  114.6 0.6 copy-done.14
  115.2 1.3 copy-done.16
  116.5 1.3 copy-done.17
  117.8 1.1 copy-done.18
  118.9 205.6 %shard_map.187 = (f32[128,2048]{1,0:T(8,128)}, f32[128,2048]{1,0:T(8,128)}, bf16[512,2048]{1,0:T(8,128)(2,1)}, bf16[512,1408]{1,0:T(8,128)(2,1)}, bf16[512,2816]...) custom-call(bf16[512,2048]{1,0:T(8,128)(2,1)} %copy-done.16, ...), custom_call_target="tpu_custom_call" | custom-call | flops 16911433728 | bytes 62914560 | tf_op jit(solution)/shard_map/pallas_call | solution.py:1276
  324.5 0.7 slice.6
  325.3 7.9 %convolution_convert_fusion.2.refs_12_ = bf16[1408,2048]{1,0:T(8,128)(2,1)} fusion(bf16[512,1408]{1,0:T(8,128)(2,1)} %get-tuple-element.50.refs_0_, bf16[512,2048]{1,0:T(8,128)(2,1)} %copy-done.17), kind=kOutput, calls=%fused_computation.2 | convolution fusion | flops 2955673600 | bytes 9306112 | tf_op jit(solution)/shard_map/dot_general | solution.py:51
  333.1 0.0 copy-done.32
  333.2 0.0 copy-done.33
  333.2 0.0 copy-start.27
  333.2 9.0 %convolution_convert_fusion.refs_11_ = bf16[2048,2816]{1,0:T(8,128)(2,1)} fusion(bf16[512,2048]{1,0:T(8,128)(2,1)S(1)} %copy-done.33, bf16[512,2816]{1,0:T(8,128)(2,1)S(1)} %copy-done.32), kind=kOutput, calls=%fused_computation | convolution fusion | flops 5911347200 | bytes 16515072 | tf_op jit(solution)/shard_map/dot_general | solution.py:51
  342.2 0.0 copy-done.20
  342.2 4.0 convolution_convert_fusion.3.refs_13_
  346.2 144.0 %shard_map.188 = (f32[128,2048]{1,0:T(8,128)}, bf16[512,2048]{1,0:T(8,128)(2,1)}, bf16[4,64,2816]{2,1,0:T(8,128)(2,1)}, f32[176,2048]{1,0:T(8,128)}, f32[64,2048]{1,0:T(8,128)}) custom-call(bf16[512,1408]{1,0:T(8,128)(2,1)} %get-tuple-element.50.refs_0_, bf16[1408,2048]{1,0:T(8,128)(2,1)} %get-tuple-element.51.refs_1_, ...), custom_call_target="tpu_custom_call" | custom-call | flops 2952790016 | bytes 62914560 | tf_op jit(solution)/shard_map/pallas_call | solution.py:1465
  490.2 5.4 collective-permute-start
  495.5 10.1 %convolution_convert_fusion.1.refs_3_ = bf16[2048,2048]{1,0:T(8,128)(2,1)} fusion(bf16[512,2048]{1,0:T(8,128)(2,1)} %copy-done.16, bf16[512,2048]{1,0:T(8,128)(2,1)} %get-tuple-element.61.refs_0_), kind=kOutput, calls=%fused_computation.1 | convolution fusion | flops 4299161600 | bytes 12582912 | tf_op jit(solution)/shard_map/dot_general | solution.py:51
  505.6 86.3 %shard_map.189 = (f32[128,2048]{1,0:T(8,128)}, f32[64,2048]{1,0:T(8,128)}, f32[64,2048]{1,0:T(8,128)}, f32[64,2048]{1,0:T(8,128)}, f32[64,2048]{1,0:T(8,128)}, /*index=5*/f32[64,5632]{1,0:T(8,128)}, f32[64,5632]{1,0:T(8,128)}) custom-call(bf16[512,2048]{1,0:T(8,128)(2,1)} %get-tuple-element.61.refs_0_, bf16[2048,2048]{1,0:T(8,128)(2,1)} %copy-done, ...), custom_call_target="tpu_custom_call" | custom-call | flops 4294967296 | bytes 62914560 | tf_op jit(solution)/shard_map/pallas_call | solution.py:1534
  591.9 1.6 fusion
  593.6 1.5 fusion.4
  595.1 0.0 collective-permute-done
  595.1 0.0 copy-done.31
  595.1 0.8 copy.29
  595.9 0.8 copy.30
  596.7 0.0 copy-done.29
  596.7 0.8 copy.31
  597.5 0.8 copy.32
  598.3 2.0 copy.33
  600.3 1.1 copy.34
  601.4 1.1 copy.35
  602.5 0.8 copy-done.21
  603.2 1.1 copy.36
  (43 shorter events, 0.1 us)
Async XLA Ops:
  0.6 1.0 copy-start.1
  1.7 1.1 copy-start.4
  2.8 1.1 copy-start.5
  3.9 1.0 copy-start.6
  5.0 0.9 copy-start.8
  5.9 0.9 copy-start.9
  6.9 0.9 copy-start.10
  7.8 0.9 copy-start.11
  8.8 0.9 copy-start.12
  9.7 0.7 copy-start.15
  108.7 3.2 copy-start
  111.9 1.4 copy-start.3
  113.3 0.7 copy-start.7
  114.0 0.6 copy-start.13
  114.6 0.6 copy-start.14
  115.2 1.3 copy-start.16
  116.5 1.3 copy-start.17
  117.8 1.1 copy-start.18
  325.3 7.9 %copy-start.32 = (bf16[512,2816]{1,0:T(8,128)(2,1)S(1)}, bf16[512,2816]{1,0:T(8,128)(2,1)}, u32[]{:S(2)}) copy-start(bf16[512,2816]{1,0:T(8,128)(2,1)} %get-tuple-element.58) | copy-start | bytes 8650756
  325.3 7.9 %copy-start.33 = (bf16[512,2048]{1,0:T(8,128)(2,1)S(1)}, bf16[512,2048]{1,0:T(8,128)(2,1)}, u32[]{:S(2)}) copy-start(bf16[512,2048]{1,0:T(8,128)(2,1)} %get-tuple-element.57) | copy-start | bytes 6291460
  333.2 9.0 %copy-start.20 = (bf16[512,2048]{1,0:T(8,128)(2,1)S(1)}, bf16[512,2048]{1,0:T(8,128)(2,1)}, u32[]{:S(2)}) copy-start(bf16[512,2048]{1,0:T(8,128)(2,1)} %get-tuple-element.52.refs_2_) | copy-start | bytes 6291460
  333.2 9.0 %copy-start.27 = (f32[512,512]{1,0:T(8,128)S(1)}, f32[512,512]{1,0:T(8,128)}, u32[]{:S(2)}) copy-start(f32[512,512]{1,0:T(8,128)} %get-tuple-element.54.refs_5_) | copy-start | bytes 3145732
  490.2 104.9 %collective-permute-start = (f32[64,2048]{1,0:T(8,128)}, f32[64,2048]{1,0:T(8,128)}, u32[]{:S(2)}, u32[]{:S(2)}) collective-permute-start(f32[64,2048]{1,0:T(8,128)} %get-tuple-element.68), channel_id=1, source_target_pairs={{0,0},{1,8},{2,16},{3,24},{4,1},{5,9},{6,17},{7,25},{8,2},{9,10},{... | collective-permute-start | bytes 1572872 | tf_op jit(solution)/shard_map/ppermute | solution.py:159
  505.6 86.3 %copy-start.2 = (bf16[128,2048]{1,0:T(8,128)(2,1)S(1)}, bf16[128,2048]{1,0:T(8,128)(2,1)}, u32[]{:S(2)}) copy-start(bf16[128,2048]{1,0:T(8,128)(2,1)} %refs_5_.1) | copy-start | bytes 1572868
  505.6 87.9 %copy-start.24 = (f32[128,2048]{1,0:T(8,128)S(1)}, f32[128,2048]{1,0:T(8,128)}, u32[]{:S(2)}) copy-start(f32[128,2048]{1,0:T(8,128)} %get-tuple-element.49) | copy-start | bytes 3145732
  505.6 87.9 %copy-start.25 = (f32[128,2048]{1,0:T(8,128)S(1)}, f32[128,2048]{1,0:T(8,128)}, u32[]{:S(2)}) copy-start(f32[128,2048]{1,0:T(8,128)} %get-tuple-element.60) | copy-start | bytes 3145732
  505.6 87.9 %copy-start.26 = (f32[128,2048]{1,0:T(8,128)S(1)}, f32[128,2048]{1,0:T(8,128)}, u32[]{:S(2)}) copy-start(f32[128,2048]{1,0:T(8,128)} %get-tuple-element.59) | copy-start | bytes 3145732
  591.9 1.6 copy-start.19
  593.6 1.5 copy-start.31
  593.6 2.3 copy-start.30
  595.1 1.6 copy-start.29
  595.1 2.4 copy-start.28
  595.9 4.4 copy-start.23
  598.3 3.1 copy-start.22
  601.4 1.9 copy-start.21

commit v6 on v5

--- a/solution.py
+++ b/solution.py
@@ -14,12 +14,10 @@
 SHORT_DEV = 64
 HEADS_DEV = 4
 TEAM = H // HEADS_DEV
-RING = (0, 2, 3, 1)
-PLACE = tuple(RING.index(i) for i in range(TEAM))
-ORDER = (0, 1, 3, 2)
 CHUNK = 64
 ATTN_SPLIT = 2
 MLP_SPLIT = 2
+DOWN_KIND = ((1, 11),)
 MESH = pl.DeviceIdType.MESH
 
 epsilon = 1e-06
@@ -66,45 +64,16 @@
         teams = [[sub * TEAM + i for i in range(TEAM)] for sub in range(self.subs)]
         self.team_groups = None if self.subs == 1 else teams
         self.sub_groups = [[sub * TEAM + i for sub in range(self.subs)] for i in range(TEAM)]
-        self.up = [(t[RING[i]], t[RING[(i + 1) % TEAM]]) for t in teams for i in range(TEAM)]
-        self.down = [(b, a) for a, b in self.up]
-
-    def to_next(self, x):
-        return lax.ppermute(x, "seq", self.up)
-
-    def to_previous(self, x):
-        return lax.ppermute(x, "seq", self.down)
-
-    def ring_gather(self, x):
-        half = x.shape[0] // 2
-        blocks = [x] + [None] * (TEAM - 1)
-        forth = back = x
-        for k in range(1, TEAM // 2):
-            forth, back = self.to_next(forth), self.to_previous(back)
-            blocks[k], blocks[TEAM - k] = forth, back
-        blocks[TEAM // 2] = jnp.concatenate(
-            [self.to_next(forth[:half]), self.to_previous(back[half:])], axis=0
-        )
-        return [blocks[k] for k in ORDER]
-
-    def ring_reduce(self, slot_part):
-        def part(k):
-            return slot_part(ORDER.index(k))
-
-        middle = part(TEAM // 2)
-        half = middle.shape[0] // 2
-        back = self.to_previous(middle[:half].astype(low))
-        forth = self.to_next(middle[half:].astype(low))
-        for k in range(TEAM // 2 - 1, 0, -1):
-            a, b = part(k), part(TEAM - k)
-            if k == TEAM // 2 - 1:
-                a = jnp.concatenate([a[:half] + back.astype(wide), a[half:]], axis=0)
-                b = jnp.concatenate([b[:half], b[half:] + forth.astype(wide)], axis=0)
-            else:
-                a, b = a + back.astype(wide), b + forth.astype(wide)
-            back = self.to_previous(a.astype(low))
-            forth = self.to_next(b.astype(low))
-        return part(0) + back.astype(wide) + forth.astype(wide)
+
+    def to_mate(self, x, k):
+        return lax.ppermute(x, "seq", [(i, i ^ k) for i in range(self.seq)])
+
+    def team_gather(self, x):
+        return jnp.concatenate([x] + [self.to_mate(x, k) for k in range(1, TEAM)], axis=0)
+
+    def team_sum(self, part):
+        others = [self.to_mate(part(k).astype(low), k).astype(wide) for k in range(1, TEAM)]
+        return sum(others, part(0))
 
     def across(self, x):
         if self.subs > 1:
@@ -170,22 +139,17 @@
         self.dp, self.seq = lax.axis_index("dp"), lax.axis_index("seq")
         self.place = self.seq % TEAM
         self.base = self.seq - self.place
-        self.spot = self.place // 2 + (self.place % 2) * (TEAM - 1 - 2 * (self.place // 2))
-        self.ahead, self.behind = self.device(1), self.device(-1)
         self.sub = self.seq // TEAM
         self.core_mate = (self.dp + 1 - 2 * (self.dp % 2), self.seq)
         self.side_mate = (self.dp + 2 - 4 * (self.dp // 2), self.seq)
         self.far_mate = (self.dp, (self.seq + TEAM) % (2 * TEAM))
 
-    def device(self, steps):
-        at = (self.spot + TEAM + steps) % TEAM
-        side = at // (TEAM // 2)
-        return (self.dp, self.base + 2 * (at + side * (TEAM - 1 - 2 * at)) + side)
-
-    def block(self, slot):
-        at = (self.spot + TEAM - ORDER[slot]) % TEAM
-        side = at // (TEAM // 2)
-        return 2 * (at + side * (TEAM - 1 - 2 * at)) + side
+    def block(self, k):
+        x, z = self.place % 2, self.place // 2
+        return 2 * (z + (k // 2) * (1 - 2 * z)) + x + (k % 2) * (1 - 2 * x)
+
+    def mate(self, k):
+        return (self.dp, self.base + self.block(k))
 
     def member(self, place):
         return (self.dp, self.base + place)
@@ -197,7 +161,7 @@
 
     def meet(self, mates=(), more=None, other=None, meanwhile=lambda: None):
         barrier = pltpu.get_barrier_semaphore()
-        others = [self.device(k) for k in range(1, TEAM)] + list(mates)
+        others = [self.mate(k) for k in range(1, TEAM)] + list(mates)
         for device in others:
             pl.semaphore_signal(barrier, inc=1, device_id=device, device_id_type=MESH)
         if more is None:
@@ -220,66 +184,57 @@
             pl.semaphore_wait(barrier, len(others))
 
 
-class RingSum:
+class TeamSum:
     def __init__(self, site, rows, part, stage, landed, send, recv):
         self.site, self.rows, self.part = site, rows, part
         self.stage, self.landed, self.send, self.recv = stage, landed, send, recv
 
-    def copy(self, way, step, chunk):
+    def copy(self, kind, chunk):
         return remote(
-            self.stage.at[way, step, chunk],
-            self.landed.at[way, step, chunk],
-            self.send.at[way, step, chunk],
-            self.recv.at[way, step, chunk],
-            self.site.ahead if way else self.site.behind,
+            self.stage.at[kind, chunk],
+            self.landed.at[kind, chunk],
+            self.send.at[kind, chunk],
+            self.recv.at[kind, chunk],
+            self.site.mate(2 if kind == 2 else 1),
         )
 
     def run(self, fill, between=lambda step: None):
         part, stage, landed, rows = self.part, self.stage, self.landed, self.rows
-        last = TEAM // 2 - 1
-        fill(TEAM - 1, 1)
-        for way in range(2):
-            stage[way, 0, way] = part[way * CHUNK : (way + 1) * CHUNK].astype(low)
-            self.copy(way, 0, way).start()
+        chunks = range(rows // CHUNK)
+        fill(3, 1)
+        for chunk in chunks:
+            stage[0, chunk] = part[chunk * CHUNK : (chunk + 1) * CHUNK].astype(low)
+            self.copy(0, chunk).start()
+        fill(1, 2)
+        for chunk in chunks:
+            stage[1, chunk] = part[chunk * CHUNK : (chunk + 1) * CHUNK].astype(low)
+            self.copy(1, chunk).start()
         between(0)
-        for step in range(1, last + 1):
-            fill(2 * (last - step) + 1, 2)
-            for turn in range(2):
-                for way in range(2):
-                    chunk = 1 - way if turn == 0 else way
-                    start = way * rows + chunk * CHUNK
-                    value = part[start : start + CHUNK]
-                    if step > 1 or chunk == way:
-                        self.copy(way, step - 1, chunk).wait_recv()
-                        value = value + landed[way, step - 1, chunk].astype(wide)
-                    stage[way, step, chunk] = value.astype(low)
-                    self.copy(way, step, chunk).start()
-            between(step)
+        for chunk in chunks:
+            start = rows + chunk * CHUNK
+            self.copy(0, chunk).wait_recv()
+            value = part[start : start + CHUNK] + landed[0, chunk].astype(wide)
+            stage[2, chunk] = value.astype(low)
+            self.copy(2, chunk).start()
         fill(0, 1)
-        for chunk in range(2):
+        between(1)
+        for chunk in chunks:
             at = pl.ds(chunk * CHUNK, CHUNK)
-            for way in range(2):
-                self.copy(way, last, chunk).wait_recv()
-            part[at] = (
-                part[at]
-                + landed[0, last, chunk].astype(wide)
-                + landed[1, last, chunk].astype(wide)
-            )
-        for way in range(2):
-            self.copy(way, 0, way).wait_send()
-            for step in range(1, last + 1):
-                for chunk in range(2):
-                    self.copy(way, step, chunk).wait_send()
-
-
-def ring_sum_scratch(rows, width):
-    steps = TEAM // 2
+            for kind in (1, 2):
+                self.copy(kind, chunk).wait_recv()
+            part[at] = part[at] + landed[1, chunk].astype(wide) + landed[2, chunk].astype(wide)
+        for kind in range(3):
+            for chunk in chunks:
+                self.copy(kind, chunk).wait_send()
+
+
+def team_sum_scratch(rows, width):
     return [
         pltpu.VMEM((2 * rows, width), wide),
-        pltpu.VMEM((2, steps, 2, CHUNK, width), low),
-        pltpu.VMEM((2, steps, 2, CHUNK, width), low),
-        pltpu.SemaphoreType.DMA((2, steps, 2)),
-        pltpu.SemaphoreType.DMA((2, steps, 2)),
+        pltpu.VMEM((3, rows // CHUNK, CHUNK, width), low),
+        pltpu.VMEM((3, rows // CHUNK, CHUNK, width), low),
+        pltpu.SemaphoreType.DMA((3, rows // CHUNK)),
+        pltpu.SemaphoreType.DMA((3, rows // CHUNK)),
     ]
 
 
@@ -461,38 +416,50 @@
 
 
 class Exchanges:
-    def __init__(self, exchanges):
-        self.exchanges = exchanges
+    def __init__(self, exchanges, depth=3):
+        self.exchanges, self.depth = exchanges, depth
         self.parts = [(exchange, j) for exchange in exchanges for j in range(exchange.count)]
-        self.sides = [(1, part) for part in self.parts] + [(0, part) for part in self.parts]
-        self.sent = self.done = 0
-
-    def start(self, depth=3):
+        count = len(self.parts)
+        self.sides = []
+        for i in range(count + depth):
+            if i < count:
+                self.sides.append((1, self.parts[i]))
+            if i >= depth:
+                self.sides.append((0, self.parts[i - depth]))
+        self.sent = self.done = self.settled = 0
+
+    def start(self):
         for exchange in self.exchanges:
             exchange.start()
-        for _ in range(depth):
-            self.next_side()
-
-    def next_side(self):
-        if self.sent < len(self.sides):
-            far, (exchange, j) = self.sides[self.sent]
+        self.send_sides(self.depth)
+
+    def send_sides(self, count):
+        for far, (exchange, j) in self.sides[self.sent : self.sent + count]:
             exchange.to_side(far, j)
-            self.sent += 1
+        self.sent += count
+
+    def settle(self):
+        if self.settled < len(self.parts):
+            exchange, j = self.parts[self.settled]
+            exchange.to_owner(j)
+            self.settled += 1
 
     def step(self, count=1):
         for _ in range(count):
-            if self.done < len(self.parts):
-                exchange, j = self.parts[self.done]
-                exchange.to_far(j)
-                self.next_side()
-                self.done += 1
+            if self.done == len(self.parts):
+                return
+            exchange, j = self.parts[self.done]
+            exchange.to_far(j)
+            self.send_sides(2)
+            if self.done >= self.depth + 1:
+                self.settle()
+            self.done += 1
 
     def finish(self):
         self.step(len(self.parts))
-        while self.sent < len(self.sides):
-            self.next_side()
-        for exchange, j in self.parts:
-            exchange.to_owner(j)
+        self.send_sides(len(self.sides))
+        while self.settled < len(self.parts):
+            self.settle()
         for exchange in self.exchanges:
             exchange.finish()
 
@@ -596,37 +563,42 @@
 
 
 class WeightStreams:
-    def __init__(self, streams, depth=2):
+    def __init__(self, streams, depth=4):
         self.streams, self.depth = streams, depth
         self.parts = [(stream, j) for stream in streams for j in range(stream.count)]
-        self.done = 0
+        self.sent = self.done = self.crossed = 0
 
     def start(self):
         for stream in self.streams:
             stream.start()
-
-    def launch(self):
-        for stream, j in self.parts[: self.depth]:
+        self.launch(self.streams[0].split)
+
+    def launch(self, until):
+        for stream, j in self.parts[self.sent : until]:
             stream.launch(j)
+            self.sent += 1
 
     def step(self, count=1):
         for _ in range(count):
             if self.done == len(self.parts):
                 return
+            self.launch(self.done + 2)
             stream, j = self.parts[self.done]
             stream.land(j)
-            if self.done + self.depth < len(self.parts):
-                stream, j = self.parts[self.done + self.depth]
-                stream.launch(j)
-            if self.done >= self.depth:
-                stream, j = self.parts[self.done - self.depth]
-                stream.cross(j)
             self.done += 1
+            self.launch(self.done + self.depth)
+            if self.done > 2:
+                self.cross()
+
+    def cross(self):
+        stream, j = self.parts[self.crossed]
+        stream.cross(j)
+        self.crossed += 1
 
     def finish(self):
         self.step(len(self.parts))
-        for stream, j in self.parts[len(self.parts) - self.depth :]:
-            stream.cross(j)
+        while self.crossed < len(self.parts):
+            self.cross()
         for stream in self.streams:
             stream.finish()
 
@@ -679,52 +651,46 @@
             self.first_copy().wait_send()
 
 
-class RingGather:
+class TeamGather:
     def __init__(self, site, rows, own, buffer, send, recv):
         self.site, self.rows, self.own, self.buffer = site, rows, own, buffer
         self.send, self.recv = send, recv
 
     @staticmethod
-    def scratch():
-        return [pltpu.SemaphoreType.DMA((2, TEAM // 2, 2))] * 2
+    def scratch(rows):
+        return [pltpu.SemaphoreType.DMA((3, rows // CHUNK))] * 2
 
     def slab(self, slot, chunk):
         return self.buffer.at[pl.ds(slot * self.rows + chunk * CHUNK, CHUNK)]
 
-    def copy(self, way, step, chunk):
-        source = self.own.at[pl.ds(chunk * CHUNK, CHUNK)]
-        if step > 1:
-            source = self.slab(2 * (step - 1) - 1 + way, chunk)
-        target = 2 * step - 1 + way if step < TEAM // 2 else TEAM - 1
+    def copy(self, kind, chunk):
+        source = self.slab(2, chunk) if kind == 2 else self.own.at[pl.ds(chunk * CHUNK, CHUNK)]
         return remote(
             source,
-            self.slab(target, chunk),
-            self.send.at[way, step - 1, chunk],
-            self.recv.at[way, step - 1, chunk],
-            self.site.behind if way else self.site.ahead,
-        )
-
-    def chunks(self, way, step):
-        return (0, 1) if step < TEAM // 2 else (way,)
+            self.slab((2, 1, 3)[kind], chunk),
+            self.send.at[kind, chunk],
+            self.recv.at[kind, chunk],
+            self.site.mate(1 if kind else 2),
+        )
+
+    def each(self, kinds, act):
+        for chunk in range(self.rows // CHUNK):
+            for kind in kinds:
+                act(self.copy(kind, chunk))
 
     def start(self):
-        for chunk in range(2):
-            for way in range(2):
-                self.copy(way, 1, chunk).start()
+        self.each((0, 1), lambda copy: copy.start())
 
     def step(self, step):
-        for chunk in range(2):
-            for way in range(2):
-                if chunk in self.chunks(way, step):
-                    self.copy(way, step, chunk).wait_recv()
-                    if step < TEAM // 2 and chunk in self.chunks(way, step + 1):
-                        self.copy(way, step + 1, chunk).start()
+        if step == 1:
+            for chunk in range(self.rows // CHUNK):
+                self.copy(0, chunk).wait_recv()
+                self.copy(2, chunk).start()
+        else:
+            self.each((1, 2), lambda copy: copy.wait_recv())
 
     def finish(self):
-        for step in range(1, TEAM // 2 + 1):
-            for way in range(2):
-                for chunk in self.chunks(way, step):
-                    self.copy(way, step, chunk).wait_send()
+        self.each((0, 1, 2), lambda copy: copy.wait_send())
 
 
 def unit_pieces(groups, piece, ref, put):
@@ -752,39 +718,71 @@
 
 
 def front_kernel(
+    tokens_hbm,
+    cotangent_hbm,
+    lengths_ref,
+    query_hbm,
+    key_hbm,
+    value_hbm,
+    unit_hbm,
+    output_rows_hbm,
+    down_hbm,
+    gate_hbm,
+    up_hbm,
+    normed_out,
+    cotangents_out,
+    weight_out,
+    output_out,
+    down_out,
+    mlp_pieces_out,
+    columns_ref,
+    rows_ref,
+    rates_ref,
     tokens_ref,
     cotangent_ref,
-    lengths_ref,
     query_ref,
     key_ref,
     value_ref,
     unit_ref,
     output_rows_ref,
+    down_ref,
     gate_ref,
     up_ref,
-    normed_out,
-    cotangents_out,
-    weight_out,
-    output_out,
-    mlp_pieces_ref,
-    columns_ref,
-    rows_ref,
-    rates_ref,
     normed,
     pieces,
+    mlp_pieces_ref,
+    load_sems,
     own_sems,
     *sems,
 ):
+    loads = {}
+    for i, (ref, source) in enumerate(
+        (
+            (query_ref, query_hbm),
+            (key_ref, key_hbm),
+            (value_ref, value_hbm),
+            (unit_ref, unit_hbm),
+            (output_rows_ref, output_rows_hbm),
+            (down_ref, down_hbm),
+            (tokens_ref, tokens_hbm),
+            (cotangent_ref, cotangent_hbm),
+            (gate_ref, gate_hbm),
+            (up_ref, up_hbm),
+        )
+    ):
+        loads[i] = pltpu.make_async_copy(source, ref, load_sems.at[i])
+        loads[i].start()
     site = Site()
     rows = tokens_ref.shape[0]
     width = HEADS_DEV * DH
     groups = 8
     piece = gate_ref.shape[1] // (groups * TEAM)
-    normed_ring = RingGather(site, rows, normed, normed_out, *sems[:2])
-    cotangent_ring = RingGather(site, rows, cotangent_ref, cotangents_out, *sems[2:4])
+    normed_ring = TeamGather(site, rows, normed, normed_out, *sems[:2])
+    cotangent_ring = TeamGather(site, rows, cotangent_ref, cotangents_out, *sems[2:4])
     attention = WeightStream(site, TEAM, ATTN_SPLIT, pieces, weight_out, sems[4:9])
-    output = SpreadStream(site, 2, output_rows_ref, output_out, sems[9:])
-    streams = WeightStreams([attention, output], 4)
+    output = SpreadStream(site, 2, output_rows_ref, output_out, sems[9:14])
+    down = WeightStream(site, 1, down_ref.shape[0] // 16, down_ref, down_out, sems[14:])
+    streams = WeightStreams([attention, output, down])
     own = [
         pltpu.make_async_copy(ref, out.at[pl.ds(0, rows)], own_sems.at[i])
         for i, (ref, out) in enumerate(((normed, normed_out), (cotangent_ref, cotangents_out)))
@@ -792,14 +790,18 @@
 
     def cut():
         for i, ref in enumerate((query_ref, key_ref, value_ref, unit_ref)):
+            loads[i].wait()
             for place in range(TEAM):
                 columns = ref[:, place * width : (place + 1) * width]
                 pieces[place, :, i * width : (i + 1) * width] = columns
 
     mates = [site.core_mate, site.side_mate, site.far_mate]
     site.meet(mates, output.elsewhere, output.origin, cut)
+    for i in (4, 5):
+        loads[i].wait()
     streams.start()
-    streams.launch()
+    for i in (6, 7):
+        loads[i].wait()
     normed[...] = normalize(tokens_ref[...].astype(wide)).astype(low)
     for copy in own:
         copy.start()
@@ -816,8 +818,11 @@
         def put(place, at, columns, start=i * hidden):
             mlp_pieces_ref[place, at, start : start + hidden] = columns.astype(low)
 
+        loads[8 + i].wait()
         unit_pieces(groups, piece, ref, put)
         streams.step(1)
+    store = pltpu.make_async_copy(mlp_pieces_ref, mlp_pieces_out, own_sems.at[2])
+    store.start()
     streams.step(1)
     normed_ring.step(1)
     cotangent_ring.start()
@@ -829,11 +834,11 @@
     cotangent_ring.step(2)
     normed_ring.finish()
     cotangent_ring.finish()
-    for copy in own:
+    for copy in own + [store]:
         copy.wait()
 
 
-def front_call(tokens, cotangent, lengths, attention, output_rows, gate, up):
+def front_call(tokens, cotangent, lengths, attention, output_rows, down, gate, up):
     rows, width = tokens.shape
     weight_rows = gate.shape[0]
     anywhere = pl.BlockSpec(memory_space=pl.ANY)
@@ -847,27 +852,34 @@
             jax.ShapeDtypeStruct((TEAM * rows, width), low),
             jax.ShapeDtypeStruct((8 * TEAM * weight_rows, 4 * head_width), low),
             jax.ShapeDtypeStruct((8 * output_rows.shape[0], output_rows.shape[1]), low),
+            jax.ShapeDtypeStruct((8 * down.shape[0], down.shape[1]), low),
             jax.ShapeDtypeStruct((TEAM, weight_rows, piece_width), low),
             jax.ShapeDtypeStruct((TEAM * rows, 8), wide),
             jax.ShapeDtypeStruct((8, TEAM * rows), wide),
             jax.ShapeDtypeStruct((8, 128), wide),
         ),
-        in_specs=[vmem, vmem, pl.BlockSpec(memory_space=pltpu.SMEM)] + [vmem] * 7,
-        out_specs=(anywhere,) * 4 + (vmem,) * 4,
+        in_specs=[anywhere, anywhere, pl.BlockSpec(memory_space=pltpu.SMEM)] + [anywhere] * 8,
+        out_specs=(anywhere,) * 6 + (vmem,) * 3,
         scratch_shapes=[
             pltpu.VMEM((rows, width), low),
+            pltpu.VMEM((rows, width), low),
+            *[pltpu.VMEM(weight.shape, low) for weight in (*attention, output_rows, down, gate, up)],
+            pltpu.VMEM((rows, width), low),
             pltpu.VMEM((TEAM, weight_rows, 4 * head_width), low),
-            pltpu.SemaphoreType.DMA((2,)),
-            *RingGather.scratch(),
-            *RingGather.scratch(),
+            pltpu.VMEM((TEAM, weight_rows, piece_width), low),
+            pltpu.SemaphoreType.DMA((10,)),
+            pltpu.SemaphoreType.DMA((3,)),
+            *TeamGather.scratch(rows),
+            *TeamGather.scratch(rows),
             *WeightStream.scratch(TEAM, ATTN_SPLIT),
             *WeightStream.scratch(1, 2),
+            *WeightStream.scratch(1, down.shape[0] // 16),
         ],
         compiler_params=pltpu.CompilerParams(
-            collective_id=3, has_side_effects=True, vmem_limit_bytes=32 * 2**20
+            collective_id=3, has_side_effects=True, vmem_limit_bytes=62 * 2**20
         ),
         cost_estimate=pl.CostEstimate(flops=0, bytes_accessed=60 * 2**20, transcendentals=0),
-    )(tokens, cotangent, lengths, *attention, output_rows, gate, up)
+    )(tokens, cotangent, lengths, *attention, output_rows, down, gate, up)
 
 
 def attention_table(site, lengths_ref, shape, axis):
@@ -900,7 +912,8 @@
 
 
 def head_lanes(part, head):
-    return pl.ds(pl.multiple_of(part * HEADS_DEV * DH + head * DH, DH), DH)
+    start = part * HEADS_DEV * DH + head * DH
+    return pl.ds(start if isinstance(start, int) else pl.multiple_of(start, DH), DH)
 
 
 class Heads:
@@ -1014,6 +1027,7 @@
 
 def middle_kernel(model_width, hidden, streamed, *refs):
     refs = iter(refs)
+    site = Site()
 
     def take(count):
         return [next(refs) for _ in range(count)]
@@ -1024,38 +1038,35 @@
         squares_ref, raw_ref = take(2)
     tokens_ref, cotangents_hbm, output_ref, mlp_hbm, down_hbm = take(5)
     middle_ref, middle_grad_ref, second_hbm, hidden_hbm, pairs_hbm, gathered_hbm = take(6)
-    coefficients_ref, down_out = take(2)
+    (coefficients_ref,) = take(1)
     if streamed:
-        z_hbm, out_hbm, state_ref = take(3)
+        z_hbm, out_hbm, state_ref, terms_hbm, grad_down_ref = take(5)
     cotangents, mlp, down, second, hiddens, pairs, gathered, proj, own_squares = take(9)
     part, stage, landed, reduce_send, reduce_recv, load_sems, store_sems = take(7)
     gather_send, gather_recv, square_send, square_recv, coef_send, coef_recv = take(6)
     if streamed:
-        stream_sems = take(10)
+        stream_sems = take(5)
         squares_ref, raw_ref, tiles, staging, unit, heads_out, increment = take(7)
-        tile_sems, z_sems, state_send, state_recv, out_sem, normed_sem = take(6)
-    site = Site()
+        tile_sems, z_sems, state_send, state_recv, out_sem, normed_sem, terms_sems = take(7)
+        exchange = exchanges_of(
+            site, DOWN_KIND, [terms_hbm], [grad_down_ref], take(Exchange.SCRATCH)
+        )
     rows = tokens_ref.shape[0]
     if streamed:
         site.meet([site.core_mate, site.side_mate, site.far_mate])
         streams = WeightStreams(
-            [
-                WeightStream(site, TEAM, MLP_SPLIT, mlp_hbm, mlp, stream_sems[:5]),
-                WeightStream(site, 1, down_hbm.shape[0] // 16, down_hbm, down, stream_sems[5:]),
-            ],
-            4,
+            [WeightStream(site, TEAM, MLP_SPLIT, mlp_hbm, mlp, stream_sems)], 2
         )
         streams.start()
-        streams.launch()
     else:
         site.meet()
 
     loads = [
         pltpu.make_async_copy(src, dst, load_sems.at[i])
         for i, (src, dst) in enumerate(
-            ((cotangents_hbm, cotangents), (mlp_hbm, mlp), (down_hbm, down))
-        )
-    ][: 1 if streamed else 3]
+            ((cotangents_hbm, cotangents), (down_hbm, down), (mlp_hbm, mlp))
+        )
+    ][: 2 if streamed else 3]
     for load in loads:
         load.start()
     eye = lax.broadcasted_iota(jnp.int32, (rows, rows), 0) == lax.broadcasted_iota(
@@ -1091,11 +1102,11 @@
 
     square_copies = [
         remote(
-            squares_ref.at[ORDER.index(k)],
+            squares_ref.at[k],
             own_squares.at[k],
             square_send.at[k],
             square_recv.at[k],
-            site.device(-k),
+            site.mate(k),
         )
         for k in range(1, TEAM)
     ]
@@ -1103,10 +1114,10 @@
         copy.start()
 
     second_ring, gathered_ring = (
-        RingGather(site, rows, buffer.at[pl.ds(0, rows)], buffer, gather_send, gather_recv)
+        TeamGather(site, rows, buffer.at[pl.ds(0, rows)], buffer, gather_send, gather_recv)
         for buffer in (second, gathered)
     )
-    ring = RingSum(site, rows, part, stage, landed, reduce_send, reduce_recv)
+    ring = TeamSum(site, rows, part, stage, landed, reduce_send, reduce_recv)
     fill_output = fill_tiles(
         part,
         model_width,
@@ -1160,11 +1171,10 @@
         units(2, 2)
     else:
         units(0, 1)
-        for step in range(1, TEAM // 2):
+        for step in range(1, TEAM // 2 + 1):
             second_ring.step(step)
-            units(2 * step - 1, 2)
-        second_ring.step(TEAM // 2)
-        units(TEAM - 1, 1)
+        units(1, 1)
+        units(2, 2)
     stores = [
         pltpu.make_async_copy(src, dst, store_sems.at[i])
         for i, (src, dst) in enumerate(
@@ -1172,15 +1182,45 @@
                 (second, second_hbm),
                 (hiddens, hidden_hbm),
                 (pairs, pairs_hbm),
-                (down, down_out),
                 (gathered, gathered_hbm),
             )
         )
     ]
-    for store in stores[:4]:
+    for store in stores[:3]:
         store.start()
 
-    ring.run(fill_pairs)
+    def between_pairs(step):
+        if streamed:
+            exchange.step(2)
+
+    if streamed:
+        tile = 128
+
+        def terms_copy(i):
+            return pltpu.make_async_copy(
+                gathered.at[pl.ds(pl.multiple_of(i % 2 * tile, tile), tile)],
+                terms_hbm.at[pl.ds(pl.multiple_of(i * tile, tile), tile)],
+                terms_sems.at[i % 2],
+            )
+
+        tiles = hidden // tile
+
+        @pl.loop(0, tiles)
+        def _(i):
+            @pl.when(i >= 2)
+            def _():
+                terms_copy(i - 2).wait()
+
+            columns = hiddens[:, pl.ds(pl.multiple_of(i * tile, tile), tile)]
+            at = pl.ds(pl.multiple_of(i % 2 * tile, tile), tile)
+            gathered[at] = outer(columns, cotangents[...]).astype(low)
+            terms_copy(i).start()
+
+        terms_copy(tiles - 2).wait()
+        terms_copy(tiles - 1).wait()
+        exchange.start()
+
+    ring.run(fill_pairs, between_pairs)
     middle_grad_ref[...] = cotangents[:rows].astype(wide) + norm_back(middle_ref[...], part[:rows])
     middle_low = middle_grad_ref[...].astype(low)
     gathered[:rows] = middle_low
@@ -1193,18 +1233,20 @@
     coef_copies = [
         remote(
             coefficients_ref.at[0],
-            coefficients_ref.at[ORDER.index(k)],
+            coefficients_ref.at[k],
             coef_send.at[k],
             coef_recv.at[k],
-            site.device(k),
+            site.mate(k),
         )
         for k in range(1, TEAM)
     ]
     for copy in coef_copies:
         copy.start()
     for step in range(1, TEAM // 2 + 1):
+        if streamed:
+            exchange.step(2)
         gathered_ring.step(step)
-    stores[4].start()
+    stores[3].start()
     gathered_ring.finish()
     for copy in coef_copies:
         copy.wait()
@@ -1213,6 +1255,7 @@
     for store in stores:
         store.wait()
     if streamed:
+        exchange.finish()
         out_copy.wait()
 
 
@@ -1221,7 +1264,7 @@
     team_rows = rows * TEAM
     streamed = plan.fused
     hidden = mlp_w.shape[-1] // 2
-    padded = 8 * down_w.shape[0] if streamed else down_w.shape[0]
+    padded = down_w.shape[0]
     head_width = HEADS_DEV * DH
     vmem, anywhere = pl.BlockSpec(memory_space=pltpu.VMEM), pl.BlockSpec(memory_space=pl.ANY)
     flops = 2 * team_rows * width * (2 * head_width + 4 * hidden + padded)
@@ -1233,9 +1276,8 @@
         jax.ShapeDtypeStruct((team_rows, 2 * hidden), low),
         jax.ShapeDtypeStruct((team_rows, width), low),
         jax.ShapeDtypeStruct((TEAM, 8, rows), wide),
-        jax.ShapeDtypeStruct((padded, width), low),
     ]
-    out_specs = [vmem, vmem] + [anywhere] * 4 + [vmem, anywhere]
+    out_specs = [vmem, vmem] + [anywhere] * 4 + [vmem]
     scratch = [
         pltpu.VMEM((team_rows, width), low),
         pltpu.VMEM((width, 2 * hidden), low),
@@ -1246,10 +1288,10 @@
         pltpu.VMEM((team_rows, width), low),
         pltpu.VMEM((rows, width), wide),
         pltpu.VMEM((TEAM, 8, rows), wide),
-        *ring_sum_scratch(rows, width),
+        *team_sum_scratch(rows, width),
         pltpu.SemaphoreType.DMA((3,)),
-        pltpu.SemaphoreType.DMA((5,)),
-        *RingGather.scratch(),
+        pltpu.SemaphoreType.DMA((4,)),
+        *TeamGather.scratch(rows),
         *[pltpu.SemaphoreType.DMA((TEAM,))] * 4,
     ]
     if streamed:
@@ -1258,11 +1300,12 @@
             jax.ShapeDtypeStruct((team_rows, 4 * head_width), wide),
             jax.ShapeDtypeStruct((team_rows, head_width), wide),
             jax.ShapeDtypeStruct(state, low),
+            jax.ShapeDtypeStruct((hidden, width), low),
+            jax.ShapeDtypeStruct((hidden // 8, width), wide),
         ]
-        out_specs += [anywhere, anywhere, vmem]
+        out_specs += [anywhere, anywhere, vmem, anywhere, vmem]
         scratch += [
             *WeightStream.scratch(TEAM, MLP_SPLIT),
-            *WeightStream.scratch(1, down_w.shape[0] // 16),
             pltpu.VMEM((TEAM, 8, rows), wide),
             pltpu.VMEM((team_rows, head_width), low),
             pltpu.VMEM((2, width, head_width), low),
@@ -1270,7 +1313,8 @@
             pltpu.VMEM((team_rows, head_width), wide),
             pltpu.VMEM((team_rows, head_width), wide),
             pltpu.VMEM(state, low),
-            *[pltpu.SemaphoreType.DMA((n,)) for n in (2, 2, 1, 1, 1, 1)],
+            *[pltpu.SemaphoreType.DMA((n,)) for n in (2, 2, 1, 1, 1, 1, 2)],
+            *Exchange.scratch(*DOWN_KIND[0], hidden // 8, width),
         ]
     first = [anywhere, anywhere, vmem, vmem, vmem] if streamed else [vmem, vmem]
     return pl.pallas_call(
@@ -1341,8 +1385,7 @@
             sigma = jax.nn.sigmoid(z)
             return sigma * (1.0 + z * (1.0 - sigma))
 
-        @pl.loop(0, HEADS_DEV)
-        def _(h):
+        for h in range(HEADS_DEV):
             query, key = mix[:, head_lanes(0, h)], mix[:, head_lanes(1, h)]
             value, key_out = mix[:, head_lanes(2, h)], mix[:, head_lanes(3, h)]
             grad = self.out_grad[:, head_lanes(0, h)]
@@ -1361,7 +1404,7 @@
             key_grad *= slope(self.z[:, head_lanes(1, h)])
             grads[:, head_lanes(1, h)] = key_grad.astype(low)
 
-        pump()
+            pump()
 
 
 def exchange_scratch(gradients):
@@ -1411,7 +1454,7 @@
         lambda start, size: left_ref[start : start + size],
         lambda value, at: dot(value, right_ref[:, at]),
     )
-    ring = RingSum(site, rows, part, stage, landed, send, recv)
+    ring = TeamSum(site, rows, part, stage, landed, send, recv)
     eye = lax.broadcasted_iota(jnp.int32, (rows, rows), 0) == lax.broadcasted_iota(
         jnp.int32, (rows, rows), 1
     )
@@ -1434,11 +1477,12 @@
     )
     z_load.wait()
     back.gate(gathered, output, out, coefficients, column)
+    exchanges.step(1)
     back.feed()
     exchanges.step(1)
     ring.run(fill, lambda step: exchanges.step(2))
     sum_ref[...] = part[:rows]
-    back.run(lambda: exchanges.step(2))
+    back.run(lambda: exchanges.step(1))
     store = pltpu.make_async_copy(grads, grads_hbm, grads_sem.at[0])
     store.start()
     exchanges.finish()
@@ -1468,7 +1512,7 @@
         in_specs=[vmem] * 4 + [anywhere] + [vmem] * 6 + [anywhere] * len(gradients),
         out_specs=(vmem, anywhere) + (vmem,) * len(gradients),
         scratch_shapes=[
-            *ring_sum_scratch(rows, width),
+            *team_sum_scratch(rows, width),
             pltpu.VMEM((team_rows, 4 * head_width), wide),
             pltpu.VMEM((team_rows, 4 * head_width), low),
             pltpu.VMEM((team_rows, head_width), low),
@@ -1504,7 +1548,7 @@
         lambda start, size: left_ref[start : start + size],
         lambda value, at: dot_t(value, right_ref[at]),
     )
-    RingSum(site, rows, part, stage, landed, send, recv).run(fill, lambda step: exchanges.step(1))
+    TeamSum(site, rows, part, stage, landed, send, recv).run(fill, lambda step: exchanges.step(1))
     sum_ref[...] = part[:rows]
     groups = 8
     hidden = pair_ref.shape[2] // 2
@@ -1537,7 +1581,7 @@
         in_specs=[vmem] * 3 + [anywhere],
         out_specs=(vmem,) * len(shapes),
         scratch_shapes=[
-            *ring_sum_scratch(rows, width),
+            *team_sum_scratch(rows, width),
             pltpu.VMEM((TEAM, weight_rows, terms.shape[1]), low),
             *exchange_scratch(gradients),
         ],
@@ -1559,8 +1603,7 @@
 
 def team_places(plan, lengths, long_rows, short_rows):
     sub = lax.axis_index("seq") // TEAM
-    spot = jnp.asarray(PLACE, jnp.int32)[lax.axis_index("seq") % TEAM]
-    blocks = jnp.asarray(RING, jnp.int32)[(spot + TEAM - jnp.asarray(ORDER)) % TEAM]
+    blocks = (lax.axis_index("seq") % TEAM) ^ jnp.arange(TEAM)
     ends = jnp.cumsum(lengths)
     starts = ends - lengths
 
@@ -1650,28 +1693,27 @@
 ):
     row_count = tokens.shape[0]
     weight_rows = w_query.shape[0]
-    piece = w_down.shape[0]
     head_width = HEADS_DEV * DH
     team_tokens = row_count * TEAM
-    normed, cotangents, attn_w, output_w, mlp_pieces, *tables = front_call(
+    normed, cotangents, attn_w, output_w, down_w, mlp_pieces, *tables = front_call(
         tokens,
         cotangent,
         short_lengths,
         (w_query, w_key, w_value, w_unit),
         w_output,
+        w_down,
         w_gate,
         w_up,
     )
-    *results, z_all, heads_out, state = middle_call(
-        plan, (normed, attn_w, *tables), tokens, cotangents, output_w, mlp_pieces, w_down
-    )
-    middle, middle_grad, second, hidden_low, pair_grads, middle_all, coefficients, down_w = results
+    *results, z_all, heads_out, state, _, grad_down = middle_call(
+        plan, (normed, attn_w, *tables), tokens, cotangents, output_w, mlp_pieces, down_w
+    )
+    middle, middle_grad, second, hidden_low, pair_grads, middle_all, coefficients = results
     scale_rows = coefficients[:, 0].reshape(team_tokens, 1)
     gated = (heads_out * scale_rows * z_all[:, 3 * head_width :]).astype(low)
     output_terms = outer(gated, middle_all).astype(low)
-    down_terms = outer(hidden_low, cotangents).astype(low)
     pair_terms = outer(second, pair_grads).astype(low)
-    down_sum, z_grads, grad_pair, grad_down, grad_output = turn_call(
+    down_sum, z_grads, grad_pair, grad_output = turn_call(
         hidden_low,
         down_w,
         row_count,
@@ -1679,7 +1721,6 @@
         tables,
         [
             (pair_terms, TEAM, MLP_SPLIT, TEAM * weight_rows),
-            (down_terms, 1, piece // 16, piece),
             (output_terms, 1, 2, weight_rows),
         ],
     )
@@ -1740,8 +1781,8 @@
     attn_w = plan.across(plan.swap(attn_pieces).reshape(TEAM * weight_rows, 4 * head_width))
     mlp_w = plan.across(plan.swap(mlp_pieces).reshape(TEAM * weight_rows, 2 * hidden))
     down_w = plan.across(w_down)
-    normed = jnp.concatenate(plan.ring_gather(normed_own), axis=0)
-    cotangents = jnp.concatenate(plan.ring_gather(cotangent), axis=0)
+    normed = plan.team_gather(normed_own)
+    cotangents = plan.team_gather(cotangent)
 
     def to_heads(x):
         x = x.reshape(TEAM, 2, LONG_DEV, HEADS_DEV, DH).transpose(1, 3, 0, 2, 4)
@@ -1776,13 +1817,13 @@
     squares = jnp.broadcast_to(squares, (TEAM, 8, row_count))
     gated_raw = (heads_out * z_all[:, 3 * head_width :]).astype(low)
     results = middle_call(plan, (squares, gated_raw), tokens, cotangents, output_w, mlp_w, down_w)
-    middle, middle_grad, second, hidden_low, pair_grads, middle_all, coefficients, down_w = results
+    middle, middle_grad, second, hidden_low, pair_grads, middle_all, coefficients = results
     z_query, z_key, _, z_unit = jnp.split(z_all, 4, axis=1)
     scale_rows = coefficients[:, 0].reshape(team_tokens, 1)
     inner_rows = coefficients[:, 1].reshape(team_tokens, 1)
     down_terms = outer(hidden_low, cotangents)
     pair_terms = outer(second, pair_grads)
-    down_sum = plan.ring_reduce(lambda i: dot(rows(hidden_low, i), down_w))
+    down_sum = plan.team_sum(lambda i: dot(rows(hidden_low, i), down_w))
     grad_down = plan.across_sum(down_terms)
     grad_pair = plan.across_sum(pair_terms).astype(low)
     grad_pair = plan.swap(grad_pair.reshape(TEAM, weight_rows, 2 * hidden))
@@ -1828,7 +1869,7 @@
         axis=1,
     )
     four_terms = outer(normed, z_grads)
-    first_grad = plan.ring_reduce(lambda i: dot_t(rows(z_grads, i), attn_w))
+    first_grad = plan.team_sum(lambda i: dot_t(rows(z_grads, i), attn_w))
     grad_four = plan.across_sum(four_terms).astype(low)
     grad_four = plan.swap(grad_four.reshape(TEAM, weight_rows, 4 * head_width))
     grad_output = plan.across_sum(output_terms)

time: 614 us -> 561 us (0.914)
  Pallas kernels: 534 us -> 508 us
  local copies, waits for them, and re-layouts: 29.9 us -> 10 us
    pallas_call x1, Pallas kernels: 144 us -> 110 us  [turn_call(): pl.pallas_call(functools.partial(turn_kernel, width, rows, kinds), out_sh...]
    pallas_call x1, Pallas kernels: 98.3 us -> 121 us  [front_call(): pl.pallas_call(front_kernel, out_shape=(jax.ShapeDtypeStruct((TEAM * rows...]
    unnamed x76 -> x36, local copies, waits for them, and re-layouts: 29.2 us -> 9.29 us
    pallas_call x1, Pallas kernels: 86.3 us -> 75.1 us  [last_call(): pl.pallas_call(functools.partial(last_kernel, width, rows, split), out_sh...]
    dot_general x4 -> x3, matrix products: 31 us -> 25.3 us  [outer(): lax.dot_general(left, right, (((0,), (0,)), ((), ())), preferred_element_...]
where the time goes in v6:
time: 561 us; the launch traced here: 553 us
  Pallas kernels  508 us (91%)
  matrix products  25.3 us (5%)
  local copies, waits for them, and re-layouts  10 us (2%)
    pallas_call x1, Pallas kernels, middle_call(): pl.pallas_call(functools.partial(middle_kernel, width, hidden, streamed),...  202 us
    pallas_call x1, Pallas kernels, front_call(): pl.pallas_call(front_kernel, out_shape=(jax.ShapeDtypeStruct((TEAM * rows...  121 us
    pallas_call x1, Pallas kernels, turn_call(): pl.pallas_call(functools.partial(turn_kernel, width, rows, kinds), out_sh...  110 us
    pallas_call x1, Pallas kernels, last_call(): pl.pallas_call(functools.partial(last_kernel, width, rows, split), out_sh...  75.1 us
    dot_general x3, matrix products, outer(): lax.dot_general(left, right, (((0,), (0,)), ((), ())), preferred_element_...  25.3 us
  transfers between devices with their start and end apart: 1, of which 0 were waited for; matrix products, arithmetic and copies ran while one was open for 2% of the time, Pallas kernels for 14%

profile of v6, /device:TPU:0, one launch (start us, length us, event | category | flops | bytes accessed | tf_op | source)
XLA Modules:
  0.0 553.1 jit_solution(4335982332252074498)
XLA Ops:
  0.6 120.6 %shard_map.186 = (bf16[512,2048]{1,0:T(8,128)(2,1)}, bf16[512,2048]{1,0:T(8,128)(2,1)}, bf16[2048,2048]{1,0:T(8,128)(2,1)}, bf16[512,2048]{1,0:T(8,128)(2,1)}, b...) custom-call(bf16[128,2048]{1,0:T(8,128)(2,1)} %refs_5_.1, ...), custom_call_target="tpu_custom_call" | custom-call | bytes 62914560 | tf_op jit(solution)/shard_map/pallas_call | solution.py:848
  121.3 202.5 %shard_map.187 = (f32[128,2048]{1,0:T(8,128)}, f32[128,2048]{1,0:T(8,128)}, bf16[512,2048]{1,0:T(8,128)(2,1)}, bf16[512,1408]{1,0:T(8,128)(2,1)}, bf16[512,2816]...) custom-call(bf16[512,2048]{1,0:T(8,128)(2,1)} %get-tuple-element.41., ...), custom_call_target="tpu_custom_call" | custom-call | flops 16911433728 | bytes 62914560 | tf_op jit(solution)/shard_map/pallas_call | solution.py:1320
  323.8 0.7 slice.6
  324.5 0.0 copy-start.2
  324.5 0.0 copy-start.9
  324.5 11.3 %convolution_convert_fusion.refs_11_ = bf16[2048,2816]{1,0:T(8,128)(2,1)} fusion(bf16[512,2048]{1,0:T(8,128)(2,1)} %get-tuple-element.57, bf16[512,2816]{1,0:T(8,128)(2,1)} %get-tuple-element.58), kind=kOutput, calls=%fused_computation | convolution fusion | flops 5911347200 | bytes 16515072 | tf_op jit(solution)/shard_map/dot_general | solution.py:49
  335.7 0.0 copy-done.2
  335.7 0.0 copy-done.9
  335.7 4.0 convolution_convert_fusion.2.refs_12_
  339.7 110.2 %shard_map.188 = (f32[128,2048]{1,0:T(8,128)}, bf16[512,2048]{1,0:T(8,128)(2,1)}, bf16[4,64,2816]{2,1,0:T(8,128)(2,1)}, f32[64,2048]{1,0:T(8,128)}) custom-call(bf16[512,1408]{1,0:T(8,128)(2,1)} %get-tuple-element.51.refs_0_, bf16[1408,2048]{1,0:T(8,128)(2,1)} %get-tuple-element.49.refs_9_.refs_1_, bf16[512,2048]{1,0:T(8,128)(2,1)} %get-tuple-element.52.refs_2_, ...), custom_call_target="tpu_custom_call" | custom-call | flops 2952790016 | bytes 62914560 | tf_op jit(solution)/shard_map/pallas_call | solution.py:1509
  449.9 5.4 collective-permute-start
  455.3 10.0 %convolution_convert_fusion.1.refs_3_ = bf16[2048,2048]{1,0:T(8,128)(2,1)} fusion(bf16[512,2048]{1,0:T(8,128)(2,1)} %get-tuple-element.41.refs_0_, bf16[512,2048]{1,0:T(8,128)(2,1)} %get-tuple-element.61.refs_0_), kind=kOutput, calls=%fused_computation.1 | convolution fusion | flops 4299161600 | bytes 12582912 | tf_op jit(solution)/shard_map/dot_general | solution.py:49
  465.3 0.0 copy-start
  465.3 0.0 copy-start.6
  465.3 0.0 copy-start.7
  465.4 0.0 copy-start.8
  465.4 75.1 %shard_map.189 = (f32[128,2048]{1,0:T(8,128)}, f32[64,2048]{1,0:T(8,128)}, f32[64,2048]{1,0:T(8,128)}, f32[64,2048]{1,0:T(8,128)}, f32[64,2048]{1,0:T(8,128)}, /*index=5*/f32[64,5632]{1,0:T(8,128)}, f32[64,5632]{1,0:T(8,128)}) custom-call(bf16[512,2048]{1,0:T(8,128)(2,1)} %get-tuple-element.61.refs_0_, bf16[2048,2048]{1,0:T(8,128)(2,1)} %get-tuple-element.42.refs_1_, ...), custom_call_target="tpu_custom_call" | custom-call | flops 4294967296 | bytes 62914560 | tf_op jit(solution)/shard_map/pallas_call | solution.py:1578
  540.5 0.0 copy-start.1
  540.5 0.0 copy-done
  540.5 1.6 fusion
  542.1 0.0 copy-done.6
  542.1 0.0 copy-done.7
  542.1 0.0 copy-done.8
  542.1 0.0 copy-done.1
  542.1 0.0 copy-start.13
  542.2 0.0 copy-start.12
  542.2 1.5 fusion.4
  543.6 0.0 copy-start.11
  543.6 0.0 copy-start.10
  543.6 0.0 collective-permute-done
  543.6 0.0 copy-done.13
  543.7 0.8 copy.29
  544.5 0.0 copy-done.12
  544.5 0.0 copy-start.5
  544.5 0.8 copy.30
  545.2 0.0 copy-done.11
  545.3 0.8 copy.31
  546.0 0.0 copy-done.10
  546.0 0.8 copy.32
  546.8 0.0 copy-start.4
  546.8 2.0 copy.33
  548.8 0.0 copy-done.5
  548.8 1.1 copy.34
  549.9 0.0 copy-done.4
  549.9 0.0 copy-start.3
  549.9 1.1 copy.35
  551.0 0.8 copy-done.3
  551.8 1.1 copy.36
  (2 shorter events, 0.0 us)
Async XLA Ops:
  324.5 11.3 %copy-start.2 = (bf16[512,2048]{1,0:T(8,128)(2,1)S(1)}, bf16[512,2048]{1,0:T(8,128)(2,1)}, u32[]{:S(2)}) copy-start(bf16[512,2048]{1,0:T(8,128)(2,1)} %get-tuple-element.52.refs_2_) | copy-start | bytes 6291460
  324.5 11.3 %copy-start.9 = (f32[512,512]{1,0:T(8,128)S(1)}, f32[512,512]{1,0:T(8,128)}, u32[]{:S(2)}) copy-start(f32[512,512]{1,0:T(8,128)} %get-tuple-element.54.refs_5_) | copy-start | bytes 3145732
  449.9 93.7 %collective-permute-start = (f32[64,2048]{1,0:T(8,128)}, f32[64,2048]{1,0:T(8,128)}, u32[]{:S(2)}, u32[]{:S(2)}) collective-permute-start(f32[64,2048]{1,0:T(8,128)} %get-tuple-element.68), channel_id=1, source_target_pairs={{0,0},{1,8},{2,16},{3,24},{4,1},{5,9},{6,17},{7,25},{8,2},{9,10},{... | collective-permute-start | bytes 1572872 | tf_op jit(solution)/shard_map/ppermute | solution.py:128
  465.3 75.2 %copy-start = (bf16[128,2048]{1,0:T(8,128)(2,1)S(1)}, bf16[128,2048]{1,0:T(8,128)(2,1)}, u32[]{:S(2)}) copy-start(bf16[128,2048]{1,0:T(8,128)(2,1)} %refs_5_.1) | copy-start | bytes 1572868
  465.3 76.8 %copy-start.6 = (f32[128,2048]{1,0:T(8,128)S(1)}, f32[128,2048]{1,0:T(8,128)}, u32[]{:S(2)}) copy-start(f32[128,2048]{1,0:T(8,128)} %get-tuple-element.50) | copy-start | bytes 3145732
  465.3 76.8 %copy-start.7 = (f32[128,2048]{1,0:T(8,128)S(1)}, f32[128,2048]{1,0:T(8,128)}, u32[]{:S(2)}) copy-start(f32[128,2048]{1,0:T(8,128)} %get-tuple-element.60) | copy-start | bytes 3145732
  465.4 76.8 %copy-start.8 = (f32[128,2048]{1,0:T(8,128)S(1)}, f32[128,2048]{1,0:T(8,128)}, u32[]{:S(2)}) copy-start(f32[128,2048]{1,0:T(8,128)} %get-tuple-element.59) | copy-start | bytes 3145732
  540.5 1.6 copy-start.1
  542.1 1.5 copy-start.13
  542.2 2.3 copy-start.12
  543.6 1.6 copy-start.11
  543.6 2.4 copy-start.10
  544.5 4.4 copy-start.5
  546.8 3.1 copy-start.4
  549.9 1.9 copy-start.3

commit v7 on v6

--- a/solution.py
+++ b/solution.py
@@ -271,8 +271,29 @@
         self.block = keep.shape[1]
         self.count = pieces * split
         self.size = self.block // self.count
+        self.compute = self.core_out = None
 
     SCRATCH = 13
+
+    def by(self, compute, core_out):
+        self.compute, self.core_out = compute, core_out
+        return self
+
+    def prepare(self, i):
+        if self.compute is None:
+            self.core_copy(i).start()
+            self.load(i).start()
+            return
+        if i < 2:
+            self.core_copy(i + 2).wait_send()
+        self.compute(self.group(1, i), self.core_out.at[i % 2])
+        self.core_copy(i).start()
+        self.compute(self.group(0, i), self.keep.at[i])
+
+    def ready(self, i):
+        if self.compute is None:
+            self.load(i).wait()
+        self.core_copy(i).wait_recv()
 
     @staticmethod
     def scratch(pieces, split, block, width):
@@ -293,16 +314,19 @@
             pltpu.SemaphoreType.DMA((pieces, split)),
         ]
 
+    def group(self, core, i):
+        return self.site.group(core, i // 2, i % 2)
+
     def terms(self, core, i):
-        group = self.site.group(core, i // 2, i % 2)
-        return self.source.at[pl.ds(pl.multiple_of(group * self.block, 16), self.block)]
+        start = pl.multiple_of(self.group(core, i) * self.block, 16)
+        return self.source.at[pl.ds(start, self.block)]
 
     def load(self, i):
         return pltpu.make_async_copy(self.terms(0, i), self.keep.at[i], self.load_sem.at[i])
 
     def core_copy(self, i):
         return remote(
-            self.terms(1, i),
+            self.terms(1, i) if self.compute is None else self.core_out.at[i % 2],
             self.core_in.at[i],
             self.core_send.at[i],
             self.core_recv.at[i],
@@ -357,23 +381,16 @@
                 total = total + term[at].astype(wide)
             into[at] = total.astype(into.dtype)
 
-    def start(self):
-        for i in (3, 2, 1, 0):
-            self.core_copy(i).start()
-            self.load(i).start()
-
     def to_side(self, far, j):
         if j == 0:
-            self.load(2 + far).wait()
-            self.core_copy(2 + far).wait_recv()
+            self.ready(2 + far)
         into = self.keep.at[2 + far]
         self.add(j, into, (into, self.core_in.at[2 + far]))
         self.side_copy(far, j).start()
 
     def to_far(self, j):
         if j == 0:
-            self.load(1).wait()
-            self.core_copy(1).wait_recv()
+            self.ready(1)
         self.side_copy(1, j).wait_recv()
         into = self.keep.at[1]
         self.add(j, into, (into, self.core_in.at[1], self.side_in.at[1]))
@@ -381,8 +398,7 @@
 
     def to_owner(self, j):
         if j == 0:
-            self.load(0).wait()
-            self.core_copy(0).wait_recv()
+            self.ready(0)
         self.side_copy(0, j).wait_recv()
         self.far_copy(j).wait_recv()
         own = self.keep.at[0]
@@ -398,7 +414,7 @@
             self.result[self.site.place, sub] = own[self.at(j)]
 
     def finish(self):
-        for i in range(4):
+        for i in range(4 if self.compute is None else 2):
             self.core_copy(i).wait_send()
 
         @pl.loop(0, self.count)
@@ -429,14 +445,19 @@
         self.sent = self.done = self.settled = 0
 
     def start(self):
+        self.prepare(3)
+        self.send_sides(1)
+        self.prepare(1)
+        self.send_sides(self.depth - 1)
+
+    def prepare(self, i):
         for exchange in self.exchanges:
-            exchange.start()
-        self.send_sides(self.depth)
+            exchange.prepare(i)
 
     def send_sides(self, count):
         for far, (exchange, j) in self.sides[self.sent : self.sent + count]:
             exchange.to_side(far, j)
-        self.sent += count
+            self.sent += 1
 
     def settle(self):
         if self.settled < len(self.parts):
@@ -450,6 +471,8 @@
                 return
             exchange, j = self.parts[self.done]
             exchange.to_far(j)
+            if self.done < 2:
+                self.prepare((2, 0)[self.done])
             self.send_sides(2)
             if self.done >= self.depth + 1:
                 self.settle()
@@ -1055,7 +1078,7 @@
     if streamed:
         site.meet([site.core_mate, site.side_mate, site.far_mate])
         streams = WeightStreams(
-            [WeightStream(site, TEAM, MLP_SPLIT, mlp_hbm, mlp, stream_sems)], 2
+            [WeightStream(site, TEAM, MLP_SPLIT, mlp_hbm, mlp, stream_sems)], 3
         )
         streams.start()
     else:
@@ -1090,7 +1113,7 @@
         attention.project(
             gathered, attn_hbm, z_hbm, tiles, staging, tile_sems, z_sems, lambda: None
         )
-        attention.run(streams.step)
+        attention.run(lambda: None)
         out_copy = pltpu.make_async_copy(heads_out, out_hbm, out_sem.at[0])
         out_copy.start()
         for slot in range(TEAM):
@@ -1191,7 +1214,7 @@
 
     def between_pairs(step):
         if streamed:
-            exchange.step(2)
+            exchange.step(3)
 
     if streamed:
         tile = 128
@@ -1244,7 +1267,7 @@
         copy.start()
     for step in range(1, TEAM // 2 + 1):
         if streamed:
-            exchange.step(2)
+            exchange.step(3)
         gathered_ring.step(step)
     stores[3].start()
     gathered_ring.finish()
@@ -1427,6 +1450,17 @@
     return Exchanges(exchanges)
 
 
+def outer_blocks(left, right, block):
+    def compute(group, ref):
+        columns = left[:, pl.ds(pl.multiple_of(group * block, 128), block)]
+        half = right.shape[1] // 2
+        for i in range(2):
+            at = slice(i * half, (i + 1) * half)
+            ref[:, at] = outer(columns, right[:, at]).astype(low)
+
+    return compute
+
+
 def turn_kernel(width, rows, kinds, *refs):
     refs = iter(refs)
 
@@ -1436,13 +1470,17 @@
     count = len(kinds)
     left_ref, right_ref, gathered, output, z_hbm, out, state, coefficients = take(8)
     columns_ref, rows_ref, rates_ref = take(3)
-    sources = take(count)
+    second, pairs = take(2)
+    sources = [None] + take(count - 1)
     sum_ref, grads_hbm = take(2)
     results = take(count)
     part, stage, landed, send, recv = take(5)
     z, mix, out_grad, grads, increment, state_in, z_sem, grads_sem, state_send, state_recv = take(10)
+    (core_out,) = take(1)
     site = Site()
     exchanges = exchanges_of(site, kinds, sources, results, list(refs))
+    first = exchanges.exchanges[0]
+    first.by(outer_blocks(second, pairs, first.block), core_out)
     z_load = pltpu.make_async_copy(z_hbm, z, z_sem.at[0])
     z_load.start()
     site.meet([site.core_mate, site.side_mate, site.far_mate])
@@ -1489,7 +1527,7 @@
     store.wait()
 
 
-def turn_call(left, right, rows, attention, tables, gradients):
+def turn_call(left, right, rows, attention, tables, pair, gradients):
     width = right.shape[1]
     team_rows = left.shape[0]
     head_width = HEADS_DEV * DH
@@ -1509,7 +1547,7 @@
     return pl.pallas_call(
         functools.partial(turn_kernel, width, rows, kinds),
         out_shape=tuple(shapes),
-        in_specs=[vmem] * 4 + [anywhere] + [vmem] * 6 + [anywhere] * len(gradients),
+        in_specs=[vmem] * 4 + [anywhere] + [vmem] * 8 + [anywhere] * (len(gradients) - 1),
         out_specs=(vmem, anywhere) + (vmem,) * len(gradients),
         scratch_shapes=[
             *team_sum_scratch(rows, width),
@@ -1520,6 +1558,7 @@
             pltpu.VMEM(state, low),
             pltpu.VMEM(state, low),
             *[pltpu.SemaphoreType.DMA((1,))] * 4,
+            pltpu.VMEM((2, gradients[0][3], pair[1].shape[1]), low),
             *exchange_scratch(gradients),
         ],
         compiler_params=pltpu.CompilerParams(
@@ -1530,15 +1569,17 @@
             bytes_accessed=60 * 2**20,
             transcendentals=0,
         ),
-    )(left, right, *attention, *tables, *[gradient[0] for gradient in gradients])
+    )(left, right, *attention, *tables, *pair, *[gradient[0] for gradient in gradients[1:]])
 
 
 def last_kernel(width, rows, split, *refs):
-    left_ref, right_ref, pair_ref, source, sum_ref, *refs = refs
+    left_ref, right_ref, pair_ref, normed_ref, sum_ref, *refs = refs
     outs, gate_out, up_out, refs = refs[:4], refs[4], refs[5], refs[6:]
-    part, stage, landed, send, recv, result, *refs = refs
+    part, stage, landed, send, recv, result, core_out, *refs = refs
     site = Site()
-    exchanges = exchanges_of(site, ((TEAM, split),), [source], [result], refs)
+    exchanges = exchanges_of(site, ((TEAM, split),), [None], [result], refs)
+    (exchange,) = exchanges.exchanges
+    exchange.by(outer_blocks(normed_ref, left_ref, exchange.block), core_out)
     site.meet([site.core_mate, site.side_mate, site.far_mate])
     exchanges.start()
     fill = fill_tiles(
@@ -1567,22 +1608,24 @@
             out[:, place * head_width : (place + 1) * head_width] = columns.astype(wide)
 
 
-def last_call(left, right, rows, pair, terms, split):
+def last_call(left, right, rows, pair, normed, split):
     width = right.shape[0]
     weight_rows = pair.shape[1]
-    vmem, anywhere = pl.BlockSpec(memory_space=pltpu.VMEM), pl.BlockSpec(memory_space=pl.ANY)
+    vmem = pl.BlockSpec(memory_space=pltpu.VMEM)
     shapes = [jax.ShapeDtypeStruct((rows, width), wide)]
     shapes += [jax.ShapeDtypeStruct((weight_rows, width), wide)] * 4
     shapes += [jax.ShapeDtypeStruct((weight_rows, TEAM * pair.shape[2] // 2), wide)] * 2
-    gradients = [(terms, TEAM, split, TEAM * weight_rows)]
+    block = TEAM * weight_rows
+    gradients = [(left, TEAM, split, block)]
     return pl.pallas_call(
         functools.partial(last_kernel, width, rows, split),
         out_shape=tuple(shapes),
-        in_specs=[vmem] * 3 + [anywhere],
+        in_specs=[vmem] * 4,
         out_specs=(vmem,) * len(shapes),
         scratch_shapes=[
             *team_sum_scratch(rows, width),
-            pltpu.VMEM((TEAM, weight_rows, terms.shape[1]), low),
+            pltpu.VMEM((TEAM, weight_rows, left.shape[1]), low),
+            pltpu.VMEM((2, block, left.shape[1]), low),
             *exchange_scratch(gradients),
         ],
         compiler_params=pltpu.CompilerParams(
@@ -1593,7 +1636,7 @@
             bytes_accessed=60 * 2**20,
             transcendentals=0,
         ),
-    )(left, right, pair, terms)
+    )(left, right, pair, normed)
 
 
 def team_rates():
@@ -1712,23 +1755,22 @@
     scale_rows = coefficients[:, 0].reshape(team_tokens, 1)
     gated = (heads_out * scale_rows * z_all[:, 3 * head_width :]).astype(low)
     output_terms = outer(gated, middle_all).astype(low)
-    pair_terms = outer(second, pair_grads).astype(low)
     down_sum, z_grads, grad_pair, grad_output = turn_call(
         hidden_low,
         down_w,
         row_count,
         (middle_all, output_w, z_all, heads_out, state, coefficients),
         tables,
+        (second, pair_grads),
         [
-            (pair_terms, TEAM, MLP_SPLIT, TEAM * weight_rows),
+            (pair_grads, TEAM, MLP_SPLIT, TEAM * weight_rows),
             (output_terms, 1, 2, weight_rows),
         ],
     )
     grad_output = plan.team_rows_back(grad_output)
     mixed = (middle + down_sum).astype(low)
-    four_terms = outer(normed, z_grads).astype(low)
     first_grad, grad_query, grad_key, grad_value, grad_unit, grad_gate, grad_up = last_call(
-        z_grads, attn_w, row_count, grad_pair, four_terms, ATTN_SPLIT
+        z_grads, attn_w, row_count, grad_pair, normed, ATTN_SPLIT
     )
     tokens_grad = (middle_grad + norm_back(tokens.astype(wide), first_grad)).astype(low)
     return (

time: 561 us -> 527 us (0.939)
  matrix products: 25.3 us -> 5 us
  Pallas kernels: 508 us -> 495 us
    dot_general x3 -> x1, matrix products: 25.3 us -> 5 us  [outer(): lax.dot_general(left, right, (((0,), (0,)), ((), ())), preferred_element_...]
    pallas_call x1, Pallas kernels: 202 us -> 187 us  [middle_call(): pl.pallas_call(functools.partial(middle_kernel, width, hidden, streamed),...]
    pallas_call x1, Pallas kernels: 75.1 us -> 81.4 us  [last_call(): pl.pallas_call(functools.partial(last_kernel, width, rows, split), out_sh...]
  transfers between devices with their start and end apart: 1 -> 1, of which waited for: 0 -> 0; matrix products, arithmetic and copies ran while one was open for 2% -> 1% of each run, Pallas kernels for 14% -> 16%
where the time goes in v7:
time: 527 us; the launch traced here: 519 us
  Pallas kernels  495 us (94%)
  local copies, waits for them, and re-layouts  10 us (2%)
  starting transfers between devices  5.38 us (1%)
    pallas_call x1, Pallas kernels, middle_call(): pl.pallas_call(functools.partial(middle_kernel, width, hidden, streamed),...  187 us
    pallas_call x1, Pallas kernels, front_call(): pl.pallas_call(front_kernel, out_shape=(jax.ShapeDtypeStruct((TEAM * rows...  121 us
    pallas_call x1, Pallas kernels, turn_call(): pl.pallas_call(functools.partial(turn_kernel, width, rows, kinds), out_sh...  106 us
    pallas_call x1, Pallas kernels, last_call(): pl.pallas_call(functools.partial(last_kernel, width, rows, split), out_sh...  81.4 us
  transfers between devices with their start and end apart: 1, of which 0 were waited for; matrix products, arithmetic and copies ran while one was open for 1% of the time, Pallas kernels for 16%

profile of v7, /device:TPU:0, one launch (start us, length us, event | category | flops | bytes accessed | tf_op | source)
XLA Modules:
  0.0 519.4 jit_solution(14347036820940205612)
XLA Ops:
  0.6 120.6 %shard_map.186 = (bf16[512,2048]{1,0:T(8,128)(2,1)}, bf16[512,2048]{1,0:T(8,128)(2,1)}, bf16[2048,2048]{1,0:T(8,128)(2,1)}, bf16[512,2048]{1,0:T(8,128)(2,1)}, b...) custom-call(bf16[128,2048]{1,0:T(8,128)(2,1)} %refs_5_.1, ...), custom_call_target="tpu_custom_call" | custom-call | bytes 62914560 | tf_op jit(solution)/shard_map/pallas_call | solution.py:871
  121.3 187.0 %shard_map.187 = (f32[128,2048]{1,0:T(8,128)}, f32[128,2048]{1,0:T(8,128)}, bf16[512,2048]{1,0:T(8,128)(2,1)}, bf16[512,1408]{1,0:T(8,128)(2,1)}, bf16[512,2816]...) custom-call(bf16[512,2048]{1,0:T(8,128)(2,1)} %get-tuple-element.41., ...), custom_call_target="tpu_custom_call" | custom-call | flops 16911433728 | bytes 62914560 | tf_op jit(solution)/shard_map/pallas_call | solution.py:1343
  308.3 0.7 slice.6
  309.0 5.0 convolution_convert_fusion.refs_13_
  314.0 105.7 %shard_map.188 = (f32[128,2048]{1,0:T(8,128)}, bf16[512,2048]{1,0:T(8,128)(2,1)}, bf16[4,64,2816]{2,1,0:T(8,128)(2,1)}, f32[64,2048]{1,0:T(8,128)}) custom-call(bf16[512,1408]{1,0:T(8,128)(2,1)} %get-tuple-element.51.refs_0_, bf16[1408,2048]{1,0:T(8,128)(2,1)} %get-tuple-element.49.refs_9_.refs_1_, bf16[512,2048]{1,0:T(8,128)(2,1)} %get-tuple-element.52.refs_2_, ...), custom_call_target="tpu_custom_call" | custom-call | flops 2952790016 | bytes 62914560 | tf_op jit(solution)/shard_map/pallas_call | solution.py:1547
  419.8 5.4 %collective-permute-start = (f32[64,2048]{1,0:T(8,128)}, f32[64,2048]{1,0:T(8,128)}, u32[]{:S(2)}, u32[]{:S(2)}) collective-permute-start(f32[64,2048]{1,0:T(8,128)} %get-tuple-element.68), channel_id=1, source_target_pairs={{0,0},{1,8},{2,16},{3,24},{4,1},{5,9},{6,17},{7,25},{8,2},{9,10},{... | collective-permute-start | bytes 1572872 | tf_op jit(solution)/shard_map/ppermute | solution.py:128
  425.2 0.0 copy-start
  425.2 0.0 copy-start.5
  425.2 0.0 copy-start.6
  425.2 0.0 copy-start.7
  425.2 81.4 %shard_map.189 = (f32[128,2048]{1,0:T(8,128)}, f32[64,2048]{1,0:T(8,128)}, f32[64,2048]{1,0:T(8,128)}, f32[64,2048]{1,0:T(8,128)}, f32[64,2048]{1,0:T(8,128)}, /*index=5*/f32[64,5632]{1,0:T(8,128)}, f32[64,5632]{1,0:T(8,128)}) custom-call(bf16[512,2048]{1,0:T(8,128)(2,1)} %get-tuple-element.61.refs_0_, bf16[2048,2048]{1,0:T(8,128)(2,1)} %get-tuple-element.42.refs_1_, ...), custom_call_target="tpu_custom_call" | custom-call | flops 4294967296 | bytes 62914560 | tf_op jit(solution)/shard_map/pallas_call | solution.py:1620
  506.6 0.0 copy-start.1
  506.6 0.0 copy-done
  506.6 1.6 fusion
  508.2 0.0 copy-done.5
  508.2 0.0 copy-done.6
  508.2 0.0 copy-done.7
  508.2 0.0 copy-done.1
  508.2 0.0 copy-start.11
  508.2 0.0 copy-start.10
  508.2 1.5 fusion.4
  509.7 0.0 copy-start.9
  509.7 0.0 copy-start.8
  509.7 0.0 collective-permute-done
  509.7 0.0 copy-done.11
  509.7 0.8 copy.29
  510.5 0.0 copy-done.10
  510.5 0.0 copy-start.4
  510.5 0.8 copy.30
  511.3 0.0 copy-done.9
  511.3 0.8 copy.31
  512.1 0.0 copy-done.8
  512.1 0.8 copy.32
  512.9 0.0 copy-start.3
  512.9 2.0 copy.33
  514.9 0.0 copy-done.4
  514.9 1.1 copy.34
  516.0 0.0 copy-done.3
  516.0 0.0 copy-start.2
  516.0 1.1 copy.35
  517.1 0.8 copy-done.2
  517.9 1.1 copy.36
  (2 shorter events, 0.0 us)
Async XLA Ops:
  419.8 89.9 %collective-permute-start = (f32[64,2048]{1,0:T(8,128)}, f32[64,2048]{1,0:T(8,128)}, u32[]{:S(2)}, u32[]{:S(2)}) collective-permute-start(f32[64,2048]{1,0:T(8,128)} %get-tuple-element.68), channel_id=1, source_target_pairs={{0,0},{1,8},{2,16},{3,24},{4,1},{5,9},{6,17},{7,25},{8,2},{9,10},{... | collective-permute-start | bytes 1572872 | tf_op jit(solution)/shard_map/ppermute | solution.py:128
  425.2 81.4 %copy-start = (bf16[128,2048]{1,0:T(8,128)(2,1)S(1)}, bf16[128,2048]{1,0:T(8,128)(2,1)}, u32[]{:S(2)}) copy-start(bf16[128,2048]{1,0:T(8,128)(2,1)} %refs_5_.1) | copy-start | bytes 1572868
  425.2 83.0 %copy-start.5 = (f32[128,2048]{1,0:T(8,128)S(1)}, f32[128,2048]{1,0:T(8,128)}, u32[]{:S(2)}) copy-start(f32[128,2048]{1,0:T(8,128)} %get-tuple-element.50) | copy-start | bytes 3145732
  425.2 83.0 %copy-start.6 = (f32[128,2048]{1,0:T(8,128)S(1)}, f32[128,2048]{1,0:T(8,128)}, u32[]{:S(2)}) copy-start(f32[128,2048]{1,0:T(8,128)} %get-tuple-element.60) | copy-start | bytes 3145732
  425.2 83.0 %copy-start.7 = (f32[128,2048]{1,0:T(8,128)S(1)}, f32[128,2048]{1,0:T(8,128)}, u32[]{:S(2)}) copy-start(f32[128,2048]{1,0:T(8,128)} %get-tuple-element.59) | copy-start | bytes 3145732
  506.6 1.6 copy-start.1
  508.2 1.5 copy-start.11
  508.2 2.3 copy-start.10
  509.7 1.6 copy-start.9
  509.7 2.4 copy-start.8
  510.5 4.4 copy-start.4
  512.9 3.1 copy-start.3
  516.0 1.9 copy-start.2

commit v8 on v7

--- a/solution.py
+++ b/solution.py
@@ -432,7 +432,7 @@
 
 
 class Exchanges:
-    def __init__(self, exchanges, depth=3):
+    def __init__(self, exchanges, depth=2):
         self.exchanges, self.depth = exchanges, depth
         self.parts = [(exchange, j) for exchange in exchanges for j in range(exchange.count)]
         count = len(self.parts)
@@ -851,10 +851,11 @@
     cotangent_ring.start()
     streams.step(3)
     normed_ring.step(2)
-    streams.step(1)
+    streams.step(3)
     cotangent_ring.step(1)
+    streams.step(4)
+    cotangent_ring.step(2)
     streams.finish()
-    cotangent_ring.step(2)
     normed_ring.finish()
     cotangent_ring.finish()
     for copy in own + [store]:

time: 527 us -> 522 us (level)
  no operation moved by 1% of the time
where the time goes in v8:
time: 522 us; the launch traced here: 515 us
  Pallas kernels  490 us (94%)
  local copies, waits for them, and re-layouts  10 us (2%)
  starting transfers between devices  5.38 us (1%)
    pallas_call x1, Pallas kernels, middle_call(): pl.pallas_call(functools.partial(middle_kernel, width, hidden, streamed),...  182 us
    pallas_call x1, Pallas kernels, front_call(): pl.pallas_call(front_kernel, out_shape=(jax.ShapeDtypeStruct((TEAM * rows...  119 us
    pallas_call x1, Pallas kernels, turn_call(): pl.pallas_call(functools.partial(turn_kernel, width, rows, kinds), out_sh...  109 us
    pallas_call x1, Pallas kernels, last_call(): pl.pallas_call(functools.partial(last_kernel, width, rows, split), out_sh...  79.9 us
  transfers between devices with their start and end apart: 1, of which 0 were waited for; matrix products, arithmetic and copies ran while one was open for 1% of the time, Pallas kernels for 16%

profile of v8, /device:TPU:0, one launch (start us, length us, event | category | flops | bytes accessed | tf_op | source)
XLA Modules:
  0.0 514.7 jit_solution(17195885184772206810)
XLA Ops:
  0.6 119.2 %shard_map.186 = (bf16[512,2048]{1,0:T(8,128)(2,1)}, bf16[512,2048]{1,0:T(8,128)(2,1)}, bf16[2048,2048]{1,0:T(8,128)(2,1)}, bf16[512,2048]{1,0:T(8,128)(2,1)}, b...) custom-call(bf16[128,2048]{1,0:T(8,128)(2,1)} %refs_5_.1, ...), custom_call_target="tpu_custom_call" | custom-call | bytes 62914560 | tf_op jit(solution)/shard_map/pallas_call | solution.py:872
  119.9 181.8 %shard_map.187 = (f32[128,2048]{1,0:T(8,128)}, f32[128,2048]{1,0:T(8,128)}, bf16[512,2048]{1,0:T(8,128)(2,1)}, bf16[512,1408]{1,0:T(8,128)(2,1)}, bf16[512,2816]...) custom-call(bf16[512,2048]{1,0:T(8,128)(2,1)} %get-tuple-element.41., ...), custom_call_target="tpu_custom_call" | custom-call | flops 16911433728 | bytes 62914560 | tf_op jit(solution)/shard_map/pallas_call | solution.py:1344
  301.7 0.7 slice.6
  302.4 5.0 convolution_convert_fusion.refs_13_
  307.4 109.1 %shard_map.188 = (f32[128,2048]{1,0:T(8,128)}, bf16[512,2048]{1,0:T(8,128)(2,1)}, bf16[4,64,2816]{2,1,0:T(8,128)(2,1)}, f32[64,2048]{1,0:T(8,128)}) custom-call(bf16[512,1408]{1,0:T(8,128)(2,1)} %get-tuple-element.51.refs_0_, bf16[1408,2048]{1,0:T(8,128)(2,1)} %get-tuple-element.49.refs_9_.refs_1_, bf16[512,2048]{1,0:T(8,128)(2,1)} %get-tuple-element.52.refs_2_, ...), custom_call_target="tpu_custom_call" | custom-call | flops 2952790016 | bytes 62914560 | tf_op jit(solution)/shard_map/pallas_call | solution.py:1548
  416.5 5.4 %collective-permute-start = (f32[64,2048]{1,0:T(8,128)}, f32[64,2048]{1,0:T(8,128)}, u32[]{:S(2)}, u32[]{:S(2)}) collective-permute-start(f32[64,2048]{1,0:T(8,128)} %get-tuple-element.68), channel_id=1, source_target_pairs={{0,0},{1,8},{2,16},{3,24},{4,1},{5,9},{6,17},{7,25},{8,2},{9,10},{... | collective-permute-start | bytes 1572872 | tf_op jit(solution)/shard_map/ppermute | solution.py:128
  421.9 0.0 copy-start
  421.9 0.0 copy-start.5
  421.9 0.0 copy-start.6
  421.9 0.0 copy-start.7
  421.9 79.9 %shard_map.189 = (f32[128,2048]{1,0:T(8,128)}, f32[64,2048]{1,0:T(8,128)}, f32[64,2048]{1,0:T(8,128)}, f32[64,2048]{1,0:T(8,128)}, f32[64,2048]{1,0:T(8,128)}, /*index=5*/f32[64,5632]{1,0:T(8,128)}, f32[64,5632]{1,0:T(8,128)}) custom-call(bf16[512,2048]{1,0:T(8,128)(2,1)} %get-tuple-element.61.refs_0_, bf16[2048,2048]{1,0:T(8,128)(2,1)} %get-tuple-element.42.refs_1_, ...), custom_call_target="tpu_custom_call" | custom-call | flops 4294967296 | bytes 62914560 | tf_op jit(solution)/shard_map/pallas_call | solution.py:1621
  501.9 0.0 copy-start.1
  501.9 0.0 copy-done
  501.9 1.6 fusion
  503.5 0.0 copy-done.5
  503.5 0.0 copy-done.6
  503.5 0.0 copy-done.7
  503.5 0.0 copy-done.1
  503.5 0.0 copy-start.11
  503.5 0.0 copy-start.10
  503.5 1.5 fusion.4
  505.0 0.0 copy-start.9
  505.0 0.0 copy-start.8
  505.0 0.0 collective-permute-done
  505.0 0.0 copy-done.11
  505.0 0.8 copy.29
  505.8 0.0 copy-done.10
  505.8 0.0 copy-start.4
  505.8 0.8 copy.30
  506.6 0.0 copy-done.9
  506.6 0.8 copy.31
  507.4 0.0 copy-done.8
  507.4 0.8 copy.32
  508.2 0.0 copy-start.3
  508.2 2.0 copy.33
  510.2 0.0 copy-done.4
  510.2 1.1 copy.34
  511.3 0.0 copy-done.3
  511.3 0.0 copy-start.2
  511.3 1.1 copy.35
  512.4 0.8 copy-done.2
  513.2 1.1 copy.36
  (2 shorter events, 0.0 us)
Async XLA Ops:
  416.5 88.5 %collective-permute-start = (f32[64,2048]{1,0:T(8,128)}, f32[64,2048]{1,0:T(8,128)}, u32[]{:S(2)}, u32[]{:S(2)}) collective-permute-start(f32[64,2048]{1,0:T(8,128)} %get-tuple-element.68), channel_id=1, source_target_pairs={{0,0},{1,8},{2,16},{3,24},{4,1},{5,9},{6,17},{7,25},{8,2},{9,10},{... | collective-permute-start | bytes 1572872 | tf_op jit(solution)/shard_map/ppermute | solution.py:128
  421.9 80.0 %copy-start = (bf16[128,2048]{1,0:T(8,128)(2,1)S(1)}, bf16[128,2048]{1,0:T(8,128)(2,1)}, u32[]{:S(2)}) copy-start(bf16[128,2048]{1,0:T(8,128)(2,1)} %refs_5_.1) | copy-start | bytes 1572868
  421.9 81.5 %copy-start.5 = (f32[128,2048]{1,0:T(8,128)S(1)}, f32[128,2048]{1,0:T(8,128)}, u32[]{:S(2)}) copy-start(f32[128,2048]{1,0:T(8,128)} %get-tuple-element.50) | copy-start | bytes 3145732
  421.9 81.6 %copy-start.6 = (f32[128,2048]{1,0:T(8,128)S(1)}, f32[128,2048]{1,0:T(8,128)}, u32[]{:S(2)}) copy-start(f32[128,2048]{1,0:T(8,128)} %get-tuple-element.60) | copy-start | bytes 3145732
  421.9 81.6 %copy-start.7 = (f32[128,2048]{1,0:T(8,128)S(1)}, f32[128,2048]{1,0:T(8,128)}, u32[]{:S(2)}) copy-start(f32[128,2048]{1,0:T(8,128)} %get-tuple-element.59) | copy-start | bytes 3145732
  501.9 1.6 copy-start.1
  503.5 1.5 copy-start.11
  503.5 2.3 copy-start.10
  505.0 1.6 copy-start.9
  505.0 2.4 copy-start.8
  505.8 4.4 copy-start.4
  508.2 3.1 copy-start.3
  511.3 1.9 copy-start.2
